TPU v7x, 256 devices: a whole 4x4x8 slice. The times are simulated.
256 devices in a mesh: rep: 32 (over z, x_hi, core), fsdp: 8 (over y, x_lo).
Axes of the slice: x: 4 (x_hi: 2, x_lo: 2; x = x_hi * 2 + x_lo), y: 4, z: 8, core: 2. Of those that a mesh axis runs over, the one named last changes fastest.
Arguments:
- tokens: bfloat16 [65536, 4096], P(('rep', 'fsdp')), may hold values from -6 to 6
- cotangent: bfloat16 [65536, 1024], P(('rep', 'fsdp')), may hold values from -0.29882812 to 0.29882812
- weight: bfloat16 [4096, 1024], P('fsdp'), may hold values from -0.09375 to 0.09375
- momentum: float32 [32, 4096, 1024], P('rep', 'fsdp'), may hold values from -6 to 6
- kept_index: int32 [4096, 16, 4], P('fsdp'), may hold values from 0 to 63, as said below
Outputs:
- projected: bfloat16 [65536, 1024], P(('rep', 'fsdp'))
- new_weight: bfloat16 [4096, 1024], P('fsdp')
- new_momentum: float32 [32, 4096, 1024], P('rep', 'fsdp')
Inputs may be any that keep to these rules, and one draw needn't show every extreme that they name: `kept_index`: the four indices of one block are distinct.
All inputs are finite; a program needn't handle non-finite values.
Results may differ from a plain program's by a relative error of at most 0.0049.
Values may be sent and summed in bfloat16 or wider, within the bound.
No kernel may reach another device: no remote copies, remote signals or barrier semaphores. Data moves between devices by JAX's collectives and lax.ppermute only.
A program may use at most 128 MiB of HBM per device.

v0:
```python
import jax
import jax.numpy as jnp
from jax import lax
from jax.sharding import PartitionSpec as P

beta_decay = 0.9
step_rate = 0.5


def dct_pair():
    index = jnp.arange(64, dtype=jnp.float32)
    freq = index[:, None]
    angle = jnp.pi * (2.0 * index[None, :] + 1.0) * freq / 128.0
    factor = jnp.where(
        freq == 0.0, jnp.sqrt(jnp.float32(1.0 / 64.0)), jnp.sqrt(jnp.float32(2.0 / 64.0))
    )
    single = factor * jnp.cos(angle)
    return jnp.kron(jnp.eye(2, dtype=jnp.float32), single)


def kept_lanes(kept_index):
    rows = kept_index.shape[0]
    pairs = kept_index.reshape(rows, kept_index.shape[1] // 2, 2, 4)
    pairs = pairs + (jnp.arange(2, dtype=jnp.int32) * 64)[None, None, :, None]
    return pairs.reshape(rows, kept_index.shape[1] // 2, 8)


def to_spectrum(field, basis):
    rows, width = field.shape
    flat = jnp.dot(
        field.reshape(-1, 128),
        basis.T,
        precision=lax.Precision.HIGHEST,
        preferred_element_type=jnp.float32,
    )
    return flat.reshape(rows, width // 128, 128)


def from_spectrum(spectrum, basis):
    rows, blocks, lanes = spectrum.shape
    flat = jnp.dot(
        spectrum.reshape(-1, 128),
        basis,
        precision=lax.Precision.HIGHEST,
        preferred_element_type=jnp.float32,
    )
    return flat.reshape(rows, blocks * lanes)


def contract_rows(left, right):
    return lax.dot_general(
        left, right, (((0,), (0,)), ((), ())), preferred_element_type=jnp.float32
    )


def body(tokens, cotangent, weight, momentum, kept_index):
    block = tokens
    gradient = lax.psum_scatter(
        contract_rows(block, cotangent), "fsdp", scatter_dimension=0, tiled=True
    )
    basis = dct_pair()
    lanes = kept_lanes(kept_index)
    mask = lanes[..., None] == jnp.arange(128, dtype=jnp.int32)
    moment = beta_decay * momentum[0] + gradient
    spectrum = to_spectrum(moment, basis)
    picked = jnp.sum(jnp.where(mask, spectrum[:, :, None, :], jnp.float32(0.0)), axis=3)
    kept = jnp.sum(jnp.where(mask, picked[..., None], jnp.float32(0.0)), axis=2)
    new_momentum = moment - from_spectrum(kept, basis)
    replicas = lax.axis_size("rep")
    total = lax.psum(kept, "rep")
    delta = from_spectrum(total, basis) / replicas
    new_weight = (weight.astype(jnp.float32) - step_rate * delta).astype(jnp.bfloat16)
    block = tokens
    projected = jnp.dot(
        block,
        lax.all_gather(new_weight, "fsdp", axis=0, tiled=True),
        preferred_element_type=jnp.float32,
    )
    return (projected.astype(jnp.bfloat16), new_weight, new_momentum[None])


def solution(mesh):
    in_specs = (
        P(("rep", "fsdp"), None),
        P(("rep", "fsdp"), None),
        P("fsdp", None),
        P("rep", "fsdp", None),
        P("fsdp", None, None),
    )
    out_specs = (P(("rep", "fsdp"), None), P("fsdp", None), P("rep", "fsdp", None))
    return jax.shard_map(body, mesh=mesh, in_specs=in_specs, out_specs=out_specs, check_vma=False)
```

profile of v0, /device:TPU:1, one launch (start us, length us, event | category | flops | bytes accessed | tf_op | source)
XLA Modules:
  0.0 855.1 jit_solution(15113450681176430520)
XLA Ops:
  7.2 1.5 copy-done
  8.8 9.2 %fusion.4 = f32[4096,1024]{1,0:T(8,128)} fusion(bf16[256,4096]{1,0:T(8,128)(2,1)S(1)} %copy-done, bf16[256,1024]{1,0:T(8,128)(2,1)} %param.6), kind=kOutput, calls=%fused_computation.19 | convolution fusion | flops 2147483648 | bytes 19398656 | tf_op jit(solution)/shard_map/dot_general | solution.py:51
  18.0 0.1 cosine_multiply_fusion
  18.5 0.3 copy-done.4
  19.1 1.9 copy.12
  21.1 329.9 %reduce-scatter.2.cloned.1.call-done = f32[512,1024]{1,0:T(8,128)} async-done(((f32[4096,1024]{1,0:T(8,128)}), f32[512,1024]{1,0:T(8,128)}) %reduce-scatter.2.cloned.1.call-update) | async-done | bytes 2097168 | tf_op jit(solution)/shard_map/reduce_scatter | solution.py:58
  350.9 2.7 fusion.1
  353.6 0.5 copy.18
  354.1 1.8 fusion.5
  355.9 10.5 %select_reduce_fusion.1 = f32[512,8,8]{2,1,0:T(8,128)S(1)} fusion(f32[512,8,128]{2,1,0:T(8,128)S(1)} %fusion.5, s32[512,8,8]{2,1,0:T(8,128)S(1)} %copy-done.1), kind=kLoop, calls=%fused_computation.1 | loop fusion | flops 12550144 | bytes 2359296 | tf_op jit(solution)/shard_map/reduce_sum | solution.py:66
  366.4 11.4 %select_reduce_fusion = f32[512,8,128]{2,1,0:T(8,128)S(1)} fusion(f32[512,8,8]{2,1,0:T(8,128)S(1)} %select_reduce_fusion.1, s32[512,8,8]{2,1,0:T(8,128)S(1)} %copy-done.1), kind=kLoop, calls=%fused_computation | loop fusion | flops 12058624 | bytes 2359296 | tf_op jit(solution)/shard_map/reduce_sum | solution.py:67
  377.8 1.3 copy-done.2
  379.1 3.1 fusion.2
  382.2 0.7 all-reduce.2.cloned.1.call-update
  383.0 0.2 all-gather.2.cloned.1.call-start
  383.2 278.3 %all-reduce.2.cloned.1.call-done = f32[4096,128]{1,0:T(8,128)} async-done(((f32[4096,128]{1,0:T(8,128)}), f32[4096,128]{1,0:T(8,128)}) %all-reduce.2.cloned.1.call-update) | async-done | bytes 2097168 | tf_op jit(solution)/shard_map/psum | solution.py:70
  661.4 4.7 convolution_multiply_fusion
  666.1 2.8 mul.178
  668.9 2.9 subtract_convert_fusion
  671.9 2.7 reshape.127
  674.6 5.1 subtract_bitcast_fusion
  679.7 162.1 %all-gather.2.cloned.1.call-done = bf16[4096,1024]{1,0:T(8,128)(2,1)} async-done(((bf16[512,1024]{1,0:T(8,128)(2,1)}), bf16[4096,1024]{1,0:T(8,128)(2,1)}) %all-gather.2.cloned.1.call-update) | async-done | bytes 8388624 | tf_op jit(solution)/shard_map/all_gather | solution.py:76
  841.8 5.8 fusion
  847.5 1.0 copy.15
  (21 shorter events, 0.8 us)
Async XLA Ops:
  7.2 1.6 copy-start
  7.2 343.7 %reduce-scatter.2.cloned.1.call-start = ((), (), s32[]{:S(2)}) async-start(), calls=%async_computation.1 | async-start | bytes 18874368 | tf_op jit(solution)/shard_map/reduce_scatter | solution.py:58
  17.9 0.9 copy-start.4
  354.1 1.8 copy-start.1
  377.8 1.3 copy-start.2
  382.2 279.2 %all-reduce.2.cloned.1.call-start = ((), (), s32[]{:S(2)}) async-start(), calls=%async_computation.2 | async-start | bytes 4194304 | tf_op jit(solution)/shard_map/psum | solution.py:70
  383.0 458.8 %all-gather.2.cloned.1.call-start = ((), (), s32[]{:S(2)}) async-start(), calls=%async_computation.3 | async-start | bytes 9437184 | tf_op jit(solution)/shard_map/all_gather | solution.py:76
  666.1 2.8 copy-start.3
Sparse Core Ops, SparseCore 0:
  18.1 332.8 reduce-scatter.1
  386.3 275.1 all-reduce.1
  672.0 169.7 all-gather.1
where the time goes:
time: 855 us
  waiting for transfers between devices  771 us (90%)
  other arithmetic  32.8 us (4%)
  matrix products  24.6 us (3%)
  between operations  13.8 us (2%)
  local copies, waits for them, and re-layouts  12.6 us (1%)
    reduce_scatter x1, waiting for transfers between devices, body(): lax.psum_scatter(contract_rows(block, cotangent), 'fsdp', scatter_dimensi...  330 us
    psum x1, waiting for transfers between devices, body(): total = lax.psum(kept, 'rep')  278 us
    all_gather x1, waiting for transfers between devices, body(): lax.all_gather(new_weight, 'fsdp', axis=0, tiled=True)  162 us
  transfers between devices with their start and end apart: 3, of which 3 were waited for; matrix products, arithmetic and copies ran while one was open for 1% of the time, Pallas kernels for 0%

commit v1 on v0

v1 whole, which is shorter than its diff:
```python
import jax
import jax.numpy as jnp
import numpy as np
from jax import lax
from jax.experimental import pallas as pl
from jax.experimental.pallas import tpu as pltpu
from jax.sharding import PartitionSpec as P

beta_decay = 0.9
step_rate = 0.5
ROWS = 512
KV = 1024
TOK = 256
BLOCK = 64
KEEP = 4
HALF = KV // 2
GROUP = 256
STEPS = KV // GROUP
PICKS = KV // BLOCK * KEEP
LANES = 128
PACK = 16
REPS = 32
VMEM_LIMIT = 24 * 1024 * 1024


def dct_group():
    n = np.arange(BLOCK, dtype=np.float64)
    single = np.cos(np.pi * (2.0 * n[None, :] + 1.0) * n[:, None] / (2 * BLOCK))
    single *= np.where(n[:, None] == 0, np.sqrt(1.0 / BLOCK), np.sqrt(2.0 / BLOCK))
    return np.kron(np.eye(GROUP // BLOCK), single).astype(np.float32)


def split_pair(values):
    high = values.astype(jnp.bfloat16)
    return high, (values - high.astype(jnp.float32)).astype(jnp.bfloat16)


def mix(left, right, dims):
    return lax.dot_general(left, right, (dims, ((), ())), preferred_element_type=jnp.float32)


def three_pass(left_pair, right_pair, dims):
    return (
        mix(left_pair[0], right_pair[0], dims)
        + mix(left_pair[0], right_pair[1], dims)
        + mix(left_pair[1], right_pair[0], dims)
    )


def expand_block(index_rows, value_rows, width):
    freq = lax.broadcasted_iota(jnp.int32, (BLOCK, width), 0)
    dense = jnp.zeros((BLOCK, width), jnp.float32)
    for j in range(KEEP):
        dense = jnp.where(index_rows[j] == freq, value_rows[j], dense)
    return dense


def spread_row(tile, row):
    return jnp.broadcast_to(tile[row : row + 1, :], (PACK, LANES)).astype(jnp.bfloat16)


def expand_tile(indices, values, dense, first, cols):
    freq = lax.broadcasted_iota(jnp.int32, (PACK, LANES), 0).astype(jnp.float32)
    for half in range(2):
        at = [spread_row(indices, half * KEEP + j) for j in range(KEEP)]
        have = [spread_row(values, half * KEEP + j) for j in range(KEEP)]
        for part in range(BLOCK // PACK):
            here = (freq + part * PACK).astype(jnp.bfloat16)
            tile = jnp.zeros((PACK, LANES), jnp.bfloat16)
            for j in range(KEEP):
                tile = jnp.where(at[j] == here, have[j], tile)
            start = first + half * BLOCK + part * PACK
            dense[start : start + PACK, cols] = tile


def four_products(cots, toks):
    total = jnp.dot(cots[0][...], toks[0][...], preferred_element_type=jnp.float32)
    for c, t in zip(cots[1:], toks[1:]):
        total += jnp.dot(c[...], t[...], preferred_element_type=jnp.float32)
    return total


def turn_kernel(cot, late_lo, late_hi, out):
    out[...] = cot[...].T


def copy_kernel(where, t0, t1, t2, t3, late, *outs):
    for t, out in zip((t0, t1, t2, t3), outs):
        out[...] = t[...]


def partial_first_kernel(c0, c1, c2, c3, t0, t1, t2, t3, idx, early, out):
    for g in range(HALF // GROUP):
        rows = slice(g * GROUP, (g + 1) * GROUP)
        cots = [c[rows, :] for c in (c0, c1, c2, c3)]
        out[rows, :] = four_products(cots, (t0, t1, t2, t3)).astype(out.dtype)
    out[HALF:, :] = idx[...].astype(jnp.float32).astype(out.dtype)


def partial_second_kernel(c0, c1, c2, c3, t0, t1, t2, t3, out):
    for g in range(HALF // GROUP):
        rows = slice(g * GROUP, (g + 1) * GROUP)
        cots = [c[rows, :] for c in (c0, c1, c2, c3)]
        out[rows, :] = four_products(cots, (t0, t1, t2, t3)).astype(out.dtype)


def own_kernel(a0, a1, a2, a3, b0, b1, b2, b3, t0, t1, t2, t3, mom, out):
    first = pl.program_id(0) < STEPS // 2
    cots = [jnp.where(first, a[...], b[...]) for a, b in zip((a0, a1, a2, a3), (b0, b1, b2, b3))]
    out[...] = four_products(cots, (t0, t1, t2, t3)) + beta_decay * mom[...].T


def received(got_a, got_b):
    first = pl.program_id(0) < STEPS // 2
    return jnp.where(first, got_a[...], got_b[...]).astype(jnp.float32)


def pick_kernel(pre, got_a, got_b, idx, ch, cl, late, picked, tiles):
    moment = pre[...] + received(got_a, got_b)
    spectrum = three_pass((ch[...], cl[...]), split_pair(moment), ((1,), (0,)))
    freq = lax.broadcasted_iota(jnp.int32, (BLOCK, ROWS), 0)
    rows = []
    for b in range(GROUP // BLOCK):
        part = spectrum[b * BLOCK : (b + 1) * BLOCK, :]
        for j in range(KEEP):
            at = idx[b * KEEP + j : b * KEEP + j + 1, :]
            rows.append(jnp.sum(jnp.where(at == freq, part, 0.0), axis=0, keepdims=True))
    values = jnp.concatenate(rows, axis=0)
    picked[...] = values
    for t in range(GROUP // BLOCK * KEEP // 8):
        for q in range(ROWS // LANES):
            tile = values[t * 8 : (t + 1) * 8, q * LANES : (q + 1) * LANES]
            tiles[t * (ROWS // LANES) + q] = tile.astype(tiles.dtype)


def share_kernel(spread, out):
    total = jnp.sum(spread[...].astype(jnp.float32), axis=0, keepdims=True)
    out[...] = jnp.broadcast_to(total, out.shape).astype(out.dtype)


def residual_kernel(pre, got_a, got_b, picked, idx, ch, cl, out):
    parts = []
    for b in range(GROUP // BLOCK):
        rows = [slice(b * KEEP + j, b * KEEP + j + 1) for j in range(KEEP)]
        parts.append(expand_block([idx[r, :] for r in rows], [picked[r, :] for r in rows], ROWS))
    kept = jnp.concatenate(parts, axis=0)
    back = three_pass((ch[...], cl[...]), split_pair(kept), ((0,), (0,)))
    out[...] = (pre[...] + received(got_a, got_b) - back).T


def base_kernel(where, o0, o1, o2, o3, p0, p1, p2, p3, w_own, w_peer, idx, got_a, *outs):
    mine = idx[...].astype(jnp.float32).astype(jnp.bfloat16)
    theirs = got_a[HALF:, :]
    first = where[0] == 0
    left, right = jnp.where(first, mine, theirs), jnp.where(first, theirs, mine)
    for own, peer, out in zip((o0, o1, o2, o3), (p0, p1, p2, p3), outs):
        total = jnp.dot(own[...], w_own[...], preferred_element_type=jnp.float32)
        total += jnp.dot(peer[...], w_peer[...], preferred_element_type=jnp.float32)
        out[:TOK, :] = total.astype(out.dtype)
        out[TOK:, :ROWS] = left
        out[TOK:, ROWS:] = right


def forward_kernel(where, tok, own, hi, far, lo, tot, ch, cl, out, dense, mixed):
    step = pl.program_id(0)
    tail = slice(TOK, TOK + PICKS)
    near = jnp.where(step == 0, own[tail, :], hi[tail, :])
    away = jnp.where(step == 2, far[tail, :], lo[tail, :])
    pairs = jnp.where(step < 2, near, away).astype(jnp.float32)

    @pl.when(step == 0)
    def _():
        mixed[...] = jnp.zeros_like(mixed)

    for g in range(STEPS):
        for t in range(2 * g, 2 * g + 2):
            for f in range(2):
                for q in range(ROWS // LANES):
                    cols = slice(f * ROWS + q * LANES, f * ROWS + (q + 1) * LANES)
                    values = tot[t * (ROWS // LANES) + q, f].astype(jnp.float32)
                    expand_tile(pairs[t * 8 : (t + 1) * 8, cols], values, dense, t * 2 * BLOCK, cols)
        span = slice(g * GROUP, (g + 1) * GROUP)
        mixed[:, span] += mix(tok[...], dense[span, :], ((1,), (1,)))

    @pl.when(step == 3)
    def _():
        for g in range(STEPS):
            span = slice(g * GROUP, (g + 1) * GROUP)
            delta = three_pass(split_pair(mixed[:, span]), (ch[...], cl[...]), ((1,), (0,)))
            base = own[:TOK, span].astype(jnp.float32) + hi[:TOK, span].astype(jnp.float32)
            base += far[:TOK, span].astype(jnp.float32) + lo[:TOK, span].astype(jnp.float32)
            out[:, span] = (base - (step_rate / REPS) * delta).astype(out.dtype)


def weight_kernel(where, weight, tot, idx, ch, cl, out, dense):
    indices = idx[...].astype(jnp.float32)
    for g in range(STEPS):
        for t in range(2 * g, 2 * g + 2):
            for q in range(ROWS // LANES):
                cols = slice(q * LANES, (q + 1) * LANES)
                values = tot[t * (ROWS // LANES) + q, 0].astype(jnp.float32)
                expand_tile(indices[t * 8 : (t + 1) * 8, cols], values, dense, t * 2 * BLOCK, cols)
        span = slice(g * GROUP, (g + 1) * GROUP)
        turned = dense[span, :].T
        delta = mix(turned, ch[...], ((1,), (0,))) + mix(turned, cl[...], ((1,), (0,)))
        out[:, span] = (weight[:, span].astype(jnp.float32) - (step_rate / REPS) * delta).astype(out.dtype)


def params():
    return pltpu.CompilerParams(vmem_limit_bytes=VMEM_LIMIT)


def cost(flops, mib):
    return pl.CostEstimate(flops=int(flops), bytes_accessed=int(mib * (1 << 20)), transcendentals=0)


def whole(*shape):
    return pl.BlockSpec(shape, lambda c, *_: (0,) * len(shape))


def by_row(rows, width):
    return pl.BlockSpec((rows, width), lambda c: (c, 0))


def by_col(rows, width):
    return pl.BlockSpec((rows, width), lambda c: (0, c))


def first_half(rows, width):
    return pl.BlockSpec((rows, width), lambda c: (jnp.minimum(c, STEPS // 2 - 1), 0))


def second_half(rows, width):
    return pl.BlockSpec((rows, width), lambda c: (jnp.maximum(c - STEPS // 2, 0), 0))


AFTER = pl.BlockSpec(memory_space=pl.ANY)
BASIS = [whole(GROUP, GROUP)] * 2
GOT = [first_half(GROUP, ROWS), second_half(GROUP, ROWS)]
BF16, F32 = jnp.bfloat16, jnp.float32


def body(tokens, cotangent, weight, momentum, kept_index):
    basis = dct_group()
    high = jnp.asarray(basis).astype(BF16)
    low = (jnp.asarray(basis) - high.astype(F32)).astype(BF16)
    fsdp = lax.axis_index("fsdp").astype(jnp.int32)
    y, side = fsdp >> 1, fsdp & 1
    other = 1 - side
    index_t = jnp.transpose(kept_index, (1, 2, 0)).reshape(PICKS, ROWS)

    plus = [(i, (i + 2) % 8) for i in range(8)]
    minus = [(i, (i + 6) % 8) for i in range(8)]
    across = [(i, (i + 4) % 8) for i in range(8)]
    swap = [(i, i ^ 1) for i in range(8)]

    def up(x):
        return lax.ppermute(x, "fsdp", plus)

    def down(x):
        return lax.ppermute(x, "fsdp", minus)

    def piece(distance, which):
        start = (((y + distance) & 3) * 2 + which) * ROWS
        return lax.dynamic_slice(tokens, (0, start), (TOK, ROWS))

    weight_peer = lax.ppermute(weight, "fsdp", swap)

    cot_a = cotangent[:, :HALF].T
    a_lo = up(cot_a)
    peer_step = down(piece(2, other))
    a_hi = down(cot_a)
    peer_lo = up(piece(1, other))
    peer_hi = down(piece(3, other))
    a_far = up(a_lo)
    peer_far = down(peer_step)
    cots_a = (cot_a, a_hi, a_far, a_lo)
    peers = (piece(0, other), peer_hi, peer_far, peer_lo)

    cot_b = pl.pallas_call(
        turn_kernel,
        grid=(1,),
        in_specs=[pl.BlockSpec((TOK, HALF), lambda c: (0, 1)), AFTER, AFTER],
        out_specs=whole(HALF, TOK),
        out_shape=jax.ShapeDtypeStruct((HALF, TOK), BF16),
        compiler_params=params(),
        cost_estimate=cost(0, 1),
    )(cotangent, a_lo, a_hi)
    b_lo = up(cot_b)
    b_hi = down(cot_b)
    b_far = down(b_hi)
    cots_b = (cot_b, b_hi, b_far, b_lo)

    own_0, own_1, own_2, own_3 = pl.pallas_call(
        copy_kernel,
        grid_spec=pltpu.PrefetchScalarGridSpec(
            num_scalar_prefetch=1,
            grid=(1,),
            in_specs=[
                pl.BlockSpec((TOK, ROWS), lambda c, s, d=d: (0, (s[0] + 2 * d) & 7)) for d in range(4)
            ]
            + [AFTER],
            out_specs=[whole(TOK, ROWS)] * 4,
        ),
        out_shape=[jax.ShapeDtypeStruct((TOK, ROWS), BF16)] * 4,
        compiler_params=params(),
        cost_estimate=cost(0, 2),
    )(fsdp.reshape(1), tokens, tokens, tokens, tokens, b_lo)
    owns = (own_0, down(own_3), up(up(own_2)), up(own_1))

    partial_a = pl.pallas_call(
        partial_first_kernel,
        grid=(1,),
        in_specs=[whole(HALF, TOK)] * 4 + [whole(TOK, ROWS)] * 4 + [whole(PICKS, ROWS), AFTER],
        out_specs=whole(HALF + PICKS, ROWS),
        out_shape=jax.ShapeDtypeStruct((HALF + PICKS, ROWS), BF16),
        compiler_params=params(),
        cost_estimate=cost(KV * KV * ROWS, 3),
    )(*cots_a, *peers, index_t, weight_peer)
    got_a = lax.ppermute(partial_a, "fsdp", swap)
    partial_b = pl.pallas_call(
        partial_second_kernel,
        grid=(1,),
        in_specs=[whole(HALF, TOK)] * 4 + [whole(TOK, ROWS)] * 4,
        out_specs=whole(HALF, ROWS),
        out_shape=jax.ShapeDtypeStruct((HALF, ROWS), BF16),
        compiler_params=params(),
        cost_estimate=cost(KV * KV * ROWS, 3),
    )(*cots_b, *peers)
    got_b = lax.ppermute(partial_b, "fsdp", swap)

    pre = pl.pallas_call(
        own_kernel,
        grid=(STEPS,),
        in_specs=[first_half(GROUP, TOK)] * 4
        + [second_half(GROUP, TOK)] * 4
        + [whole(TOK, ROWS)] * 4
        + [by_col(ROWS, GROUP)],
        out_specs=by_row(GROUP, ROWS),
        out_shape=jax.ShapeDtypeStruct((KV, ROWS), F32),
        compiler_params=params(),
        cost_estimate=cost(2 * KV * KV * ROWS, 7),
    )(*cots_a, *cots_b, *owns, momentum[0])

    based = pl.pallas_call(
        base_kernel,
        grid_spec=pltpu.PrefetchScalarGridSpec(
            num_scalar_prefetch=1,
            grid=(1,),
            in_specs=[whole(TOK, ROWS)] * 8
            + [whole(ROWS, KV)] * 2
            + [whole(PICKS, ROWS), whole(HALF + PICKS, ROWS)],
            out_specs=[whole(TOK + PICKS, KV)] * 4,
        ),
        out_shape=[jax.ShapeDtypeStruct((TOK + PICKS, KV), BF16)] * 4,
        compiler_params=params(),
        cost_estimate=cost(4 * KV * KV * ROWS, 7),
    )(side.reshape(1), *owns, *peers, weight, weight_peer, index_t, got_a)
    base_lo = up(based[1])
    base_far = lax.ppermute(based[2], "fsdp", across)
    base_hi = down(based[3])

    picked, tiles = pl.pallas_call(
        pick_kernel,
        grid=(STEPS,),
        in_specs=[by_row(GROUP, ROWS)] + GOT + [by_row(PICKS // STEPS, ROWS)] + BASIS + [AFTER],
        out_specs=[
            by_row(PICKS // STEPS, ROWS),
            pl.BlockSpec((REPS // STEPS, 8, LANES), lambda c: (c, 0, 0)),
        ],
        out_shape=[
            jax.ShapeDtypeStruct((PICKS, ROWS), F32),
            jax.ShapeDtypeStruct((REPS, 8, LANES), BF16),
        ],
        compiler_params=params(),
        cost_estimate=cost(6 * KV * GROUP * ROWS, 4),
    )(pre, got_a, got_b, index_t, high, low, based[0])

    spread = lax.all_to_all(tiles, "rep", 0, 0)
    copies = pl.pallas_call(
        share_kernel,
        grid=(1,),
        in_specs=[whole(REPS, 8, LANES)],
        out_specs=whole(REPS * 8, 8, LANES),
        out_shape=jax.ShapeDtypeStruct((REPS * 8, 8, LANES), BF16),
        compiler_params=params(),
        cost_estimate=cost(0, 1),
    )(spread)
    totals = lax.all_to_all(copies, ("rep", "fsdp"), 0, 0).reshape(REPS, 8, 8, LANES)

    new_momentum = pl.pallas_call(
        residual_kernel,
        grid=(STEPS,),
        in_specs=[by_row(GROUP, ROWS)] + GOT + [by_row(PICKS // STEPS, ROWS)] * 2 + BASIS,
        out_specs=by_col(ROWS, GROUP),
        out_shape=jax.ShapeDtypeStruct((ROWS, KV), F32),
        compiler_params=params(),
        cost_estimate=cost(6 * KV * GROUP * ROWS, 6),
    )(pre, got_a, got_b, picked, index_t, high, low)

    projected = pl.pallas_call(
        forward_kernel,
        grid_spec=pltpu.PrefetchScalarGridSpec(
            num_scalar_prefetch=1,
            grid=(4,),
            in_specs=[pl.BlockSpec((TOK, 2 * ROWS), lambda c, s: (0, (s[0] + c) & 3))]
            + [whole(TOK + PICKS, KV)] * 4
            + [pl.BlockSpec((REPS, 2, 8, LANES), lambda c, s: (0, (s[0] + c) & 3, 0, 0))]
            + BASIS,
            out_specs=whole(TOK, KV),
            scratch_shapes=[pltpu.VMEM((KV, 2 * ROWS), BF16), pltpu.VMEM((TOK, KV), F32)],
        ),
        out_shape=jax.ShapeDtypeStruct((TOK, KV), BF16),
        compiler_params=params(),
        cost_estimate=cost(8 * KV * KV * ROWS, 8),
    )(y.reshape(1), tokens, based[0], base_hi, base_far, base_lo, totals, high, low)

    new_weight = pl.pallas_call(
        weight_kernel,
        grid_spec=pltpu.PrefetchScalarGridSpec(
            num_scalar_prefetch=1,
            grid=(1,),
            in_specs=[
                whole(ROWS, KV),
                pl.BlockSpec((REPS, 1, 8, LANES), lambda c, s: (0, s[0], 0, 0)),
                whole(PICKS, ROWS),
            ]
            + BASIS,
            out_specs=whole(ROWS, KV),
            scratch_shapes=[pltpu.VMEM((KV, ROWS), BF16)],
        ),
        out_shape=jax.ShapeDtypeStruct((ROWS, KV), BF16),
        compiler_params=params(),
        cost_estimate=cost(4 * KV * GROUP * ROWS, 3),
    )(fsdp.reshape(1), weight, totals, index_t, high, low)
    return (projected, new_weight, new_momentum[None])


def solution(mesh):
    in_specs = (
        P(("rep", "fsdp"), None),
        P(("rep", "fsdp"), None),
        P("fsdp", None),
        P("rep", "fsdp", None),
        P("fsdp", None, None),
    )
    out_specs = (P(("rep", "fsdp"), None), P("fsdp", None), P("rep", "fsdp", None))
    return jax.shard_map(body, mesh=mesh, in_specs=in_specs, out_specs=out_specs, check_vma=False)
```

time: 855 us -> 145 us (0.17)
  waiting for transfers between devices: 771 us -> 44.8 us
  other arithmetic: 32.8 us -> 0 us
  Pallas kernels: 0 us -> 31 us
  blocking collectives: 0 us -> 27.4 us
  starting transfers between devices: 0.26 us -> 26.3 us
  matrix products: 24.6 us -> 0 us
  between operations: 13.8 us -> 1 us
    reduce_scatter x1 -> x0, waiting for transfers between devices: 330 us -> none  [body(): lax.psum_scatter(contract_rows(block, cotangent), 'fsdp', scatter_dimensi...]
    psum x1 -> x0, waiting for transfers between devices: 278 us -> none  [body(): total = lax.psum(kept, 'rep')]
    all_gather x1 -> x0, waiting for transfers between devices: 162 us -> none  [body(): lax.all_gather(new_weight, 'fsdp', axis=0, tiled=True)]
    ppermute x0 -> x20, waiting for transfers between devices: none -> 35.2 us  [the longest x8 27.5 us: up(): return lax.ppermute(x, 'fsdp', plus)]
    pallas_call x0 -> x11, Pallas kernels: none -> 31 us  [the longest x1 9.99 us: body(): pl.pallas_call(forward_kernel, grid_spec=pltpu.PrefetchScalarGridSpec(num...]
    all_to_all x0 -> x1, blocking collectives: none -> 27.4 us  [body(): spread = lax.all_to_all(tiles, 'rep', 0, 0)]
    dot_general x5 -> x0, matrix products: 24.6 us -> none  [the longest x1 9.16 us: contract_rows(): lax.dot_general(left, right, (((0,), (0,)), ((), ())), preferred_element_...]
    reduce_sum x2 -> x0, other arithmetic: 21.9 us -> none  [the longest x1 11.4 us: body(): kept = jnp.sum(jnp.where(mask, picked[..., None], jnp.float32(0.0)), axis=2)]
  transfers between devices with their start and end apart: 3 -> 21, of which waited for: 3 -> 11; matrix products, arithmetic and copies ran while one was open for 1% -> 3% of each run, Pallas kernels for 0% -> 12%
where the time goes in v1:
time: 145 us; the launch traced here: 144 us
  waiting for transfers between devices  44.8 us (31%)
  Pallas kernels  31 us (21%)
  blocking collectives  27.4 us (19%)
  starting transfers between devices  26.3 us (18%)
  local copies, waits for them, and re-layouts  13.9 us (10%)
    ppermute x8, waiting for transfers between devices, up(): return lax.ppermute(x, 'fsdp', plus)  27.5 us
    all_to_all x1, blocking collectives, body(): spread = lax.all_to_all(tiles, 'rep', 0, 0)  27.4 us
    ppermute x8, starting transfers between devices, down(): return lax.ppermute(x, 'fsdp', minus)  13.8 us
    pallas_call x1, Pallas kernels, body(): pl.pallas_call(forward_kernel, grid_spec=pltpu.PrefetchScalarGridSpec(num...  9.99 us
    unnamed x65, local copies, waits for them, and re-layouts  9.92 us
    all_to_all x1, waiting for transfers between devices, body(): lax.all_to_all(copies, ('rep', 'fsdp'), 0, 0).reshape(REPS, 8, 8, LANES)  9.56 us
    ppermute x8, waiting for transfers between devices, down(): return lax.ppermute(x, 'fsdp', minus)  6.2 us
    all_to_all x1, starting transfers between devices, body(): lax.all_to_all(copies, ('rep', 'fsdp'), 0, 0).reshape(REPS, 8, 8, LANES)  5.43 us
  transfers between devices with their start and end apart: 21, of which 11 were waited for; matrix products, arithmetic and copies ran while one was open for 3% of the time, Pallas kernels for 12%

profile of v1, /device:TPU:1, one launch (start us, length us, event | category | flops | bytes accessed | tf_op | source)
XLA Modules:
  0.0 144.2 jit_solution(14149499754554850188)
XLA Ops:
  0.6 2.1 %collective-permute-start.11 = (bf16[512,1024]{1,0:T(8,128)(2,1)}, bf16[512,1024]{1,0:T(8,128)(2,1)}, u32[]{:S(2)}, u32[]{:S(2)}) collective-permute-start(bf16[512,1024]{1,0:T(8,128)(2,1)} %weight.1), channel_id=1, source_target_pairs={{0,1},{1,0},{2,3},{3,2},{4,5},{5,4},{6,7},{7,6},{8,9},{9,8},{10,11... | collective-permute-start | bytes 3145736 | tf_op jit(solution)/shard_map/ppermute | solution.py:267
  3.9 2.8 %collective-permute-start.1 = (bf16[512,256]{1,0:T(8,128)(2,1)S(1)}, bf16[512,256]{1,0:T(8,128)(2,1)S(1)}, u32[]{:S(2)}, u32[]{:S(2)}) collective-permute-start(bf16[512,256]{1,0:T(8,128)(2,1)S(1)} %bitcast.8), channel_id=1, source_target_pairs={{0,6},{1,7},{2,0},{3,1},{4,2},{5,3},{6,4},{7,5},{8,14},{9,15},{10,... | collective-permute-start | bytes 786440 | tf_op jit(solution)/shard_map/ppermute | solution.py:261
  6.7 2.0 %constant_dynamic-slice_fusion = (bf16[256,512]{1,0:T(8,128)(2,1)S(1)}, bf16[256,512]{1,0:T(8,128)(2,1)S(1)}, bf16[256,512]{1,0:T(8,128)(2,1)}, bf16[256,512]{1,0:T(8,128)(2,1)S(1)}) fusion(bf16[256,4096]{1,0:T(8,128)(2,1)} %tok.1, s32[]{:T(128)S(6)} %select_n.15, s32[]{:T(128)S(6)} %select_n.14, s32[]{:T(128)S(6)} %select_n.13, s32[]{:T(128)S(6)} %select_n.12), kind=kLoop, calls=%fused_computation | loop fusion | bytes 2097168 | tf_op jit(solution)/shard_map/dynamic_slice | solution.py:265
  8.8 2.7 %collective-permute-start.8 = (bf16[256,512]{1,0:T(8,128)(2,1)S(1)}, bf16[256,512]{1,0:T(8,128)(2,1)}, u32[]{:S(2)}, u32[]{:S(2)}) collective-permute-start(bf16[256,512]{1,0:T(8,128)(2,1)S(1)} %get-tuple-element.24), channel_id=1, source_target_pairs={{0,6},{1,7},{2,0},{3,1},{4,2},{5,3},{6,4},{7,5},{8,14},{9,15},{10,... | collective-permute-start | bytes 786440 | tf_op jit(solution)/shard_map/ppermute | solution.py:261
  11.4 3.0 %collective-permute-done.late_lo.c3.a3 = bf16[512,256]{1,0:T(8,128)(2,1)S(1)} collective-permute-done((bf16[512,256]{1,0:T(8,128)(2,1)S(1)}, bf16[512,256]{1,0:T(8,128)(2,1)S(1)}, u32[]{:S(2)}, u32[]{:S(2)}) %collective-permute-start) | collective-permute-done | bytes 262176 | tf_op jit(solution)/shard_map/ppermute | solution.py:258
  14.7 2.7 %collective-permute-start.7 = (bf16[256,512]{1,0:T(8,128)(2,1)}, bf16[256,512]{1,0:T(8,128)(2,1)}, u32[]{:S(2)}, u32[]{:S(2)}) collective-permute-start(bf16[256,512]{1,0:T(8,128)(2,1)} %get-tuple-element.25), channel_id=1, source_target_pairs={{0,6},{1,7},{2,0},{3,1},{4,2},{5,3},{6,4},{7,5},{8,14},{9,15},{10,... | collective-permute-start | bytes 786440 | tf_op jit(solution)/shard_map/ppermute | solution.py:261
  17.4 2.7 %collective-permute-done.10.t3.p3 = bf16[256,512]{1,0:T(8,128)(2,1)S(1)} collective-permute-done((bf16[256,512]{1,0:T(8,128)(2,1)S(1)}, bf16[256,512]{1,0:T(8,128)(2,1)S(1)}, u32[]{:S(2)}, u32[]{:S(2)}) %collective-permute-start.10) | collective-permute-done | bytes 262176 | tf_op jit(solution)/shard_map/ppermute | solution.py:258
  22.3 3.4 %collective-permute-done.2.late.b3.c3 = bf16[512,256]{1,0:T(8,128)(2,1)S(1)} collective-permute-done((bf16[512,256]{1,0:T(8,128)(2,1)S(1)}, bf16[512,256]{1,0:T(8,128)(2,1)S(1)}, u32[]{:S(2)}, u32[]{:S(2)}) %collective-permute-start.2) | collective-permute-done | bytes 262176 | tf_op jit(solution)/shard_map/ppermute | solution.py:258
  29.6 1.9 %collective-permute-done.12.c2.a2 = bf16[512,256]{1,0:T(8,128)(2,1)} collective-permute-done((bf16[512,256]{1,0:T(8,128)(2,1)S(1)}, bf16[512,256]{1,0:T(8,128)(2,1)}, u32[]{:S(2)}, u32[]{:S(2)}) %collective-permute-start.12) | collective-permute-done | bytes 262176 | tf_op jit(solution)/shard_map/ppermute | solution.py:258
  31.4 2.6 %collective-permute-done.9.t2.p2 = bf16[256,512]{1,0:T(8,128)(2,1)} collective-permute-done((bf16[256,512]{1,0:T(8,128)(2,1)}, bf16[256,512]{1,0:T(8,128)(2,1)}, u32[]{:S(2)}, u32[]{:S(2)}) %collective-permute-start.9) | collective-permute-done | bytes 262176 | tf_op jit(solution)/shard_map/ppermute | solution.py:261
  34.1 2.0 %shard_map.87 = bf16[576,512]{1,0:T(8,128)(2,1)S(1)} custom-call(bf16[512,256]{1,0:T(8,128)(2,1)S(1)} %bitcast.10, bf16[512,256]{1,0:T(8,128)(2,1)S(1)} %collective-permute-done.1.late_hi.c1.a1, bf16[512,256]{1,0:T(8,128)(2,1)} %collective-permute-done.12.c2.a2, bf16[512,256]{1,0:T(8,128)(2,1)S(1)} %collective-permute-done.late_lo.c3.a3, ...), custom_call_target="tpu_custom_call" | custom-call | flops 536870912 | bytes 3145728 | tf_op jit(solution)/shard_map/pallas_call | solution.py:311
  42.7 2.1 %collective-permute-done.3.o1.t1 = bf16[256,512]{1,0:T(8,128)(2,1)S(1)} collective-permute-done((bf16[256,512]{1,0:T(8,128)(2,1)S(1)}, bf16[256,512]{1,0:T(8,128)(2,1)S(1)}, u32[]{:S(2)}, u32[]{:S(2)}) %collective-permute-start.3) | collective-permute-done | bytes 262176 | tf_op jit(solution)/shard_map/ppermute | solution.py:261
  44.7 2.5 %collective-permute-done.5.o2.t2 = bf16[256,512]{1,0:T(8,128)(2,1)S(1)} collective-permute-done((bf16[256,512]{1,0:T(8,128)(2,1)S(1)}, bf16[256,512]{1,0:T(8,128)(2,1)S(1)}, u32[]{:S(2)}, u32[]{:S(2)}) %collective-permute-start.5) | collective-permute-done | bytes 262176 | tf_op jit(solution)/shard_map/ppermute | solution.py:258
  47.3 3.5 %shard_map.89.pre = f32[1024,512]{1,0:T(8,128)S(1)} custom-call(bf16[512,256]{1,0:T(8,128)(2,1)S(1)} %bitcast.11, bf16[512,256]{1,0:T(8,128)(2,1)S(1)} %copy-done.4, bf16[512,256]{1,0:T(8,128)(2,1)} %collective-permute-done.12.c2.a2, bf16[512,256]{1,0:T(8,128)(2,1)S(1)} %copy-done.6, bf16[512,256]{1,0:T(8,128)(2,1)S(1)} %shard_map.85.b0.c0, ...), custom_call_target="tpu_custom_call" | custom-call | flops 1073741824 | bytes 7340032 | tf_op jit(solution)/shard_map/pallas_call | solution.py:332
  50.9 4.6 %shard_map.88 = (bf16[320,1024]{1,0:T(8,128)(2,1)S(1)}, bf16[320,1024]{1,0:T(8,128)(2,1)S(1)}, bf16[320,1024]{1,0:T(8,128)(2,1)S(1)}, bf16[320,1024]{1,0:T(8,128)(2,1)S(1)}) custom-call(s32[1]{0:T(128)} %bitcast.1.where, bf16[256,512]{1,0:T(8,128)(2,1)S(1)} %get-tuple-element.13.o0.t0, bf16[256,512]{1,0:T(8,128)(2,1)S(1)} %collective-permute-done.3.o1.t1, ...), custom_call_target="tpu_custom_call" | custom-call | flops 2147483648 | bytes 7340032 | tf_op jit(solution)/shard_map/pallas_call | solution.py:345
  57.1 2.9 %shard_map.91 = (f32[64,512]{1,0:T(8,128)S(1)}, bf16[32,8,128]{2,1,0:T(8,128)(2,1)S(1)}) custom-call(f32[1024,512]{1,0:T(8,128)S(1)} %shard_map.89.pre, bf16[576,512]{1,0:T(8,128)(2,1)S(1)} %collective-permute-done.13.got_a, bf16[512,512]{1,0:T(8,128)(2,1)S(1)} %collective-permute-done.19.got_b, s32[64,512]{1,0:T(8,128)S(1)} %reshape.25.idx, ...), custom_call_target="tpu_custom_call" | custom-call | flops 805306368 | bytes 4194304 | tf_op jit(solution)/shard_map/pallas_call | solution.py:363
  60.7 27.4 %all_to_all.10.spread = bf16[32,8,128]{2,1,0:T(8,128)(2,1)S(1)} all-to-all(bf16[32,8,128]{2,1,0:T(8,128)(2,1)S(1)} %get-tuple-element.21), channel_id=1, replica_groups=mesh['rep'=32,'fsdp'=8] {'rep'}, dimensions={0} | all-to-all | bytes 131072 | tf_op jit(solution)/shard_map/all_to_all | solution.py:379
  88.9 5.4 %all-to-all-start.1 = ((bf16[256,8,128]{2,1,0:T(8,128)(2,1)}), bf16[256,8,128]{2,1,0:T(8,128)(2,1)S(1)}, u32[]{:S(2)}, u32[]{:S(2)}) async-start(bf16[256,8,128]{2,1,0:T(8,128)(2,1)} %copy-done.13), calls=%async_computation.1 | async-start | bytes 1048576 | tf_op jit(solution)/shard_map/all_to_all | solution.py:389
  94.4 2.9 %collective-permute-start.14 = (bf16[320,1024]{1,0:T(8,128)(2,1)}, bf16[320,1024]{1,0:T(8,128)(2,1)}, u32[]{:S(2)}, u32[]{:S(2)}) collective-permute-start(bf16[320,1024]{1,0:T(8,128)(2,1)} %copy-done.31), channel_id=1, source_target_pairs={{0,6},{1,7},{2,0},{3,1},{4,2},{5,3},{6,4},{7,5},{8,14},{9,15},{10,... | collective-permute-start | bytes 1966088 | tf_op jit(solution)/shard_map/ppermute | solution.py:261
  102.8 3.7 %shard_map.95 = f32[512,1024]{1,0:T(8,128)} custom-call(f32[1024,512]{1,0:T(8,128)S(1)} %copy-done.2, bf16[576,512]{1,0:T(8,128)(2,1)S(1)} %collective-permute-done.13.got_a, bf16[512,512]{1,0:T(8,128)(2,1)S(1)} %copy-done.15, f32[64,512]{1,0:T(8,128)S(1)} %copy-done.28, s32[64,512]{1,0:T(8,128)S(1)} %reshape.25.idx, bf16[256,256]{1,0:T(8,128)(2,1)S(1)} %copy-done.18, ...), custom_call_target="tpu_custom_call" | custom-call | flops 805306368 | bytes 6291456 | tf_op jit(solution)/shard_map/pallas_call | solution.py:391
  106.5 9.6 %all-to-all-done.1 = bf16[256,8,128]{2,1,0:T(8,128)(2,1)S(1)} async-done(((bf16[256,8,128]{2,1,0:T(8,128)(2,1)}), bf16[256,8,128]{2,1,0:T(8,128)(2,1)S(1)}, u32[]{:S(2)}, u32[]{:S(2)}) %all-to-all-start.1) | async-done | bytes 524320 | tf_op jit(solution)/shard_map/all_to_all | solution.py:389
  118.2 2.2 %shard_map.94 = bf16[512,1024]{1,0:T(8,128)(2,1)} custom-call(s32[1]{0:T(128)} %bitcast.2.where, bf16[512,1024]{1,0:T(8,128)(2,1)S(1)} %copy-done.22, bf16[32,8,8,128]{3,2,1,0:T(8,128)(2,1)S(1)} %bitcast.13, s32[64,512]{1,0:T(8,128)S(1)} %reshape.25.idx, bf16[256,256]{1,0:T(8,128)(2,1)S(1)} %copy-done.19, bf16[256,256]{1,0:T(8,128)(2,1)S(1)} %copy-done.16), custom_call_target="tpu_custom_call" | custom-call | flops 536870912 | bytes 3145728 | tf_op jit(solution)/shard_map/pallas_call | solution.py:418
  120.4 13.9 %collective-permute-done.16.lo = bf16[320,1024]{1,0:T(8,128)(2,1)} collective-permute-done((bf16[320,1024]{1,0:T(8,128)(2,1)}, bf16[320,1024]{1,0:T(8,128)(2,1)}, u32[]{:S(2)}, u32[]{:S(2)}) %collective-permute-start.16) | collective-permute-done | bytes 655392 | tf_op jit(solution)/shard_map/ppermute | solution.py:258
  134.2 10.0 %shard_map.93 = bf16[256,1024]{1,0:T(8,128)(2,1)} custom-call(s32[1]{0:T(128)} %bitcast.where, bf16[256,4096]{1,0:T(8,128)(2,1)S(1)} %copy-done, bf16[320,1024]{1,0:T(8,128)(2,1)S(1)} %copy-done.26, bf16[320,1024]{1,0:T(8,128)(2,1)} %collective-permute-done.14.hi, bf16[320,1024]{1,0:T(8,128)(2,1)} %collective-permute-done.15.far, ...), custom_call_target="tpu_custom_call" | custom-call | flops 4294967296 | bytes 8388608 | tf_op jit(solution)/shard_map/pallas_call | solution.py:401
  (98 shorter events, 24.7 us)
Async XLA Ops:
  0.6 33.4 %collective-permute-start.11 = (bf16[512,1024]{1,0:T(8,128)(2,1)}, bf16[512,1024]{1,0:T(8,128)(2,1)}, u32[]{:S(2)}, u32[]{:S(2)}) collective-permute-start(bf16[512,1024]{1,0:T(8,128)(2,1)} %weight.1), channel_id=1, source_target_pairs={{0,1},{1,0},{2,3},{3,2},{4,5},{5,4},{6,7},{7,6},{8,9},{9,8},{10,11... | collective-permute-start | bytes 3145736 | tf_op jit(solution)/shard_map/ppermute | solution.py:267
  3.9 7.5 %collective-permute-start.1 = (bf16[512,256]{1,0:T(8,128)(2,1)S(1)}, bf16[512,256]{1,0:T(8,128)(2,1)S(1)}, u32[]{:S(2)}, u32[]{:S(2)}) collective-permute-start(bf16[512,256]{1,0:T(8,128)(2,1)S(1)} %bitcast.8), channel_id=1, source_target_pairs={{0,6},{1,7},{2,0},{3,1},{4,2},{5,3},{6,4},{7,5},{8,14},{9,15},{10,... | collective-permute-start | bytes 786440 | tf_op jit(solution)/shard_map/ppermute | solution.py:261
  6.7 7.8 %collective-permute-start = (bf16[512,256]{1,0:T(8,128)(2,1)S(1)}, bf16[512,256]{1,0:T(8,128)(2,1)S(1)}, u32[]{:S(2)}, u32[]{:S(2)}) collective-permute-start(bf16[512,256]{1,0:T(8,128)(2,1)S(1)} %bitcast.9), channel_id=1, source_target_pairs={{0,2},{1,3},{2,4},{3,5},{4,6},{5,7},{6,0},{7,1},{8,10},{9,11},{10,... | collective-permute-start | bytes 786440 | tf_op jit(solution)/shard_map/ppermute | solution.py:258
  8.7 11.3 %collective-permute-start.10 = (bf16[256,512]{1,0:T(8,128)(2,1)S(1)}, bf16[256,512]{1,0:T(8,128)(2,1)S(1)}, u32[]{:S(2)}, u32[]{:S(2)}) collective-permute-start(bf16[256,512]{1,0:T(8,128)(2,1)S(1)} %get-tuple-element.23), channel_id=1, source_target_pairs={{0,2},{1,3},{2,4},{3,5},{4,6},{5,7},{6,0},{7,1},{8,10},{9,11},{10,... | collective-permute-start | bytes 786440 | tf_op jit(solution)/shard_map/ppermute | solution.py:258
  8.8 12.0 %collective-permute-start.8 = (bf16[256,512]{1,0:T(8,128)(2,1)S(1)}, bf16[256,512]{1,0:T(8,128)(2,1)}, u32[]{:S(2)}, u32[]{:S(2)}) collective-permute-start(bf16[256,512]{1,0:T(8,128)(2,1)S(1)} %get-tuple-element.24), channel_id=1, source_target_pairs={{0,6},{1,7},{2,0},{3,1},{4,2},{5,3},{6,4},{7,5},{8,14},{9,15},{10,... | collective-permute-start | bytes 786440 | tf_op jit(solution)/shard_map/ppermute | solution.py:261
  14.6 11.1 %collective-permute-start.2 = (bf16[512,256]{1,0:T(8,128)(2,1)S(1)}, bf16[512,256]{1,0:T(8,128)(2,1)S(1)}, u32[]{:S(2)}, u32[]{:S(2)}) collective-permute-start(bf16[512,256]{1,0:T(8,128)(2,1)S(1)} %shard_map.85.b0.c0), channel_id=1, source_target_pairs={{0,2},{1,3},{2,4},{3,5},{4,6},{5,7},{6,0},{7,1},{8,10},{9,11},{10,... | collective-permute-start | bytes 786440 | tf_op jit(solution)/shard_map/ppermute | solution.py:258
  14.7 12.1 %collective-permute-start.7 = (bf16[256,512]{1,0:T(8,128)(2,1)}, bf16[256,512]{1,0:T(8,128)(2,1)}, u32[]{:S(2)}, u32[]{:S(2)}) collective-permute-start(bf16[256,512]{1,0:T(8,128)(2,1)} %get-tuple-element.25), channel_id=1, source_target_pairs={{0,6},{1,7},{2,0},{3,1},{4,2},{5,3},{6,4},{7,5},{8,14},{9,15},{10,... | collective-permute-start | bytes 786440 | tf_op jit(solution)/shard_map/ppermute | solution.py:261
  20.8 7.5 %collective-permute-start.17 = (bf16[512,256]{1,0:T(8,128)(2,1)S(1)}, bf16[512,256]{1,0:T(8,128)(2,1)}, u32[]{:S(2)}, u32[]{:S(2)}) collective-permute-start(bf16[512,256]{1,0:T(8,128)(2,1)S(1)} %shard_map.85.b0.c0), channel_id=1, source_target_pairs={{0,6},{1,7},{2,0},{3,1},{4,2},{5,3},{6,4},{7,5},{8,14},{9,15},{10,... | collective-permute-start | bytes 786440 | tf_op jit(solution)/shard_map/ppermute | solution.py:261
  20.8 10.6 %collective-permute-start.12 = (bf16[512,256]{1,0:T(8,128)(2,1)S(1)}, bf16[512,256]{1,0:T(8,128)(2,1)}, u32[]{:S(2)}, u32[]{:S(2)}) collective-permute-start(bf16[512,256]{1,0:T(8,128)(2,1)S(1)} %collective-permute-done.late_lo.c3.a3), channel_id=1, source_target_pairs={{0,2},{1,3},{2,4},{3,5},{4,6},{5,7},{6,0},{7,1},{8,10},{9,11},{10,... | collective-permute-start | bytes 786440 | tf_op jit(solution)/shard_map/ppermute | solution.py:258
  25.7 8.3 %collective-permute-start.9 = (bf16[256,512]{1,0:T(8,128)(2,1)}, bf16[256,512]{1,0:T(8,128)(2,1)}, u32[]{:S(2)}, u32[]{:S(2)}) collective-permute-start(bf16[256,512]{1,0:T(8,128)(2,1)} %collective-permute-done.8), channel_id=1, source_target_pairs={{0,6},{1,7},{2,0},{3,1},{4,2},{5,3},{6,4},{7,5},{8,14},{9,15},{10,... | collective-permute-start | bytes 786440 | tf_op jit(solution)/shard_map/ppermute | solution.py:261
  26.8 11.2 %collective-permute-start.4 = (bf16[256,512]{1,0:T(8,128)(2,1)S(1)}, bf16[256,512]{1,0:T(8,128)(2,1)S(1)}, u32[]{:S(2)}, u32[]{:S(2)}) collective-permute-start(bf16[256,512]{1,0:T(8,128)(2,1)S(1)} %get-tuple-element.15), channel_id=1, source_target_pairs={{0,2},{1,3},{2,4},{3,5},{4,6},{5,7},{6,0},{7,1},{8,10},{9,11},{10,... | collective-permute-start | bytes 786440 | tf_op jit(solution)/shard_map/ppermute | solution.py:258
  28.3 11.2 %collective-permute-start.18 = (bf16[512,256]{1,0:T(8,128)(2,1)}, bf16[512,256]{1,0:T(8,128)(2,1)S(1)}, u32[]{:S(2)}, u32[]{:S(2)}) collective-permute-start(bf16[512,256]{1,0:T(8,128)(2,1)} %collective-permute-done.17.b1.c1), channel_id=1, source_target_pairs={{0,6},{1,7},{2,0},{3,1},{4,2},{5,3},{6,4},{7,5},{8,14},{9,15},{10,... | collective-permute-start | bytes 786440 | tf_op jit(solution)/shard_map/ppermute | solution.py:261
  36.1 14.8 %collective-permute-start.13 = (bf16[576,512]{1,0:T(8,128)(2,1)S(1)}, bf16[576,512]{1,0:T(8,128)(2,1)S(1)}, u32[]{:S(2)}, u32[]{:S(2)}) collective-permute-start(bf16[576,512]{1,0:T(8,128)(2,1)S(1)} %shard_map.87), channel_id=1, source_target_pairs={{0,1},{1,0},{2,3},{3,2},{4,5},{5,4},{6,7},{7,6},{8,9},{9,8},{10,11... | collective-permute-start | bytes 1769480 | tf_op jit(solution)/shard_map/ppermute | solution.py:320
  36.4 8.3 %collective-permute-start.3 = (bf16[256,512]{1,0:T(8,128)(2,1)S(1)}, bf16[256,512]{1,0:T(8,128)(2,1)S(1)}, u32[]{:S(2)}, u32[]{:S(2)}) collective-permute-start(bf16[256,512]{1,0:T(8,128)(2,1)S(1)} %get-tuple-element.14), channel_id=1, source_target_pairs={{0,6},{1,7},{2,0},{3,1},{4,2},{5,3},{6,4},{7,5},{8,14},{9,15},{10,... | collective-permute-start | bytes 786440 | tf_op jit(solution)/shard_map/ppermute | solution.py:261
  38.0 6.7 %collective-permute-start.6 = (bf16[256,512]{1,0:T(8,128)(2,1)S(1)}, bf16[256,512]{1,0:T(8,128)(2,1)S(1)}, u32[]{:S(2)}, u32[]{:S(2)}) collective-permute-start(bf16[256,512]{1,0:T(8,128)(2,1)S(1)} %get-tuple-element.16), channel_id=1, source_target_pairs={{0,2},{1,3},{2,4},{3,5},{4,6},{5,7},{6,0},{7,1},{8,10},{9,11},{10,... | collective-permute-start | bytes 786440 | tf_op jit(solution)/shard_map/ppermute | solution.py:258
  38.0 9.2 %collective-permute-start.5 = (bf16[256,512]{1,0:T(8,128)(2,1)S(1)}, bf16[256,512]{1,0:T(8,128)(2,1)S(1)}, u32[]{:S(2)}, u32[]{:S(2)}) collective-permute-start(bf16[256,512]{1,0:T(8,128)(2,1)S(1)} %collective-permute-done.4), channel_id=1, source_target_pairs={{0,2},{1,3},{2,4},{3,5},{4,6},{5,7},{6,0},{7,1},{8,10},{9,11},{10,... | collective-permute-start | bytes 786440 | tf_op jit(solution)/shard_map/ppermute | solution.py:258
  42.3 14.8 %collective-permute-start.19 = (bf16[512,512]{1,0:T(8,128)(2,1)S(1)}, bf16[512,512]{1,0:T(8,128)(2,1)S(1)}, u32[]{:S(2)}, u32[]{:S(2)}) collective-permute-start(bf16[512,512]{1,0:T(8,128)(2,1)S(1)} %shard_map.90), channel_id=1, source_target_pairs={{0,1},{1,0},{2,3},{3,2},{4,5},{5,4},{6,7},{7,6},{8,9},{9,8},{10,11... | collective-permute-start | bytes 1572872 | tf_op jit(solution)/shard_map/ppermute | solution.py:330
  55.5 32.6 %copy-start.29 = (bf16[320,1024]{1,0:T(8,128)(2,1)}, bf16[320,1024]{1,0:T(8,128)(2,1)S(1)}, u32[]{:S(2)}) copy-start(bf16[320,1024]{1,0:T(8,128)(2,1)S(1)} %get-tuple-element.20) | copy-start | bytes 1966084
  55.5 32.6 %copy-start.30 = (bf16[320,1024]{1,0:T(8,128)(2,1)}, bf16[320,1024]{1,0:T(8,128)(2,1)S(1)}, u32[]{:S(2)}) copy-start(bf16[320,1024]{1,0:T(8,128)(2,1)S(1)} %get-tuple-element.19) | copy-start | bytes 1966084
  55.5 32.5 %copy-start.31 = (bf16[320,1024]{1,0:T(8,128)(2,1)}, bf16[320,1024]{1,0:T(8,128)(2,1)S(1)}, u32[]{:S(2)}) copy-start(bf16[320,1024]{1,0:T(8,128)(2,1)S(1)} %get-tuple-element.18) | copy-start | bytes 1966084
  88.9 27.1 %all-to-all-start.1 = ((bf16[256,8,128]{2,1,0:T(8,128)(2,1)}), bf16[256,8,128]{2,1,0:T(8,128)(2,1)S(1)}, u32[]{:S(2)}, u32[]{:S(2)}) async-start(bf16[256,8,128]{2,1,0:T(8,128)(2,1)} %copy-done.13), calls=%async_computation.1 | async-start | bytes 1048576 | tf_op jit(solution)/shard_map/all_to_all | solution.py:389
  94.4 26.0 %collective-permute-start.14 = (bf16[320,1024]{1,0:T(8,128)(2,1)}, bf16[320,1024]{1,0:T(8,128)(2,1)}, u32[]{:S(2)}, u32[]{:S(2)}) collective-permute-start(bf16[320,1024]{1,0:T(8,128)(2,1)} %copy-done.31), channel_id=1, source_target_pairs={{0,6},{1,7},{2,0},{3,1},{4,2},{5,3},{6,4},{7,5},{8,14},{9,15},{10,... | collective-permute-start | bytes 1966088 | tf_op jit(solution)/shard_map/ppermute | solution.py:261
  97.3 23.1 %collective-permute-start.15 = (bf16[320,1024]{1,0:T(8,128)(2,1)}, bf16[320,1024]{1,0:T(8,128)(2,1)}, u32[]{:S(2)}, u32[]{:S(2)}) collective-permute-start(bf16[320,1024]{1,0:T(8,128)(2,1)} %copy-done.30), channel_id=1, source_target_pairs={{0,4},{1,5},{2,6},{3,7},{4,0},{5,1},{6,2},{7,3},{8,12},{9,13},{10,... | collective-permute-start | bytes 1966088 | tf_op jit(solution)/shard_map/ppermute | solution.py:360
  97.7 36.5 %collective-permute-start.16 = (bf16[320,1024]{1,0:T(8,128)(2,1)}, bf16[320,1024]{1,0:T(8,128)(2,1)}, u32[]{:S(2)}, u32[]{:S(2)}) collective-permute-start(bf16[320,1024]{1,0:T(8,128)(2,1)} %copy-done.29), channel_id=1, source_target_pairs={{0,2},{1,3},{2,4},{3,5},{4,6},{5,7},{6,0},{7,1},{8,10},{9,11},{10,... | collective-permute-start | bytes 1966088 | tf_op jit(solution)/shard_map/ppermute | solution.py:258
  (29 other events, 215.1 us)

commit v2 on v1

v2 whole, which is shorter than its diff:
```python
import jax
import jax.numpy as jnp
import numpy as np
from jax import lax
from jax.experimental import pallas as pl
from jax.experimental.pallas import tpu as pltpu
from jax.sharding import PartitionSpec as P

beta_decay = 0.9
step_rate = 0.5
ROWS = 512
KV = 1024
TOK = 256
BLOCK = 64
KEEP = 4
HALF = KV // 2
GROUP = 256
STEPS = KV // GROUP
PICKS = KV // BLOCK * KEEP
LANES = 128
FAR = TOK // 2
PACK = 16
REPS = 32
VMEM_LIMIT = 24 * 1024 * 1024


def dct_group():
    n = np.arange(BLOCK, dtype=np.float64)
    single = np.cos(np.pi * (2.0 * n[None, :] + 1.0) * n[:, None] / (2 * BLOCK))
    single *= np.where(n[:, None] == 0, np.sqrt(1.0 / BLOCK), np.sqrt(2.0 / BLOCK))
    return np.kron(np.eye(GROUP // BLOCK), single).astype(np.float32)


def split_pair(values):
    high = values.astype(jnp.bfloat16)
    return high, (values - high.astype(jnp.float32)).astype(jnp.bfloat16)


def mix(left, right, dims):
    return lax.dot_general(left, right, (dims, ((), ())), preferred_element_type=jnp.float32)


def three_pass(left_pair, right_pair, dims):
    return (
        mix(left_pair[0], right_pair[0], dims)
        + mix(left_pair[0], right_pair[1], dims)
        + mix(left_pair[1], right_pair[0], dims)
    )


def expand_block(index_rows, value_rows, width):
    freq = lax.broadcasted_iota(jnp.int32, (BLOCK, width), 0)
    dense = jnp.zeros((BLOCK, width), jnp.float32)
    for j in range(KEEP):
        dense = jnp.where(index_rows[j] == freq, value_rows[j], dense)
    return dense


def spread_row(tile, row):
    return jnp.broadcast_to(tile[row : row + 1, :], (PACK, LANES)).astype(jnp.bfloat16)


def expand_tile(indices, values, dense, first, cols):
    freq = lax.broadcasted_iota(jnp.int32, (PACK, LANES), 0).astype(jnp.float32)
    for half in range(2):
        at = [spread_row(indices, half * KEEP + j) for j in range(KEEP)]
        have = [spread_row(values, half * KEEP + j) for j in range(KEEP)]
        for part in range(BLOCK // PACK):
            here = (freq + part * PACK).astype(jnp.bfloat16)
            tile = jnp.zeros((PACK, LANES), jnp.bfloat16)
            for j in range(KEEP):
                tile = jnp.where(at[j] == here, have[j], tile)
            start = first + half * BLOCK + part * PACK
            dense[start : start + PACK, cols] = tile


def four_products(cots, toks):
    total = jnp.dot(cots[0], toks[0], preferred_element_type=jnp.float32)
    for c, t in zip(cots[1:], toks[1:]):
        total += jnp.dot(c, t, preferred_element_type=jnp.float32)
    return total


def cot_of(message):
    return message[:, :TOK]


def tok_of(message):
    return jnp.concatenate([message[:TOK, TOK:], message[TOK:, TOK:]], axis=1)


def pack_first_kernel(where, cot, t0, t1, t2, t3, to_up, to_down, far, mine):
    turned = cot[...].T
    for out, t in ((to_up, t1), (to_down, t3)):
        out[:, :TOK] = turned
        out[:TOK, TOK:] = t[:, :TOK]
        out[TOK:, TOK:] = t[:, TOK:]
    far[...] = t2[...]
    mine[...] = t0[...]


def pack_second_kernel(cot, late_lo, late_hi, out):
    out[...] = cot[...].T


def pack_own_kernel(where, t0, t1, t2, t3, late, to_up, to_down, mine):
    to_up[:TOK, :] = t1[...]
    to_up[TOK:, :] = t2[...]
    to_down[...] = t3[...]
    mine[...] = t0[...]


def partial_first_kernel(sent, hi, far, lo, t0, t2, idx, early, out):
    cots = (cot_of(sent), cot_of(hi), far[...], cot_of(lo))
    toks = (t0[...], tok_of(hi), t2[...], tok_of(lo))
    out[:HALF, :] = four_products(cots, toks).astype(out.dtype)
    out[HALF:, :] = idx[...].astype(jnp.float32).astype(out.dtype)


def partial_second_kernel(c0, c1, c2, c3, t0, hi, t2, lo, out):
    cots = (c0[...], c1[...], c2[...], c3[...])
    out[...] = four_products(cots, (t0[...], tok_of(hi), t2[...], tok_of(lo))).astype(out.dtype)


def own_kernel(sent, a1, a2, a3, b0, b1, b2, b3, t0, t1, t2, t3, mom, out):
    step = pl.program_id(0)
    toks = (t0[...], t1[...], t2[...], t3[...])

    @pl.when(step < STEPS // 2)
    def _():
        cots = (sent[:, :TOK], a1[:, :TOK], a2[...], a3[:, :TOK])
        out[...] = four_products(cots, toks) + beta_decay * mom[...].T

    @pl.when(step >= STEPS // 2)
    def _():
        cots = (b0[...], b1[...], b2[...], b3[...])
        out[...] = four_products(cots, toks) + beta_decay * mom[...].T


def received(got_a, got_b):
    first = pl.program_id(0) < STEPS // 2
    return jnp.where(first, got_a[...], got_b[...]).astype(jnp.float32)


def pick_kernel(pre, got_a, got_b, idx, ch, cl, late, picked, tiles):
    moment = pre[...] + received(got_a, got_b)
    spectrum = three_pass((ch[...], cl[...]), split_pair(moment), ((1,), (0,)))
    freq = lax.broadcasted_iota(jnp.int32, (BLOCK, ROWS), 0)
    rows = []
    for b in range(GROUP // BLOCK):
        part = spectrum[b * BLOCK : (b + 1) * BLOCK, :]
        for j in range(KEEP):
            at = idx[b * KEEP + j : b * KEEP + j + 1, :]
            rows.append(jnp.sum(jnp.where(at == freq, part, 0.0), axis=0, keepdims=True))
    values = jnp.concatenate(rows, axis=0)
    picked[...] = values
    for t in range(GROUP // BLOCK * KEEP // 8):
        for q in range(ROWS // LANES):
            tile = values[t * 8 : (t + 1) * 8, q * LANES : (q + 1) * LANES]
            tiles[t * (ROWS // LANES) + q] = tile.astype(tiles.dtype)


def share_kernel(spread, late, out):
    total = jnp.sum(spread[...].astype(jnp.float32), axis=0, keepdims=True)
    out[...] = jnp.broadcast_to(total, out.shape).astype(out.dtype)


def residual_kernel(pre, got_a, got_b, picked, idx, ch, cl, late, out):
    parts = []
    for b in range(GROUP // BLOCK):
        rows = [slice(b * KEEP + j, b * KEEP + j + 1) for j in range(KEEP)]
        parts.append(expand_block([idx[r, :] for r in rows], [picked[r, :] for r in rows], ROWS))
    kept = jnp.concatenate(parts, axis=0)
    back = three_pass((ch[...], cl[...]), split_pair(kept), ((0,), (0,)))
    out[...] = (pre[...] + received(got_a, got_b) - back).T


def base_far_kernel(where, own, peer, w_own, w_peer, idx, got_a, to_up, to_down):
    total = jnp.dot(own[...], w_own[...], preferred_element_type=jnp.float32)
    total += jnp.dot(peer[...], w_peer[...], preferred_element_type=jnp.float32)
    low = total.astype(to_up.dtype)
    mine = idx[...].astype(jnp.float32).astype(jnp.bfloat16)
    theirs = got_a[HALF:, :]
    first = where[0] == 0
    left, right = jnp.where(first, mine, theirs), jnp.where(first, theirs, mine)
    for out, rows in ((to_up, low[:FAR]), (to_down, low[FAR:])):
        out[:FAR, :] = rows
        out[FAR:, :ROWS] = left
        out[FAR:, ROWS:] = right


def base_near_kernel(o0, o1, o3, p0, first_hi, first_lo, w_own, w_peer, lo, hi, late, base, to_up, to_down):
    def product(own, peer):
        total = jnp.dot(own[...], w_own[...], preferred_element_type=jnp.float32)
        return total + jnp.dot(peer, w_peer[...], preferred_element_type=jnp.float32)

    base[...] = product(o0, p0[...])
    total = product(o1, tok_of(first_hi))
    to_up[:FAR, :] = (total[:FAR] + lo[:FAR, :].astype(jnp.float32)).astype(to_up.dtype)
    to_up[FAR:TOK, :] = total[FAR:].astype(to_up.dtype)
    to_up[TOK:, :] = lo[FAR:, :]
    total = product(o3, tok_of(first_lo))
    to_down[:FAR, :] = total[:FAR].astype(to_down.dtype)
    to_down[FAR:, :] = (total[FAR:] + hi[:FAR, :].astype(jnp.float32)).astype(to_down.dtype)


def forward_kernel(where, tok, base, own, near_hi, near_lo, lo, hi, tot, weight, ch, cl, out, out_weight, dense, mixed):
    step = pl.program_id(0)
    near = jnp.where(step == 0, own[FAR:, :], near_hi[FAR:, :])
    away = jnp.where(step == 2, lo[TOK:, :], near_lo[FAR:, :])
    pairs = jnp.where(step < 2, near, away).astype(jnp.float32)

    @pl.when(step == 0)
    def _():
        mixed[...] = jnp.zeros_like(mixed)

    for g in range(STEPS):
        for t in range(2 * g, 2 * g + 2):
            for f in range(2):
                for q in range(ROWS // LANES):
                    cols = slice(f * ROWS + q * LANES, f * ROWS + (q + 1) * LANES)
                    values = tot[t * (ROWS // LANES) + q, f].astype(jnp.float32)
                    expand_tile(pairs[t * 8 : (t + 1) * 8, cols], values, dense, t * 2 * BLOCK, cols)
        span = slice(g * GROUP, (g + 1) * GROUP)
        mixed[span, :] += mix(dense[span, :], tok[...], ((1,), (1,)))

    @pl.when(step == 0)
    def _():
        cols = pl.ds(pl.multiple_of((where[0] & 1) * ROWS, ROWS), ROWS)
        for g in range(STEPS):
            span = slice(g * GROUP, (g + 1) * GROUP)
            turned = dense[span, cols].T
            delta = mix(turned, ch[...], ((1,), (0,))) + mix(turned, cl[...], ((1,), (0,)))
            new = weight[:, span].astype(jnp.float32) - (step_rate / REPS) * delta
            out_weight[:, span] = new.astype(out_weight.dtype)

    @pl.when(step == 3)
    def _():
        for g in range(STEPS):
            span = slice(g * GROUP, (g + 1) * GROUP)
            delta = three_pass(split_pair(mixed[span, :].T), (ch[...], cl[...]), ((1,), (0,)))
            near = lo[:TOK, span].astype(jnp.float32) + hi[:, span].astype(jnp.float32)
            out[:, span] = (base[:, span] + near - (step_rate / REPS) * delta).astype(out.dtype)


def params():
    return pltpu.CompilerParams(vmem_limit_bytes=VMEM_LIMIT)


def cost(flops, mib):
    return pl.CostEstimate(flops=int(flops), bytes_accessed=int(mib * (1 << 20)), transcendentals=0)


def whole(*shape):
    return pl.BlockSpec(shape, lambda c, *_: (0,) * len(shape))


def by_row(rows, width):
    return pl.BlockSpec((rows, width), lambda c: (c, 0))


def by_col(rows, width):
    return pl.BlockSpec((rows, width), lambda c: (0, c))


def first_half(rows, width):
    return pl.BlockSpec((rows, width), lambda c: (jnp.minimum(c, STEPS // 2 - 1), 0))


def second_half(rows, width):
    return pl.BlockSpec((rows, width), lambda c: (jnp.maximum(c - STEPS // 2, 0), 0))


AFTER = pl.BlockSpec(memory_space=pl.ANY)
BASIS = [whole(GROUP, GROUP)] * 2
GOT = [first_half(GROUP, ROWS), second_half(GROUP, ROWS)]
BF16, F32 = jnp.bfloat16, jnp.float32


def body(tokens, cotangent, weight, momentum, kept_index):
    basis = dct_group()
    high = jnp.asarray(basis).astype(BF16)
    low = (jnp.asarray(basis) - high.astype(F32)).astype(BF16)
    fsdp = lax.axis_index("fsdp").astype(jnp.int32)
    y, side = fsdp >> 1, fsdp & 1
    other = 1 - side
    index_t = jnp.transpose(kept_index, (1, 2, 0)).reshape(PICKS, ROWS)

    plus = [(i, (i + 2) % 8) for i in range(8)]
    minus = [(i, (i + 6) % 8) for i in range(8)]
    across = [(i, (i + 4) % 8) for i in range(8)]
    swap = [(i, i ^ 1) for i in range(8)]

    def up(x):
        return lax.ppermute(x, "fsdp", plus)

    def down(x):
        return lax.ppermute(x, "fsdp", minus)

    weight_peer = lax.ppermute(weight, "fsdp", swap)

    def columns():
        return [pl.BlockSpec((TOK, ROWS), lambda c, s, d=d: (0, (s[0] + 2 * d) & 7)) for d in range(4)]

    first_up, first_down, far_send, peer_0 = pl.pallas_call(
        pack_first_kernel,
        grid_spec=pltpu.PrefetchScalarGridSpec(
            num_scalar_prefetch=1,
            grid=(1,),
            in_specs=[whole(TOK, HALF)] + columns(),
            out_specs=[whole(HALF, 2 * TOK)] * 2 + [whole(TOK, ROWS)] * 2,
        ),
        out_shape=[jax.ShapeDtypeStruct((HALF, 2 * TOK), BF16)] * 2
        + [jax.ShapeDtypeStruct((TOK, ROWS), BF16)] * 2,
        compiler_params=params(),
        cost_estimate=cost(0, 3),
    )((fsdp ^ 1).reshape(1), cotangent, tokens, tokens, tokens, tokens)
    first_lo = up(first_up)
    first_hi = down(first_down)
    peer_far = down(down(far_send))
    a_far = up(first_lo[:, :TOK])

    cot_b = pl.pallas_call(
        pack_second_kernel,
        grid=(1,),
        in_specs=[pl.BlockSpec((TOK, HALF), lambda c: (0, 1)), AFTER, AFTER],
        out_specs=whole(HALF, TOK),
        out_shape=jax.ShapeDtypeStruct((HALF, TOK), BF16),
        compiler_params=params(),
        cost_estimate=cost(0, 1),
    )(cotangent, first_lo, first_hi)
    b_lo = up(cot_b)
    b_hi = down(cot_b)
    b_far = down(b_hi)
    cots_b = (cot_b, b_hi, b_far, b_lo)

    own_up, own_down, own_0 = pl.pallas_call(
        pack_own_kernel,
        grid_spec=pltpu.PrefetchScalarGridSpec(
            num_scalar_prefetch=1,
            grid=(1,),
            in_specs=columns() + [AFTER],
            out_specs=[whole(2 * TOK, ROWS), whole(TOK, ROWS), whole(TOK, ROWS)],
        ),
        out_shape=[
            jax.ShapeDtypeStruct((2 * TOK, ROWS), BF16),
            jax.ShapeDtypeStruct((TOK, ROWS), BF16),
            jax.ShapeDtypeStruct((TOK, ROWS), BF16),
        ],
        compiler_params=params(),
        cost_estimate=cost(0, 2),
    )(fsdp.reshape(1), tokens, tokens, tokens, tokens, b_lo)
    own_lo = up(own_up)
    own_hi = down(own_down)
    own_far = up(own_lo[TOK:])
    owns = (own_0, own_hi, own_far, own_lo)

    partial_a = pl.pallas_call(
        partial_first_kernel,
        grid=(1,),
        in_specs=[whole(HALF, 2 * TOK)] * 2
        + [whole(HALF, TOK), whole(HALF, 2 * TOK)]
        + [whole(TOK, ROWS)] * 2
        + [whole(PICKS, ROWS), AFTER],
        out_specs=whole(HALF + PICKS, ROWS),
        out_shape=jax.ShapeDtypeStruct((HALF + PICKS, ROWS), BF16),
        compiler_params=params(),
        cost_estimate=cost(KV * KV * ROWS, 3),
    )(first_up, first_hi, a_far, first_lo, peer_0, peer_far, index_t, weight_peer)
    got_a = lax.ppermute(partial_a, "fsdp", swap)
    partial_b = pl.pallas_call(
        partial_second_kernel,
        grid=(1,),
        in_specs=[whole(HALF, TOK)] * 4
        + [whole(TOK, ROWS), whole(HALF, 2 * TOK), whole(TOK, ROWS), whole(HALF, 2 * TOK)],
        out_specs=whole(HALF, ROWS),
        out_shape=jax.ShapeDtypeStruct((HALF, ROWS), BF16),
        compiler_params=params(),
        cost_estimate=cost(KV * KV * ROWS, 3),
    )(*cots_b, peer_0, first_hi, peer_far, first_lo)
    got_b = lax.ppermute(partial_b, "fsdp", swap)

    pre = pl.pallas_call(
        own_kernel,
        grid=(STEPS,),
        in_specs=[first_half(GROUP, 2 * TOK)] * 2
        + [first_half(GROUP, TOK), first_half(GROUP, 2 * TOK)]
        + [second_half(GROUP, TOK)] * 4
        + [whole(TOK, ROWS)] * 4
        + [by_col(ROWS, GROUP)],
        out_specs=by_row(GROUP, ROWS),
        out_shape=jax.ShapeDtypeStruct((KV, ROWS), F32),
        compiler_params=params(),
        cost_estimate=cost(2 * KV * KV * ROWS, 7),
    )(first_up, first_hi, a_far, first_lo, *cots_b, *owns, momentum[0])

    far_up, far_down = pl.pallas_call(
        base_far_kernel,
        grid_spec=pltpu.PrefetchScalarGridSpec(
            num_scalar_prefetch=1,
            grid=(1,),
            in_specs=[whole(TOK, ROWS)] * 2
            + [whole(ROWS, KV)] * 2
            + [whole(PICKS, ROWS), whole(HALF + PICKS, ROWS)],
            out_specs=[whole(FAR + PICKS, KV)] * 2,
        ),
        out_shape=[jax.ShapeDtypeStruct((FAR + PICKS, KV), BF16)] * 2,
        compiler_params=params(),
        cost_estimate=cost(KV * KV * ROWS, 4),
    )(side.reshape(1), own_far, peer_far, weight, weight_peer, index_t, got_a)
    far_lo = up(far_up)
    far_hi = down(far_down)

    picked, tiles = pl.pallas_call(
        pick_kernel,
        grid=(STEPS,),
        in_specs=[by_row(GROUP, ROWS)] + GOT + [by_row(PICKS // STEPS, ROWS)] + BASIS + [AFTER],
        out_specs=[
            by_row(PICKS // STEPS, ROWS),
            pl.BlockSpec((REPS // STEPS, 8, LANES), lambda c: (c, 0, 0)),
        ],
        out_shape=[
            jax.ShapeDtypeStruct((PICKS, ROWS), F32),
            jax.ShapeDtypeStruct((REPS, 8, LANES), BF16),
        ],
        compiler_params=params(),
        cost_estimate=cost(6 * KV * GROUP * ROWS, 4),
    )(pre, got_a, got_b, index_t, high, low, far_up)

    base, near_up, near_down = pl.pallas_call(
        base_near_kernel,
        grid=(1,),
        in_specs=[whole(TOK, ROWS)] * 4
        + [whole(HALF, 2 * TOK)] * 2
        + [whole(ROWS, KV)] * 2
        + [whole(FAR + PICKS, KV)] * 2 + [AFTER],
        out_specs=[whole(TOK, KV), whole(TOK + PICKS, KV), whole(TOK, KV)],
        out_shape=[
            jax.ShapeDtypeStruct((TOK, KV), F32),
            jax.ShapeDtypeStruct((TOK + PICKS, KV), BF16),
            jax.ShapeDtypeStruct((TOK, KV), BF16),
        ],
        compiler_params=params(),
        cost_estimate=cost(3 * KV * KV * ROWS, 7),
    )(own_0, own_hi, own_lo, peer_0, first_hi, first_lo, weight, weight_peer, far_lo, far_hi, tiles)
    near_lo = up(near_up)
    near_hi = down(near_down)

    spread = lax.all_to_all(tiles, "rep", 0, 0)
    copies = pl.pallas_call(
        share_kernel,
        grid=(1,),
        in_specs=[whole(REPS, 8, LANES), AFTER],
        out_specs=whole(REPS * 8, 8, LANES),
        out_shape=jax.ShapeDtypeStruct((REPS * 8, 8, LANES), BF16),
        compiler_params=params(),
        cost_estimate=cost(0, 1),
    )(spread, near_down)
    totals = lax.all_to_all(copies, ("rep", "fsdp"), 0, 0).reshape(REPS, 8, 8, LANES)

    new_momentum = pl.pallas_call(
        residual_kernel,
        grid=(STEPS,),
        in_specs=[by_row(GROUP, ROWS)] + GOT + [by_row(PICKS // STEPS, ROWS)] * 2 + BASIS + [AFTER],
        out_specs=by_col(ROWS, GROUP),
        out_shape=jax.ShapeDtypeStruct((ROWS, KV), F32),
        compiler_params=params(),
        cost_estimate=cost(6 * KV * GROUP * ROWS, 6),
    )(pre, got_a, got_b, picked, index_t, high, low, copies)

    projected, new_weight = pl.pallas_call(
        forward_kernel,
        grid_spec=pltpu.PrefetchScalarGridSpec(
            num_scalar_prefetch=1,
            grid=(4,),
            in_specs=[pl.BlockSpec((TOK, 2 * ROWS), lambda c, s: (0, ((s[0] >> 1) + c) & 3))]
            + [whole(TOK, KV)]
            + [whole(FAR + PICKS, KV)] * 3
            + [whole(TOK + PICKS, KV), whole(TOK, KV)]
            + [pl.BlockSpec((REPS, 2, 8, LANES), lambda c, s: (0, ((s[0] >> 1) + c) & 3, 0, 0))]
            + [whole(ROWS, KV)]
            + BASIS,
            out_specs=[whole(TOK, KV), whole(ROWS, KV)],
            scratch_shapes=[pltpu.VMEM((KV, 2 * ROWS), BF16), pltpu.VMEM((KV, TOK), F32)],
        ),
        out_shape=[
            jax.ShapeDtypeStruct((TOK, KV), BF16),
            jax.ShapeDtypeStruct((ROWS, KV), BF16),
        ],
        compiler_params=params(),
        cost_estimate=cost(8 * KV * KV * ROWS, 8),
    )(fsdp.reshape(1), tokens, base, far_up, far_hi, far_lo, near_lo, near_hi, totals, weight, high, low)
    return (projected, new_weight, new_momentum[None])


def solution(mesh):
    in_specs = (
        P(("rep", "fsdp"), None),
        P(("rep", "fsdp"), None),
        P("fsdp", None),
        P("rep", "fsdp", None),
        P("fsdp", None, None),
    )
    out_specs = (P(("rep", "fsdp"), None), P("fsdp", None), P("rep", "fsdp", None))
    return jax.shard_map(body, mesh=mesh, in_specs=in_specs, out_specs=out_specs, check_vma=False)
```

time: 145 us -> 150 us (1.034)
  blocking collectives: 27.4 us -> 0 us
  starting transfers between devices: 26.3 us -> 50.6 us
  waiting for transfers between devices: 44.8 us -> 31.4 us
  local copies, waits for them, and re-layouts: 13.9 us -> 26.1 us
  Pallas kernels: 31 us -> 39.4 us
    all_to_all x1 -> x0, blocking collectives: 27.4 us -> none  [body(): spread = lax.all_to_all(tiles, 'rep', 0, 0)]
    all_to_all x0 -> x1, starting transfers between devices: none -> 16.3 us  [body(): spread = lax.all_to_all(tiles, 'rep', 0, 0)]
    unnamed x65 -> x80, local copies, waits for them, and re-layouts: 9.92 us -> 22.7 us
    ppermute x8 -> x7, waiting for transfers between devices: 27.5 us -> 17.6 us  [up(): return lax.ppermute(x, 'fsdp', plus)]
    all_to_all x1, waiting for transfers between devices: 9.56 us -> 0.01 us  [body(): lax.all_to_all(copies, ('rep', 'fsdp'), 0, 0).reshape(REPS, 8, 8, LANES)]
    ppermute x8, waiting for transfers between devices: 6.2 us -> 13.1 us  [down(): return lax.ppermute(x, 'fsdp', minus)]
    all_to_all x1, starting transfers between devices: 5.43 us -> 10.5 us  [body(): lax.all_to_all(copies, ('rep', 'fsdp'), 0, 0).reshape(REPS, 8, 8, LANES)]
    pallas_call x7 -> x8, Pallas kernels: 12.5 us -> 16.5 us  [the longest x1 4.18 us: body(): pl.pallas_call(base_near_kernel, grid=(1,), in_specs=[whole(TOK, ROWS)] *...]
  transfers between devices with their start and end apart: 21 -> 20, of which waited for: 11 -> 9; matrix products, arithmetic and copies ran while one was open for 3% -> 2% of each run, Pallas kernels for 12% -> 18%
where the time goes in v2:
time: 150 us; the launch traced here: 148 us
  starting transfers between devices  50.6 us (34%)
  Pallas kernels  39.4 us (26%)
  waiting for transfers between devices  31.4 us (21%)
  local copies, waits for them, and re-layouts  26.1 us (17%)
    unnamed x80, local copies, waits for them, and re-layouts  22.7 us
    ppermute x7, waiting for transfers between devices, up(): return lax.ppermute(x, 'fsdp', plus)  17.6 us
    ppermute x8, starting transfers between devices, down(): return lax.ppermute(x, 'fsdp', minus)  17.3 us
    all_to_all x1, starting transfers between devices, body(): spread = lax.all_to_all(tiles, 'rep', 0, 0)  16.3 us
    ppermute x8, waiting for transfers between devices, down(): return lax.ppermute(x, 'fsdp', minus)  13.1 us
    pallas_call x1, Pallas kernels, body(): pl.pallas_call(forward_kernel, grid_spec=pltpu.PrefetchScalarGridSpec(num...  10.8 us
    all_to_all x1, starting transfers between devices, body(): lax.all_to_all(copies, ('rep', 'fsdp'), 0, 0).reshape(REPS, 8, 8, LANES)  10.5 us
    pallas_call x1, Pallas kernels, body(): pl.pallas_call(residual_kernel, grid=(STEPS,), in_specs=[by_row(GROUP, RO...  5.22 us
  transfers between devices with their start and end apart: 20, of which 9 were waited for; matrix products, arithmetic and copies ran while one was open for 2% of the time, Pallas kernels for 18%

profile of v2, /device:TPU:1, one launch (start us, length us, event | category | flops | bytes accessed | tf_op | source)
XLA Modules:
  0.0 148.4 jit_solution(2824973754774996237)
XLA Ops:
  0.6 2.1 %collective-permute-start.5 = (bf16[512,1024]{1,0:T(8,128)(2,1)}, bf16[512,1024]{1,0:T(8,128)(2,1)}, u32[]{:S(2)}, u32[]{:S(2)}) collective-permute-start(bf16[512,1024]{1,0:T(8,128)(2,1)} %weight.1), channel_id=1, source_target_pairs={{0,1},{1,0},{2,3},{3,2},{4,5},{5,4},{6,7},{7,6},{8,9},{9,8},{10,11... | collective-permute-start | bytes 3145736 | tf_op jit(solution)/shard_map/ppermute | solution.py:300
  2.8 1.6 %copy-done = bf16[256,4096]{1,0:T(8,128)(2,1)S(1)} copy-done((bf16[256,4096]{1,0:T(8,128)(2,1)S(1)}, bf16[256,4096]{1,0:T(8,128)(2,1)}, u32[]{:S(2)}) %copy-start) | copy-done | bytes 2097176
  9.9 9.3 %collective-permute-done.late_lo.lo.a3.first_lo = bf16[512,512]{1,0:T(8,128)(2,1)S(1)} collective-permute-done((bf16[512,512]{1,0:T(8,128)(2,1)S(1)}, bf16[512,512]{1,0:T(8,128)(2,1)S(1)}, u32[]{:S(2)}, u32[]{:S(2)}) %collective-permute-start) | collective-permute-done | bytes 524320 | tf_op jit(solution)/shard_map/ppermute | solution.py:295
  20.7 4.1 %collective-permute-done.7 = bf16[256,512]{1,0:T(8,128)(2,1)} collective-permute-done((bf16[256,512]{1,0:T(8,128)(2,1)S(1)}, bf16[256,512]{1,0:T(8,128)(2,1)}, u32[]{:S(2)}, u32[]{:S(2)}) %collective-permute-start.7) | collective-permute-done | bytes 262176 | tf_op jit(solution)/shard_map/ppermute | solution.py:298
  24.8 2.6 %collective-permute-start.8 = (bf16[256,512]{1,0:T(8,128)(2,1)}, bf16[256,512]{1,0:T(8,128)(2,1)}, u32[]{:S(2)}, u32[]{:S(2)}) collective-permute-start(bf16[256,512]{1,0:T(8,128)(2,1)} %collective-permute-done.7), channel_id=1, source_target_pairs={{0,6},{1,7},{2,0},{3,1},{4,2},{5,3},{6,4},{7,5},{8,14},{9,15},{10,... | collective-permute-start | bytes 786440 | tf_op jit(solution)/shard_map/ppermute | solution.py:298
  30.0 2.5 %collective-permute-start.13 = (bf16[512,256]{1,0:T(8,128)(2,1)S(1)}, bf16[512,256]{1,0:T(8,128)(2,1)}, u32[]{:S(2)}, u32[]{:S(2)}) collective-permute-start(bf16[512,256]{1,0:T(8,128)(2,1)S(1)} %shard_map.86.b0.c0), channel_id=1, source_target_pairs={{0,6},{1,7},{2,0},{3,1},{4,2},{5,3},{6,4},{7,5},{8,14},{9,15},{10,... | collective-permute-start | bytes 786440 | tf_op jit(solution)/shard_map/ppermute | solution.py:298
  36.9 2.6 %shard_map.88 = bf16[576,512]{1,0:T(8,128)(2,1)} custom-call(bf16[512,512]{1,0:T(8,128)(2,1)S(1)} %copy-done.10, bf16[512,512]{1,0:T(8,128)(2,1)S(1)} %collective-permute-done.1.late_hi.hi.a1.first_hi, bf16[512,256]{1,0:T(8,128)(2,1)} %collective-permute-done.9.far.a2, bf16[512,512]{1,0:T(8,128)(2,1)S(1)} %collective-permute-done.late_lo.lo.a3.first_lo, ...), custom_call_target="tpu_custom_call" | custom-call | flops 536870912 | bytes 3145728 | tf_op jit(solution)/shard_map/pallas_call | solution.py:358
  39.5 2.4 %collective-permute-start.14 = (bf16[512,256]{1,0:T(8,128)(2,1)}, bf16[512,256]{1,0:T(8,128)(2,1)S(1)}, u32[]{:S(2)}, u32[]{:S(2)}) collective-permute-start(bf16[512,256]{1,0:T(8,128)(2,1)} %collective-permute-done.13.b1.c1), channel_id=1, source_target_pairs={{0,6},{1,7},{2,0},{3,1},{4,2},{5,3},{6,4},{7,5},{8,14},{9,15},{10,... | collective-permute-start | bytes 786440 | tf_op jit(solution)/shard_map/ppermute | solution.py:298
  42.0 4.2 %collective-permute-done.4.t3.o3 = bf16[512,512]{1,0:T(8,128)(2,1)} collective-permute-done((bf16[512,512]{1,0:T(8,128)(2,1)}, bf16[512,512]{1,0:T(8,128)(2,1)}, u32[]{:S(2)}, u32[]{:S(2)}) %collective-permute-start.4) | collective-permute-done | bytes 524320 | tf_op jit(solution)/shard_map/ppermute | solution.py:295
  46.2 1.7 %slice.8 = bf16[256,512]{1,0:T(8,128)(2,1)} slice(bf16[512,512]{1,0:T(8,128)(2,1)} %collective-permute-done.4.t3.o3), slice={[256:512], [0:512]} | slice | bytes 524288 | tf_op jit(solution)/shard_map/slice | solution.py:355
  47.9 2.6 %shard_map.91 = bf16[512,512]{1,0:T(8,128)(2,1)} custom-call(bf16[512,256]{1,0:T(8,128)(2,1)S(1)} %shard_map.86.b0.c0, bf16[512,256]{1,0:T(8,128)(2,1)} %collective-permute-done.13.b1.c1, bf16[512,256]{1,0:T(8,128)(2,1)S(1)} %collective-permute-done.14.b2.c2, bf16[512,256]{1,0:T(8,128)(2,1)S(1)} %copy-done.5, bf16[256,512]{1,0:T(8,128)(2,1)S(1)} %copy-done.13, ...), custom_call_target="tpu_custom_call" | custom-call | flops 536870912 | bytes 3145728 | tf_op jit(solution)/shard_map/pallas_call | solution.py:371
  50.6 2.7 %collective-permute-start.3 = (bf16[256,512]{1,0:T(8,128)(2,1)}, bf16[256,512]{1,0:T(8,128)(2,1)S(1)}, u32[]{:S(2)}, u32[]{:S(2)}) collective-permute-start(bf16[256,512]{1,0:T(8,128)(2,1)} %copy-done.37), channel_id=1, source_target_pairs={{0,6},{1,7},{2,0},{3,1},{4,2},{5,3},{6,4},{7,5},{8,14},{9,15},{10,... | collective-permute-start | bytes 786440 | tf_op jit(solution)/shard_map/ppermute | solution.py:298
  55.8 3.1 %shard_map.89 = (bf16[192,1024]{1,0:T(8,128)(2,1)}, bf16[192,1024]{1,0:T(8,128)(2,1)}) custom-call(s32[1]{0:T(128)} %bitcast.2.where, bf16[256,512]{1,0:T(8,128)(2,1)} %collective-permute-done.6.own.t2, bf16[256,512]{1,0:T(8,128)(2,1)} %collective-permute-done.8.t2.peer, bf16[512,1024]{1,0:T(8,128)(2,1)S(1)} %copy-done.17, ...), custom_call_target="tpu_custom_call" | custom-call | flops 536870912 | bytes 4194304 | tf_op jit(solution)/shard_map/pallas_call | solution.py:397
  59.0 2.7 %collective-permute-start.12 = (bf16[192,1024]{1,0:T(8,128)(2,1)}, bf16[192,1024]{1,0:T(8,128)(2,1)}, u32[]{:S(2)}, u32[]{:S(2)}) collective-permute-start(bf16[192,1024]{1,0:T(8,128)(2,1)} %get-tuple-element.27), channel_id=1, source_target_pairs={{0,6},{1,7},{2,0},{3,1},{4,2},{5,3},{6,4},{7,5},{8,14},{9,15},{10,... | collective-permute-start | bytes 1179656 | tf_op jit(solution)/shard_map/ppermute | solution.py:298
  62.7 3.8 %shard_map.90.pre = f32[1024,512]{1,0:T(8,128)S(1)} custom-call(bf16[512,512]{1,0:T(8,128)(2,1)S(1)} %copy-done.11, bf16[512,512]{1,0:T(8,128)(2,1)S(1)} %collective-permute-done.1.late_hi.hi.a1.first_hi, bf16[512,256]{1,0:T(8,128)(2,1)} %collective-permute-done.9.far.a2, bf16[512,512]{1,0:T(8,128)(2,1)S(1)} %collective-permute-done.late_lo.lo.a3.first_lo, ...), custom_call_target="tpu_custom_call" | custom-call | flops 1073741824 | bytes 7340032 | tf_op jit(solution)/shard_map/pallas_call | solution.py:383
  66.6 4.2 %shard_map.92 = (f32[64,512]{1,0:T(8,128)S(1)}, bf16[32,8,128]{2,1,0:T(8,128)(2,1)S(1)}) custom-call(f32[1024,512]{1,0:T(8,128)S(1)} %shard_map.90.pre, bf16[576,512]{1,0:T(8,128)(2,1)} %collective-permute-done.10.got_a, bf16[512,512]{1,0:T(8,128)(2,1)} %collective-permute-done.15.got_b, s32[64,512]{1,0:T(8,128)S(1)} %reshape.25.idx, ...), custom_call_target="tpu_custom_call" | custom-call | flops 805306368 | bytes 4194304 | tf_op jit(solution)/shard_map/pallas_call | solution.py:414
  73.4 16.3 %all-to-all-start = ((bf16[32,8,128]{2,1,0:T(8,128)(2,1)}), bf16[32,8,128]{2,1,0:T(8,128)(2,1)}, u32[]{:S(2)}, u32[]{:S(2)}) async-start(bf16[32,8,128]{2,1,0:T(8,128)(2,1)} %copy-done.31), calls=%async_computation | async-start | bytes 131072 | tf_op jit(solution)/shard_map/all_to_all | solution.py:449
  93.7 4.2 %shard_map.93 = (f32[256,1024]{1,0:T(8,128)S(1)}, bf16[320,1024]{1,0:T(8,128)(2,1)}, bf16[256,1024]{1,0:T(8,128)(2,1)}) custom-call(bf16[256,512]{1,0:T(8,128)(2,1)S(1)} %copy-done.26, bf16[256,512]{1,0:T(8,128)(2,1)S(1)} %copy-done.28, bf16[512,512]{1,0:T(8,128)(2,1)} %collective-permute-done.4.t3.o3, bf16[256,512]{1,0:T(8,128)(2,1)S(1)} %copy-done.14, ...), custom_call_target="tpu_custom_call" | custom-call | flops 1610612736 | bytes 7340032 | tf_op jit(solution)/shard_map/pallas_call | solution.py:430
  99.6 1.7 %shard_map.94.late = bf16[256,8,128]{2,1,0:T(8,128)(2,1)} custom-call(bf16[32,8,128]{2,1,0:T(8,128)(2,1)} %all-to-all-done.spread, bf16[256,1024]{1,0:T(8,128)(2,1)} %get-tuple-element.31.late), custom_call_target="tpu_custom_call" | custom-call | bytes 1048576 | tf_op jit(solution)/shard_map/pallas_call | solution.py:450
  101.3 10.5 %all-to-all-start.1 = ((bf16[256,8,128]{2,1,0:T(8,128)(2,1)}), bf16[256,8,128]{2,1,0:T(8,128)(2,1)}, u32[]{:S(2)}, u32[]{:S(2)}) async-start(bf16[256,8,128]{2,1,0:T(8,128)(2,1)} %shard_map.94.late), calls=%async_computation.1 | async-start | bytes 1048576 | tf_op jit(solution)/shard_map/all_to_all | solution.py:459
  114.7 1.6 %copy-done.3 = f32[1024,512]{1,0:T(8,128)S(1)} copy-done((f32[1024,512]{1,0:T(8,128)S(1)}, f32[1024,512]{1,0:T(8,128)}, u32[]{:S(2)}) %copy-start.3) | copy-done | bytes 2097176
  117.2 5.2 %shard_map.96 = f32[512,1024]{1,0:T(8,128)} custom-call(f32[1024,512]{1,0:T(8,128)S(1)} %copy-done.3, bf16[576,512]{1,0:T(8,128)(2,1)} %collective-permute-done.10.got_a, bf16[512,512]{1,0:T(8,128)(2,1)} %collective-permute-done.15.got_b, f32[64,512]{1,0:T(8,128)S(1)} %copy-done.30, s32[64,512]{1,0:T(8,128)S(1)} %reshape.25.idx, ...), custom_call_target="tpu_custom_call" | custom-call | flops 805306368 | bytes 6291456 | tf_op jit(solution)/shard_map/pallas_call | solution.py:461
  122.4 8.9 %collective-permute-done.17.hi = bf16[256,1024]{1,0:T(8,128)(2,1)S(1)} collective-permute-done((bf16[256,1024]{1,0:T(8,128)(2,1)}, bf16[256,1024]{1,0:T(8,128)(2,1)S(1)}, u32[]{:S(2)}, u32[]{:S(2)}) %collective-permute-start.17) | collective-permute-done | bytes 524320 | tf_op jit(solution)/shard_map/ppermute | solution.py:298
  137.7 10.8 %shard_map.95 = (bf16[256,1024]{1,0:T(8,128)(2,1)}, bf16[512,1024]{1,0:T(8,128)(2,1)}) custom-call(s32[1]{0:T(128)} %bitcast.where, bf16[256,4096]{1,0:T(8,128)(2,1)S(1)} %copy-done.1, f32[256,1024]{1,0:T(8,128)S(1)} %copy-done.39, bf16[192,1024]{1,0:T(8,128)(2,1)} %get-tuple-element.26.late.own, bf16[192,1024]{1,0:T(8,128)(2,1)} %collective-permute-done.12.hi.near_hi, ...), custom_call_target="tpu_custom_call" | custom-call | flops 4294967296 | bytes 8388608 | tf_op jit(solution)/shard_map/pallas_call | solution.py:471
  (111 shorter events, 35.9 us)
Async XLA Ops:
  0.6 34.3 %collective-permute-start.5 = (bf16[512,1024]{1,0:T(8,128)(2,1)}, bf16[512,1024]{1,0:T(8,128)(2,1)}, u32[]{:S(2)}, u32[]{:S(2)}) collective-permute-start(bf16[512,1024]{1,0:T(8,128)(2,1)} %weight.1), channel_id=1, source_target_pairs={{0,1},{1,0},{2,3},{3,2},{4,5},{5,4},{6,7},{7,6},{8,9},{9,8},{10,11... | collective-permute-start | bytes 3145736 | tf_op jit(solution)/shard_map/ppermute | solution.py:300
  5.5 22.7 %copy-start.9 = (bf16[512,512]{1,0:T(8,128)(2,1)}, bf16[512,512]{1,0:T(8,128)(2,1)S(1)}, u32[]{:S(2)}) copy-start(bf16[512,512]{1,0:T(8,128)(2,1)S(1)} %get-tuple-element.19.sent) | copy-start | bytes 1572868
  5.6 23.6 %copy-start.12 = (bf16[256,512]{1,0:T(8,128)(2,1)}, bf16[256,512]{1,0:T(8,128)(2,1)S(1)}, u32[]{:S(2)}) copy-start(bf16[256,512]{1,0:T(8,128)(2,1)S(1)} %get-tuple-element.24.t0.p0) | copy-start | bytes 786436
  5.6 22.6 %copy-start.1 = (bf16[256,4096]{1,0:T(8,128)(2,1)S(1)}, bf16[256,4096]{1,0:T(8,128)(2,1)}, u32[]{:S(2)}) copy-start(bf16[256,4096]{1,0:T(8,128)(2,1)} %tok.1) | copy-start | bytes 6291460
  5.6 13.6 %collective-permute-start = (bf16[512,512]{1,0:T(8,128)(2,1)S(1)}, bf16[512,512]{1,0:T(8,128)(2,1)S(1)}, u32[]{:S(2)}, u32[]{:S(2)}) collective-permute-start(bf16[512,512]{1,0:T(8,128)(2,1)S(1)} %get-tuple-element.19.sent), channel_id=1, source_target_pairs={{0,2},{1,3},{2,4},{3,5},{4,6},{5,7},{6,0},{7,1},{8,10},{9,11},{10,... | collective-permute-start | bytes 1572872 | tf_op jit(solution)/shard_map/ppermute | solution.py:295
  6.9 12.3 %collective-permute-start.1 = (bf16[512,512]{1,0:T(8,128)(2,1)S(1)}, bf16[512,512]{1,0:T(8,128)(2,1)S(1)}, u32[]{:S(2)}, u32[]{:S(2)}) collective-permute-start(bf16[512,512]{1,0:T(8,128)(2,1)S(1)} %get-tuple-element.20), channel_id=1, source_target_pairs={{0,6},{1,7},{2,0},{3,1},{4,2},{5,3},{6,4},{7,5},{8,14},{9,15},{10,... | collective-permute-start | bytes 1572872 | tf_op jit(solution)/shard_map/ppermute | solution.py:298
  8.5 16.4 %collective-permute-start.7 = (bf16[256,512]{1,0:T(8,128)(2,1)S(1)}, bf16[256,512]{1,0:T(8,128)(2,1)}, u32[]{:S(2)}, u32[]{:S(2)}) collective-permute-start(bf16[256,512]{1,0:T(8,128)(2,1)S(1)} %get-tuple-element.25), channel_id=1, source_target_pairs={{0,6},{1,7},{2,0},{3,1},{4,2},{5,3},{6,4},{7,5},{8,14},{9,15},{10,... | collective-permute-start | bytes 786440 | tf_op jit(solution)/shard_map/ppermute | solution.py:298
  19.4 8.8 %collective-permute-start.2 = (bf16[512,256]{1,0:T(8,128)(2,1)S(1)}, bf16[512,256]{1,0:T(8,128)(2,1)S(1)}, u32[]{:S(2)}, u32[]{:S(2)}) collective-permute-start(bf16[512,256]{1,0:T(8,128)(2,1)S(1)} %shard_map.86.b0.c0), channel_id=1, source_target_pairs={{0,2},{1,3},{2,4},{3,5},{4,6},{5,7},{6,0},{7,1},{8,10},{9,11},{10,... | collective-permute-start | bytes 786440 | tf_op jit(solution)/shard_map/ppermute | solution.py:295
  24.8 8.6 %collective-permute-start.8 = (bf16[256,512]{1,0:T(8,128)(2,1)}, bf16[256,512]{1,0:T(8,128)(2,1)}, u32[]{:S(2)}, u32[]{:S(2)}) collective-permute-start(bf16[256,512]{1,0:T(8,128)(2,1)} %collective-permute-done.7), channel_id=1, source_target_pairs={{0,6},{1,7},{2,0},{3,1},{4,2},{5,3},{6,4},{7,5},{8,14},{9,15},{10,... | collective-permute-start | bytes 786440 | tf_op jit(solution)/shard_map/ppermute | solution.py:298
  28.2 6.7 %collective-permute-start.9 = (bf16[512,256]{1,0:T(8,128)(2,1)}, bf16[512,256]{1,0:T(8,128)(2,1)}, u32[]{:S(2)}, u32[]{:S(2)}) collective-permute-start(bf16[512,256]{1,0:T(8,128)(2,1)} %slice.9), channel_id=1, source_target_pairs={{0,2},{1,3},{2,4},{3,5},{4,6},{5,7},{6,0},{7,1},{8,10},{9,11},{10,... | collective-permute-start | bytes 786440 | tf_op jit(solution)/shard_map/ppermute | solution.py:295
  29.8 16.4 %collective-permute-start.4 = (bf16[512,512]{1,0:T(8,128)(2,1)}, bf16[512,512]{1,0:T(8,128)(2,1)}, u32[]{:S(2)}, u32[]{:S(2)}) collective-permute-start(bf16[512,512]{1,0:T(8,128)(2,1)} %get-tuple-element.23), channel_id=1, source_target_pairs={{0,2},{1,3},{2,4},{3,5},{4,6},{5,7},{6,0},{7,1},{8,10},{9,11},{10,... | collective-permute-start | bytes 1572872 | tf_op jit(solution)/shard_map/ppermute | solution.py:295
  30.0 9.6 %collective-permute-start.13 = (bf16[512,256]{1,0:T(8,128)(2,1)S(1)}, bf16[512,256]{1,0:T(8,128)(2,1)}, u32[]{:S(2)}, u32[]{:S(2)}) collective-permute-start(bf16[512,256]{1,0:T(8,128)(2,1)S(1)} %shard_map.86.b0.c0), channel_id=1, source_target_pairs={{0,6},{1,7},{2,0},{3,1},{4,2},{5,3},{6,4},{7,5},{8,14},{9,15},{10,... | collective-permute-start | bytes 786440 | tf_op jit(solution)/shard_map/ppermute | solution.py:298
  39.5 15.1 %collective-permute-start.10 = (bf16[576,512]{1,0:T(8,128)(2,1)}, bf16[576,512]{1,0:T(8,128)(2,1)}, u32[]{:S(2)}, u32[]{:S(2)}) collective-permute-start(bf16[576,512]{1,0:T(8,128)(2,1)} %shard_map.88), channel_id=1, source_target_pairs={{0,1},{1,0},{2,3},{3,2},{4,5},{5,4},{6,7},{7,6},{8,9},{9,8},{10,11... | collective-permute-start | bytes 1769480 | tf_op jit(solution)/shard_map/ppermute | solution.py:370
  39.5 8.3 %collective-permute-start.14 = (bf16[512,256]{1,0:T(8,128)(2,1)}, bf16[512,256]{1,0:T(8,128)(2,1)S(1)}, u32[]{:S(2)}, u32[]{:S(2)}) collective-permute-start(bf16[512,256]{1,0:T(8,128)(2,1)} %collective-permute-done.13.b1.c1), channel_id=1, source_target_pairs={{0,6},{1,7},{2,0},{3,1},{4,2},{5,3},{6,4},{7,5},{8,14},{9,15},{10,... | collective-permute-start | bytes 786440 | tf_op jit(solution)/shard_map/ppermute | solution.py:298
  47.9 6.7 %collective-permute-start.6 = (bf16[256,512]{1,0:T(8,128)(2,1)}, bf16[256,512]{1,0:T(8,128)(2,1)}, u32[]{:S(2)}, u32[]{:S(2)}) collective-permute-start(bf16[256,512]{1,0:T(8,128)(2,1)} %slice.8), channel_id=1, source_target_pairs={{0,2},{1,3},{2,4},{3,5},{4,6},{5,7},{6,0},{7,1},{8,10},{9,11},{10,... | collective-permute-start | bytes 786440 | tf_op jit(solution)/shard_map/ppermute | solution.py:295
  50.5 16.0 %collective-permute-start.15 = (bf16[512,512]{1,0:T(8,128)(2,1)}, bf16[512,512]{1,0:T(8,128)(2,1)}, u32[]{:S(2)}, u32[]{:S(2)}) collective-permute-start(bf16[512,512]{1,0:T(8,128)(2,1)} %shard_map.91), channel_id=1, source_target_pairs={{0,1},{1,0},{2,3},{3,2},{4,5},{5,4},{6,7},{7,6},{8,9},{9,8},{10,11... | collective-permute-start | bytes 1572872 | tf_op jit(solution)/shard_map/ppermute | solution.py:381
  50.6 11.1 %collective-permute-start.3 = (bf16[256,512]{1,0:T(8,128)(2,1)}, bf16[256,512]{1,0:T(8,128)(2,1)S(1)}, u32[]{:S(2)}, u32[]{:S(2)}) collective-permute-start(bf16[256,512]{1,0:T(8,128)(2,1)} %copy-done.37), channel_id=1, source_target_pairs={{0,6},{1,7},{2,0},{3,1},{4,2},{5,3},{6,4},{7,5},{8,14},{9,15},{10,... | collective-permute-start | bytes 786440 | tf_op jit(solution)/shard_map/ppermute | solution.py:298
  59.0 30.8 %collective-permute-start.11 = (bf16[192,1024]{1,0:T(8,128)(2,1)}, bf16[192,1024]{1,0:T(8,128)(2,1)}, u32[]{:S(2)}, u32[]{:S(2)}) collective-permute-start(bf16[192,1024]{1,0:T(8,128)(2,1)} %get-tuple-element.26.late.own), channel_id=1, source_target_pairs={{0,2},{1,3},{2,4},{3,5},{4,6},{5,7},{6,0},{7,1},{8,10},{9,11},{10,... | collective-permute-start | bytes 1179656 | tf_op jit(solution)/shard_map/ppermute | solution.py:295
  59.0 30.8 %collective-permute-start.12 = (bf16[192,1024]{1,0:T(8,128)(2,1)}, bf16[192,1024]{1,0:T(8,128)(2,1)}, u32[]{:S(2)}, u32[]{:S(2)}) collective-permute-start(bf16[192,1024]{1,0:T(8,128)(2,1)} %get-tuple-element.27), channel_id=1, source_target_pairs={{0,6},{1,7},{2,0},{3,1},{4,2},{5,3},{6,4},{7,5},{8,14},{9,15},{10,... | collective-permute-start | bytes 1179656 | tf_op jit(solution)/shard_map/ppermute | solution.py:298
  66.5 23.3 %copy-start.14 = (bf16[256,512]{1,0:T(8,128)(2,1)S(1)}, bf16[256,512]{1,0:T(8,128)(2,1)}, u32[]{:S(2)}) copy-start(bf16[256,512]{1,0:T(8,128)(2,1)} %copy-done.12) | copy-start | bytes 786436
  73.4 26.2 %all-to-all-start = ((bf16[32,8,128]{2,1,0:T(8,128)(2,1)}), bf16[32,8,128]{2,1,0:T(8,128)(2,1)}, u32[]{:S(2)}, u32[]{:S(2)}) async-start(bf16[32,8,128]{2,1,0:T(8,128)(2,1)} %copy-done.31), calls=%async_computation | async-start | bytes 131072 | tf_op jit(solution)/shard_map/all_to_all | solution.py:449
  101.3 32.9 %all-to-all-start.1 = ((bf16[256,8,128]{2,1,0:T(8,128)(2,1)}), bf16[256,8,128]{2,1,0:T(8,128)(2,1)}, u32[]{:S(2)}, u32[]{:S(2)}) async-start(bf16[256,8,128]{2,1,0:T(8,128)(2,1)} %shard_map.94.late), calls=%async_computation.1 | async-start | bytes 1048576 | tf_op jit(solution)/shard_map/all_to_all | solution.py:459
  111.9 21.5 %collective-permute-start.16 = (bf16[320,1024]{1,0:T(8,128)(2,1)}, bf16[320,1024]{1,0:T(8,128)(2,1)S(1)}, u32[]{:S(2)}, u32[]{:S(2)}) collective-permute-start(bf16[320,1024]{1,0:T(8,128)(2,1)} %get-tuple-element.30), channel_id=1, source_target_pairs={{0,2},{1,3},{2,4},{3,5},{4,6},{5,7},{6,0},{7,1},{8,10},{9,11},{10,... | collective-permute-start | bytes 1966088 | tf_op jit(solution)/shard_map/ppermute | solution.py:295
  113.4 18.0 %collective-permute-start.17 = (bf16[256,1024]{1,0:T(8,128)(2,1)}, bf16[256,1024]{1,0:T(8,128)(2,1)S(1)}, u32[]{:S(2)}, u32[]{:S(2)}) collective-permute-start(bf16[256,1024]{1,0:T(8,128)(2,1)} %get-tuple-element.31.late), channel_id=1, source_target_pairs={{0,6},{1,7},{2,0},{3,1},{4,2},{5,3},{6,4},{7,5},{8,14},{9,15},{10,... | collective-permute-start | bytes 1572872 | tf_op jit(solution)/shard_map/ppermute | solution.py:298
  (36 other events, 145.6 us)

commit v3 on v2

v3 whole, which is shorter than its diff:
```python
import jax
import jax.numpy as jnp
import numpy as np
from jax import lax
from jax.experimental import pallas as pl
from jax.experimental.pallas import tpu as pltpu
from jax.sharding import PartitionSpec as P

beta_decay = 0.9
step_rate = 0.5
ROWS = 512
KV = 1024
TOK = 256
BLOCK = 64
KEEP = 4
HALF = KV // 2
GROUP = 256
STEPS = KV // GROUP
PICKS = KV // BLOCK * KEEP
LANES = 128
PACK = 16
REPS = 32
VMEM_LIMIT = 16 * 1024 * 1024
VMEM_MOST = 60 * 1024 * 1024


def dct_group():
    n = np.arange(BLOCK, dtype=np.float64)
    single = np.cos(np.pi * (2.0 * n[None, :] + 1.0) * n[:, None] / (2 * BLOCK))
    single *= np.where(n[:, None] == 0, np.sqrt(1.0 / BLOCK), np.sqrt(2.0 / BLOCK))
    return np.kron(np.eye(GROUP // BLOCK), single).astype(np.float32)


def split_pair(values):
    high = values.astype(jnp.bfloat16)
    return high, (values - high.astype(jnp.float32)).astype(jnp.bfloat16)


def mix(left, right, dims):
    return lax.dot_general(left, right, (dims, ((), ())), preferred_element_type=jnp.float32)


def three_pass(left_pair, right_pair, dims):
    return (
        mix(left_pair[0], right_pair[0], dims)
        + mix(left_pair[0], right_pair[1], dims)
        + mix(left_pair[1], right_pair[0], dims)
    )


def expand_block(index_rows, value_rows, width):
    freq = lax.broadcasted_iota(jnp.int32, (BLOCK, width), 0)
    dense = jnp.zeros((BLOCK, width), jnp.float32)
    for j in range(KEEP):
        dense = jnp.where(index_rows[j] == freq, value_rows[j], dense)
    return dense


def spread_row(tile, row):
    return jnp.broadcast_to(tile[row : row + 1, :], (PACK, LANES)).astype(jnp.bfloat16)


def expand_tile(indices, values, dense, first, cols):
    freq = lax.broadcasted_iota(jnp.int32, (PACK, LANES), 0).astype(jnp.float32)
    for half in range(2):
        at = [spread_row(indices, half * KEEP + j) for j in range(KEEP)]
        have = [spread_row(values, half * KEEP + j) for j in range(KEEP)]
        for part in range(BLOCK // PACK):
            here = (freq + part * PACK).astype(jnp.bfloat16)
            tile = jnp.zeros((PACK, LANES), jnp.bfloat16)
            for j in range(KEEP):
                tile = jnp.where(at[j] == here, have[j], tile)
            start = first + half * BLOCK + part * PACK
            dense[start : start + PACK, cols] = tile


def four_products(cots, toks):
    total = jnp.dot(cots[0], toks[0], preferred_element_type=jnp.float32)
    for c, t in zip(cots[1:], toks[1:]):
        total += jnp.dot(c, t, preferred_element_type=jnp.float32)
    return total


def cot_of(message):
    return message[:, :TOK]


def tok_of(message):
    return jnp.concatenate([message[:TOK, TOK:], message[TOK:, TOK:]], axis=1)


def flat_index(idx):
    rows = [idx[b].astype(jnp.float32) for b in range(KV // BLOCK)]
    return jnp.concatenate(rows, axis=0).astype(jnp.bfloat16)


def pack_first_kernel(where, cot, t0, t1, t2, t3, to_up, to_far, to_down, mine):
    turned = cot[...].T
    for out, t in ((to_up, t1), (to_far, t2), (to_down, t3)):
        out[:, :TOK] = turned
        out[:TOK, TOK:] = t[:, :TOK]
        out[TOK:, TOK:] = t[:, TOK:]
    mine[...] = t0[...]


def pack_second_kernel(cot, late_lo, late_hi, out):
    out[...] = cot[...].T


def pack_own_kernel(where, t0, t1, t2, t3, late_lo, late_hi, mine, to_up, to_far, to_down):
    for out, t in ((mine, t0), (to_up, t1), (to_far, t2), (to_down, t3)):
        out[...] = t[...]


def partial_first_kernel(sent, hi, far, lo, t0, idx, early, turned, out):
    cots = (cot_of(sent), cot_of(hi), cot_of(far), cot_of(lo))
    toks = (t0[...], tok_of(hi), tok_of(far), tok_of(lo))
    out[:HALF, :] = four_products(cots, toks).astype(out.dtype)
    out[HALF:, :] = flat_index(idx)


def partial_second_kernel(c0, c1, c2, c3, t0, hi, far, lo, out):
    cots = (c0[...], c1[...], c2[...], c3[...])
    toks = (t0[...], tok_of(hi), tok_of(far), tok_of(lo))
    out[...] = four_products(cots, toks).astype(out.dtype)


def own_kernel(a0, a1, a2, a3, b0, b1, b2, b3, t0, t1, t2, t3, mom, out):
    step = pl.program_id(0)
    toks = (t0[...], t1[...], t2[...], t3[...])

    @pl.when(step < STEPS // 2)
    def _():
        cots = (cot_of(a0), cot_of(a1), cot_of(a2), cot_of(a3))
        out[...] = four_products(cots, toks) + beta_decay * mom[...].T

    @pl.when(step >= STEPS // 2)
    def _():
        cots = (b0[...], b1[...], b2[...], b3[...])
        out[...] = four_products(cots, toks) + beta_decay * mom[...].T


def pick_rows(moment, idx, ch, cl):
    spectrum = three_pass((ch[...], cl[...]), split_pair(moment), ((1,), (0,)))
    freq = lax.broadcasted_iota(jnp.int32, (BLOCK, ROWS), 0)
    rows = []
    for b in range(GROUP // BLOCK):
        part = spectrum[b * BLOCK : (b + 1) * BLOCK, :]
        for j in range(KEEP):
            here = idx[b, j : j + 1, :] == freq
            rows.append(jnp.sum(jnp.where(here, part, 0.0), axis=0, keepdims=True))
    return rows


def pick_kernel(pre, got_a, got_b, idx, ch, cl, late, moment, tiles):
    first = pl.program_id(0) < STEPS // 2
    got = jnp.where(first, got_a[...], got_b[...]).astype(jnp.float32)
    total = pre[...] + got
    moment[...] = total
    values = jnp.concatenate(pick_rows(total, idx, ch, cl), axis=0)
    for t in range(GROUP // BLOCK * KEEP // 8):
        for q in range(ROWS // LANES):
            tile = values[t * 8 : (t + 1) * 8, q * LANES : (q + 1) * LANES]
            tiles[t * (ROWS // LANES) + q] = tile.astype(tiles.dtype)


def share_kernel(spread, late_0, late_1, late_2, out):
    total = jnp.sum(spread[...].astype(jnp.float32), axis=0, keepdims=True)
    out[...] = jnp.broadcast_to(total, out.shape).astype(out.dtype)


def residual_kernel(moment, idx, ch, cl, late, out):
    total = moment[...]
    rows = pick_rows(total, idx, ch, cl)
    parts = []
    for b in range(GROUP // BLOCK):
        at = [idx[b, j : j + 1, :] for j in range(KEEP)]
        parts.append(expand_block(at, rows[b * KEEP : (b + 1) * KEEP], ROWS))
    kept = jnp.concatenate(parts, axis=0)
    back = three_pass((ch[...], cl[...]), split_pair(kept), ((0,), (0,)))
    out[...] = (total - back).T


def base_kernel(where, o0, o1, o2, o3, p0, p1, p2, p3, w_own, w_peer, idx, got_a, *outs):
    mine, theirs = flat_index(idx), got_a[HALF:, :]
    first = (where[0] & 1) == 0
    left, right = jnp.where(first, mine, theirs), jnp.where(first, theirs, mine)
    peers = (p0[...], tok_of(p1), tok_of(p2), tok_of(p3))
    for own, peer, out in zip((o0, o1, o2, o3), peers, outs):
        total = jnp.dot(own[...], w_own[...], preferred_element_type=jnp.float32)
        total += jnp.dot(peer, w_peer[...], preferred_element_type=jnp.float32)
        out[:TOK, :] = total.astype(out.dtype)
        out[TOK:, :ROWS] = left
        out[TOK:, ROWS:] = right


def forward_kernel(where, tok, own, hi, far, lo, tot, weight, ch, cl, out, out_weight, dense, mixed):
    step = pl.program_id(0)
    tail = slice(TOK, TOK + PICKS)
    near = jnp.where(step == 0, own[tail, :], hi[tail, :])
    away = jnp.where(step == 2, far[tail, :], lo[tail, :])
    pairs = jnp.where(step < 2, near, away).astype(jnp.float32)

    @pl.when(step == 0)
    def _():
        mixed[...] = jnp.zeros_like(mixed)

    for g in range(STEPS):
        for t in range(2 * g, 2 * g + 2):
            for f in range(2):
                for q in range(ROWS // LANES):
                    cols = slice(f * ROWS + q * LANES, f * ROWS + (q + 1) * LANES)
                    values = tot[t * (ROWS // LANES) + q, f].astype(jnp.float32)
                    expand_tile(pairs[t * 8 : (t + 1) * 8, cols], values, dense, t * 2 * BLOCK, cols)
        span = slice(g * GROUP, (g + 1) * GROUP)
        mixed[span, :] += mix(dense[span, :], tok[...], ((1,), (1,)))

    @pl.when(step == 0)
    def _():
        cols = pl.ds(pl.multiple_of((where[0] & 1) * ROWS, ROWS), ROWS)
        for g in range(STEPS):
            span = slice(g * GROUP, (g + 1) * GROUP)
            turned = dense[span, cols].T
            delta = mix(turned, ch[...], ((1,), (0,))) + mix(turned, cl[...], ((1,), (0,)))
            new = weight[:, span].astype(jnp.float32) - (step_rate / REPS) * delta
            out_weight[:, span] = new.astype(out_weight.dtype)

    @pl.when(step == 3)
    def _():
        for g in range(STEPS):
            span = slice(g * GROUP, (g + 1) * GROUP)
            delta = three_pass(split_pair(mixed[span, :].T), (ch[...], cl[...]), ((1,), (0,)))
            base = own[:TOK, span].astype(jnp.float32) + hi[:TOK, span].astype(jnp.float32)
            base += far[:TOK, span].astype(jnp.float32) + lo[:TOK, span].astype(jnp.float32)
            out[:, span] = (base - (step_rate / REPS) * delta).astype(out.dtype)


def params(limit=VMEM_LIMIT):
    return pltpu.CompilerParams(vmem_limit_bytes=limit)


def cost(flops, mib):
    return pl.CostEstimate(flops=int(flops), bytes_accessed=int(mib * (1 << 20)), transcendentals=0)


def whole(*shape):
    return pl.BlockSpec(shape, lambda c, *_: (0,) * len(shape))


def by_row(rows, width):
    return pl.BlockSpec((rows, width), lambda c: (c, 0))


def by_col(rows, width):
    return pl.BlockSpec((rows, width), lambda c: (0, c))


def first_half(rows, width):
    return pl.BlockSpec((rows, width), lambda c: (jnp.minimum(c, STEPS // 2 - 1), 0))


def second_half(rows, width):
    return pl.BlockSpec((rows, width), lambda c: (jnp.maximum(c - STEPS // 2, 0), 0))


AFTER = pl.BlockSpec(memory_space=pl.ANY)
BASIS = [whole(GROUP, GROUP)] * 2
GOT = [first_half(GROUP, ROWS), second_half(GROUP, ROWS)]
BF16, F32 = jnp.bfloat16, jnp.float32
INDEX = pl.BlockSpec((KV // BLOCK, KEEP, ROWS), lambda c, *_: (0, 0, 0))
INDEX_STEP = pl.BlockSpec((GROUP // BLOCK, KEEP, ROWS), lambda c: (c, 0, 0))
MESSAGE = whole(HALF, 2 * TOK)
PIECE = whole(TOK, ROWS)


def shape(*dims, dtype=BF16):
    return jax.ShapeDtypeStruct(dims, dtype)


def body(tokens, cotangent, weight, momentum, kept_index):
    basis = dct_group()
    high = jnp.asarray(basis).astype(BF16)
    low = (jnp.asarray(basis) - high.astype(F32)).astype(BF16)
    place = lax.axis_index("fsdp").astype(jnp.int32).reshape(1)
    index_t = jnp.transpose(kept_index, (1, 2, 0))

    def up(x):
        return lax.ppermute(x, "fsdp", [(i, (i + 2) % 8) for i in range(8)])

    def down(x):
        return lax.ppermute(x, "fsdp", [(i, (i + 6) % 8) for i in range(8)])

    def across(x):
        return lax.ppermute(x, "fsdp", [(i, (i + 4) % 8) for i in range(8)])

    def swap(x):
        return lax.ppermute(x, "fsdp", [(i, i ^ 1) for i in range(8)])

    def columns(flip):
        return [pl.BlockSpec((TOK, ROWS), lambda c, s, d=d: (0, ((s[0] ^ flip) + 2 * d) & 7)) for d in range(4)]

    weight_peer = swap(weight)

    first_up, first_far, first_down, peer_0 = pl.pallas_call(
        pack_first_kernel,
        grid_spec=pltpu.PrefetchScalarGridSpec(
            num_scalar_prefetch=1,
            grid=(1,),
            in_specs=[whole(TOK, HALF)] + columns(1),
            out_specs=[MESSAGE] * 3 + [PIECE],
        ),
        out_shape=[shape(HALF, 2 * TOK)] * 3 + [shape(TOK, ROWS)],
        compiler_params=params(),
        cost_estimate=cost(0, 4),
    )(place, cotangent, tokens, tokens, tokens, tokens)
    first_lo = up(first_up)
    first_hi = down(first_down)
    first_x = across(first_far)
    firsts = (first_up, first_hi, first_x, first_lo)

    cot_b = pl.pallas_call(
        pack_second_kernel,
        grid=(1,),
        in_specs=[pl.BlockSpec((TOK, HALF), lambda c: (0, 1)), AFTER, AFTER],
        out_specs=whole(HALF, TOK),
        out_shape=shape(HALF, TOK),
        compiler_params=params(),
        cost_estimate=cost(0, 1),
    )(cotangent, first_lo, first_hi)
    b_lo, b_hi, b_far = up(cot_b), down(cot_b), across(cot_b)
    cots_b = (cot_b, b_hi, b_far, b_lo)

    own_0, own_up, own_across, own_down = pl.pallas_call(
        pack_own_kernel,
        grid_spec=pltpu.PrefetchScalarGridSpec(
            num_scalar_prefetch=1,
            grid=(1,),
            in_specs=columns(0) + [AFTER, AFTER],
            out_specs=[PIECE] * 4,
        ),
        out_shape=[shape(TOK, ROWS)] * 4,
        compiler_params=params(),
        cost_estimate=cost(0, 2),
    )(place, tokens, tokens, tokens, tokens, b_lo, b_hi)
    owns = (own_0, down(own_down), across(own_across), up(own_up))

    partial_a = pl.pallas_call(
        partial_first_kernel,
        grid=(1,),
        in_specs=[MESSAGE] * 4 + [PIECE, INDEX, AFTER, AFTER],
        out_specs=whole(HALF + PICKS, ROWS),
        out_shape=shape(HALF + PICKS, ROWS),
        compiler_params=params(),
        cost_estimate=cost(KV * KV * ROWS, 3),
    )(*firsts, peer_0, index_t, weight_peer, cot_b)
    got_a = swap(partial_a)
    partial_b = pl.pallas_call(
        partial_second_kernel,
        grid=(1,),
        in_specs=[whole(HALF, TOK)] * 4 + [PIECE] + [MESSAGE] * 3,
        out_specs=whole(HALF, ROWS),
        out_shape=shape(HALF, ROWS),
        compiler_params=params(),
        cost_estimate=cost(KV * KV * ROWS, 3),
    )(*cots_b, peer_0, *firsts[1:])
    got_b = swap(partial_b)

    pre = pl.pallas_call(
        own_kernel,
        grid=(STEPS,),
        in_specs=[first_half(GROUP, 2 * TOK)] * 4
        + [second_half(GROUP, TOK)] * 4
        + [PIECE] * 4
        + [by_col(ROWS, GROUP)],
        out_specs=by_row(GROUP, ROWS),
        out_shape=shape(KV, ROWS, dtype=F32),
        compiler_params=params(),
        cost_estimate=cost(2 * KV * KV * ROWS, 7),
    )(*firsts, *cots_b, *owns, momentum[0])

    base, base_up, base_across, base_down = pl.pallas_call(
        base_kernel,
        grid_spec=pltpu.PrefetchScalarGridSpec(
            num_scalar_prefetch=1,
            grid=(1,),
            in_specs=[PIECE] * 5
            + [MESSAGE] * 3
            + [whole(ROWS, KV)] * 2
            + [INDEX, whole(HALF + PICKS, ROWS)],
            out_specs=[whole(TOK + PICKS, KV)] * 4,
        ),
        out_shape=[shape(TOK + PICKS, KV)] * 4,
        compiler_params=params(2 * VMEM_LIMIT),
        cost_estimate=cost(4 * KV * KV * ROWS, 7),
    )(place, *owns, peer_0, *firsts[1:], weight, weight_peer, index_t, got_a)
    base_lo, base_hi, base_far = up(base_up), down(base_down), across(base_across)

    moment, tiles = pl.pallas_call(
        pick_kernel,
        grid=(STEPS,),
        in_specs=[by_row(GROUP, ROWS)] + GOT + [INDEX_STEP] + BASIS + [AFTER],
        out_specs=[by_row(GROUP, ROWS), pl.BlockSpec((REPS // STEPS, 8, LANES), lambda c: (c, 0, 0))],
        out_shape=[shape(KV, ROWS, dtype=F32), shape(REPS, 8, LANES)],
        compiler_params=params(),
        cost_estimate=cost(6 * KV * GROUP * ROWS, 6),
    )(pre, got_a, got_b, index_t, high, low, base)

    spread = lax.all_to_all(tiles, "rep", 0, 0)
    copies = pl.pallas_call(
        share_kernel,
        grid=(1,),
        in_specs=[whole(REPS, 8, LANES), AFTER, AFTER, AFTER],
        out_specs=whole(REPS * 8, 8, LANES),
        out_shape=shape(REPS * 8, 8, LANES),
        compiler_params=params(),
        cost_estimate=cost(0, 1),
    )(spread, base_lo, base_hi, base_far)
    totals = lax.all_to_all(copies, ("rep", "fsdp"), 0, 0).reshape(REPS, 8, 8, LANES)

    new_momentum = pl.pallas_call(
        residual_kernel,
        grid=(STEPS,),
        in_specs=[by_row(GROUP, ROWS), INDEX_STEP] + BASIS + [AFTER],
        out_specs=by_col(ROWS, GROUP),
        out_shape=shape(ROWS, KV, dtype=F32),
        compiler_params=params(VMEM_MOST),
        cost_estimate=cost(12 * KV * GROUP * ROWS, 5),
    )(moment, index_t, high, low, copies)

    projected, new_weight = pl.pallas_call(
        forward_kernel,
        grid_spec=pltpu.PrefetchScalarGridSpec(
            num_scalar_prefetch=1,
            grid=(4,),
            in_specs=[pl.BlockSpec((TOK, 2 * ROWS), lambda c, s: (0, ((s[0] >> 1) + c) & 3))]
            + [whole(TOK + PICKS, KV)] * 4
            + [pl.BlockSpec((REPS, 2, 8, LANES), lambda c, s: (0, ((s[0] >> 1) + c) & 3, 0, 0))]
            + [whole(ROWS, KV)]
            + BASIS,
            out_specs=[whole(TOK, KV), whole(ROWS, KV)],
            scratch_shapes=[pltpu.VMEM((KV, 2 * ROWS), BF16), pltpu.VMEM((KV, TOK), F32)],
        ),
        out_shape=[shape(TOK, KV), shape(ROWS, KV)],
        compiler_params=params(VMEM_MOST),
        cost_estimate=cost(8 * KV * KV * ROWS, 8),
    )(place, tokens, base, base_hi, base_far, base_lo, totals, weight, high, low)
    return (projected, new_weight, new_momentum[None])


def solution(mesh):
    in_specs = (
        P(("rep", "fsdp"), None),
        P(("rep", "fsdp"), None),
        P("fsdp", None),
        P("rep", "fsdp", None),
        P("fsdp", None, None),
    )
    out_specs = (P(("rep", "fsdp"), None), P("fsdp", None), P("rep", "fsdp", None))
    return jax.shard_map(body, mesh=mesh, in_specs=in_specs, out_specs=out_specs, check_vma=False)
```

time: 150 us -> 141 us (0.940)
  blocking collectives: 0 us -> 25.4 us
  local copies, waits for them, and re-layouts: 26.1 us -> 4.79 us
  starting transfers between devices: 50.6 us -> 31.4 us
  waiting for transfers between devices: 31.4 us -> 48.3 us
  Pallas kernels: 39.4 us -> 29.5 us
    all_to_all x0 -> x1, blocking collectives: none -> 25.4 us  [body(): spread = lax.all_to_all(tiles, 'rep', 0, 0)]
    unnamed x80 -> x28, local copies, waits for them, and re-layouts: 22.7 us -> 4.79 us
    all_to_all x1 -> x0, starting transfers between devices: 16.3 us -> none  [body(): spread = lax.all_to_all(tiles, 'rep', 0, 0)]
    all_to_all x1, waiting for transfers between devices: 0.01 us -> 13.9 us  [body(): lax.all_to_all(copies, ('rep', 'fsdp'), 0, 0).reshape(REPS, 8, 8, LANES)]
    pallas_call x3 -> x2, Pallas kernels: 9.89 us -> 3.1 us  [the longest x1 2.39 us: body(): pl.pallas_call(base_kernel, grid_spec=pltpu.PrefetchScalarGridSpec(num_sc...]
    ppermute x18 -> x15, starting transfers between devices: 23.8 us -> 19.9 us  [the longest x4 10.1 us: down(): return lax.ppermute(x, 'fsdp', [(i, (i + 6) % 8) for i in range(8)])]
    ppermute x18 -> x15, waiting for transfers between devices: 30.7 us -> 34.4 us  [the longest x4 15 us: up(): return lax.ppermute(x, 'fsdp', [(i, (i + 2) % 8) for i in range(8)])]
    slice x2 -> x0, local copies, waits for them, and re-layouts: 2.39 us -> none  [the longest x1 1.67 us: body(): own_far = up(own_lo[TOK:])]
  transfers between devices with their start and end apart: 20 -> 16, of which waited for: 9 -> 7; matrix products, arithmetic and copies ran while one was open for 2% -> 0% of each run, Pallas kernels for 18% -> 12%
where the time goes in v3:
time: 141 us; the launch traced here: 140 us
  waiting for transfers between devices  48.3 us (34%)
  starting transfers between devices  31.4 us (22%)
  Pallas kernels  29.5 us (21%)
  blocking collectives  25.4 us (18%)
  local copies, waits for them, and re-layouts  4.79 us (3%)
    all_to_all x1, blocking collectives, body(): spread = lax.all_to_all(tiles, 'rep', 0, 0)  25.4 us
    ppermute x4, waiting for transfers between devices, up(): return lax.ppermute(x, 'fsdp', [(i, (i + 2) % 8) for i in range(8)])  15 us
    all_to_all x1, waiting for transfers between devices, body(): lax.all_to_all(copies, ('rep', 'fsdp'), 0, 0).reshape(REPS, 8, 8, LANES)  13.9 us
    ppermute x4, waiting for transfers between devices, across(): return lax.ppermute(x, 'fsdp', [(i, (i + 4) % 8) for i in range(8)])  12.5 us
    pallas_call x1, Pallas kernels, body(): pl.pallas_call(forward_kernel, grid_spec=pltpu.PrefetchScalarGridSpec(num...  11.7 us
    all_to_all x1, starting transfers between devices, body(): lax.all_to_all(copies, ('rep', 'fsdp'), 0, 0).reshape(REPS, 8, 8, LANES)  11.5 us
    ppermute x4, starting transfers between devices, down(): return lax.ppermute(x, 'fsdp', [(i, (i + 6) % 8) for i in range(8)])  10.1 us
    pallas_call x1, Pallas kernels, body(): pl.pallas_call(residual_kernel, grid=(STEPS,), in_specs=[by_row(GROUP, RO...  7.55 us
  transfers between devices with their start and end apart: 16, of which 7 were waited for; matrix products, arithmetic and copies ran while one was open for 0% of the time, Pallas kernels for 12%

profile of v3, /device:TPU:1, one launch (start us, length us, event | category | flops | bytes accessed | tf_op | source)
XLA Modules:
  0.0 140.3 jit_solution(14523806594894629086)
XLA Ops:
  0.6 2.1 %collective-permute-start.8 = (bf16[512,1024]{1,0:T(8,128)(2,1)}, bf16[512,1024]{1,0:T(8,128)(2,1)S(1)}, u32[]{:S(2)}, u32[]{:S(2)}) collective-permute-start(bf16[512,1024]{1,0:T(8,128)(2,1)} %weight.1), channel_id=1, source_target_pairs={{0,1},{1,0},{2,3},{3,2},{4,5},{5,4},{6,7},{7,6},{8,9},{9,8},{10,11... | collective-permute-start | bytes 3145736 | tf_op jit(solution)/shard_map/ppermute | solution.py:297
  2.8 1.6 %copy-done = bf16[256,4096]{1,0:T(8,128)(2,1)S(1)} copy-done((bf16[256,4096]{1,0:T(8,128)(2,1)S(1)}, bf16[256,4096]{1,0:T(8,128)(2,1)}, u32[]{:S(2)}) %copy-start) | copy-done | bytes 2097176
  5.6 1.4 collective-permute-start
  6.9 1.5 %collective-permute-start.1 = (bf16[512,512]{1,0:T(8,128)(2,1)S(1)}, bf16[512,512]{1,0:T(8,128)(2,1)S(1)}, u32[]{:S(2)}, u32[]{:S(2)}) collective-permute-start(bf16[512,512]{1,0:T(8,128)(2,1)S(1)} %get-tuple-element.20), channel_id=1, source_target_pairs={{0,6},{1,7},{2,0},{3,1},{4,2},{5,3},{6,4},{7,5},{8,14},{9,15},{10,... | collective-permute-start | bytes 1572872 | tf_op jit(solution)/shard_map/ppermute | solution.py:291
  8.5 1.6 %collective-permute-start.7 = (bf16[512,512]{1,0:T(8,128)(2,1)S(1)}, bf16[512,512]{1,0:T(8,128)(2,1)S(1)}, u32[]{:S(2)}, u32[]{:S(2)}) collective-permute-start(bf16[512,512]{1,0:T(8,128)(2,1)S(1)} %get-tuple-element.26), channel_id=1, source_target_pairs={{0,4},{1,5},{2,6},{3,7},{4,0},{5,1},{6,2},{7,3},{8,12},{9,13},{10,... | collective-permute-start | bytes 1572872 | tf_op jit(solution)/shard_map/ppermute | solution.py:294
  10.0 9.2 %collective-permute-done.late_lo.lo.p3.a3 = bf16[512,512]{1,0:T(8,128)(2,1)S(1)} collective-permute-done((bf16[512,512]{1,0:T(8,128)(2,1)S(1)}, bf16[512,512]{1,0:T(8,128)(2,1)S(1)}, u32[]{:S(2)}, u32[]{:S(2)}) %collective-permute-start) | collective-permute-done | bytes 524320 | tf_op jit(solution)/shard_map/ppermute | solution.py:288
  19.3 12.5 %collective-permute-done.7.far.p2.a2 = bf16[512,512]{1,0:T(8,128)(2,1)S(1)} collective-permute-done((bf16[512,512]{1,0:T(8,128)(2,1)S(1)}, bf16[512,512]{1,0:T(8,128)(2,1)S(1)}, u32[]{:S(2)}, u32[]{:S(2)}) %collective-permute-start.7) | collective-permute-done | bytes 524320 | tf_op jit(solution)/shard_map/ppermute | solution.py:294
  33.4 2.1 %collective-permute-start.3 = (bf16[512,256]{1,0:T(8,128)(2,1)S(1)}, bf16[512,256]{1,0:T(8,128)(2,1)S(1)}, u32[]{:S(2)}, u32[]{:S(2)}) collective-permute-start(bf16[512,256]{1,0:T(8,128)(2,1)S(1)} %shard_map.86.turned.b0.c0), channel_id=1, source_target_pairs={{0,6},{1,7},{2,0},{3,1},{4,2},{5,3},{6,4},{7,5},{8,14},{9,15},{10,... | collective-permute-start | bytes 786440 | tf_op jit(solution)/shard_map/ppermute | solution.py:291
  35.5 4.2 %collective-permute-done.2.late_lo.b3.c3 = bf16[512,256]{1,0:T(8,128)(2,1)S(1)} collective-permute-done((bf16[512,256]{1,0:T(8,128)(2,1)S(1)}, bf16[512,256]{1,0:T(8,128)(2,1)S(1)}, u32[]{:S(2)}, u32[]{:S(2)}) %collective-permute-start.2) | collective-permute-done | bytes 262176 | tf_op jit(solution)/shard_map/ppermute | solution.py:288
  41.0 4.0 %collective-permute-start.4 = (bf16[256,512]{1,0:T(8,128)(2,1)S(1)}, bf16[256,512]{1,0:T(8,128)(2,1)S(1)}, u32[]{:S(2)}, u32[]{:S(2)}) collective-permute-start(bf16[256,512]{1,0:T(8,128)(2,1)S(1)} %get-tuple-element.22), channel_id=1, source_target_pairs={{0,6},{1,7},{2,0},{3,1},{4,2},{5,3},{6,4},{7,5},{8,14},{9,15},{10,... | collective-permute-start | bytes 786440 | tf_op jit(solution)/shard_map/ppermute | solution.py:291
  46.4 1.3 collective-permute-start.14
  47.7 5.7 %collective-permute-done.4.o1.t1 = bf16[256,512]{1,0:T(8,128)(2,1)S(1)} collective-permute-done((bf16[256,512]{1,0:T(8,128)(2,1)S(1)}, bf16[256,512]{1,0:T(8,128)(2,1)S(1)}, u32[]{:S(2)}, u32[]{:S(2)}) %collective-permute-start.4) | collective-permute-done | bytes 262176 | tf_op jit(solution)/shard_map/ppermute | solution.py:291
  53.4 1.7 %collective-permute-done.6.o3.t3 = bf16[256,512]{1,0:T(8,128)(2,1)S(1)} collective-permute-done((bf16[256,512]{1,0:T(8,128)(2,1)S(1)}, bf16[256,512]{1,0:T(8,128)(2,1)S(1)}, u32[]{:S(2)}, u32[]{:S(2)}) %collective-permute-start.6) | collective-permute-done | bytes 262176 | tf_op jit(solution)/shard_map/ppermute | solution.py:288
  55.0 2.4 %shard_map.89 = (bf16[320,1024]{1,0:T(8,128)(2,1)S(1)}, bf16[320,1024]{1,0:T(8,128)(2,1)S(1)}, bf16[320,1024]{1,0:T(8,128)(2,1)S(1)}, bf16[320,1024]{1,0:T(8,128)(2,1)S(1)}) custom-call(s32[1]{0:T(128)} %bitcast.where, bf16[256,512]{1,0:T(8,128)(2,1)S(1)} %get-tuple-element.21.o0.t0, bf16[256,512]{1,0:T(8,128)(2,1)S(1)} %collective-permute-done.4.o1.t1, ...), custom_call_target="tpu_custom_call" | custom-call | flops 2147483648 | bytes 7340032 | tf_op jit(solution)/shard_map/pallas_call | solution.py:381
  57.5 2.5 %collective-permute-start.10 = (bf16[320,1024]{1,0:T(8,128)(2,1)S(1)}, bf16[320,1024]{1,0:T(8,128)(2,1)S(1)}, u32[]{:S(2)}, u32[]{:S(2)}) collective-permute-start(bf16[320,1024]{1,0:T(8,128)(2,1)S(1)} %get-tuple-element.28), channel_id=1, source_target_pairs={{0,6},{1,7},{2,0},{3,1},{4,2},{5,3},{6,4},{7,5},{8,14},{9,15},{10,... | collective-permute-start | bytes 1966088 | tf_op jit(solution)/shard_map/ppermute | solution.py:291
  60.0 1.8 %collective-permute-start.11 = (bf16[320,1024]{1,0:T(8,128)(2,1)S(1)}, bf16[320,1024]{1,0:T(8,128)(2,1)S(1)}, u32[]{:S(2)}, u32[]{:S(2)}) collective-permute-start(bf16[320,1024]{1,0:T(8,128)(2,1)S(1)} %get-tuple-element.29), channel_id=1, source_target_pairs={{0,4},{1,5},{2,6},{3,7},{4,0},{5,1},{6,2},{7,3},{8,12},{9,13},{10,... | collective-permute-start | bytes 1966088 | tf_op jit(solution)/shard_map/ppermute | solution.py:294
  61.8 2.3 %shard_map.90.pre = f32[1024,512]{1,0:T(8,128)S(1)} custom-call(bf16[512,512]{1,0:T(8,128)(2,1)S(1)} %get-tuple-element.19.sent.a0, bf16[512,512]{1,0:T(8,128)(2,1)S(1)} %collective-permute-done.1.late_hi.hi.p1.a1, bf16[512,512]{1,0:T(8,128)(2,1)S(1)} %collective-permute-done.7.far.p2.a2, bf16[512,512]{1,0:T(8,128)(2,1)S(1)} %collective-permute-done.late_lo.lo.p3.a3, ...), custom_call_target="tpu_custom_call" | custom-call | flops 1073741824 | bytes 7340032 | tf_op jit(solution)/shard_map/pallas_call | solution.py:368
  64.1 2.9 %shard_map.92 = (f32[1024,512]{1,0:T(8,128)S(1)}, bf16[32,8,128]{2,1,0:T(8,128)(2,1)S(1)}) custom-call(f32[1024,512]{1,0:T(8,128)S(1)} %shard_map.90.pre, bf16[576,512]{1,0:T(8,128)(2,1)S(1)} %collective-permute-done.9.got_a, bf16[512,512]{1,0:T(8,128)(2,1)S(1)} %collective-permute-done.14.got_b, s32[16,4,512]{2,1,0:T(4,128)S(1)} %bitcast.9, ...), custom_call_target="tpu_custom_call" | custom-call | flops 805306368 | bytes 6291456 | tf_op jit(solution)/shard_map/pallas_call | solution.py:398
  67.1 1.3 copy-done.11
  68.4 25.4 %all_to_all.10.spread = bf16[32,8,128]{2,1,0:T(8,128)(2,1)S(1)} all-to-all(bf16[32,8,128]{2,1,0:T(8,128)(2,1)S(1)} %get-tuple-element.31), channel_id=1, replica_groups=mesh['rep'=32,'fsdp'=8] {'rep'}, dimensions={0} | all-to-all | bytes 131072 | tf_op jit(solution)/shard_map/all_to_all | solution.py:408
  94.8 11.5 %all-to-all-start.1 = ((bf16[256,8,128]{2,1,0:T(8,128)(2,1)}), bf16[256,8,128]{2,1,0:T(8,128)(2,1)S(1)}, u32[]{:S(2)}, u32[]{:S(2)}) async-start(bf16[256,8,128]{2,1,0:T(8,128)(2,1)} %shard_map.93.late), calls=%async_computation.1 | async-start | bytes 1048576 | tf_op jit(solution)/shard_map/all_to_all | solution.py:418
  106.4 7.5 %shard_map.95 = f32[512,1024]{1,0:T(8,128)} custom-call(f32[1024,512]{1,0:T(8,128)} %copy-done.11, s32[16,4,512]{2,1,0:T(4,128)} %bitcast.6, bf16[256,256]{1,0:T(8,128)(2,1)} %constant.8.ch, bf16[256,256]{1,0:T(8,128)(2,1)} %constant.11.cl, bf16[256,8,128]{2,1,0:T(8,128)(2,1)} %shard_map.93.late), custom_call_target="tpu_custom_call" | custom-call | flops 1610612736 | bytes 5242880 | tf_op jit(solution)/shard_map/pallas_call | solution.py:420
  113.9 13.9 %all-to-all-done.1 = bf16[256,8,128]{2,1,0:T(8,128)(2,1)S(1)} async-done(((bf16[256,8,128]{2,1,0:T(8,128)(2,1)}), bf16[256,8,128]{2,1,0:T(8,128)(2,1)S(1)}, u32[]{:S(2)}, u32[]{:S(2)}) %all-to-all-start.1) | async-done | bytes 524320 | tf_op jit(solution)/shard_map/all_to_all | solution.py:418
  128.6 11.7 %shard_map.94 = (bf16[256,1024]{1,0:T(8,128)(2,1)}, bf16[512,1024]{1,0:T(8,128)(2,1)}) custom-call(s32[1]{0:T(128)} %bitcast.where, bf16[256,4096]{1,0:T(8,128)(2,1)} %tok.1, bf16[320,1024]{1,0:T(8,128)(2,1)} %copy-done.7, bf16[320,1024]{1,0:T(8,128)(2,1)} %copy-done.4, bf16[320,1024]{1,0:T(8,128)(2,1)} %copy-done.5, bf16[320,1024]{1,0:T(8,128)(2,1)} %copy-done.6, ...), custom_call_target="tpu_custom_call" | custom-call | flops 4294967296 | bytes 8388608 | tf_op jit(solution)/shard_map/pallas_call | solution.py:430
  (48 shorter events, 7.3 us)
Async XLA Ops:
  0.6 31.2 %collective-permute-start.8 = (bf16[512,1024]{1,0:T(8,128)(2,1)}, bf16[512,1024]{1,0:T(8,128)(2,1)S(1)}, u32[]{:S(2)}, u32[]{:S(2)}) collective-permute-start(bf16[512,1024]{1,0:T(8,128)(2,1)} %weight.1), channel_id=1, source_target_pairs={{0,1},{1,0},{2,3},{3,2},{4,5},{5,4},{6,7},{7,6},{8,9},{9,8},{10,11... | collective-permute-start | bytes 3145736 | tf_op jit(solution)/shard_map/ppermute | solution.py:297
  5.4 26.4 %copy-start.8 = (s32[512,16,4]{0,2,1:T(4,128)S(1)}, s32[512,16,4]{0,2,1:T(4,128)}, u32[]{:S(2)}) copy-start(s32[512,16,4]{0,2,1:T(4,128)} %param.10) | copy-start | bytes 393220
  5.6 13.6 %collective-permute-start = (bf16[512,512]{1,0:T(8,128)(2,1)S(1)}, bf16[512,512]{1,0:T(8,128)(2,1)S(1)}, u32[]{:S(2)}, u32[]{:S(2)}) collective-permute-start(bf16[512,512]{1,0:T(8,128)(2,1)S(1)} %get-tuple-element.19.sent.a0), channel_id=1, source_target_pairs={{0,2},{1,3},{2,4},{3,5},{4,6},{5,7},{6,0},{7,1},{8,10},{9,11},{10,... | collective-permute-start | bytes 1572872 | tf_op jit(solution)/shard_map/ppermute | solution.py:288
  6.9 12.2 %collective-permute-start.1 = (bf16[512,512]{1,0:T(8,128)(2,1)S(1)}, bf16[512,512]{1,0:T(8,128)(2,1)S(1)}, u32[]{:S(2)}, u32[]{:S(2)}) collective-permute-start(bf16[512,512]{1,0:T(8,128)(2,1)S(1)} %get-tuple-element.20), channel_id=1, source_target_pairs={{0,6},{1,7},{2,0},{3,1},{4,2},{5,3},{6,4},{7,5},{8,14},{9,15},{10,... | collective-permute-start | bytes 1572872 | tf_op jit(solution)/shard_map/ppermute | solution.py:291
  8.5 23.3 %collective-permute-start.7 = (bf16[512,512]{1,0:T(8,128)(2,1)S(1)}, bf16[512,512]{1,0:T(8,128)(2,1)S(1)}, u32[]{:S(2)}, u32[]{:S(2)}) collective-permute-start(bf16[512,512]{1,0:T(8,128)(2,1)S(1)} %get-tuple-element.26), channel_id=1, source_target_pairs={{0,4},{1,5},{2,6},{3,7},{4,0},{5,1},{6,2},{7,3},{8,12},{9,13},{10,... | collective-permute-start | bytes 1572872 | tf_op jit(solution)/shard_map/ppermute | solution.py:294
  31.8 9.1 %copy-start.1 = (bf16[256,4096]{1,0:T(8,128)(2,1)S(1)}, bf16[256,4096]{1,0:T(8,128)(2,1)}, u32[]{:S(2)}) copy-start(bf16[256,4096]{1,0:T(8,128)(2,1)} %tok.1) | copy-start | bytes 6291460
  32.5 22.5 %collective-permute-start.9 = (bf16[576,512]{1,0:T(8,128)(2,1)S(1)}, bf16[576,512]{1,0:T(8,128)(2,1)S(1)}, u32[]{:S(2)}, u32[]{:S(2)}) collective-permute-start(bf16[576,512]{1,0:T(8,128)(2,1)S(1)} %shard_map.88), channel_id=1, source_target_pairs={{0,1},{1,0},{2,3},{3,2},{4,5},{5,4},{6,7},{7,6},{8,9},{9,8},{10,11... | collective-permute-start | bytes 1769480 | tf_op jit(solution)/shard_map/ppermute | solution.py:297
  32.9 6.9 %collective-permute-start.2 = (bf16[512,256]{1,0:T(8,128)(2,1)S(1)}, bf16[512,256]{1,0:T(8,128)(2,1)S(1)}, u32[]{:S(2)}, u32[]{:S(2)}) collective-permute-start(bf16[512,256]{1,0:T(8,128)(2,1)S(1)} %shard_map.86.turned.b0.c0), channel_id=1, source_target_pairs={{0,2},{1,3},{2,4},{3,5},{4,6},{5,7},{6,0},{7,1},{8,10},{9,11},{10,... | collective-permute-start | bytes 786440 | tf_op jit(solution)/shard_map/ppermute | solution.py:288
  33.4 7.4 %collective-permute-start.3 = (bf16[512,256]{1,0:T(8,128)(2,1)S(1)}, bf16[512,256]{1,0:T(8,128)(2,1)S(1)}, u32[]{:S(2)}, u32[]{:S(2)}) collective-permute-start(bf16[512,256]{1,0:T(8,128)(2,1)S(1)} %shard_map.86.turned.b0.c0), channel_id=1, source_target_pairs={{0,6},{1,7},{2,0},{3,1},{4,2},{5,3},{6,4},{7,5},{8,14},{9,15},{10,... | collective-permute-start | bytes 786440 | tf_op jit(solution)/shard_map/ppermute | solution.py:291
  35.5 10.1 %collective-permute-start.13 = (bf16[512,256]{1,0:T(8,128)(2,1)S(1)}, bf16[512,256]{1,0:T(8,128)(2,1)S(1)}, u32[]{:S(2)}, u32[]{:S(2)}) collective-permute-start(bf16[512,256]{1,0:T(8,128)(2,1)S(1)} %shard_map.86.turned.b0.c0), channel_id=1, source_target_pairs={{0,4},{1,5},{2,6},{3,7},{4,0},{5,1},{6,2},{7,3},{8,12},{9,13},{10,... | collective-permute-start | bytes 786440 | tf_op jit(solution)/shard_map/ppermute | solution.py:294
  41.0 14.1 %copy-start.12 = (bf16[512,1024]{1,0:T(8,128)(2,1)S(1)}, bf16[512,1024]{1,0:T(8,128)(2,1)}, u32[]{:S(2)}) copy-start(bf16[512,1024]{1,0:T(8,128)(2,1)} %weight.1) | copy-start | bytes 3145732
  41.0 12.4 %collective-permute-start.4 = (bf16[256,512]{1,0:T(8,128)(2,1)S(1)}, bf16[256,512]{1,0:T(8,128)(2,1)S(1)}, u32[]{:S(2)}, u32[]{:S(2)}) collective-permute-start(bf16[256,512]{1,0:T(8,128)(2,1)S(1)} %get-tuple-element.22), channel_id=1, source_target_pairs={{0,6},{1,7},{2,0},{3,1},{4,2},{5,3},{6,4},{7,5},{8,14},{9,15},{10,... | collective-permute-start | bytes 786440 | tf_op jit(solution)/shard_map/ppermute | solution.py:291
  45.0 8.4 %collective-permute-start.5 = (bf16[256,512]{1,0:T(8,128)(2,1)S(1)}, bf16[256,512]{1,0:T(8,128)(2,1)S(1)}, u32[]{:S(2)}, u32[]{:S(2)}) collective-permute-start(bf16[256,512]{1,0:T(8,128)(2,1)S(1)} %get-tuple-element.23), channel_id=1, source_target_pairs={{0,4},{1,5},{2,6},{3,7},{4,0},{5,1},{6,2},{7,3},{8,12},{9,13},{10,... | collective-permute-start | bytes 786440 | tf_op jit(solution)/shard_map/ppermute | solution.py:294
  45.0 10.1 %collective-permute-start.6 = (bf16[256,512]{1,0:T(8,128)(2,1)S(1)}, bf16[256,512]{1,0:T(8,128)(2,1)S(1)}, u32[]{:S(2)}, u32[]{:S(2)}) collective-permute-start(bf16[256,512]{1,0:T(8,128)(2,1)S(1)} %get-tuple-element.24), channel_id=1, source_target_pairs={{0,2},{1,3},{2,4},{3,5},{4,6},{5,7},{6,0},{7,1},{8,10},{9,11},{10,... | collective-permute-start | bytes 786440 | tf_op jit(solution)/shard_map/ppermute | solution.py:288
  46.4 17.7 %collective-permute-start.14 = (bf16[512,512]{1,0:T(8,128)(2,1)S(1)}, bf16[512,512]{1,0:T(8,128)(2,1)S(1)}, u32[]{:S(2)}, u32[]{:S(2)}) collective-permute-start(bf16[512,512]{1,0:T(8,128)(2,1)S(1)} %shard_map.91), channel_id=1, source_target_pairs={{0,1},{1,0},{2,3},{3,2},{4,5},{5,4},{6,7},{7,6},{8,9},{9,8},{10,11... | collective-permute-start | bytes 1572872 | tf_op jit(solution)/shard_map/ppermute | solution.py:297
  55.0 6.8 %copy-start.3 = (f32[1,512,1024]{2,1,0:T(8,128)S(1)}, f32[1,512,1024]{2,1,0:T(8,128)}, u32[]{:S(2)}) copy-start(f32[1,512,1024]{2,1,0:T(8,128)} %param.9) | copy-start | bytes 6291460
  57.4 6.7 %copy-start.7 = (bf16[320,1024]{1,0:T(8,128)(2,1)}, bf16[320,1024]{1,0:T(8,128)(2,1)S(1)}, u32[]{:S(2)}) copy-start(bf16[320,1024]{1,0:T(8,128)(2,1)S(1)} %get-tuple-element.27.late.own) | copy-start | bytes 1966084
  57.5 36.4 %collective-permute-start.10 = (bf16[320,1024]{1,0:T(8,128)(2,1)S(1)}, bf16[320,1024]{1,0:T(8,128)(2,1)S(1)}, u32[]{:S(2)}, u32[]{:S(2)}) collective-permute-start(bf16[320,1024]{1,0:T(8,128)(2,1)S(1)} %get-tuple-element.28), channel_id=1, source_target_pairs={{0,6},{1,7},{2,0},{3,1},{4,2},{5,3},{6,4},{7,5},{8,14},{9,15},{10,... | collective-permute-start | bytes 1966088 | tf_op jit(solution)/shard_map/ppermute | solution.py:291
  60.0 33.9 %collective-permute-start.11 = (bf16[320,1024]{1,0:T(8,128)(2,1)S(1)}, bf16[320,1024]{1,0:T(8,128)(2,1)S(1)}, u32[]{:S(2)}, u32[]{:S(2)}) collective-permute-start(bf16[320,1024]{1,0:T(8,128)(2,1)S(1)} %get-tuple-element.29), channel_id=1, source_target_pairs={{0,4},{1,5},{2,6},{3,7},{4,0},{5,1},{6,2},{7,3},{8,12},{9,13},{10,... | collective-permute-start | bytes 1966088 | tf_op jit(solution)/shard_map/ppermute | solution.py:294
  61.8 32.1 %collective-permute-start.12 = (bf16[320,1024]{1,0:T(8,128)(2,1)S(1)}, bf16[320,1024]{1,0:T(8,128)(2,1)S(1)}, u32[]{:S(2)}, u32[]{:S(2)}) collective-permute-start(bf16[320,1024]{1,0:T(8,128)(2,1)S(1)} %get-tuple-element.30), channel_id=1, source_target_pairs={{0,2},{1,3},{2,4},{3,5},{4,6},{5,7},{6,0},{7,1},{8,10},{9,11},{10,... | collective-permute-start | bytes 1966088 | tf_op jit(solution)/shard_map/ppermute | solution.py:288
  93.8 20.1 %copy-start.4 = (bf16[320,1024]{1,0:T(8,128)(2,1)}, bf16[320,1024]{1,0:T(8,128)(2,1)S(1)}, u32[]{:S(2)}) copy-start(bf16[320,1024]{1,0:T(8,128)(2,1)S(1)} %collective-permute-done.10.late_1.hi) | copy-start | bytes 1966084
  93.8 20.1 %copy-start.5 = (bf16[320,1024]{1,0:T(8,128)(2,1)}, bf16[320,1024]{1,0:T(8,128)(2,1)S(1)}, u32[]{:S(2)}) copy-start(bf16[320,1024]{1,0:T(8,128)(2,1)S(1)} %collective-permute-done.11.late_2.far) | copy-start | bytes 1966084
  93.9 20.0 %copy-start.6 = (bf16[320,1024]{1,0:T(8,128)(2,1)}, bf16[320,1024]{1,0:T(8,128)(2,1)S(1)}, u32[]{:S(2)}) copy-start(bf16[320,1024]{1,0:T(8,128)(2,1)S(1)} %collective-permute-done.12.late_0.lo) | copy-start | bytes 1966084
  94.8 33.0 %all-to-all-start.1 = ((bf16[256,8,128]{2,1,0:T(8,128)(2,1)}), bf16[256,8,128]{2,1,0:T(8,128)(2,1)S(1)}, u32[]{:S(2)}, u32[]{:S(2)}) async-start(bf16[256,8,128]{2,1,0:T(8,128)(2,1)} %shard_map.93.late), calls=%async_computation.1 | async-start | bytes 1048576 | tf_op jit(solution)/shard_map/all_to_all | solution.py:418
  (6 other events, 9.4 us)

commit v4 on v3

--- a/solution.py
+++ b/solution.py
@@ -20,8 +20,8 @@
 LANES = 128
 PACK = 16
 REPS = 32
+TILES = PICKS * ROWS // (8 * LANES)
 VMEM_LIMIT = 16 * 1024 * 1024
-VMEM_MOST = 60 * 1024 * 1024
 
 
 def dct_group():
@@ -152,33 +152,52 @@
     return rows
 
 
-def pick_kernel(pre, got_a, got_b, idx, ch, cl, late, moment, tiles):
-    first = pl.program_id(0) < STEPS // 2
+def pick_kernel(where, pre, got_a, got_b, idx, ch, cl, late, moment, picked, keep, send):
+    step = pl.program_id(0)
+    first = step < STEPS // 2
     got = jnp.where(first, got_a[...], got_b[...]).astype(jnp.float32)
     total = pre[...] + got
     moment[...] = total
     values = jnp.concatenate(pick_rows(total, idx, ch, cl), axis=0)
-    for t in range(GROUP // BLOCK * KEEP // 8):
-        for q in range(ROWS // LANES):
-            tile = values[t * 8 : (t + 1) * 8, q * LANES : (q + 1) * LANES]
-            tiles[t * (ROWS // LANES) + q] = tile.astype(tiles.dtype)
-
-
-def share_kernel(spread, late_0, late_1, late_2, out):
-    total = jnp.sum(spread[...].astype(jnp.float32), axis=0, keepdims=True)
-    out[...] = jnp.broadcast_to(total, out.shape).astype(out.dtype)
-
-
-def residual_kernel(moment, idx, ch, cl, late, out):
-    total = moment[...]
-    rows = pick_rows(total, idx, ch, cl)
+    picked[...] = values
+
+    def put(out):
+        for t in range(GROUP // BLOCK * KEEP // 8):
+            for q in range(ROWS // LANES):
+                tile = values[t * 8 : (t + 1) * 8, q * LANES : (q + 1) * LANES]
+                out[(step & 1) * (TILES // STEPS) + t * (ROWS // LANES) + q] = tile
+
+    here = (step >> 1) == (where[1] & 1)
+    pl.when(here)(lambda: put(keep))
+    pl.when(jnp.logical_not(here))(lambda: put(send))
+
+
+def add_two_kernel(a, b, out):
+    out[...] = (a[...] + b[...]).astype(out.dtype)
+
+
+def add_four_kernel(a, b, c, d, out):
+    out[...] = (a[...] + b[...]) + (c[...] + d[...])
+
+
+def pair_kernel(where, half, core, across, corner, late_0, late_1, late_2, out):
+    side, mine = where[0] & 1, (where[1] & 1) * (TILES // 2)
+    other = TILES // 2 - mine
+    out[side, pl.ds(mine, TILES // 2)] = half[...]
+    out[side, pl.ds(other, TILES // 2)] = core[...]
+    out[1 - side, pl.ds(mine, TILES // 2)] = across[...]
+    out[1 - side, pl.ds(other, TILES // 2)] = corner[...]
+
+
+def residual_kernel(moment, picked, idx, ch, cl, late, out):
     parts = []
     for b in range(GROUP // BLOCK):
         at = [idx[b, j : j + 1, :] for j in range(KEEP)]
-        parts.append(expand_block(at, rows[b * KEEP : (b + 1) * KEEP], ROWS))
+        have = [picked[b * KEEP + j : b * KEEP + j + 1, :] for j in range(KEEP)]
+        parts.append(expand_block(at, have, ROWS))
     kept = jnp.concatenate(parts, axis=0)
     back = three_pass((ch[...], cl[...]), split_pair(kept), ((0,), (0,)))
-    out[...] = (total - back).T
+    out[...] = (moment[...] - back).T
 
 
 def base_kernel(where, o0, o1, o2, o3, p0, p1, p2, p3, w_own, w_peer, idx, got_a, *outs):
@@ -194,45 +213,40 @@
         out[TOK:, ROWS:] = right
 
 
-def forward_kernel(where, tok, own, hi, far, lo, tot, weight, ch, cl, out, out_weight, dense, mixed):
-    step = pl.program_id(0)
-    tail = slice(TOK, TOK + PICKS)
-    near = jnp.where(step == 0, own[tail, :], hi[tail, :])
-    away = jnp.where(step == 2, far[tail, :], lo[tail, :])
-    pairs = jnp.where(step < 2, near, away).astype(jnp.float32)
-
-    @pl.when(step == 0)
-    def _():
-        mixed[...] = jnp.zeros_like(mixed)
-
+def expand_group(g, pairs, tot, dense):
+    for t in range(2 * g, 2 * g + 2):
+        for f in range(2):
+            for q in range(ROWS // LANES):
+                cols = slice(f * ROWS + q * LANES, f * ROWS + (q + 1) * LANES)
+                values = tot[f, t * (ROWS // LANES) + q].astype(jnp.float32)
+                expand_tile(pairs[t * 8 : (t + 1) * 8, cols], values, dense, t * 2 * BLOCK, cols)
+
+
+def forward_own_kernel(where, tok, own, tot, weight, ch, cl, mixed, out_weight, dense):
+    pairs = own[TOK:, :].astype(jnp.float32)
+    cols = pl.ds(pl.multiple_of((where[0] & 1) * ROWS, ROWS), ROWS)
     for g in range(STEPS):
-        for t in range(2 * g, 2 * g + 2):
-            for f in range(2):
-                for q in range(ROWS // LANES):
-                    cols = slice(f * ROWS + q * LANES, f * ROWS + (q + 1) * LANES)
-                    values = tot[t * (ROWS // LANES) + q, f].astype(jnp.float32)
-                    expand_tile(pairs[t * 8 : (t + 1) * 8, cols], values, dense, t * 2 * BLOCK, cols)
+        expand_group(g, pairs, tot, dense)
         span = slice(g * GROUP, (g + 1) * GROUP)
-        mixed[span, :] += mix(dense[span, :], tok[...], ((1,), (1,)))
-
-    @pl.when(step == 0)
-    def _():
-        cols = pl.ds(pl.multiple_of((where[0] & 1) * ROWS, ROWS), ROWS)
-        for g in range(STEPS):
-            span = slice(g * GROUP, (g + 1) * GROUP)
-            turned = dense[span, cols].T
-            delta = mix(turned, ch[...], ((1,), (0,))) + mix(turned, cl[...], ((1,), (0,)))
-            new = weight[:, span].astype(jnp.float32) - (step_rate / REPS) * delta
-            out_weight[:, span] = new.astype(out_weight.dtype)
-
-    @pl.when(step == 3)
-    def _():
-        for g in range(STEPS):
-            span = slice(g * GROUP, (g + 1) * GROUP)
-            delta = three_pass(split_pair(mixed[span, :].T), (ch[...], cl[...]), ((1,), (0,)))
-            base = own[:TOK, span].astype(jnp.float32) + hi[:TOK, span].astype(jnp.float32)
-            base += far[:TOK, span].astype(jnp.float32) + lo[:TOK, span].astype(jnp.float32)
-            out[:, span] = (base - (step_rate / REPS) * delta).astype(out.dtype)
+        mixed[span, :] = mix(dense[span, :], tok[...], ((1,), (1,)))
+        turned = dense[span, cols].T
+        delta = mix(turned, ch[...], ((1,), (0,))) + mix(turned, cl[...], ((1,), (0,)))
+        new = weight[:, span].astype(jnp.float32) - (step_rate / REPS) * delta
+        out_weight[:, span] = new.astype(out_weight.dtype)
+
+
+def forward_kernel(where, tok_1, tok_2, tok_3, own, hi, far, lo, tot_1, tot_2, tot_3, mixed, ch, cl, out, *dense):
+    pairs = [near[TOK:, :].astype(jnp.float32) for near in (hi, far, lo)]
+    for g in range(STEPS):
+        span = slice(g * GROUP, (g + 1) * GROUP)
+        total = mixed[span, :]
+        for tok, index, tot, buffer in zip((tok_1, tok_2, tok_3), pairs, (tot_1, tot_2, tot_3), dense):
+            expand_group(g, index, tot, buffer)
+            total += mix(buffer[span, :], tok[...], ((1,), (1,)))
+        delta = three_pass(split_pair(total.T), (ch[...], cl[...]), ((1,), (0,)))
+        base = own[:TOK, span].astype(jnp.float32) + hi[:TOK, span].astype(jnp.float32)
+        base += far[:TOK, span].astype(jnp.float32) + lo[:TOK, span].astype(jnp.float32)
+        out[:, span] = (base - (step_rate / REPS) * delta).astype(out.dtype)
 
 
 def params(limit=VMEM_LIMIT):
@@ -248,19 +262,19 @@
 
 
 def by_row(rows, width):
-    return pl.BlockSpec((rows, width), lambda c: (c, 0))
+    return pl.BlockSpec((rows, width), lambda c, *_: (c, 0))
 
 
 def by_col(rows, width):
-    return pl.BlockSpec((rows, width), lambda c: (0, c))
+    return pl.BlockSpec((rows, width), lambda c, *_: (0, c))
 
 
 def first_half(rows, width):
-    return pl.BlockSpec((rows, width), lambda c: (jnp.minimum(c, STEPS // 2 - 1), 0))
+    return pl.BlockSpec((rows, width), lambda c, *_: (jnp.minimum(c, STEPS // 2 - 1), 0))
 
 
 def second_half(rows, width):
-    return pl.BlockSpec((rows, width), lambda c: (jnp.maximum(c - STEPS // 2, 0), 0))
+    return pl.BlockSpec((rows, width), lambda c, *_: (jnp.maximum(c - STEPS // 2, 0), 0))
 
 
 AFTER = pl.BlockSpec(memory_space=pl.ANY)
@@ -268,7 +282,7 @@
 GOT = [first_half(GROUP, ROWS), second_half(GROUP, ROWS)]
 BF16, F32 = jnp.bfloat16, jnp.float32
 INDEX = pl.BlockSpec((KV // BLOCK, KEEP, ROWS), lambda c, *_: (0, 0, 0))
-INDEX_STEP = pl.BlockSpec((GROUP // BLOCK, KEEP, ROWS), lambda c: (c, 0, 0))
+INDEX_STEP = pl.BlockSpec((GROUP // BLOCK, KEEP, ROWS), lambda c, *_: (c, 0, 0))
 MESSAGE = whole(HALF, 2 * TOK)
 PIECE = whole(TOK, ROWS)
 
@@ -281,7 +295,7 @@
     basis = dct_group()
     high = jnp.asarray(basis).astype(BF16)
     low = (jnp.asarray(basis) - high.astype(F32)).astype(BF16)
-    place = lax.axis_index("fsdp").astype(jnp.int32).reshape(1)
+    place = jnp.stack([lax.axis_index("fsdp"), lax.axis_index("rep")]).astype(jnp.int32)
     index_t = jnp.transpose(kept_index, (1, 2, 0))
 
     def up(x):
@@ -395,55 +409,100 @@
     )(place, *owns, peer_0, *firsts[1:], weight, weight_peer, index_t, got_a)
     base_lo, base_hi, base_far = up(base_up), down(base_down), across(base_across)
 
-    moment, tiles = pl.pallas_call(
+    halves = whole(TILES // 2, 8, LANES)
+    half_shape = shape(TILES // 2, 8, LANES, dtype=F32)
+    moment, picked, keep, send = pl.pallas_call(
         pick_kernel,
-        grid=(STEPS,),
-        in_specs=[by_row(GROUP, ROWS)] + GOT + [INDEX_STEP] + BASIS + [AFTER],
-        out_specs=[by_row(GROUP, ROWS), pl.BlockSpec((REPS // STEPS, 8, LANES), lambda c: (c, 0, 0))],
-        out_shape=[shape(KV, ROWS, dtype=F32), shape(REPS, 8, LANES)],
+        grid_spec=pltpu.PrefetchScalarGridSpec(
+            num_scalar_prefetch=1,
+            grid=(STEPS,),
+            in_specs=[by_row(GROUP, ROWS)] + GOT + [INDEX_STEP] + BASIS + [AFTER],
+            out_specs=[by_row(GROUP, ROWS), by_row(PICKS // STEPS, ROWS), halves, halves],
+        ),
+        out_shape=[shape(KV, ROWS, dtype=F32), shape(PICKS, ROWS, dtype=F32), half_shape, half_shape],
         compiler_params=params(),
         cost_estimate=cost(6 * KV * GROUP * ROWS, 6),
-    )(pre, got_a, got_b, index_t, high, low, base)
-
-    spread = lax.all_to_all(tiles, "rep", 0, 0)
-    copies = pl.pallas_call(
-        share_kernel,
-        grid=(1,),
-        in_specs=[whole(REPS, 8, LANES), AFTER, AFTER, AFTER],
-        out_specs=whole(REPS * 8, 8, LANES),
-        out_shape=shape(REPS * 8, 8, LANES),
-        compiler_params=params(),
-        cost_estimate=cost(0, 1),
-    )(spread, base_lo, base_hi, base_far)
-    totals = lax.all_to_all(copies, ("rep", "fsdp"), 0, 0).reshape(REPS, 8, 8, LANES)
+    )(place, pre, got_a, got_b, index_t, high, low, base)
+
+    def partner(x, bits):
+        return lax.ppermute(x, "rep", [(i, i ^ bits) for i in range(REPS)])
+
+    def add(kernel, result, *parts):
+        return pl.pallas_call(
+            kernel,
+            grid=(1,),
+            in_specs=[halves] * len(parts),
+            out_specs=halves,
+            out_shape=result,
+            compiler_params=params(),
+            cost_estimate=cost(0, 0.25),
+        )(*parts)
+
+    value = add(add_two_kernel, half_shape, keep, partner(send, 1))
+    value = add(add_two_kernel, half_shape, value, partner(value, 2))
+    value = add(add_four_kernel, half_shape, value, partner(value, 4), partner(value, 8), partner(value, 12))
+    half = add(add_two_kernel, shape(TILES // 2, 8, LANES), value, partner(value, 16))
+
+    corner = lax.ppermute(half, ("rep", "fsdp"), [(i, i ^ 9) for i in range(REPS * 8)])
+    pair_spec = whole(2, TILES, 8, LANES)
+    pair = pl.pallas_call(
+        pair_kernel,
+        grid_spec=pltpu.PrefetchScalarGridSpec(
+            num_scalar_prefetch=1,
+            grid=(1,),
+            in_specs=[halves] * 4 + [AFTER] * 3,
+            out_specs=pair_spec,
+        ),
+        out_shape=shape(2, TILES, 8, LANES),
+        compiler_params=params(),
+        cost_estimate=cost(0, 0.25),
+    )(place, half, partner(half, 1), swap(half), corner, base_lo, base_hi, base_far)
+    pair_far, pair_lo, pair_hi = across(pair), up(pair), down(pair)
+
+    def token_block(d):
+        return pl.BlockSpec((TOK, 2 * ROWS), lambda c, s: (0, ((s[0] >> 1) + d) & 3))
+
+    mixed, new_weight = pl.pallas_call(
+        forward_own_kernel,
+        grid_spec=pltpu.PrefetchScalarGridSpec(
+            num_scalar_prefetch=1,
+            grid=(1,),
+            in_specs=[token_block(0), whole(TOK + PICKS, KV), pair_spec, whole(ROWS, KV)] + BASIS,
+            out_specs=[whole(KV, TOK), whole(ROWS, KV)],
+            scratch_shapes=[pltpu.VMEM((KV, 2 * ROWS), BF16)],
+        ),
+        out_shape=[shape(KV, TOK, dtype=F32), shape(ROWS, KV)],
+        compiler_params=params(),
+        cost_estimate=cost(3 * KV * KV * ROWS, 4),
+    )(place, tokens, base, pair, weight, high, low)
 
     new_momentum = pl.pallas_call(
         residual_kernel,
         grid=(STEPS,),
-        in_specs=[by_row(GROUP, ROWS), INDEX_STEP] + BASIS + [AFTER],
+        in_specs=[by_row(GROUP, ROWS), by_row(PICKS // STEPS, ROWS), INDEX_STEP] + BASIS + [AFTER],
         out_specs=by_col(ROWS, GROUP),
         out_shape=shape(ROWS, KV, dtype=F32),
-        compiler_params=params(VMEM_MOST),
-        cost_estimate=cost(12 * KV * GROUP * ROWS, 5),
-    )(moment, index_t, high, low, copies)
-
-    projected, new_weight = pl.pallas_call(
+        compiler_params=params(),
+        cost_estimate=cost(6 * KV * GROUP * ROWS, 5),
+    )(moment, picked, index_t, high, low, pair)
+
+    projected = pl.pallas_call(
         forward_kernel,
         grid_spec=pltpu.PrefetchScalarGridSpec(
             num_scalar_prefetch=1,
-            grid=(4,),
-            in_specs=[pl.BlockSpec((TOK, 2 * ROWS), lambda c, s: (0, ((s[0] >> 1) + c) & 3))]
+            grid=(1,),
+            in_specs=[token_block(d) for d in (1, 2, 3)]
             + [whole(TOK + PICKS, KV)] * 4
-            + [pl.BlockSpec((REPS, 2, 8, LANES), lambda c, s: (0, ((s[0] >> 1) + c) & 3, 0, 0))]
-            + [whole(ROWS, KV)]
+            + [pair_spec] * 3
+            + [whole(KV, TOK)]
             + BASIS,
-            out_specs=[whole(TOK, KV), whole(ROWS, KV)],
-            scratch_shapes=[pltpu.VMEM((KV, 2 * ROWS), BF16), pltpu.VMEM((KV, TOK), F32)],
-        ),
-        out_shape=[shape(TOK, KV), shape(ROWS, KV)],
-        compiler_params=params(VMEM_MOST),
-        cost_estimate=cost(8 * KV * KV * ROWS, 8),
-    )(place, tokens, base, base_hi, base_far, base_lo, totals, weight, high, low)
+            out_specs=whole(TOK, KV),
+            scratch_shapes=[pltpu.VMEM((KV, 2 * ROWS), BF16)] * 3,
+        ),
+        out_shape=shape(TOK, KV),
+        compiler_params=params(2 * VMEM_LIMIT),
+        cost_estimate=cost(6 * KV * KV * ROWS, 7),
+    )(place, tokens, tokens, tokens, base, base_hi, base_far, base_lo, pair_hi, pair_far, pair_lo, mixed, high, low)
     return (projected, new_weight, new_momentum[None])
 
 

time: 141 us -> 126 us (0.89)
  blocking collectives: 25.4 us -> 0 us
  starting transfers between devices: 31.4 us -> 52.1 us
  waiting for transfers between devices: 48.3 us -> 44 us
  Pallas kernels: 29.5 us -> 26.1 us
  local copies, waits for them, and re-layouts: 4.79 us -> 2.66 us
    ppermute x0 -> x8, starting transfers between devices: none -> 28.1 us  [the longest x7 27 us: partner(): return lax.ppermute(x, 'rep', [(i, i ^ bits) for i in range(REPS)])]
    all_to_all x1 -> x0, blocking collectives: 25.4 us -> none  [body(): spread = lax.all_to_all(tiles, 'rep', 0, 0)]
    all_to_all x1 -> x0, waiting for transfers between devices: 13.9 us -> none  [body(): lax.all_to_all(copies, ('rep', 'fsdp'), 0, 0).reshape(REPS, 8, 8, LANES)]
    all_to_all x1 -> x0, starting transfers between devices: 11.5 us -> none  [body(): lax.all_to_all(copies, ('rep', 'fsdp'), 0, 0).reshape(REPS, 8, 8, LANES)]
    ppermute x0 -> x8, waiting for transfers between devices: none -> 9.06 us  [the longest x7 7.23 us: partner(): return lax.ppermute(x, 'rep', [(i, i ^ bits) for i in range(REPS)])]
    pallas_call x1, Pallas kernels: 11.7 us -> 6.57 us  [body(): pl.pallas_call(forward_kernel, grid_spec=pltpu.PrefetchScalarGridSpec(num...]
    pallas_call x2 -> x7, Pallas kernels: 3.88 us -> 7.74 us  [the longest x1 3.65 us: body(): pl.pallas_call(forward_own_kernel, grid_spec=pltpu.PrefetchScalarGridSpec...]
    pallas_call x1, Pallas kernels: 7.55 us -> 3.71 us  [body(): pl.pallas_call(residual_kernel, grid=(STEPS,), in_specs=[by_row(GROUP, RO...]
  transfers between devices with their start and end apart: 16 -> 27, of which waited for: 7 -> 13; matrix products, arithmetic and copies ran while one was open for 0% -> 0% of each run, Pallas kernels for 12% -> 15%
where the time goes in v4:
time: 126 us
  starting transfers between devices  52.1 us (41%)
  waiting for transfers between devices  44 us (35%)
  Pallas kernels  26.1 us (21%)
  local copies, waits for them, and re-layouts  2.66 us (2%)
    ppermute x7, starting transfers between devices, partner(): return lax.ppermute(x, 'rep', [(i, i ^ bits) for i in range(REPS)])  27 us
    ppermute x5, waiting for transfers between devices, up(): return lax.ppermute(x, 'fsdp', [(i, (i + 2) % 8) for i in range(8)])  16.3 us
    ppermute x5, waiting for transfers between devices, across(): return lax.ppermute(x, 'fsdp', [(i, (i + 4) % 8) for i in range(8)])  12.5 us
    ppermute x5, starting transfers between devices, down(): return lax.ppermute(x, 'fsdp', [(i, (i + 6) % 8) for i in range(8)])  12 us
    ppermute x7, waiting for transfers between devices, partner(): return lax.ppermute(x, 'rep', [(i, i ^ bits) for i in range(REPS)])  7.23 us
    pallas_call x1, Pallas kernels, body(): pl.pallas_call(forward_kernel, grid_spec=pltpu.PrefetchScalarGridSpec(num...  6.57 us
    ppermute x5, waiting for transfers between devices, down(): return lax.ppermute(x, 'fsdp', [(i, (i + 6) % 8) for i in range(8)])  5.64 us
    ppermute x4, starting transfers between devices, swap(): return lax.ppermute(x, 'fsdp', [(i, i ^ 1) for i in range(8)])  5.03 us
  transfers between devices with their start and end apart: 27, of which 13 were waited for; matrix products, arithmetic and copies ran while one was open for 0% of the time, Pallas kernels for 15%

profile of v4, /device:TPU:1, one launch (start us, length us, event | category | flops | bytes accessed | tf_op | source)
XLA Modules:
  0.0 125.8 jit_solution(16001066228441697361)
XLA Ops:
  0.6 2.1 %collective-permute-start.8 = (bf16[512,1024]{1,0:T(8,128)(2,1)}, bf16[512,1024]{1,0:T(8,128)(2,1)S(1)}, u32[]{:S(2)}, u32[]{:S(2)}) collective-permute-start(bf16[512,1024]{1,0:T(8,128)(2,1)} %weight.1), channel_id=1, source_target_pairs={{0,1},{1,0},{2,3},{3,2},{4,5},{5,4},{6,7},{7,6},{8,9},{9,8},{10,11... | collective-permute-start | bytes 3145736 | tf_op jit(solution)/shard_map/ppermute | solution.py:311
  10.6 9.2 %collective-permute-done.late_lo.lo.p3.a3 = bf16[512,512]{1,0:T(8,128)(2,1)S(1)} collective-permute-done((bf16[512,512]{1,0:T(8,128)(2,1)S(1)}, bf16[512,512]{1,0:T(8,128)(2,1)S(1)}, u32[]{:S(2)}, u32[]{:S(2)}) %collective-permute-start) | collective-permute-done | bytes 524320 | tf_op jit(solution)/shard_map/ppermute | solution.py:302
  19.9 12.5 %collective-permute-done.7.far.p2.a2 = bf16[512,512]{1,0:T(8,128)(2,1)S(1)} collective-permute-done((bf16[512,512]{1,0:T(8,128)(2,1)S(1)}, bf16[512,512]{1,0:T(8,128)(2,1)S(1)}, u32[]{:S(2)}, u32[]{:S(2)}) %collective-permute-start.7) | collective-permute-done | bytes 524320 | tf_op jit(solution)/shard_map/ppermute | solution.py:308
  34.0 2.1 %collective-permute-start.3 = (bf16[512,256]{1,0:T(8,128)(2,1)S(1)}, bf16[512,256]{1,0:T(8,128)(2,1)S(1)}, u32[]{:S(2)}, u32[]{:S(2)}) collective-permute-start(bf16[512,256]{1,0:T(8,128)(2,1)S(1)} %shard_map.86.turned.b0.c0), channel_id=1, source_target_pairs={{0,6},{1,7},{2,0},{3,1},{4,2},{5,3},{6,4},{7,5},{8,14},{9,15},{10,... | collective-permute-start | bytes 786440 | tf_op jit(solution)/shard_map/ppermute | solution.py:305
  36.2 4.2 %collective-permute-done.2.late_lo.b3.c3 = bf16[512,256]{1,0:T(8,128)(2,1)S(1)} collective-permute-done((bf16[512,256]{1,0:T(8,128)(2,1)S(1)}, bf16[512,256]{1,0:T(8,128)(2,1)S(1)}, u32[]{:S(2)}, u32[]{:S(2)}) %collective-permute-start.2) | collective-permute-done | bytes 262176 | tf_op jit(solution)/shard_map/ppermute | solution.py:302
  42.1 4.0 %collective-permute-start.4 = (bf16[256,512]{1,0:T(8,128)(2,1)S(1)}, bf16[256,512]{1,0:T(8,128)(2,1)S(1)}, u32[]{:S(2)}, u32[]{:S(2)}) collective-permute-start(bf16[256,512]{1,0:T(8,128)(2,1)S(1)} %get-tuple-element.24), channel_id=1, source_target_pairs={{0,6},{1,7},{2,0},{3,1},{4,2},{5,3},{6,4},{7,5},{8,14},{9,15},{10,... | collective-permute-start | bytes 786440 | tf_op jit(solution)/shard_map/ppermute | solution.py:305
  48.8 4.5 %collective-permute-done.4.o1.t1 = bf16[256,512]{1,0:T(8,128)(2,1)S(1)} collective-permute-done((bf16[256,512]{1,0:T(8,128)(2,1)S(1)}, bf16[256,512]{1,0:T(8,128)(2,1)S(1)}, u32[]{:S(2)}, u32[]{:S(2)}) %collective-permute-start.4) | collective-permute-done | bytes 262176 | tf_op jit(solution)/shard_map/ppermute | solution.py:305
  53.3 2.6 %collective-permute-done.6.o3.t3 = bf16[256,512]{1,0:T(8,128)(2,1)S(1)} collective-permute-done((bf16[256,512]{1,0:T(8,128)(2,1)S(1)}, bf16[256,512]{1,0:T(8,128)(2,1)S(1)}, u32[]{:S(2)}, u32[]{:S(2)}) %collective-permute-start.6) | collective-permute-done | bytes 262176 | tf_op jit(solution)/shard_map/ppermute | solution.py:302
  56.0 3.0 %shard_map.89 = (bf16[320,1024]{1,0:T(8,128)(2,1)S(1)}, bf16[320,1024]{1,0:T(8,128)(2,1)S(1)}, bf16[320,1024]{1,0:T(8,128)(2,1)S(1)}, bf16[320,1024]{1,0:T(8,128)(2,1)S(1)}) custom-call(s32[2]{0:T(128)S(1)} %pad_add_fusion.where, bf16[256,512]{1,0:T(8,128)(2,1)S(1)} %get-tuple-element.23.o0.t0, bf16[256,512]{1,0:T(8,128)(2,1)S(1)} %collective-permute-done.4.o1.t1, ...), custom_call_target="tpu_custom_call" | custom-call | flops 2147483648 | bytes 7340032 | tf_op jit(solution)/shard_map/pallas_call | solution.py:395
  58.9 2.5 %collective-permute-start.10 = (bf16[320,1024]{1,0:T(8,128)(2,1)S(1)}, bf16[320,1024]{1,0:T(8,128)(2,1)S(1)}, u32[]{:S(2)}, u32[]{:S(2)}) collective-permute-start(bf16[320,1024]{1,0:T(8,128)(2,1)S(1)} %get-tuple-element.30), channel_id=1, source_target_pairs={{0,6},{1,7},{2,0},{3,1},{4,2},{5,3},{6,4},{7,5},{8,14},{9,15},{10,... | collective-permute-start | bytes 1966088 | tf_op jit(solution)/shard_map/ppermute | solution.py:305
  62.3 2.3 %shard_map.90.pre = f32[1024,512]{1,0:T(8,128)S(1)} custom-call(bf16[512,512]{1,0:T(8,128)(2,1)S(1)} %get-tuple-element.21.sent.a0, bf16[512,512]{1,0:T(8,128)(2,1)S(1)} %collective-permute-done.1.late_hi.hi.p1.a1, bf16[512,512]{1,0:T(8,128)(2,1)S(1)} %collective-permute-done.7.far.p2.a2, bf16[512,512]{1,0:T(8,128)(2,1)S(1)} %collective-permute-done.late_lo.lo.p3.a3, ...), custom_call_target="tpu_custom_call" | custom-call | flops 1073741824 | bytes 7340032 | tf_op jit(solution)/shard_map/pallas_call | solution.py:382
  64.6 3.5 %shard_map.92 = (f32[1024,512]{1,0:T(8,128)S(1)}, f32[64,512]{1,0:T(8,128)S(1)}, f32[16,8,128]{2,1,0:T(8,128)S(1)}, f32[16,8,128]{2,1,0:T(8,128)S(1)}) custom-call(s32[2]{0:T(128)S(1)} %pad_add_fusion.where, f32[1024,512]{1,0:T(8,128)S(1)} %shard_map.90.pre, bf16[576,512]{1,0:T(8,128)(2,1)S(1)} %collective-permute-done.9.got_a, ...), custom_call_target="tpu_custom_call" | custom-call | flops 805306368 | bytes 6291456 | tf_op jit(solution)/shard_map/pallas_call | solution.py:414
  68.1 5.7 %collective-permute-start.15 = (f32[16,8,128]{2,1,0:T(8,128)S(1)}, f32[16,8,128]{2,1,0:T(8,128)S(1)}, u32[]{:S(2)}, u32[]{:S(2)}) collective-permute-start(f32[16,8,128]{2,1,0:T(8,128)S(1)} %get-tuple-element.34), channel_id=1, source_target_pairs={{0,8},{8,0},{16,24},{24,16},{32,40},{40,32},{48,56},{56,48},{64,72... | collective-permute-start | bytes 196616 | tf_op jit(solution)/shard_map/ppermute | solution.py:428
  74.7 2.8 %collective-permute-start.16 = (f32[16,8,128]{2,1,0:T(8,128)S(1)}, f32[16,8,128]{2,1,0:T(8,128)S(1)}, u32[]{:S(2)}, u32[]{:S(2)}) collective-permute-start(f32[16,8,128]{2,1,0:T(8,128)S(1)} %shard_map.93.a), channel_id=1, source_target_pairs={{0,16},{8,24},{16,0},{24,8},{32,48},{40,56},{48,32},{56,40},{64,80... | collective-permute-start | bytes 196616 | tf_op jit(solution)/shard_map/ppermute | solution.py:428
  77.5 2.2 %collective-permute-done.16.b = f32[16,8,128]{2,1,0:T(8,128)S(1)} collective-permute-done((f32[16,8,128]{2,1,0:T(8,128)S(1)}, f32[16,8,128]{2,1,0:T(8,128)S(1)}, u32[]{:S(2)}, u32[]{:S(2)}) %collective-permute-start.16) | collective-permute-done | bytes 65568 | tf_op jit(solution)/shard_map/ppermute | solution.py:428
  81.4 3.0 %collective-permute-start.18 = (f32[16,8,128]{2,1,0:T(8,128)S(1)}, f32[16,8,128]{2,1,0:T(8,128)S(1)}, u32[]{:S(2)}, u32[]{:S(2)}) collective-permute-start(f32[16,8,128]{2,1,0:T(8,128)S(1)} %shard_map.94.a), channel_id=1, source_target_pairs={{0,64},{8,72},{16,80},{24,88},{32,96},{40,104},{48,112},{56,120},{... | collective-permute-start | bytes 196616 | tf_op jit(solution)/shard_map/ppermute | solution.py:428
  84.4 3.1 %collective-permute-start.19 = (f32[16,8,128]{2,1,0:T(8,128)S(1)}, f32[16,8,128]{2,1,0:T(8,128)S(1)}, u32[]{:S(2)}, u32[]{:S(2)}) collective-permute-start(f32[16,8,128]{2,1,0:T(8,128)S(1)} %shard_map.94.a), channel_id=1, source_target_pairs={{0,96},{8,104},{16,112},{24,120},{32,64},{40,72},{48,80},{56,88},{... | collective-permute-start | bytes 196616 | tf_op jit(solution)/shard_map/ppermute | solution.py:428
  89.5 5.7 %collective-permute-start.20 = (f32[16,8,128]{2,1,0:T(8,128)S(1)}, f32[16,8,128]{2,1,0:T(8,128)S(1)}, u32[]{:S(2)}, u32[]{:S(2)}) collective-permute-start(f32[16,8,128]{2,1,0:T(8,128)S(1)} %shard_map.95.a), channel_id=1, source_target_pairs={{0,128},{8,136},{16,144},{24,152},{32,160},{40,168},{48,176},{56,1... | collective-permute-start | bytes 196616 | tf_op jit(solution)/shard_map/ppermute | solution.py:428
  95.1 2.3 %collective-permute-done.20.b = f32[16,8,128]{2,1,0:T(8,128)S(1)} collective-permute-done((f32[16,8,128]{2,1,0:T(8,128)S(1)}, f32[16,8,128]{2,1,0:T(8,128)S(1)}, u32[]{:S(2)}, u32[]{:S(2)}) %collective-permute-start.20) | collective-permute-done | bytes 65568 | tf_op jit(solution)/shard_map/ppermute | solution.py:428
  97.4 5.0 %collective-permute-start.21 = (bf16[16,8,128]{2,1,0:T(8,128)(2,1)S(1)}, bf16[16,8,128]{2,1,0:T(8,128)(2,1)S(1)}, u32[]{:S(2)}, u32[]{:S(2)}) collective-permute-start(bf16[16,8,128]{2,1,0:T(8,128)(2,1)S(1)} %shard_map.96.half), channel_id=1, source_target_pairs={{0,8},{8,0},{16,24},{24,16},{32,40},{40,32},{48,56},{56,48},{64,72... | collective-permute-start | bytes 98312 | tf_op jit(solution)/shard_map/ppermute | solution.py:428
  107.6 1.9 %collective-permute-start.24 = (bf16[2,32,8,128]{3,2,1,0:T(8,128)(2,1)S(1)}, bf16[2,32,8,128]{3,2,1,0:T(8,128)(2,1)S(1)}, u32[]{:S(2)}, u32[]{:S(2)}) collective-permute-start(bf16[2,32,8,128]{3,2,1,0:T(8,128)(2,1)S(1)} %shard_map.97.tot.late), channel_id=1, source_target_pairs={{0,6},{1,7},{2,0},{3,1},{4,2},{5,3},{6,4},{7,5},{8,14},{9,15},{10,... | collective-permute-start | bytes 393224 | tf_op jit(solution)/shard_map/ppermute | solution.py:305
  111.5 3.7 %shard_map.100 = f32[512,1024]{1,0:T(8,128)} custom-call(f32[1024,512]{1,0:T(8,128)S(1)} %get-tuple-element.37.moment, f32[64,512]{1,0:T(8,128)S(1)} %get-tuple-element.38.picked, s32[16,4,512]{2,1,0:T(4,128)S(1)} %bitcast.9, bf16[256,256]{1,0:T(8,128)(2,1)S(1)} %copy-done.5, bf16[256,256]{1,0:T(8,128)(2,1)S(1)} %copy-done.6, ...), custom_call_target="tpu_custom_call" | custom-call | flops 805306368 | bytes 5242880 | tf_op jit(solution)/shard_map/pallas_call | solution.py:479
  115.2 3.6 %shard_map.98 = (f32[1024,256]{1,0:T(8,128)S(1)}, bf16[512,1024]{1,0:T(8,128)(2,1)}) custom-call(s32[2]{0:T(128)S(1)} %pad_add_fusion.where, bf16[256,4096]{1,0:T(8,128)(2,1)S(1)} %copy-done.1, bf16[320,1024]{1,0:T(8,128)(2,1)S(1)} %get-tuple-element.29.late.own, bf16[2,32,8,128]{3,2,1,0:T(8,128)(2,1)S(1)} %shard_map.97.tot.late, ...), custom_call_target="tpu_custom_call" | custom-call | flops 1610612736 | bytes 4194304 | tf_op jit(solution)/shard_map/pallas_call | solution.py:465
  119.2 6.6 %shard_map.99 = bf16[256,1024]{1,0:T(8,128)(2,1)} custom-call(s32[2]{0:T(128)S(1)} %pad_add_fusion.where, bf16[256,4096]{1,0:T(8,128)(2,1)S(1)} %copy-done.1, bf16[256,4096]{1,0:T(8,128)(2,1)S(1)} %copy-done.1, bf16[256,4096]{1,0:T(8,128)(2,1)S(1)} %copy-done.1, bf16[320,1024]{1,0:T(8,128)(2,1)S(1)} %get-tuple-element.29.late.own, ...), custom_call_target="tpu_custom_call" | custom-call | flops 3221225472 | bytes 7340032 | tf_op jit(solution)/shard_map/pallas_call | solution.py:489
  (63 shorter events, 27.0 us)
Async XLA Ops:
  0.6 31.8 %collective-permute-start.8 = (bf16[512,1024]{1,0:T(8,128)(2,1)}, bf16[512,1024]{1,0:T(8,128)(2,1)S(1)}, u32[]{:S(2)}, u32[]{:S(2)}) collective-permute-start(bf16[512,1024]{1,0:T(8,128)(2,1)} %weight.1), channel_id=1, source_target_pairs={{0,1},{1,0},{2,3},{3,2},{4,5},{5,4},{6,7},{7,6},{8,9},{9,8},{10,11... | collective-permute-start | bytes 3145736 | tf_op jit(solution)/shard_map/ppermute | solution.py:311
  6.2 13.6 %collective-permute-start = (bf16[512,512]{1,0:T(8,128)(2,1)S(1)}, bf16[512,512]{1,0:T(8,128)(2,1)S(1)}, u32[]{:S(2)}, u32[]{:S(2)}) collective-permute-start(bf16[512,512]{1,0:T(8,128)(2,1)S(1)} %get-tuple-element.21.sent.a0), channel_id=1, source_target_pairs={{0,2},{1,3},{2,4},{3,5},{4,6},{5,7},{6,0},{7,1},{8,10},{9,11},{10,... | collective-permute-start | bytes 1572872 | tf_op jit(solution)/shard_map/ppermute | solution.py:302
  7.5 12.2 %collective-permute-start.1 = (bf16[512,512]{1,0:T(8,128)(2,1)S(1)}, bf16[512,512]{1,0:T(8,128)(2,1)S(1)}, u32[]{:S(2)}, u32[]{:S(2)}) collective-permute-start(bf16[512,512]{1,0:T(8,128)(2,1)S(1)} %get-tuple-element.22), channel_id=1, source_target_pairs={{0,6},{1,7},{2,0},{3,1},{4,2},{5,3},{6,4},{7,5},{8,14},{9,15},{10,... | collective-permute-start | bytes 1572872 | tf_op jit(solution)/shard_map/ppermute | solution.py:305
  9.1 23.3 %collective-permute-start.7 = (bf16[512,512]{1,0:T(8,128)(2,1)S(1)}, bf16[512,512]{1,0:T(8,128)(2,1)S(1)}, u32[]{:S(2)}, u32[]{:S(2)}) collective-permute-start(bf16[512,512]{1,0:T(8,128)(2,1)S(1)} %get-tuple-element.28), channel_id=1, source_target_pairs={{0,4},{1,5},{2,6},{3,7},{4,0},{5,1},{6,2},{7,3},{8,12},{9,13},{10,... | collective-permute-start | bytes 1572872 | tf_op jit(solution)/shard_map/ppermute | solution.py:308
  33.1 22.8 %collective-permute-start.9 = (bf16[576,512]{1,0:T(8,128)(2,1)S(1)}, bf16[576,512]{1,0:T(8,128)(2,1)S(1)}, u32[]{:S(2)}, u32[]{:S(2)}) collective-permute-start(bf16[576,512]{1,0:T(8,128)(2,1)S(1)} %shard_map.88), channel_id=1, source_target_pairs={{0,1},{1,0},{2,3},{3,2},{4,5},{5,4},{6,7},{7,6},{8,9},{9,8},{10,11... | collective-permute-start | bytes 1769480 | tf_op jit(solution)/shard_map/ppermute | solution.py:311
  33.5 6.9 %collective-permute-start.2 = (bf16[512,256]{1,0:T(8,128)(2,1)S(1)}, bf16[512,256]{1,0:T(8,128)(2,1)S(1)}, u32[]{:S(2)}, u32[]{:S(2)}) collective-permute-start(bf16[512,256]{1,0:T(8,128)(2,1)S(1)} %shard_map.86.turned.b0.c0), channel_id=1, source_target_pairs={{0,2},{1,3},{2,4},{3,5},{4,6},{5,7},{6,0},{7,1},{8,10},{9,11},{10,... | collective-permute-start | bytes 786440 | tf_op jit(solution)/shard_map/ppermute | solution.py:302
  34.0 7.4 %collective-permute-start.3 = (bf16[512,256]{1,0:T(8,128)(2,1)S(1)}, bf16[512,256]{1,0:T(8,128)(2,1)S(1)}, u32[]{:S(2)}, u32[]{:S(2)}) collective-permute-start(bf16[512,256]{1,0:T(8,128)(2,1)S(1)} %shard_map.86.turned.b0.c0), channel_id=1, source_target_pairs={{0,6},{1,7},{2,0},{3,1},{4,2},{5,3},{6,4},{7,5},{8,14},{9,15},{10,... | collective-permute-start | bytes 786440 | tf_op jit(solution)/shard_map/ppermute | solution.py:305
  36.2 10.6 %collective-permute-start.13 = (bf16[512,256]{1,0:T(8,128)(2,1)S(1)}, bf16[512,256]{1,0:T(8,128)(2,1)S(1)}, u32[]{:S(2)}, u32[]{:S(2)}) collective-permute-start(bf16[512,256]{1,0:T(8,128)(2,1)S(1)} %shard_map.86.turned.b0.c0), channel_id=1, source_target_pairs={{0,4},{1,5},{2,6},{3,7},{4,0},{5,1},{6,2},{7,3},{8,12},{9,13},{10,... | collective-permute-start | bytes 786440 | tf_op jit(solution)/shard_map/ppermute | solution.py:308
  42.1 11.2 %collective-permute-start.4 = (bf16[256,512]{1,0:T(8,128)(2,1)S(1)}, bf16[256,512]{1,0:T(8,128)(2,1)S(1)}, u32[]{:S(2)}, u32[]{:S(2)}) collective-permute-start(bf16[256,512]{1,0:T(8,128)(2,1)S(1)} %get-tuple-element.24), channel_id=1, source_target_pairs={{0,6},{1,7},{2,0},{3,1},{4,2},{5,3},{6,4},{7,5},{8,14},{9,15},{10,... | collective-permute-start | bytes 786440 | tf_op jit(solution)/shard_map/ppermute | solution.py:305
  46.1 7.2 %collective-permute-start.5 = (bf16[256,512]{1,0:T(8,128)(2,1)S(1)}, bf16[256,512]{1,0:T(8,128)(2,1)S(1)}, u32[]{:S(2)}, u32[]{:S(2)}) collective-permute-start(bf16[256,512]{1,0:T(8,128)(2,1)S(1)} %get-tuple-element.25), channel_id=1, source_target_pairs={{0,4},{1,5},{2,6},{3,7},{4,0},{5,1},{6,2},{7,3},{8,12},{9,13},{10,... | collective-permute-start | bytes 786440 | tf_op jit(solution)/shard_map/ppermute | solution.py:308
  46.1 9.8 %collective-permute-start.6 = (bf16[256,512]{1,0:T(8,128)(2,1)S(1)}, bf16[256,512]{1,0:T(8,128)(2,1)S(1)}, u32[]{:S(2)}, u32[]{:S(2)}) collective-permute-start(bf16[256,512]{1,0:T(8,128)(2,1)S(1)} %get-tuple-element.26), channel_id=1, source_target_pairs={{0,2},{1,3},{2,4},{3,5},{4,6},{5,7},{6,0},{7,1},{8,10},{9,11},{10,... | collective-permute-start | bytes 786440 | tf_op jit(solution)/shard_map/ppermute | solution.py:302
  47.5 17.0 %collective-permute-start.14 = (bf16[512,512]{1,0:T(8,128)(2,1)S(1)}, bf16[512,512]{1,0:T(8,128)(2,1)S(1)}, u32[]{:S(2)}, u32[]{:S(2)}) collective-permute-start(bf16[512,512]{1,0:T(8,128)(2,1)S(1)} %shard_map.91), channel_id=1, source_target_pairs={{0,1},{1,0},{2,3},{3,2},{4,5},{5,4},{6,7},{7,6},{8,9},{9,8},{10,11... | collective-permute-start | bytes 1572872 | tf_op jit(solution)/shard_map/ppermute | solution.py:311
  58.9 48.1 %collective-permute-start.10 = (bf16[320,1024]{1,0:T(8,128)(2,1)S(1)}, bf16[320,1024]{1,0:T(8,128)(2,1)S(1)}, u32[]{:S(2)}, u32[]{:S(2)}) collective-permute-start(bf16[320,1024]{1,0:T(8,128)(2,1)S(1)} %get-tuple-element.30), channel_id=1, source_target_pairs={{0,6},{1,7},{2,0},{3,1},{4,2},{5,3},{6,4},{7,5},{8,14},{9,15},{10,... | collective-permute-start | bytes 1966088 | tf_op jit(solution)/shard_map/ppermute | solution.py:305
  61.4 45.6 %collective-permute-start.11 = (bf16[320,1024]{1,0:T(8,128)(2,1)S(1)}, bf16[320,1024]{1,0:T(8,128)(2,1)S(1)}, u32[]{:S(2)}, u32[]{:S(2)}) collective-permute-start(bf16[320,1024]{1,0:T(8,128)(2,1)S(1)} %get-tuple-element.31), channel_id=1, source_target_pairs={{0,4},{1,5},{2,6},{3,7},{4,0},{5,1},{6,2},{7,3},{8,12},{9,13},{10,... | collective-permute-start | bytes 1966088 | tf_op jit(solution)/shard_map/ppermute | solution.py:308
  61.9 45.1 %collective-permute-start.12 = (bf16[320,1024]{1,0:T(8,128)(2,1)S(1)}, bf16[320,1024]{1,0:T(8,128)(2,1)S(1)}, u32[]{:S(2)}, u32[]{:S(2)}) collective-permute-start(bf16[320,1024]{1,0:T(8,128)(2,1)S(1)} %get-tuple-element.32), channel_id=1, source_target_pairs={{0,2},{1,3},{2,4},{3,5},{4,6},{5,7},{6,0},{7,1},{8,10},{9,11},{10,... | collective-permute-start | bytes 1966088 | tf_op jit(solution)/shard_map/ppermute | solution.py:302
  68.1 6.6 %collective-permute-start.15 = (f32[16,8,128]{2,1,0:T(8,128)S(1)}, f32[16,8,128]{2,1,0:T(8,128)S(1)}, u32[]{:S(2)}, u32[]{:S(2)}) collective-permute-start(f32[16,8,128]{2,1,0:T(8,128)S(1)} %get-tuple-element.34), channel_id=1, source_target_pairs={{0,8},{8,0},{16,24},{24,16},{32,40},{40,32},{48,56},{56,48},{64,72... | collective-permute-start | bytes 196616 | tf_op jit(solution)/shard_map/ppermute | solution.py:428
  74.7 5.0 %collective-permute-start.16 = (f32[16,8,128]{2,1,0:T(8,128)S(1)}, f32[16,8,128]{2,1,0:T(8,128)S(1)}, u32[]{:S(2)}, u32[]{:S(2)}) collective-permute-start(f32[16,8,128]{2,1,0:T(8,128)S(1)} %shard_map.93.a), channel_id=1, source_target_pairs={{0,16},{8,24},{16,0},{24,8},{32,48},{40,56},{48,32},{56,40},{64,80... | collective-permute-start | bytes 196616 | tf_op jit(solution)/shard_map/ppermute | solution.py:428
  81.4 6.1 %collective-permute-start.18 = (f32[16,8,128]{2,1,0:T(8,128)S(1)}, f32[16,8,128]{2,1,0:T(8,128)S(1)}, u32[]{:S(2)}, u32[]{:S(2)}) collective-permute-start(f32[16,8,128]{2,1,0:T(8,128)S(1)} %shard_map.94.a), channel_id=1, source_target_pairs={{0,64},{8,72},{16,80},{24,88},{32,96},{40,104},{48,112},{56,120},{... | collective-permute-start | bytes 196616 | tf_op jit(solution)/shard_map/ppermute | solution.py:428
  84.4 5.0 %collective-permute-start.19 = (f32[16,8,128]{2,1,0:T(8,128)S(1)}, f32[16,8,128]{2,1,0:T(8,128)S(1)}, u32[]{:S(2)}, u32[]{:S(2)}) collective-permute-start(f32[16,8,128]{2,1,0:T(8,128)S(1)} %shard_map.94.a), channel_id=1, source_target_pairs={{0,96},{8,104},{16,112},{24,120},{32,64},{40,72},{48,80},{56,88},{... | collective-permute-start | bytes 196616 | tf_op jit(solution)/shard_map/ppermute | solution.py:428
  89.5 7.9 %collective-permute-start.20 = (f32[16,8,128]{2,1,0:T(8,128)S(1)}, f32[16,8,128]{2,1,0:T(8,128)S(1)}, u32[]{:S(2)}, u32[]{:S(2)}) collective-permute-start(f32[16,8,128]{2,1,0:T(8,128)S(1)} %shard_map.95.a), channel_id=1, source_target_pairs={{0,128},{8,136},{16,144},{24,152},{32,160},{40,168},{48,176},{56,1... | collective-permute-start | bytes 196616 | tf_op jit(solution)/shard_map/ppermute | solution.py:428
  97.4 6.3 %collective-permute-start.21 = (bf16[16,8,128]{2,1,0:T(8,128)(2,1)S(1)}, bf16[16,8,128]{2,1,0:T(8,128)(2,1)S(1)}, u32[]{:S(2)}, u32[]{:S(2)}) collective-permute-start(bf16[16,8,128]{2,1,0:T(8,128)(2,1)S(1)} %shard_map.96.half), channel_id=1, source_target_pairs={{0,8},{8,0},{16,24},{24,16},{32,40},{40,32},{48,56},{56,48},{64,72... | collective-permute-start | bytes 98312 | tf_op jit(solution)/shard_map/ppermute | solution.py:428
  107.6 11.2 %collective-permute-start.24 = (bf16[2,32,8,128]{3,2,1,0:T(8,128)(2,1)S(1)}, bf16[2,32,8,128]{3,2,1,0:T(8,128)(2,1)S(1)}, u32[]{:S(2)}, u32[]{:S(2)}) collective-permute-start(bf16[2,32,8,128]{3,2,1,0:T(8,128)(2,1)S(1)} %shard_map.97.tot.late), channel_id=1, source_target_pairs={{0,6},{1,7},{2,0},{3,1},{4,2},{5,3},{6,4},{7,5},{8,14},{9,15},{10,... | collective-permute-start | bytes 393224 | tf_op jit(solution)/shard_map/ppermute | solution.py:305
  109.5 9.3 %collective-permute-start.25 = (bf16[2,32,8,128]{3,2,1,0:T(8,128)(2,1)S(1)}, bf16[2,32,8,128]{3,2,1,0:T(8,128)(2,1)S(1)}, u32[]{:S(2)}, u32[]{:S(2)}) collective-permute-start(bf16[2,32,8,128]{3,2,1,0:T(8,128)(2,1)S(1)} %shard_map.97.tot.late), channel_id=1, source_target_pairs={{0,4},{1,5},{2,6},{3,7},{4,0},{5,1},{6,2},{7,3},{8,12},{9,13},{10,... | collective-permute-start | bytes 393224 | tf_op jit(solution)/shard_map/ppermute | solution.py:308
  110.7 8.5 %collective-permute-start.26 = (bf16[2,32,8,128]{3,2,1,0:T(8,128)(2,1)S(1)}, bf16[2,32,8,128]{3,2,1,0:T(8,128)(2,1)S(1)}, u32[]{:S(2)}, u32[]{:S(2)}) collective-permute-start(bf16[2,32,8,128]{3,2,1,0:T(8,128)(2,1)S(1)} %shard_map.97.tot.late), channel_id=1, source_target_pairs={{0,2},{1,3},{2,4},{3,5},{4,6},{5,7},{6,0},{7,1},{8,10},{9,11},{10,... | collective-permute-start | bytes 393224 | tf_op jit(solution)/shard_map/ppermute | solution.py:302
  (11 other events, 74.3 us)

commit v5 on v4

--- a/solution.py
+++ b/solution.py
@@ -107,7 +107,7 @@
     out[...] = cot[...].T
 
 
-def pack_own_kernel(where, t0, t1, t2, t3, late_lo, late_hi, mine, to_up, to_far, to_down):
+def pack_own_kernel(where, t0, t1, t2, t3, late, turned, mine, to_up, to_far, to_down):
     for out, t in ((mine, t0), (to_up, t1), (to_far, t2), (to_down, t3)):
         out[...] = t[...]
 
@@ -152,7 +152,7 @@
     return rows
 
 
-def pick_kernel(where, pre, got_a, got_b, idx, ch, cl, late, moment, picked, keep, send):
+def pick_kernel(where, pre, got_a, got_b, idx, ch, cl, moment, picked, keep, send):
     step = pl.program_id(0)
     first = step < STEPS // 2
     got = jnp.where(first, got_a[...], got_b[...]).astype(jnp.float32)
@@ -172,11 +172,11 @@
     pl.when(jnp.logical_not(here))(lambda: put(send))
 
 
-def add_two_kernel(a, b, out):
+def add_two_kernel(a, b, late, out):
     out[...] = (a[...] + b[...]).astype(out.dtype)
 
 
-def add_four_kernel(a, b, c, d, out):
+def add_four_kernel(a, b, c, d, late, out):
     out[...] = (a[...] + b[...]) + (c[...] + d[...])
 
 
@@ -189,7 +189,7 @@
     out[1 - side, pl.ds(other, TILES // 2)] = corner[...]
 
 
-def residual_kernel(moment, picked, idx, ch, cl, late, out):
+def residual_kernel(moment, picked, idx, ch, cl, late, out, mark):
     parts = []
     for b in range(GROUP // BLOCK):
         at = [idx[b, j : j + 1, :] for j in range(KEEP)]
@@ -198,9 +198,10 @@
     kept = jnp.concatenate(parts, axis=0)
     back = three_pass((ch[...], cl[...]), split_pair(kept), ((0,), (0,)))
     out[...] = (moment[...] - back).T
-
-
-def base_kernel(where, o0, o1, o2, o3, p0, p1, p2, p3, w_own, w_peer, idx, got_a, *outs):
+    mark[...] = back[:8, :LANES]
+
+
+def base_kernel(where, o0, o1, o2, o3, p0, p1, p2, p3, w_own, w_peer, idx, got_a, late, *outs):
     mine, theirs = flat_index(idx), got_a[HALF:, :]
     first = (where[0] & 1) == 0
     left, right = jnp.where(first, mine, theirs), jnp.where(first, theirs, mine)
@@ -355,7 +356,7 @@
         out_shape=[shape(TOK, ROWS)] * 4,
         compiler_params=params(),
         cost_estimate=cost(0, 2),
-    )(place, tokens, tokens, tokens, tokens, b_lo, b_hi)
+    )(place, tokens, tokens, tokens, tokens, first_x, cot_b)
     owns = (own_0, down(own_down), across(own_across), up(own_up))
 
     partial_a = pl.pallas_call(
@@ -392,23 +393,6 @@
         cost_estimate=cost(2 * KV * KV * ROWS, 7),
     )(*firsts, *cots_b, *owns, momentum[0])
 
-    base, base_up, base_across, base_down = pl.pallas_call(
-        base_kernel,
-        grid_spec=pltpu.PrefetchScalarGridSpec(
-            num_scalar_prefetch=1,
-            grid=(1,),
-            in_specs=[PIECE] * 5
-            + [MESSAGE] * 3
-            + [whole(ROWS, KV)] * 2
-            + [INDEX, whole(HALF + PICKS, ROWS)],
-            out_specs=[whole(TOK + PICKS, KV)] * 4,
-        ),
-        out_shape=[shape(TOK + PICKS, KV)] * 4,
-        compiler_params=params(2 * VMEM_LIMIT),
-        cost_estimate=cost(4 * KV * KV * ROWS, 7),
-    )(place, *owns, peer_0, *firsts[1:], weight, weight_peer, index_t, got_a)
-    base_lo, base_hi, base_far = up(base_up), down(base_down), across(base_across)
-
     halves = whole(TILES // 2, 8, LANES)
     half_shape = shape(TILES // 2, 8, LANES, dtype=F32)
     moment, picked, keep, send = pl.pallas_call(
@@ -416,32 +400,62 @@
         grid_spec=pltpu.PrefetchScalarGridSpec(
             num_scalar_prefetch=1,
             grid=(STEPS,),
-            in_specs=[by_row(GROUP, ROWS)] + GOT + [INDEX_STEP] + BASIS + [AFTER],
+            in_specs=[by_row(GROUP, ROWS)] + GOT + [INDEX_STEP] + BASIS,
             out_specs=[by_row(GROUP, ROWS), by_row(PICKS // STEPS, ROWS), halves, halves],
         ),
         out_shape=[shape(KV, ROWS, dtype=F32), shape(PICKS, ROWS, dtype=F32), half_shape, half_shape],
         compiler_params=params(),
         cost_estimate=cost(6 * KV * GROUP * ROWS, 6),
-    )(place, pre, got_a, got_b, index_t, high, low, base)
+    )(place, pre, got_a, got_b, index_t, high, low)
 
     def partner(x, bits):
         return lax.ppermute(x, "rep", [(i, i ^ bits) for i in range(REPS)])
 
-    def add(kernel, result, *parts):
+    from_core, from_hi, from_corner = partner(send, 1), partner(keep, 2), partner(send, 3)
+
+    base, base_up, base_across, base_down = pl.pallas_call(
+        base_kernel,
+        grid_spec=pltpu.PrefetchScalarGridSpec(
+            num_scalar_prefetch=1,
+            grid=(1,),
+            in_specs=[PIECE] * 5
+            + [MESSAGE] * 3
+            + [whole(ROWS, KV)] * 2
+            + [INDEX, whole(HALF + PICKS, ROWS), AFTER],
+            out_specs=[whole(TOK + PICKS, KV)] * 4,
+        ),
+        out_shape=[shape(TOK + PICKS, KV)] * 4,
+        compiler_params=params(2 * VMEM_LIMIT),
+        cost_estimate=cost(4 * KV * KV * ROWS, 7),
+    )(place, *owns, peer_0, *firsts[1:], weight, weight_peer, index_t, got_a, from_core)
+    base_lo, base_hi, base_far = up(base_up), down(base_down), across(base_across)
+
+    def add(kernel, result, after, *parts):
         return pl.pallas_call(
             kernel,
             grid=(1,),
-            in_specs=[halves] * len(parts),
+            in_specs=[halves] * len(parts) + [AFTER],
             out_specs=halves,
             out_shape=result,
             compiler_params=params(),
             cost_estimate=cost(0, 0.25),
-        )(*parts)
-
-    value = add(add_two_kernel, half_shape, keep, partner(send, 1))
-    value = add(add_two_kernel, half_shape, value, partner(value, 2))
-    value = add(add_four_kernel, half_shape, value, partner(value, 4), partner(value, 8), partner(value, 12))
-    half = add(add_two_kernel, shape(TILES // 2, 8, LANES), value, partner(value, 16))
+        )(*parts, after)
+
+    value = add(add_four_kernel, half_shape, base, keep, from_core, from_hi, from_corner)
+    value = add(
+        add_four_kernel, half_shape, keep, value, partner(value, 4), partner(value, 8), partner(value, 12)
+    )
+    last = partner(value, 16)
+    new_momentum, mark = pl.pallas_call(
+        residual_kernel,
+        grid=(STEPS,),
+        in_specs=[by_row(GROUP, ROWS), by_row(PICKS // STEPS, ROWS), INDEX_STEP] + BASIS + [AFTER],
+        out_specs=[by_col(ROWS, GROUP), whole(8, LANES)],
+        out_shape=[shape(ROWS, KV, dtype=F32), shape(8, LANES, dtype=F32)],
+        compiler_params=params(),
+        cost_estimate=cost(6 * KV * GROUP * ROWS, 5),
+    )(moment, picked, index_t, high, low, value)
+    half = add(add_two_kernel, shape(TILES // 2, 8, LANES), mark, value, last)
 
     corner = lax.ppermute(half, ("rep", "fsdp"), [(i, i ^ 9) for i in range(REPS * 8)])
     pair_spec = whole(2, TILES, 8, LANES)
@@ -475,16 +489,6 @@
         compiler_params=params(),
         cost_estimate=cost(3 * KV * KV * ROWS, 4),
     )(place, tokens, base, pair, weight, high, low)
-
-    new_momentum = pl.pallas_call(
-        residual_kernel,
-        grid=(STEPS,),
-        in_specs=[by_row(GROUP, ROWS), by_row(PICKS // STEPS, ROWS), INDEX_STEP] + BASIS + [AFTER],
-        out_specs=by_col(ROWS, GROUP),
-        out_shape=shape(ROWS, KV, dtype=F32),
-        compiler_params=params(),
-        cost_estimate=cost(6 * KV * GROUP * ROWS, 5),
-    )(moment, picked, index_t, high, low, pair)
 
     projected = pl.pallas_call(
         forward_kernel,

time: 126 us -> 132 us (1.048)
  waiting for transfers between devices: 44 us -> 51.3 us
  starting transfers between devices: 52.1 us -> 50.4 us
    ppermute x5, waiting for transfers between devices: 5.64 us -> 15.8 us  [down(): return lax.ppermute(x, 'fsdp', [(i, (i + 6) % 8) for i in range(8)])]
    ppermute x7 -> x8, starting transfers between devices: 27 us -> 19 us  [partner(): return lax.ppermute(x, 'rep', [(i, i ^ bits) for i in range(REPS)])]
    ppermute x7 -> x8, waiting for transfers between devices: 7.23 us -> 13.5 us  [partner(): return lax.ppermute(x, 'rep', [(i, i ^ bits) for i in range(REPS)])]
    ppermute x4, starting transfers between devices: 5.03 us -> 11.3 us  [swap(): return lax.ppermute(x, 'fsdp', [(i, i ^ 1) for i in range(8)])]
    ppermute x5, waiting for transfers between devices: 12.5 us -> 7.19 us  [across(): return lax.ppermute(x, 'fsdp', [(i, (i + 4) % 8) for i in range(8)])]
    ppermute x5, starting transfers between devices: 12 us -> 8.14 us  [down(): return lax.ppermute(x, 'fsdp', [(i, (i + 6) % 8) for i in range(8)])]
    ppermute x5, starting transfers between devices: 3.25 us -> 5.82 us  [across(): return lax.ppermute(x, 'fsdp', [(i, (i + 4) % 8) for i in range(8)])]
    ppermute x5, waiting for transfers between devices: 16.3 us -> 14.2 us  [up(): return lax.ppermute(x, 'fsdp', [(i, (i + 2) % 8) for i in range(8)])]
  transfers between devices with their start and end apart: 27 -> 28, of which waited for: 13 -> 16; matrix products, arithmetic and copies ran while one was open for 0% -> 0% of each run, Pallas kernels for 15% -> 10%
where the time goes in v5:
time: 132 us; the launch traced here: 131 us
  waiting for transfers between devices  51.3 us (39%)
  starting transfers between devices  50.4 us (38%)
  Pallas kernels  26.1 us (20%)
  local copies, waits for them, and re-layouts  2.66 us (2%)
    ppermute x8, starting transfers between devices, partner(): return lax.ppermute(x, 'rep', [(i, i ^ bits) for i in range(REPS)])  19 us
    ppermute x5, waiting for transfers between devices, down(): return lax.ppermute(x, 'fsdp', [(i, (i + 6) % 8) for i in range(8)])  15.8 us
    ppermute x5, waiting for transfers between devices, up(): return lax.ppermute(x, 'fsdp', [(i, (i + 2) % 8) for i in range(8)])  14.2 us
    ppermute x8, waiting for transfers between devices, partner(): return lax.ppermute(x, 'rep', [(i, i ^ bits) for i in range(REPS)])  13.5 us
    ppermute x4, starting transfers between devices, swap(): return lax.ppermute(x, 'fsdp', [(i, i ^ 1) for i in range(8)])  11.3 us
    ppermute x5, starting transfers between devices, down(): return lax.ppermute(x, 'fsdp', [(i, (i + 6) % 8) for i in range(8)])  8.14 us
    ppermute x5, waiting for transfers between devices, across(): return lax.ppermute(x, 'fsdp', [(i, (i + 4) % 8) for i in range(8)])  7.19 us
    pallas_call x1, Pallas kernels, body(): pl.pallas_call(forward_kernel, grid_spec=pltpu.PrefetchScalarGridSpec(num...  6.57 us
  transfers between devices with their start and end apart: 28, of which 16 were waited for; matrix products, arithmetic and copies ran while one was open for 0% of the time, Pallas kernels for 10%

profile of v5, /device:TPU:1, one launch (start us, length us, event | category | flops | bytes accessed | tf_op | source)
XLA Modules:
  0.0 131.4 jit_solution(8937242203112257165)
XLA Ops:
  6.2 2.8 %collective-permute-start.2 = (bf16[512,512]{1,0:T(8,128)(2,1)S(1)}, bf16[512,512]{1,0:T(8,128)(2,1)S(1)}, u32[]{:S(2)}, u32[]{:S(2)}) collective-permute-start(bf16[512,512]{1,0:T(8,128)(2,1)S(1)} %get-tuple-element.25), channel_id=1, source_target_pairs={{0,6},{1,7},{2,0},{3,1},{4,2},{5,3},{6,4},{7,5},{8,14},{9,15},{10,... | collective-permute-start | bytes 1572872 | tf_op jit(solution)/shard_map/ppermute | solution.py:306
  10.6 10.0 %collective-permute-done.2.late_hi.hi.a1.p1 = bf16[512,512]{1,0:T(8,128)(2,1)S(1)} collective-permute-done((bf16[512,512]{1,0:T(8,128)(2,1)S(1)}, bf16[512,512]{1,0:T(8,128)(2,1)S(1)}, u32[]{:S(2)}, u32[]{:S(2)}) %collective-permute-start.2) | collective-permute-done | bytes 524320 | tf_op jit(solution)/shard_map/ppermute | solution.py:306
  20.6 2.8 %collective-permute-done.1.late_lo.lo.a3.p3 = bf16[512,512]{1,0:T(8,128)(2,1)S(1)} collective-permute-done((bf16[512,512]{1,0:T(8,128)(2,1)S(1)}, bf16[512,512]{1,0:T(8,128)(2,1)S(1)}, u32[]{:S(2)}, u32[]{:S(2)}) %collective-permute-start.1) | collective-permute-done | bytes 524320 | tf_op jit(solution)/shard_map/ppermute | solution.py:303
  23.6 2.2 %collective-permute-start.9 = (bf16[512,256]{1,0:T(8,128)(2,1)S(1)}, bf16[512,256]{1,0:T(8,128)(2,1)S(1)}, u32[]{:S(2)}, u32[]{:S(2)}) collective-permute-start(bf16[512,256]{1,0:T(8,128)(2,1)S(1)} %shard_map.86.turned.b0.c0), channel_id=1, source_target_pairs={{0,4},{1,5},{2,6},{3,7},{4,0},{5,1},{6,2},{7,3},{8,12},{9,13},{10,... | collective-permute-start | bytes 786440 | tf_op jit(solution)/shard_map/ppermute | solution.py:309
  26.3 6.3 %collective-permute-done.late.far.a2.p2 = bf16[512,512]{1,0:T(8,128)(2,1)S(1)} collective-permute-done((bf16[512,512]{1,0:T(8,128)(2,1)S(1)}, bf16[512,512]{1,0:T(8,128)(2,1)S(1)}, u32[]{:S(2)}, u32[]{:S(2)}) %collective-permute-start) | collective-permute-done | bytes 524320 | tf_op jit(solution)/shard_map/ppermute | solution.py:309
  33.4 3.0 %collective-permute-start.7 = (bf16[576,512]{1,0:T(8,128)(2,1)S(1)}, bf16[576,512]{1,0:T(8,128)(2,1)S(1)}, u32[]{:S(2)}, u32[]{:S(2)}) collective-permute-start(bf16[576,512]{1,0:T(8,128)(2,1)S(1)} %shard_map.88), channel_id=1, source_target_pairs={{0,1},{1,0},{2,3},{3,2},{4,5},{5,4},{6,7},{7,6},{8,9},{9,8},{10,11... | collective-permute-start | bytes 1769480 | tf_op jit(solution)/shard_map/ppermute | solution.py:312
  36.4 4.3 %collective-permute-done.10.b3.c3 = bf16[512,256]{1,0:T(8,128)(2,1)S(1)} collective-permute-done((bf16[512,256]{1,0:T(8,128)(2,1)S(1)}, bf16[512,256]{1,0:T(8,128)(2,1)S(1)}, u32[]{:S(2)}, u32[]{:S(2)}) %collective-permute-start.10) | collective-permute-done | bytes 262176 | tf_op jit(solution)/shard_map/ppermute | solution.py:303
  41.4 5.0 %collective-permute-start.11 = (bf16[512,512]{1,0:T(8,128)(2,1)S(1)}, bf16[512,512]{1,0:T(8,128)(2,1)S(1)}, u32[]{:S(2)}, u32[]{:S(2)}) collective-permute-start(bf16[512,512]{1,0:T(8,128)(2,1)S(1)} %shard_map.90), channel_id=1, source_target_pairs={{0,1},{1,0},{2,3},{3,2},{4,5},{5,4},{6,7},{7,6},{8,9},{9,8},{10,11... | collective-permute-start | bytes 1572872 | tf_op jit(solution)/shard_map/ppermute | solution.py:312
  47.1 2.2 %collective-permute-start.3 = (bf16[256,512]{1,0:T(8,128)(2,1)S(1)}, bf16[256,512]{1,0:T(8,128)(2,1)S(1)}, u32[]{:S(2)}, u32[]{:S(2)}) collective-permute-start(bf16[256,512]{1,0:T(8,128)(2,1)S(1)} %get-tuple-element.27), channel_id=1, source_target_pairs={{0,6},{1,7},{2,0},{3,1},{4,2},{5,3},{6,4},{7,5},{8,14},{9,15},{10,... | collective-permute-start | bytes 786440 | tf_op jit(solution)/shard_map/ppermute | solution.py:306
  50.0 5.8 %collective-permute-done.3.t1.o1 = bf16[256,512]{1,0:T(8,128)(2,1)S(1)} collective-permute-done((bf16[256,512]{1,0:T(8,128)(2,1)S(1)}, bf16[256,512]{1,0:T(8,128)(2,1)S(1)}, u32[]{:S(2)}, u32[]{:S(2)}) %collective-permute-start.3) | collective-permute-done | bytes 262176 | tf_op jit(solution)/shard_map/ppermute | solution.py:306
  56.1 7.1 %collective-permute-done.5.t3.o3 = bf16[256,512]{1,0:T(8,128)(2,1)S(1)} collective-permute-done((bf16[256,512]{1,0:T(8,128)(2,1)S(1)}, bf16[256,512]{1,0:T(8,128)(2,1)S(1)}, u32[]{:S(2)}, u32[]{:S(2)}) %collective-permute-start.5) | collective-permute-done | bytes 262176 | tf_op jit(solution)/shard_map/ppermute | solution.py:303
  63.2 2.3 %shard_map.89.pre = f32[1024,512]{1,0:T(8,128)S(1)} custom-call(bf16[512,512]{1,0:T(8,128)(2,1)S(1)} %get-tuple-element.24.sent.a0, bf16[512,512]{1,0:T(8,128)(2,1)S(1)} %collective-permute-done.2.late_hi.hi.a1.p1, bf16[512,512]{1,0:T(8,128)(2,1)S(1)} %collective-permute-done.late.far.a2.p2, bf16[512,512]{1,0:T(8,128)(2,1)S(1)} %collective-permute-done.1.late_lo.lo.a3.p3, ...), custom_call_target="tpu_custom_call" | custom-call | flops 1073741824 | bytes 7340032 | tf_op jit(solution)/shard_map/pallas_call | solution.py:383
  65.6 3.5 %shard_map.91 = (f32[1024,512]{1,0:T(8,128)S(1)}, f32[64,512]{1,0:T(8,128)S(1)}, f32[16,8,128]{2,1,0:T(8,128)S(1)}, f32[16,8,128]{2,1,0:T(8,128)S(1)}) custom-call(s32[2]{0:T(128)S(1)} %pad_add_fusion.where, f32[1024,512]{1,0:T(8,128)S(1)} %shard_map.89.pre, bf16[576,512]{1,0:T(8,128)(2,1)S(1)} %collective-permute-done.7.got_a, ...), custom_call_target="tpu_custom_call" | custom-call | flops 805306368 | bytes 6291456 | tf_op jit(solution)/shard_map/pallas_call | solution.py:398
  71.8 3.0 %shard_map.92 = (bf16[320,1024]{1,0:T(8,128)(2,1)S(1)}, bf16[320,1024]{1,0:T(8,128)(2,1)S(1)}, bf16[320,1024]{1,0:T(8,128)(2,1)S(1)}, bf16[320,1024]{1,0:T(8,128)(2,1)S(1)}) custom-call(s32[2]{0:T(128)S(1)} %pad_add_fusion.where, bf16[256,512]{1,0:T(8,128)(2,1)S(1)} %get-tuple-element.26.t0.o0, bf16[256,512]{1,0:T(8,128)(2,1)S(1)} %collective-permute-done.3.t1.o1, ...), custom_call_target="tpu_custom_call" | custom-call | flops 2147483648 | bytes 7340032 | tf_op jit(solution)/shard_map/pallas_call | solution.py:416
  76.4 5.1 %collective-permute-start.17 = (f32[16,8,128]{2,1,0:T(8,128)S(1)}, f32[16,8,128]{2,1,0:T(8,128)S(1)}, u32[]{:S(2)}, u32[]{:S(2)}) collective-permute-start(f32[16,8,128]{2,1,0:T(8,128)S(1)} %get-tuple-element.31), channel_id=1, source_target_pairs={{0,24},{8,16},{16,8},{24,0},{32,56},{40,48},{48,40},{56,32},{64,88... | collective-permute-start | bytes 196616 | tf_op jit(solution)/shard_map/ppermute | solution.py:412
  81.5 2.2 %collective-permute-done.17.d = f32[16,8,128]{2,1,0:T(8,128)S(1)} collective-permute-done((f32[16,8,128]{2,1,0:T(8,128)S(1)}, f32[16,8,128]{2,1,0:T(8,128)S(1)}, u32[]{:S(2)}, u32[]{:S(2)}) %collective-permute-start.17) | collective-permute-done | bytes 65568 | tf_op jit(solution)/shard_map/ppermute | solution.py:412
  83.7 3.3 %collective-permute-done.16.c = f32[16,8,128]{2,1,0:T(8,128)S(1)} collective-permute-done((f32[16,8,128]{2,1,0:T(8,128)S(1)}, f32[16,8,128]{2,1,0:T(8,128)S(1)}, u32[]{:S(2)}, u32[]{:S(2)}) %collective-permute-start.16) | collective-permute-done | bytes 65568 | tf_op jit(solution)/shard_map/ppermute | solution.py:412
  87.0 4.4 %collective-permute-start.20 = (f32[16,8,128]{2,1,0:T(8,128)S(1)}, f32[16,8,128]{2,1,0:T(8,128)S(1)}, u32[]{:S(2)}, u32[]{:S(2)}) collective-permute-start(f32[16,8,128]{2,1,0:T(8,128)S(1)} %shard_map.93.a), channel_id=1, source_target_pairs={{0,96},{8,104},{16,112},{24,120},{32,64},{40,72},{48,80},{56,88},{... | collective-permute-start | bytes 196616 | tf_op jit(solution)/shard_map/ppermute | solution.py:412
  93.5 2.8 %collective-permute-done.19.c = f32[16,8,128]{2,1,0:T(8,128)S(1)} collective-permute-done((f32[16,8,128]{2,1,0:T(8,128)S(1)}, f32[16,8,128]{2,1,0:T(8,128)S(1)}, u32[]{:S(2)}, u32[]{:S(2)}) %collective-permute-start.19) | collective-permute-done | bytes 65568 | tf_op jit(solution)/shard_map/ppermute | solution.py:412
  97.8 6.1 %collective-permute-start.21 = (f32[16,8,128]{2,1,0:T(8,128)S(1)}, f32[16,8,128]{2,1,0:T(8,128)S(1)}, u32[]{:S(2)}, u32[]{:S(2)}) collective-permute-start(f32[16,8,128]{2,1,0:T(8,128)S(1)} %shard_map.94.late.a), channel_id=1, source_target_pairs={{0,128},{8,136},{16,144},{24,152},{32,160},{40,168},{48,176},{56,1... | collective-permute-start | bytes 196616 | tf_op jit(solution)/shard_map/ppermute | solution.py:412
  103.9 3.7 %shard_map.95 = (f32[512,1024]{1,0:T(8,128)}, f32[8,128]{1,0:T(8,128)S(1)}) custom-call(f32[1024,512]{1,0:T(8,128)S(1)} %get-tuple-element.37.moment, f32[64,512]{1,0:T(8,128)S(1)} %get-tuple-element.38.picked, s32[16,4,512]{2,1,0:T(4,128)S(1)} %bitcast.9, bf16[256,256]{1,0:T(8,128)(2,1)S(1)} %copy-done.6, bf16[256,256]{1,0:T(8,128)(2,1)S(1)} %copy-done.5, ...), custom_call_target="tpu_custom_call" | custom-call | flops 805306368 | bytes 5242880 | tf_op jit(solution)/shard_map/pallas_call | solution.py:449
  107.6 2.9 %collective-permute-start.24 = (bf16[16,8,128]{2,1,0:T(8,128)(2,1)S(1)}, bf16[16,8,128]{2,1,0:T(8,128)(2,1)S(1)}, u32[]{:S(2)}, u32[]{:S(2)}) collective-permute-start(bf16[16,8,128]{2,1,0:T(8,128)(2,1)S(1)} %shard_map.96.half), channel_id=1, source_target_pairs={{0,9},{1,8},{2,11},{3,10},{4,13},{5,12},{6,15},{7,14},{8,1},{9,0},... | collective-permute-start | bytes 98312 | tf_op jit(solution)/shard_map/ppermute | solution.py:460
  120.6 3.6 %shard_map.98 = (f32[1024,256]{1,0:T(8,128)S(1)}, bf16[512,1024]{1,0:T(8,128)(2,1)}) custom-call(s32[2]{0:T(128)S(1)} %pad_add_fusion.where, bf16[256,4096]{1,0:T(8,128)(2,1)S(1)} %copy-done.1, bf16[320,1024]{1,0:T(8,128)(2,1)S(1)} %get-tuple-element.32.late.own, bf16[2,32,8,128]{3,2,1,0:T(8,128)(2,1)S(1)} %shard_map.97.tot, ...), custom_call_target="tpu_custom_call" | custom-call | flops 1610612736 | bytes 4194304 | tf_op jit(solution)/shard_map/pallas_call | solution.py:479
  124.8 6.6 %shard_map.99 = bf16[256,1024]{1,0:T(8,128)(2,1)} custom-call(s32[2]{0:T(128)S(1)} %pad_add_fusion.where, bf16[256,4096]{1,0:T(8,128)(2,1)S(1)} %copy-done.1, bf16[256,4096]{1,0:T(8,128)(2,1)S(1)} %copy-done.1, bf16[256,4096]{1,0:T(8,128)(2,1)S(1)} %copy-done.1, bf16[320,1024]{1,0:T(8,128)(2,1)S(1)} %get-tuple-element.32.late.own, ...), custom_call_target="tpu_custom_call" | custom-call | flops 3221225472 | bytes 7340032 | tf_op jit(solution)/shard_map/pallas_call | solution.py:493
  (64 shorter events, 29.4 us)
Async XLA Ops:
  0.6 32.0 %collective-permute-start.6 = (bf16[512,1024]{1,0:T(8,128)(2,1)}, bf16[512,1024]{1,0:T(8,128)(2,1)S(1)}, u32[]{:S(2)}, u32[]{:S(2)}) collective-permute-start(bf16[512,1024]{1,0:T(8,128)(2,1)} %weight.1), channel_id=1, source_target_pairs={{0,1},{1,0},{2,3},{3,2},{4,5},{5,4},{6,7},{7,6},{8,9},{9,8},{10,11... | collective-permute-start | bytes 3145736 | tf_op jit(solution)/shard_map/ppermute | solution.py:312
  6.2 14.4 %collective-permute-start.2 = (bf16[512,512]{1,0:T(8,128)(2,1)S(1)}, bf16[512,512]{1,0:T(8,128)(2,1)S(1)}, u32[]{:S(2)}, u32[]{:S(2)}) collective-permute-start(bf16[512,512]{1,0:T(8,128)(2,1)S(1)} %get-tuple-element.25), channel_id=1, source_target_pairs={{0,6},{1,7},{2,0},{3,1},{4,2},{5,3},{6,4},{7,5},{8,14},{9,15},{10,... | collective-permute-start | bytes 1572872 | tf_op jit(solution)/shard_map/ppermute | solution.py:306
  9.0 14.4 %collective-permute-start.1 = (bf16[512,512]{1,0:T(8,128)(2,1)S(1)}, bf16[512,512]{1,0:T(8,128)(2,1)S(1)}, u32[]{:S(2)}, u32[]{:S(2)}) collective-permute-start(bf16[512,512]{1,0:T(8,128)(2,1)S(1)} %get-tuple-element.24.sent.a0), channel_id=1, source_target_pairs={{0,2},{1,3},{2,4},{3,5},{4,6},{5,7},{6,0},{7,1},{8,10},{9,11},{10,... | collective-permute-start | bytes 1572872 | tf_op jit(solution)/shard_map/ppermute | solution.py:303
  9.0 23.6 %collective-permute-start = (bf16[512,512]{1,0:T(8,128)(2,1)S(1)}, bf16[512,512]{1,0:T(8,128)(2,1)S(1)}, u32[]{:S(2)}, u32[]{:S(2)}) collective-permute-start(bf16[512,512]{1,0:T(8,128)(2,1)S(1)} %get-tuple-element.23), channel_id=1, source_target_pairs={{0,4},{1,5},{2,6},{3,7},{4,0},{5,1},{6,2},{7,3},{8,12},{9,13},{10,... | collective-permute-start | bytes 1572872 | tf_op jit(solution)/shard_map/ppermute | solution.py:309
  23.5 17.2 %collective-permute-start.10 = (bf16[512,256]{1,0:T(8,128)(2,1)S(1)}, bf16[512,256]{1,0:T(8,128)(2,1)S(1)}, u32[]{:S(2)}, u32[]{:S(2)}) collective-permute-start(bf16[512,256]{1,0:T(8,128)(2,1)S(1)} %shard_map.86.turned.b0.c0), channel_id=1, source_target_pairs={{0,2},{1,3},{2,4},{3,5},{4,6},{5,7},{6,0},{7,1},{8,10},{9,11},{10,... | collective-permute-start | bytes 786440 | tf_op jit(solution)/shard_map/ppermute | solution.py:303
  23.6 17.1 %collective-permute-start.9 = (bf16[512,256]{1,0:T(8,128)(2,1)S(1)}, bf16[512,256]{1,0:T(8,128)(2,1)S(1)}, u32[]{:S(2)}, u32[]{:S(2)}) collective-permute-start(bf16[512,256]{1,0:T(8,128)(2,1)S(1)} %shard_map.86.turned.b0.c0), channel_id=1, source_target_pairs={{0,4},{1,5},{2,6},{3,7},{4,0},{5,1},{6,2},{7,3},{8,12},{9,13},{10,... | collective-permute-start | bytes 786440 | tf_op jit(solution)/shard_map/ppermute | solution.py:309
  25.8 14.9 %collective-permute-start.8 = (bf16[512,256]{1,0:T(8,128)(2,1)S(1)}, bf16[512,256]{1,0:T(8,128)(2,1)S(1)}, u32[]{:S(2)}, u32[]{:S(2)}) collective-permute-start(bf16[512,256]{1,0:T(8,128)(2,1)S(1)} %shard_map.86.turned.b0.c0), channel_id=1, source_target_pairs={{0,6},{1,7},{2,0},{3,1},{4,2},{5,3},{6,4},{7,5},{8,14},{9,15},{10,... | collective-permute-start | bytes 786440 | tf_op jit(solution)/shard_map/ppermute | solution.py:306
  33.4 32.2 %collective-permute-start.7 = (bf16[576,512]{1,0:T(8,128)(2,1)S(1)}, bf16[576,512]{1,0:T(8,128)(2,1)S(1)}, u32[]{:S(2)}, u32[]{:S(2)}) collective-permute-start(bf16[576,512]{1,0:T(8,128)(2,1)S(1)} %shard_map.88), channel_id=1, source_target_pairs={{0,1},{1,0},{2,3},{3,2},{4,5},{5,4},{6,7},{7,6},{8,9},{9,8},{10,11... | collective-permute-start | bytes 1769480 | tf_op jit(solution)/shard_map/ppermute | solution.py:312
  41.4 24.1 %collective-permute-start.11 = (bf16[512,512]{1,0:T(8,128)(2,1)S(1)}, bf16[512,512]{1,0:T(8,128)(2,1)S(1)}, u32[]{:S(2)}, u32[]{:S(2)}) collective-permute-start(bf16[512,512]{1,0:T(8,128)(2,1)S(1)} %shard_map.90), channel_id=1, source_target_pairs={{0,1},{1,0},{2,3},{3,2},{4,5},{5,4},{6,7},{7,6},{8,9},{9,8},{10,11... | collective-permute-start | bytes 1572872 | tf_op jit(solution)/shard_map/ppermute | solution.py:312
  47.1 8.7 %collective-permute-start.3 = (bf16[256,512]{1,0:T(8,128)(2,1)S(1)}, bf16[256,512]{1,0:T(8,128)(2,1)S(1)}, u32[]{:S(2)}, u32[]{:S(2)}) collective-permute-start(bf16[256,512]{1,0:T(8,128)(2,1)S(1)} %get-tuple-element.27), channel_id=1, source_target_pairs={{0,6},{1,7},{2,0},{3,1},{4,2},{5,3},{6,4},{7,5},{8,14},{9,15},{10,... | collective-permute-start | bytes 786440 | tf_op jit(solution)/shard_map/ppermute | solution.py:306
  49.3 6.8 %collective-permute-start.4 = (bf16[256,512]{1,0:T(8,128)(2,1)S(1)}, bf16[256,512]{1,0:T(8,128)(2,1)S(1)}, u32[]{:S(2)}, u32[]{:S(2)}) collective-permute-start(bf16[256,512]{1,0:T(8,128)(2,1)S(1)} %get-tuple-element.28), channel_id=1, source_target_pairs={{0,4},{1,5},{2,6},{3,7},{4,0},{5,1},{6,2},{7,3},{8,12},{9,13},{10,... | collective-permute-start | bytes 786440 | tf_op jit(solution)/shard_map/ppermute | solution.py:309
  49.3 13.9 %collective-permute-start.5 = (bf16[256,512]{1,0:T(8,128)(2,1)S(1)}, bf16[256,512]{1,0:T(8,128)(2,1)S(1)}, u32[]{:S(2)}, u32[]{:S(2)}) collective-permute-start(bf16[256,512]{1,0:T(8,128)(2,1)S(1)} %get-tuple-element.29), channel_id=1, source_target_pairs={{0,2},{1,3},{2,4},{3,5},{4,6},{5,7},{6,0},{7,1},{8,10},{9,11},{10,... | collective-permute-start | bytes 786440 | tf_op jit(solution)/shard_map/ppermute | solution.py:303
  74.8 39.7 %collective-permute-start.13 = (bf16[320,1024]{1,0:T(8,128)(2,1)S(1)}, bf16[320,1024]{1,0:T(8,128)(2,1)S(1)}, u32[]{:S(2)}, u32[]{:S(2)}) collective-permute-start(bf16[320,1024]{1,0:T(8,128)(2,1)S(1)} %get-tuple-element.33), channel_id=1, source_target_pairs={{0,6},{1,7},{2,0},{3,1},{4,2},{5,3},{6,4},{7,5},{8,14},{9,15},{10,... | collective-permute-start | bytes 1966088 | tf_op jit(solution)/shard_map/ppermute | solution.py:306
  75.6 38.9 %collective-permute-start.14 = (bf16[320,1024]{1,0:T(8,128)(2,1)S(1)}, bf16[320,1024]{1,0:T(8,128)(2,1)S(1)}, u32[]{:S(2)}, u32[]{:S(2)}) collective-permute-start(bf16[320,1024]{1,0:T(8,128)(2,1)S(1)} %get-tuple-element.34), channel_id=1, source_target_pairs={{0,4},{1,5},{2,6},{3,7},{4,0},{5,1},{6,2},{7,3},{8,12},{9,13},{10,... | collective-permute-start | bytes 1966088 | tf_op jit(solution)/shard_map/ppermute | solution.py:309
  75.6 38.9 %collective-permute-start.15 = (bf16[320,1024]{1,0:T(8,128)(2,1)S(1)}, bf16[320,1024]{1,0:T(8,128)(2,1)S(1)}, u32[]{:S(2)}, u32[]{:S(2)}) collective-permute-start(bf16[320,1024]{1,0:T(8,128)(2,1)S(1)} %get-tuple-element.35), channel_id=1, source_target_pairs={{0,2},{1,3},{2,4},{3,5},{4,6},{5,7},{6,0},{7,1},{8,10},{9,11},{10,... | collective-permute-start | bytes 1966088 | tf_op jit(solution)/shard_map/ppermute | solution.py:303
  76.4 7.3 %collective-permute-start.17 = (f32[16,8,128]{2,1,0:T(8,128)S(1)}, f32[16,8,128]{2,1,0:T(8,128)S(1)}, u32[]{:S(2)}, u32[]{:S(2)}) collective-permute-start(f32[16,8,128]{2,1,0:T(8,128)S(1)} %get-tuple-element.31), channel_id=1, source_target_pairs={{0,24},{8,16},{16,8},{24,0},{32,56},{40,48},{48,40},{56,32},{64,88... | collective-permute-start | bytes 196616 | tf_op jit(solution)/shard_map/ppermute | solution.py:412
  81.5 5.6 %collective-permute-start.16 = (f32[16,8,128]{2,1,0:T(8,128)S(1)}, f32[16,8,128]{2,1,0:T(8,128)S(1)}, u32[]{:S(2)}, u32[]{:S(2)}) collective-permute-start(f32[16,8,128]{2,1,0:T(8,128)S(1)} %get-tuple-element.36.a.late), channel_id=1, source_target_pairs={{0,16},{8,24},{16,0},{24,8},{32,48},{40,56},{48,32},{56,40},{64,80... | collective-permute-start | bytes 196616 | tf_op jit(solution)/shard_map/ppermute | solution.py:412
  87.0 6.5 %collective-permute-start.20 = (f32[16,8,128]{2,1,0:T(8,128)S(1)}, f32[16,8,128]{2,1,0:T(8,128)S(1)}, u32[]{:S(2)}, u32[]{:S(2)}) collective-permute-start(f32[16,8,128]{2,1,0:T(8,128)S(1)} %shard_map.93.a), channel_id=1, source_target_pairs={{0,96},{8,104},{16,112},{24,120},{32,64},{40,72},{48,80},{56,88},{... | collective-permute-start | bytes 196616 | tf_op jit(solution)/shard_map/ppermute | solution.py:412
  91.5 4.9 %collective-permute-start.19 = (f32[16,8,128]{2,1,0:T(8,128)S(1)}, f32[16,8,128]{2,1,0:T(8,128)S(1)}, u32[]{:S(2)}, u32[]{:S(2)}) collective-permute-start(f32[16,8,128]{2,1,0:T(8,128)S(1)} %shard_map.93.a), channel_id=1, source_target_pairs={{0,64},{8,72},{16,80},{24,88},{32,96},{40,104},{48,112},{56,120},{... | collective-permute-start | bytes 196616 | tf_op jit(solution)/shard_map/ppermute | solution.py:412
  97.8 9.8 %collective-permute-start.21 = (f32[16,8,128]{2,1,0:T(8,128)S(1)}, f32[16,8,128]{2,1,0:T(8,128)S(1)}, u32[]{:S(2)}, u32[]{:S(2)}) collective-permute-start(f32[16,8,128]{2,1,0:T(8,128)S(1)} %shard_map.94.late.a), channel_id=1, source_target_pairs={{0,128},{8,136},{16,144},{24,152},{32,160},{40,168},{48,176},{56,1... | collective-permute-start | bytes 196616 | tf_op jit(solution)/shard_map/ppermute | solution.py:412
  107.6 4.5 %collective-permute-start.24 = (bf16[16,8,128]{2,1,0:T(8,128)(2,1)S(1)}, bf16[16,8,128]{2,1,0:T(8,128)(2,1)S(1)}, u32[]{:S(2)}, u32[]{:S(2)}) collective-permute-start(bf16[16,8,128]{2,1,0:T(8,128)(2,1)S(1)} %shard_map.96.half), channel_id=1, source_target_pairs={{0,9},{1,8},{2,11},{3,10},{4,13},{5,12},{6,15},{7,14},{8,1},{9,0},... | collective-permute-start | bytes 98312 | tf_op jit(solution)/shard_map/ppermute | solution.py:460
  115.1 9.2 %collective-permute-start.27 = (bf16[2,32,8,128]{3,2,1,0:T(8,128)(2,1)S(1)}, bf16[2,32,8,128]{3,2,1,0:T(8,128)(2,1)S(1)}, u32[]{:S(2)}, u32[]{:S(2)}) collective-permute-start(bf16[2,32,8,128]{3,2,1,0:T(8,128)(2,1)S(1)} %shard_map.97.tot), channel_id=1, source_target_pairs={{0,2},{1,3},{2,4},{3,5},{4,6},{5,7},{6,0},{7,1},{8,10},{9,11},{10,... | collective-permute-start | bytes 393224 | tf_op jit(solution)/shard_map/ppermute | solution.py:303
  116.7 8.0 %collective-permute-start.26 = (bf16[2,32,8,128]{3,2,1,0:T(8,128)(2,1)S(1)}, bf16[2,32,8,128]{3,2,1,0:T(8,128)(2,1)S(1)}, u32[]{:S(2)}, u32[]{:S(2)}) collective-permute-start(bf16[2,32,8,128]{3,2,1,0:T(8,128)(2,1)S(1)} %shard_map.97.tot), channel_id=1, source_target_pairs={{0,4},{1,5},{2,6},{3,7},{4,0},{5,1},{6,2},{7,3},{8,12},{9,13},{10,... | collective-permute-start | bytes 393224 | tf_op jit(solution)/shard_map/ppermute | solution.py:309
  118.7 6.1 %collective-permute-start.25 = (bf16[2,32,8,128]{3,2,1,0:T(8,128)(2,1)S(1)}, bf16[2,32,8,128]{3,2,1,0:T(8,128)(2,1)S(1)}, u32[]{:S(2)}, u32[]{:S(2)}) collective-permute-start(bf16[2,32,8,128]{3,2,1,0:T(8,128)(2,1)S(1)} %shard_map.97.tot), channel_id=1, source_target_pairs={{0,6},{1,7},{2,0},{3,1},{4,2},{5,3},{6,4},{7,5},{8,14},{9,15},{10,... | collective-permute-start | bytes 393224 | tf_op jit(solution)/shard_map/ppermute | solution.py:306
  (12 other events, 88.2 us)

commit v6 on v4

--- a/solution.py
+++ b/solution.py
@@ -56,15 +56,15 @@
     return dense
 
 
-def spread_row(tile, row):
-    return jnp.broadcast_to(tile[row : row + 1, :], (PACK, LANES)).astype(jnp.bfloat16)
+def spread_row(row):
+    return jnp.broadcast_to(row, (PACK, LANES)).astype(jnp.bfloat16)
 
 
 def expand_tile(indices, values, dense, first, cols):
     freq = lax.broadcasted_iota(jnp.int32, (PACK, LANES), 0).astype(jnp.float32)
     for half in range(2):
-        at = [spread_row(indices, half * KEEP + j) for j in range(KEEP)]
-        have = [spread_row(values, half * KEEP + j) for j in range(KEEP)]
+        at = [spread_row(indices(half * KEEP + j)) for j in range(KEEP)]
+        have = [spread_row(values(half * KEEP + j)) for j in range(KEEP)]
         for part in range(BLOCK // PACK):
             here = (freq + part * PACK).astype(jnp.bfloat16)
             tile = jnp.zeros((PACK, LANES), jnp.bfloat16)
@@ -94,20 +94,31 @@
     return jnp.concatenate(rows, axis=0).astype(jnp.bfloat16)
 
 
-def pack_first_kernel(where, cot, t0, t1, t2, t3, to_up, to_far, to_down, mine):
-    turned = cot[...].T
-    for out, t in ((to_up, t1), (to_far, t2), (to_down, t3)):
+def pack_first_kernel(where, cot, tok, to_up, to_far, to_down, mine, own_cot, sems):
+    head = pltpu.make_async_copy(cot.at[:, pl.ds(0, HALF)], own_cot, sems.at[0])
+    head.start()
+    copies = []
+    for d, out in enumerate((mine, to_up, to_far, to_down)):
+        first = pl.multiple_of((((where[0] ^ 1) + 2 * d) & 7) * ROWS, ROWS)
+        if d == 0:
+            copies.append(pltpu.make_async_copy(tok.at[:, pl.ds(first, ROWS)], out, sems.at[1]))
+            continue
+        for h in range(2):
+            source = tok.at[:, pl.ds(first + h * TOK, TOK)]
+            target = out.at[pl.ds(h * TOK, TOK), pl.ds(TOK, TOK)]
+            copies.append(pltpu.make_async_copy(source, target, sems.at[2 * d + h]))
+    for copy in copies:
+        copy.start()
+    head.wait()
+    turned = own_cot[...].T
+    for out in (to_up, to_far, to_down):
         out[:, :TOK] = turned
-        out[:TOK, TOK:] = t[:, :TOK]
-        out[TOK:, TOK:] = t[:, TOK:]
-    mine[...] = t0[...]
-
-
-def pack_second_kernel(cot, late_lo, late_hi, out):
-    out[...] = cot[...].T
-
-
-def pack_own_kernel(where, t0, t1, t2, t3, late_lo, late_hi, mine, to_up, to_far, to_down):
+    for copy in copies:
+        copy.wait()
+
+
+def pack_second_kernel(where, cot, t0, t1, t2, t3, late_lo, late_hi, turned, mine, to_up, to_far, to_down):
+    turned[...] = cot[...].T
     for out, t in ((mine, t0), (to_up, t1), (to_far, t2), (to_down, t3)):
         out[...] = t[...]
 
@@ -172,7 +183,8 @@
     pl.when(jnp.logical_not(here))(lambda: put(send))
 
 
-def add_two_kernel(a, b, out):
+def add_two_kernel(a, b, *rest):
+    out = rest[-1]
     out[...] = (a[...] + b[...]).astype(out.dtype)
 
 
@@ -189,7 +201,7 @@
     out[1 - side, pl.ds(other, TILES // 2)] = corner[...]
 
 
-def residual_kernel(moment, picked, idx, ch, cl, late, out):
+def residual_kernel(moment, picked, idx, ch, cl, late, out, mark):
     parts = []
     for b in range(GROUP // BLOCK):
         at = [idx[b, j : j + 1, :] for j in range(KEEP)]
@@ -198,6 +210,7 @@
     kept = jnp.concatenate(parts, axis=0)
     back = three_pass((ch[...], cl[...]), split_pair(kept), ((0,), (0,)))
     out[...] = (moment[...] - back).T
+    mark[...] = back[:8, :LANES]
 
 
 def base_kernel(where, o0, o1, o2, o3, p0, p1, p2, p3, w_own, w_peer, idx, got_a, *outs):
@@ -218,15 +231,22 @@
         for f in range(2):
             for q in range(ROWS // LANES):
                 cols = slice(f * ROWS + q * LANES, f * ROWS + (q + 1) * LANES)
-                values = tot[f, t * (ROWS // LANES) + q].astype(jnp.float32)
-                expand_tile(pairs[t * 8 : (t + 1) * 8, cols], values, dense, t * 2 * BLOCK, cols)
-
-
-def forward_own_kernel(where, tok, own, tot, weight, ch, cl, mixed, out_weight, dense):
-    pairs = own[TOK:, :].astype(jnp.float32)
+                tile = t * (ROWS // LANES) + q
+                expand_tile(
+                    lambda s, t=t, cols=cols: pairs[t * 8 + s : t * 8 + s + 1, cols],
+                    lambda s, f=f, tile=tile: tot[f, tile, s : s + 1, :],
+                    dense,
+                    t * 2 * BLOCK,
+                    cols,
+                )
+
+
+def forward_own_kernel(where, tok, own, tot, weight, ch, cl, mixed, out_weight, dense, pairs, values):
+    pairs[...] = own[TOK:, :].astype(jnp.float32)
+    values[...] = tot[...].astype(jnp.float32)
     cols = pl.ds(pl.multiple_of((where[0] & 1) * ROWS, ROWS), ROWS)
     for g in range(STEPS):
-        expand_group(g, pairs, tot, dense)
+        expand_group(g, pairs, values, dense)
         span = slice(g * GROUP, (g + 1) * GROUP)
         mixed[span, :] = mix(dense[span, :], tok[...], ((1,), (1,)))
         turned = dense[span, cols].T
@@ -235,13 +255,16 @@
         out_weight[:, span] = new.astype(out_weight.dtype)
 
 
-def forward_kernel(where, tok_1, tok_2, tok_3, own, hi, far, lo, tot_1, tot_2, tot_3, mixed, ch, cl, out, *dense):
-    pairs = [near[TOK:, :].astype(jnp.float32) for near in (hi, far, lo)]
+def forward_kernel(where, tok_1, tok_2, tok_3, own, hi, far, lo, tot_1, tot_2, tot_3, mixed, ch, cl, out, *scratch):
+    toks, dense, pairs, values = (tok_1, tok_2, tok_3), scratch[:3], scratch[3:6], scratch[6:]
+    for near, pair, tot, value in zip((hi, far, lo), pairs, (tot_1, tot_2, tot_3), values):
+        pair[...] = near[TOK:, :].astype(jnp.float32)
+        value[...] = tot[...].astype(jnp.float32)
     for g in range(STEPS):
         span = slice(g * GROUP, (g + 1) * GROUP)
         total = mixed[span, :]
-        for tok, index, tot, buffer in zip((tok_1, tok_2, tok_3), pairs, (tot_1, tot_2, tot_3), dense):
-            expand_group(g, index, tot, buffer)
+        for tok, pair, value, buffer in zip(toks, pairs, values, dense):
+            expand_group(g, pair, value, buffer)
             total += mix(buffer[span, :], tok[...], ((1,), (1,)))
         delta = three_pass(split_pair(total.T), (ch[...], cl[...]), ((1,), (0,)))
         base = own[:TOK, span].astype(jnp.float32) + hi[:TOK, span].astype(jnp.float32)
@@ -285,6 +308,9 @@
 INDEX_STEP = pl.BlockSpec((GROUP // BLOCK, KEEP, ROWS), lambda c, *_: (c, 0, 0))
 MESSAGE = whole(HALF, 2 * TOK)
 PIECE = whole(TOK, ROWS)
+DENSE = pltpu.VMEM((KV, 2 * ROWS), BF16)
+PAIRS = pltpu.VMEM((PICKS, 2 * ROWS), F32)
+VALUES = pltpu.VMEM((2, TILES, 8, LANES), F32)
 
 
 def shape(*dims, dtype=BF16):
@@ -320,42 +346,33 @@
         grid_spec=pltpu.PrefetchScalarGridSpec(
             num_scalar_prefetch=1,
             grid=(1,),
-            in_specs=[whole(TOK, HALF)] + columns(1),
+            in_specs=[pl.BlockSpec(memory_space=pltpu.HBM)] * 2,
             out_specs=[MESSAGE] * 3 + [PIECE],
+            scratch_shapes=[pltpu.VMEM((TOK, HALF), BF16), pltpu.SemaphoreType.DMA((8,))],
         ),
         out_shape=[shape(HALF, 2 * TOK)] * 3 + [shape(TOK, ROWS)],
         compiler_params=params(),
         cost_estimate=cost(0, 4),
-    )(place, cotangent, tokens, tokens, tokens, tokens)
+    )(place, cotangent, tokens)
     first_lo = up(first_up)
     first_hi = down(first_down)
     first_x = across(first_far)
     firsts = (first_up, first_hi, first_x, first_lo)
 
-    cot_b = pl.pallas_call(
+    cot_b, own_0, own_up, own_across, own_down = pl.pallas_call(
         pack_second_kernel,
-        grid=(1,),
-        in_specs=[pl.BlockSpec((TOK, HALF), lambda c: (0, 1)), AFTER, AFTER],
-        out_specs=whole(HALF, TOK),
-        out_shape=shape(HALF, TOK),
-        compiler_params=params(),
-        cost_estimate=cost(0, 1),
-    )(cotangent, first_lo, first_hi)
+        grid_spec=pltpu.PrefetchScalarGridSpec(
+            num_scalar_prefetch=1,
+            grid=(1,),
+            in_specs=[pl.BlockSpec((TOK, HALF), lambda c, *_: (0, 1))] + columns(0) + [AFTER, AFTER],
+            out_specs=[whole(HALF, TOK)] + [PIECE] * 4,
+        ),
+        out_shape=[shape(HALF, TOK)] + [shape(TOK, ROWS)] * 4,
+        compiler_params=params(),
+        cost_estimate=cost(0, 3),
+    )(place, cotangent, tokens, tokens, tokens, tokens, first_lo, first_hi)
     b_lo, b_hi, b_far = up(cot_b), down(cot_b), across(cot_b)
     cots_b = (cot_b, b_hi, b_far, b_lo)
-
-    own_0, own_up, own_across, own_down = pl.pallas_call(
-        pack_own_kernel,
-        grid_spec=pltpu.PrefetchScalarGridSpec(
-            num_scalar_prefetch=1,
-            grid=(1,),
-            in_specs=columns(0) + [AFTER, AFTER],
-            out_specs=[PIECE] * 4,
-        ),
-        out_shape=[shape(TOK, ROWS)] * 4,
-        compiler_params=params(),
-        cost_estimate=cost(0, 2),
-    )(place, tokens, tokens, tokens, tokens, b_lo, b_hi)
     owns = (own_0, down(own_down), across(own_across), up(own_up))
 
     partial_a = pl.pallas_call(
@@ -427,21 +444,31 @@
     def partner(x, bits):
         return lax.ppermute(x, "rep", [(i, i ^ bits) for i in range(REPS)])
 
-    def add(kernel, result, *parts):
+    def add(kernel, result, *parts, after=()):
         return pl.pallas_call(
             kernel,
             grid=(1,),
-            in_specs=[halves] * len(parts),
+            in_specs=[halves] * len(parts) + [AFTER] * len(after),
             out_specs=halves,
             out_shape=result,
             compiler_params=params(),
             cost_estimate=cost(0, 0.25),
-        )(*parts)
+        )(*parts, *after)
 
     value = add(add_two_kernel, half_shape, keep, partner(send, 1))
     value = add(add_two_kernel, half_shape, value, partner(value, 2))
     value = add(add_four_kernel, half_shape, value, partner(value, 4), partner(value, 8), partner(value, 12))
-    half = add(add_two_kernel, shape(TILES // 2, 8, LANES), value, partner(value, 16))
+    last = partner(value, 16)
+    new_momentum, mark = pl.pallas_call(
+        residual_kernel,
+        grid=(STEPS,),
+        in_specs=[by_row(GROUP, ROWS), by_row(PICKS // STEPS, ROWS), INDEX_STEP] + BASIS + [AFTER],
+        out_specs=[by_col(ROWS, GROUP), whole(8, LANES)],
+        out_shape=[shape(ROWS, KV, dtype=F32), shape(8, LANES, dtype=F32)],
+        compiler_params=params(),
+        cost_estimate=cost(6 * KV * GROUP * ROWS, 5),
+    )(moment, picked, index_t, high, low, value)
+    half = add(add_two_kernel, shape(TILES // 2, 8, LANES), value, last, after=(mark,))
 
     corner = lax.ppermute(half, ("rep", "fsdp"), [(i, i ^ 9) for i in range(REPS * 8)])
     pair_spec = whole(2, TILES, 8, LANES)
@@ -469,22 +496,12 @@
             grid=(1,),
             in_specs=[token_block(0), whole(TOK + PICKS, KV), pair_spec, whole(ROWS, KV)] + BASIS,
             out_specs=[whole(KV, TOK), whole(ROWS, KV)],
-            scratch_shapes=[pltpu.VMEM((KV, 2 * ROWS), BF16)],
+            scratch_shapes=[DENSE, PAIRS, VALUES],
         ),
         out_shape=[shape(KV, TOK, dtype=F32), shape(ROWS, KV)],
         compiler_params=params(),
         cost_estimate=cost(3 * KV * KV * ROWS, 4),
     )(place, tokens, base, pair, weight, high, low)
-
-    new_momentum = pl.pallas_call(
-        residual_kernel,
-        grid=(STEPS,),
-        in_specs=[by_row(GROUP, ROWS), by_row(PICKS // STEPS, ROWS), INDEX_STEP] + BASIS + [AFTER],
-        out_specs=by_col(ROWS, GROUP),
-        out_shape=shape(ROWS, KV, dtype=F32),
-        compiler_params=params(),
-        cost_estimate=cost(6 * KV * GROUP * ROWS, 5),
-    )(moment, picked, index_t, high, low, pair)
 
     projected = pl.pallas_call(
         forward_kernel,
@@ -497,7 +514,7 @@
             + [whole(KV, TOK)]
             + BASIS,
             out_specs=whole(TOK, KV),
-            scratch_shapes=[pltpu.VMEM((KV, 2 * ROWS), BF16)] * 3,
+            scratch_shapes=[DENSE] * 3 + [PAIRS] * 3 + [VALUES] * 3,
         ),
         out_shape=shape(TOK, KV),
         compiler_params=params(2 * VMEM_LIMIT),

time: 126 us -> 127 us (level)
    ppermute x5, waiting for transfers between devices: 16.3 us -> 22.8 us  [up(): return lax.ppermute(x, 'fsdp', [(i, (i + 2) % 8) for i in range(8)])]
    ppermute x5, waiting for transfers between devices: 5.64 us -> 0.63 us  [down(): return lax.ppermute(x, 'fsdp', [(i, (i + 6) % 8) for i in range(8)])]
    ppermute x5, starting transfers between devices: 3.25 us -> 7.49 us  [across(): return lax.ppermute(x, 'fsdp', [(i, (i + 4) % 8) for i in range(8)])]
    ppermute x5, starting transfers between devices: 12 us -> 9.15 us  [down(): return lax.ppermute(x, 'fsdp', [(i, (i + 6) % 8) for i in range(8)])]
    ppermute x7, starting transfers between devices: 27 us -> 24.4 us  [partner(): return lax.ppermute(x, 'rep', [(i, i ^ bits) for i in range(REPS)])]
    ppermute x7, waiting for transfers between devices: 7.23 us -> 4.91 us  [partner(): return lax.ppermute(x, 'rep', [(i, i ^ bits) for i in range(REPS)])]
    ppermute x5, starting transfers between devices: 3.72 us -> 5.6 us  [up(): return lax.ppermute(x, 'fsdp', [(i, (i + 2) % 8) for i in range(8)])]
where the time goes in v6:
time: 127 us
  starting transfers between devices  53 us (42%)
  waiting for transfers between devices  44.2 us (35%)
  Pallas kernels  26 us (20%)
  local copies, waits for them, and re-layouts  2.66 us (2%)
    ppermute x7, starting transfers between devices, partner(): return lax.ppermute(x, 'rep', [(i, i ^ bits) for i in range(REPS)])  24.4 us
    ppermute x5, waiting for transfers between devices, up(): return lax.ppermute(x, 'fsdp', [(i, (i + 2) % 8) for i in range(8)])  22.8 us
    ppermute x5, waiting for transfers between devices, across(): return lax.ppermute(x, 'fsdp', [(i, (i + 4) % 8) for i in range(8)])  13.6 us
    ppermute x5, starting transfers between devices, down(): return lax.ppermute(x, 'fsdp', [(i, (i + 6) % 8) for i in range(8)])  9.15 us
    ppermute x5, starting transfers between devices, across(): return lax.ppermute(x, 'fsdp', [(i, (i + 4) % 8) for i in range(8)])  7.49 us
    pallas_call x1, Pallas kernels, body(): pl.pallas_call(forward_kernel, grid_spec=pltpu.PrefetchScalarGridSpec(num...  6.21 us
    ppermute x5, starting transfers between devices, up(): return lax.ppermute(x, 'fsdp', [(i, (i + 2) % 8) for i in range(8)])  5.6 us
    ppermute x4, starting transfers between devices, swap(): return lax.ppermute(x, 'fsdp', [(i, i ^ 1) for i in range(8)])  5.28 us
  transfers between devices with their start and end apart: 27, of which 13 were waited for; matrix products, arithmetic and copies ran while one was open for 0% of the time, Pallas kernels for 15%

profile of v6, /device:TPU:1, one launch (start us, length us, event | category | flops | bytes accessed | tf_op | source)
XLA Modules:
  0.0 126.7 jit_solution(478369032491963762)
XLA Ops:
  0.6 2.1 %collective-permute-start.6 = (bf16[512,1024]{1,0:T(8,128)(2,1)}, bf16[512,1024]{1,0:T(8,128)(2,1)S(1)}, u32[]{:S(2)}, u32[]{:S(2)}) collective-permute-start(bf16[512,1024]{1,0:T(8,128)(2,1)} %weight.1), channel_id=1, source_target_pairs={{0,1},{1,0},{2,3},{3,2},{4,5},{5,4},{6,7},{7,6},{8,9},{9,8},{10,11... | collective-permute-start | bytes 3145736 | tf_op jit(solution)/shard_map/ppermute | solution.py:337
  10.9 9.2 %collective-permute-done.late_lo.lo.p3.a3 = bf16[512,512]{1,0:T(8,128)(2,1)S(1)} collective-permute-done((bf16[512,512]{1,0:T(8,128)(2,1)S(1)}, bf16[512,512]{1,0:T(8,128)(2,1)S(1)}, u32[]{:S(2)}, u32[]{:S(2)}) %collective-permute-start) | collective-permute-done | bytes 524320 | tf_op jit(solution)/shard_map/ppermute | solution.py:328
  20.7 12.0 %collective-permute-done.5.far.p2.a2 = bf16[512,512]{1,0:T(8,128)(2,1)S(1)} collective-permute-done((bf16[512,512]{1,0:T(8,128)(2,1)S(1)}, bf16[512,512]{1,0:T(8,128)(2,1)S(1)}, u32[]{:S(2)}, u32[]{:S(2)}) %collective-permute-start.5) | collective-permute-done | bytes 524320 | tf_op jit(solution)/shard_map/ppermute | solution.py:334
  36.1 2.7 %collective-permute-start.2 = (bf16[256,512]{1,0:T(8,128)(2,1)S(1)}, bf16[256,512]{1,0:T(8,128)(2,1)S(1)}, u32[]{:S(2)}, u32[]{:S(2)}) collective-permute-start(bf16[256,512]{1,0:T(8,128)(2,1)S(1)} %get-tuple-element.27), channel_id=1, source_target_pairs={{0,6},{1,7},{2,0},{3,1},{4,2},{5,3},{6,4},{7,5},{8,14},{9,15},{10,... | collective-permute-start | bytes 786440 | tf_op jit(solution)/shard_map/ppermute | solution.py:331
  41.4 2.9 %collective-permute-start.4 = (bf16[256,512]{1,0:T(8,128)(2,1)S(1)}, bf16[256,512]{1,0:T(8,128)(2,1)S(1)}, u32[]{:S(2)}, u32[]{:S(2)}) collective-permute-start(bf16[256,512]{1,0:T(8,128)(2,1)S(1)} %get-tuple-element.29), channel_id=1, source_target_pairs={{0,2},{1,3},{2,4},{3,5},{4,6},{5,7},{6,0},{7,1},{8,10},{9,11},{10,... | collective-permute-start | bytes 786440 | tf_op jit(solution)/shard_map/ppermute | solution.py:328
  44.3 6.5 %collective-permute-done.13.b3.c3 = bf16[512,256]{1,0:T(8,128)(2,1)S(1)} collective-permute-done((bf16[512,256]{1,0:T(8,128)(2,1)S(1)}, bf16[512,256]{1,0:T(8,128)(2,1)S(1)}, u32[]{:S(2)}, u32[]{:S(2)}) %collective-permute-start.13) | collective-permute-done | bytes 262176 | tf_op jit(solution)/shard_map/ppermute | solution.py:328
  53.0 3.4 %collective-permute-done.4.o3.t3 = bf16[256,512]{1,0:T(8,128)(2,1)S(1)} collective-permute-done((bf16[256,512]{1,0:T(8,128)(2,1)S(1)}, bf16[256,512]{1,0:T(8,128)(2,1)S(1)}, u32[]{:S(2)}, u32[]{:S(2)}) %collective-permute-start.4) | collective-permute-done | bytes 262176 | tf_op jit(solution)/shard_map/ppermute | solution.py:328
  56.4 3.1 %shard_map.88 = (bf16[320,1024]{1,0:T(8,128)(2,1)S(1)}, bf16[320,1024]{1,0:T(8,128)(2,1)S(1)}, bf16[320,1024]{1,0:T(8,128)(2,1)S(1)}, bf16[320,1024]{1,0:T(8,128)(2,1)S(1)}) custom-call(s32[2]{0:T(128)S(1)} %pad_add_fusion.where, bf16[256,512]{1,0:T(8,128)(2,1)S(1)} %get-tuple-element.26.o0.t0, bf16[256,512]{1,0:T(8,128)(2,1)S(1)} %collective-permute-done.2.o1.t1, ...), custom_call_target="tpu_custom_call" | custom-call | flops 2147483648 | bytes 7340032 | tf_op jit(solution)/shard_map/pallas_call | solution.py:412
  59.5 1.9 %collective-permute-start.8 = (bf16[320,1024]{1,0:T(8,128)(2,1)S(1)}, bf16[320,1024]{1,0:T(8,128)(2,1)S(1)}, u32[]{:S(2)}, u32[]{:S(2)}) collective-permute-start(bf16[320,1024]{1,0:T(8,128)(2,1)S(1)} %get-tuple-element.34), channel_id=1, source_target_pairs={{0,6},{1,7},{2,0},{3,1},{4,2},{5,3},{6,4},{7,5},{8,14},{9,15},{10,... | collective-permute-start | bytes 1966088 | tf_op jit(solution)/shard_map/ppermute | solution.py:331
  61.4 2.5 %collective-permute-start.9 = (bf16[320,1024]{1,0:T(8,128)(2,1)S(1)}, bf16[320,1024]{1,0:T(8,128)(2,1)S(1)}, u32[]{:S(2)}, u32[]{:S(2)}) collective-permute-start(bf16[320,1024]{1,0:T(8,128)(2,1)S(1)} %get-tuple-element.35), channel_id=1, source_target_pairs={{0,4},{1,5},{2,6},{3,7},{4,0},{5,1},{6,2},{7,3},{8,12},{9,13},{10,... | collective-permute-start | bytes 1966088 | tf_op jit(solution)/shard_map/ppermute | solution.py:334
  64.5 2.3 %shard_map.89.pre = f32[1024,512]{1,0:T(8,128)S(1)} custom-call(bf16[512,512]{1,0:T(8,128)(2,1)S(1)} %get-tuple-element.24.sent.a0, bf16[512,512]{1,0:T(8,128)(2,1)S(1)} %collective-permute-done.1.late_hi.hi.p1.a1, bf16[512,512]{1,0:T(8,128)(2,1)S(1)} %collective-permute-done.5.far.p2.a2, bf16[512,512]{1,0:T(8,128)(2,1)S(1)} %collective-permute-done.late_lo.lo.p3.a3, ...), custom_call_target="tpu_custom_call" | custom-call | flops 1073741824 | bytes 7340032 | tf_op jit(solution)/shard_map/pallas_call | solution.py:399
  66.8 3.5 %shard_map.91 = (f32[1024,512]{1,0:T(8,128)S(1)}, f32[64,512]{1,0:T(8,128)S(1)}, f32[16,8,128]{2,1,0:T(8,128)S(1)}, f32[16,8,128]{2,1,0:T(8,128)S(1)}) custom-call(s32[2]{0:T(128)S(1)} %pad_add_fusion.where, f32[1024,512]{1,0:T(8,128)S(1)} %shard_map.89.pre, bf16[576,512]{1,0:T(8,128)(2,1)S(1)} %collective-permute-done.7.got_a, ...), custom_call_target="tpu_custom_call" | custom-call | flops 805306368 | bytes 6291456 | tf_op jit(solution)/shard_map/pallas_call | solution.py:431
  70.3 3.6 %collective-permute-start.15 = (f32[16,8,128]{2,1,0:T(8,128)S(1)}, f32[16,8,128]{2,1,0:T(8,128)S(1)}, u32[]{:S(2)}, u32[]{:S(2)}) collective-permute-start(f32[16,8,128]{2,1,0:T(8,128)S(1)} %get-tuple-element.38), channel_id=1, source_target_pairs={{0,8},{8,0},{16,24},{24,16},{32,40},{40,32},{48,56},{56,48},{64,72... | collective-permute-start | bytes 196616 | tf_op jit(solution)/shard_map/ppermute | solution.py:445
  74.8 2.9 %collective-permute-start.16 = (f32[16,8,128]{2,1,0:T(8,128)S(1)}, f32[16,8,128]{2,1,0:T(8,128)S(1)}, u32[]{:S(2)}, u32[]{:S(2)}) collective-permute-start(f32[16,8,128]{2,1,0:T(8,128)S(1)} %shard_map.92.a), channel_id=1, source_target_pairs={{0,16},{8,24},{16,0},{24,8},{32,48},{40,56},{48,32},{56,40},{64,80... | collective-permute-start | bytes 196616 | tf_op jit(solution)/shard_map/ppermute | solution.py:445
  77.7 2.1 %collective-permute-done.16.b = f32[16,8,128]{2,1,0:T(8,128)S(1)} collective-permute-done((f32[16,8,128]{2,1,0:T(8,128)S(1)}, f32[16,8,128]{2,1,0:T(8,128)S(1)}, u32[]{:S(2)}, u32[]{:S(2)}) %collective-permute-start.16) | collective-permute-done | bytes 65568 | tf_op jit(solution)/shard_map/ppermute | solution.py:445
  81.6 3.0 %collective-permute-start.18 = (f32[16,8,128]{2,1,0:T(8,128)S(1)}, f32[16,8,128]{2,1,0:T(8,128)S(1)}, u32[]{:S(2)}, u32[]{:S(2)}) collective-permute-start(f32[16,8,128]{2,1,0:T(8,128)S(1)} %shard_map.93.a), channel_id=1, source_target_pairs={{0,64},{8,72},{16,80},{24,88},{32,96},{40,104},{48,112},{56,120},{... | collective-permute-start | bytes 196616 | tf_op jit(solution)/shard_map/ppermute | solution.py:445
  84.6 3.1 %collective-permute-start.19 = (f32[16,8,128]{2,1,0:T(8,128)S(1)}, f32[16,8,128]{2,1,0:T(8,128)S(1)}, u32[]{:S(2)}, u32[]{:S(2)}) collective-permute-start(f32[16,8,128]{2,1,0:T(8,128)S(1)} %shard_map.93.a), channel_id=1, source_target_pairs={{0,96},{8,104},{16,112},{24,120},{32,64},{40,72},{48,80},{56,88},{... | collective-permute-start | bytes 196616 | tf_op jit(solution)/shard_map/ppermute | solution.py:445
  89.6 5.7 %collective-permute-start.20 = (f32[16,8,128]{2,1,0:T(8,128)S(1)}, f32[16,8,128]{2,1,0:T(8,128)S(1)}, u32[]{:S(2)}, u32[]{:S(2)}) collective-permute-start(f32[16,8,128]{2,1,0:T(8,128)S(1)} %shard_map.94.late.a), channel_id=1, source_target_pairs={{0,128},{8,136},{16,144},{24,152},{32,160},{40,168},{48,176},{56,1... | collective-permute-start | bytes 196616 | tf_op jit(solution)/shard_map/ppermute | solution.py:445
  95.3 3.7 %shard_map.95 = (f32[512,1024]{1,0:T(8,128)}, f32[8,128]{1,0:T(8,128)S(1)}) custom-call(f32[1024,512]{1,0:T(8,128)S(1)} %get-tuple-element.39.moment, f32[64,512]{1,0:T(8,128)S(1)} %get-tuple-element.40.picked, s32[16,4,512]{2,1,0:T(4,128)S(1)} %bitcast.9, bf16[256,256]{1,0:T(8,128)(2,1)S(1)} %copy-done.5, bf16[256,256]{1,0:T(8,128)(2,1)S(1)} %copy-done.6, ...), custom_call_target="tpu_custom_call" | custom-call | flops 805306368 | bytes 5242880 | tf_op jit(solution)/shard_map/pallas_call | solution.py:462
  99.0 4.4 %collective-permute-start.21 = (bf16[16,8,128]{2,1,0:T(8,128)(2,1)S(1)}, bf16[16,8,128]{2,1,0:T(8,128)(2,1)S(1)}, u32[]{:S(2)}, u32[]{:S(2)}) collective-permute-start(bf16[16,8,128]{2,1,0:T(8,128)(2,1)S(1)} %shard_map.96.half), channel_id=1, source_target_pairs={{0,8},{8,0},{16,24},{24,16},{32,40},{40,32},{48,56},{56,48},{64,72... | collective-permute-start | bytes 98312 | tf_op jit(solution)/shard_map/ppermute | solution.py:445
  108.5 2.2 %collective-permute-start.24 = (bf16[2,32,8,128]{3,2,1,0:T(8,128)(2,1)S(1)}, bf16[2,32,8,128]{3,2,1,0:T(8,128)(2,1)S(1)}, u32[]{:S(2)}, u32[]{:S(2)}) collective-permute-start(bf16[2,32,8,128]{3,2,1,0:T(8,128)(2,1)S(1)} %shard_map.97.tot), channel_id=1, source_target_pairs={{0,6},{1,7},{2,0},{3,1},{4,2},{5,3},{6,4},{7,5},{8,14},{9,15},{10,... | collective-permute-start | bytes 393224 | tf_op jit(solution)/shard_map/ppermute | solution.py:331
  112.3 3.6 %shard_map.98 = (f32[1024,256]{1,0:T(8,128)S(1)}, bf16[512,1024]{1,0:T(8,128)(2,1)}) custom-call(s32[2]{0:T(128)S(1)} %pad_add_fusion.where, bf16[256,4096]{1,0:T(8,128)(2,1)S(1)} %copy-done.1, bf16[320,1024]{1,0:T(8,128)(2,1)S(1)} %get-tuple-element.33.late.own, bf16[2,32,8,128]{3,2,1,0:T(8,128)(2,1)S(1)} %shard_map.97.tot, ...), custom_call_target="tpu_custom_call" | custom-call | flops 1610612736 | bytes 4194304 | tf_op jit(solution)/shard_map/pallas_call | solution.py:492
  116.7 3.8 %collective-permute-done.26.tot_3 = bf16[2,32,8,128]{3,2,1,0:T(8,128)(2,1)S(1)} collective-permute-done((bf16[2,32,8,128]{3,2,1,0:T(8,128)(2,1)S(1)}, bf16[2,32,8,128]{3,2,1,0:T(8,128)(2,1)S(1)}, u32[]{:S(2)}, u32[]{:S(2)}) %collective-permute-start.26) | collective-permute-done | bytes 131104 | tf_op jit(solution)/shard_map/ppermute | solution.py:328
  120.5 6.2 %shard_map.99 = bf16[256,1024]{1,0:T(8,128)(2,1)} custom-call(s32[2]{0:T(128)S(1)} %pad_add_fusion.where, bf16[256,4096]{1,0:T(8,128)(2,1)S(1)} %copy-done.1, bf16[256,4096]{1,0:T(8,128)(2,1)S(1)} %copy-done.1, bf16[256,4096]{1,0:T(8,128)(2,1)S(1)} %copy-done.1, bf16[320,1024]{1,0:T(8,128)(2,1)S(1)} %get-tuple-element.33.late.own, ...), custom_call_target="tpu_custom_call" | custom-call | flops 3221225472 | bytes 7340032 | tf_op jit(solution)/shard_map/pallas_call | solution.py:506
  (62 shorter events, 29.8 us)
Async XLA Ops:
  0.6 32.0 %collective-permute-start.6 = (bf16[512,1024]{1,0:T(8,128)(2,1)}, bf16[512,1024]{1,0:T(8,128)(2,1)S(1)}, u32[]{:S(2)}, u32[]{:S(2)}) collective-permute-start(bf16[512,1024]{1,0:T(8,128)(2,1)} %weight.1), channel_id=1, source_target_pairs={{0,1},{1,0},{2,3},{3,2},{4,5},{5,4},{6,7},{7,6},{8,9},{9,8},{10,11... | collective-permute-start | bytes 3145736 | tf_op jit(solution)/shard_map/ppermute | solution.py:337
  6.4 13.6 %collective-permute-start = (bf16[512,512]{1,0:T(8,128)(2,1)S(1)}, bf16[512,512]{1,0:T(8,128)(2,1)S(1)}, u32[]{:S(2)}, u32[]{:S(2)}) collective-permute-start(bf16[512,512]{1,0:T(8,128)(2,1)S(1)} %get-tuple-element.24.sent.a0), channel_id=1, source_target_pairs={{0,2},{1,3},{2,4},{3,5},{4,6},{5,7},{6,0},{7,1},{8,10},{9,11},{10,... | collective-permute-start | bytes 1572872 | tf_op jit(solution)/shard_map/ppermute | solution.py:328
  7.8 12.2 %collective-permute-start.1 = (bf16[512,512]{1,0:T(8,128)(2,1)S(1)}, bf16[512,512]{1,0:T(8,128)(2,1)S(1)}, u32[]{:S(2)}, u32[]{:S(2)}) collective-permute-start(bf16[512,512]{1,0:T(8,128)(2,1)S(1)} %get-tuple-element.25), channel_id=1, source_target_pairs={{0,6},{1,7},{2,0},{3,1},{4,2},{5,3},{6,4},{7,5},{8,14},{9,15},{10,... | collective-permute-start | bytes 1572872 | tf_op jit(solution)/shard_map/ppermute | solution.py:331
  9.3 23.3 %collective-permute-start.5 = (bf16[512,512]{1,0:T(8,128)(2,1)S(1)}, bf16[512,512]{1,0:T(8,128)(2,1)S(1)}, u32[]{:S(2)}, u32[]{:S(2)}) collective-permute-start(bf16[512,512]{1,0:T(8,128)(2,1)S(1)} %get-tuple-element.31), channel_id=1, source_target_pairs={{0,4},{1,5},{2,6},{3,7},{4,0},{5,1},{6,2},{7,3},{8,12},{9,13},{10,... | collective-permute-start | bytes 1572872 | tf_op jit(solution)/shard_map/ppermute | solution.py:334
  33.4 23.0 %collective-permute-start.7 = (bf16[576,512]{1,0:T(8,128)(2,1)S(1)}, bf16[576,512]{1,0:T(8,128)(2,1)S(1)}, u32[]{:S(2)}, u32[]{:S(2)}) collective-permute-start(bf16[576,512]{1,0:T(8,128)(2,1)S(1)} %shard_map.87), channel_id=1, source_target_pairs={{0,1},{1,0},{2,3},{3,2},{4,5},{5,4},{6,7},{7,6},{8,9},{9,8},{10,11... | collective-permute-start | bytes 1769480 | tf_op jit(solution)/shard_map/ppermute | solution.py:337
  33.7 5.7 %collective-permute-start.11 = (bf16[512,256]{1,0:T(8,128)(2,1)S(1)}, bf16[512,256]{1,0:T(8,128)(2,1)S(1)}, u32[]{:S(2)}, u32[]{:S(2)}) collective-permute-start(bf16[512,256]{1,0:T(8,128)(2,1)S(1)} %get-tuple-element.32.turned.b0.c0), channel_id=1, source_target_pairs={{0,6},{1,7},{2,0},{3,1},{4,2},{5,3},{6,4},{7,5},{8,14},{9,15},{10,... | collective-permute-start | bytes 786440 | tf_op jit(solution)/shard_map/ppermute | solution.py:331
  34.5 6.8 %collective-permute-start.12 = (bf16[512,256]{1,0:T(8,128)(2,1)S(1)}, bf16[512,256]{1,0:T(8,128)(2,1)S(1)}, u32[]{:S(2)}, u32[]{:S(2)}) collective-permute-start(bf16[512,256]{1,0:T(8,128)(2,1)S(1)} %get-tuple-element.32.turned.b0.c0), channel_id=1, source_target_pairs={{0,4},{1,5},{2,6},{3,7},{4,0},{5,1},{6,2},{7,3},{8,12},{9,13},{10,... | collective-permute-start | bytes 786440 | tf_op jit(solution)/shard_map/ppermute | solution.py:334
  36.1 14.6 %collective-permute-start.13 = (bf16[512,256]{1,0:T(8,128)(2,1)S(1)}, bf16[512,256]{1,0:T(8,128)(2,1)S(1)}, u32[]{:S(2)}, u32[]{:S(2)}) collective-permute-start(bf16[512,256]{1,0:T(8,128)(2,1)S(1)} %get-tuple-element.32.turned.b0.c0), channel_id=1, source_target_pairs={{0,2},{1,3},{2,4},{3,5},{4,6},{5,7},{6,0},{7,1},{8,10},{9,11},{10,... | collective-permute-start | bytes 786440 | tf_op jit(solution)/shard_map/ppermute | solution.py:328
  36.1 16.9 %collective-permute-start.2 = (bf16[256,512]{1,0:T(8,128)(2,1)S(1)}, bf16[256,512]{1,0:T(8,128)(2,1)S(1)}, u32[]{:S(2)}, u32[]{:S(2)}) collective-permute-start(bf16[256,512]{1,0:T(8,128)(2,1)S(1)} %get-tuple-element.27), channel_id=1, source_target_pairs={{0,6},{1,7},{2,0},{3,1},{4,2},{5,3},{6,4},{7,5},{8,14},{9,15},{10,... | collective-permute-start | bytes 786440 | tf_op jit(solution)/shard_map/ppermute | solution.py:331
  39.4 13.6 %collective-permute-start.3 = (bf16[256,512]{1,0:T(8,128)(2,1)S(1)}, bf16[256,512]{1,0:T(8,128)(2,1)S(1)}, u32[]{:S(2)}, u32[]{:S(2)}) collective-permute-start(bf16[256,512]{1,0:T(8,128)(2,1)S(1)} %get-tuple-element.28), channel_id=1, source_target_pairs={{0,4},{1,5},{2,6},{3,7},{4,0},{5,1},{6,2},{7,3},{8,12},{9,13},{10,... | collective-permute-start | bytes 786440 | tf_op jit(solution)/shard_map/ppermute | solution.py:334
  41.4 15.0 %collective-permute-start.4 = (bf16[256,512]{1,0:T(8,128)(2,1)S(1)}, bf16[256,512]{1,0:T(8,128)(2,1)S(1)}, u32[]{:S(2)}, u32[]{:S(2)}) collective-permute-start(bf16[256,512]{1,0:T(8,128)(2,1)S(1)} %get-tuple-element.29), channel_id=1, source_target_pairs={{0,2},{1,3},{2,4},{3,5},{4,6},{5,7},{6,0},{7,1},{8,10},{9,11},{10,... | collective-permute-start | bytes 786440 | tf_op jit(solution)/shard_map/ppermute | solution.py:328
  51.4 15.3 %collective-permute-start.14 = (bf16[512,512]{1,0:T(8,128)(2,1)S(1)}, bf16[512,512]{1,0:T(8,128)(2,1)S(1)}, u32[]{:S(2)}, u32[]{:S(2)}) collective-permute-start(bf16[512,512]{1,0:T(8,128)(2,1)S(1)} %shard_map.90), channel_id=1, source_target_pairs={{0,1},{1,0},{2,3},{3,2},{4,5},{5,4},{6,7},{7,6},{8,9},{9,8},{10,11... | collective-permute-start | bytes 1572872 | tf_op jit(solution)/shard_map/ppermute | solution.py:337
  59.5 48.5 %collective-permute-start.8 = (bf16[320,1024]{1,0:T(8,128)(2,1)S(1)}, bf16[320,1024]{1,0:T(8,128)(2,1)S(1)}, u32[]{:S(2)}, u32[]{:S(2)}) collective-permute-start(bf16[320,1024]{1,0:T(8,128)(2,1)S(1)} %get-tuple-element.34), channel_id=1, source_target_pairs={{0,6},{1,7},{2,0},{3,1},{4,2},{5,3},{6,4},{7,5},{8,14},{9,15},{10,... | collective-permute-start | bytes 1966088 | tf_op jit(solution)/shard_map/ppermute | solution.py:331
  61.4 46.6 %collective-permute-start.9 = (bf16[320,1024]{1,0:T(8,128)(2,1)S(1)}, bf16[320,1024]{1,0:T(8,128)(2,1)S(1)}, u32[]{:S(2)}, u32[]{:S(2)}) collective-permute-start(bf16[320,1024]{1,0:T(8,128)(2,1)S(1)} %get-tuple-element.35), channel_id=1, source_target_pairs={{0,4},{1,5},{2,6},{3,7},{4,0},{5,1},{6,2},{7,3},{8,12},{9,13},{10,... | collective-permute-start | bytes 1966088 | tf_op jit(solution)/shard_map/ppermute | solution.py:334
  63.9 44.1 %collective-permute-start.10 = (bf16[320,1024]{1,0:T(8,128)(2,1)S(1)}, bf16[320,1024]{1,0:T(8,128)(2,1)S(1)}, u32[]{:S(2)}, u32[]{:S(2)}) collective-permute-start(bf16[320,1024]{1,0:T(8,128)(2,1)S(1)} %get-tuple-element.36), channel_id=1, source_target_pairs={{0,2},{1,3},{2,4},{3,5},{4,6},{5,7},{6,0},{7,1},{8,10},{9,11},{10,... | collective-permute-start | bytes 1966088 | tf_op jit(solution)/shard_map/ppermute | solution.py:328
  74.8 5.0 %collective-permute-start.16 = (f32[16,8,128]{2,1,0:T(8,128)S(1)}, f32[16,8,128]{2,1,0:T(8,128)S(1)}, u32[]{:S(2)}, u32[]{:S(2)}) collective-permute-start(f32[16,8,128]{2,1,0:T(8,128)S(1)} %shard_map.92.a), channel_id=1, source_target_pairs={{0,16},{8,24},{16,0},{24,8},{32,48},{40,56},{48,32},{56,40},{64,80... | collective-permute-start | bytes 196616 | tf_op jit(solution)/shard_map/ppermute | solution.py:445
  79.8 4.8 %collective-permute-start.17 = (f32[16,8,128]{2,1,0:T(8,128)S(1)}, f32[16,8,128]{2,1,0:T(8,128)S(1)}, u32[]{:S(2)}, u32[]{:S(2)}) collective-permute-start(f32[16,8,128]{2,1,0:T(8,128)S(1)} %shard_map.93.a), channel_id=1, source_target_pairs={{0,32},{8,40},{16,48},{24,56},{32,0},{40,8},{48,16},{56,24},{64,96... | collective-permute-start | bytes 196616 | tf_op jit(solution)/shard_map/ppermute | solution.py:445
  81.6 6.1 %collective-permute-start.18 = (f32[16,8,128]{2,1,0:T(8,128)S(1)}, f32[16,8,128]{2,1,0:T(8,128)S(1)}, u32[]{:S(2)}, u32[]{:S(2)}) collective-permute-start(f32[16,8,128]{2,1,0:T(8,128)S(1)} %shard_map.93.a), channel_id=1, source_target_pairs={{0,64},{8,72},{16,80},{24,88},{32,96},{40,104},{48,112},{56,120},{... | collective-permute-start | bytes 196616 | tf_op jit(solution)/shard_map/ppermute | solution.py:445
  84.6 5.0 %collective-permute-start.19 = (f32[16,8,128]{2,1,0:T(8,128)S(1)}, f32[16,8,128]{2,1,0:T(8,128)S(1)}, u32[]{:S(2)}, u32[]{:S(2)}) collective-permute-start(f32[16,8,128]{2,1,0:T(8,128)S(1)} %shard_map.93.a), channel_id=1, source_target_pairs={{0,96},{8,104},{16,112},{24,120},{32,64},{40,72},{48,80},{56,88},{... | collective-permute-start | bytes 196616 | tf_op jit(solution)/shard_map/ppermute | solution.py:445
  89.6 9.4 %collective-permute-start.20 = (f32[16,8,128]{2,1,0:T(8,128)S(1)}, f32[16,8,128]{2,1,0:T(8,128)S(1)}, u32[]{:S(2)}, u32[]{:S(2)}) collective-permute-start(f32[16,8,128]{2,1,0:T(8,128)S(1)} %shard_map.94.late.a), channel_id=1, source_target_pairs={{0,128},{8,136},{16,144},{24,152},{32,160},{40,168},{48,176},{56,1... | collective-permute-start | bytes 196616 | tf_op jit(solution)/shard_map/ppermute | solution.py:445
  99.0 5.6 %collective-permute-start.21 = (bf16[16,8,128]{2,1,0:T(8,128)(2,1)S(1)}, bf16[16,8,128]{2,1,0:T(8,128)(2,1)S(1)}, u32[]{:S(2)}, u32[]{:S(2)}) collective-permute-start(bf16[16,8,128]{2,1,0:T(8,128)(2,1)S(1)} %shard_map.96.half), channel_id=1, source_target_pairs={{0,8},{8,0},{16,24},{24,16},{32,40},{40,32},{48,56},{56,48},{64,72... | collective-permute-start | bytes 98312 | tf_op jit(solution)/shard_map/ppermute | solution.py:445
  108.5 7.4 %collective-permute-start.24 = (bf16[2,32,8,128]{3,2,1,0:T(8,128)(2,1)S(1)}, bf16[2,32,8,128]{3,2,1,0:T(8,128)(2,1)S(1)}, u32[]{:S(2)}, u32[]{:S(2)}) collective-permute-start(bf16[2,32,8,128]{3,2,1,0:T(8,128)(2,1)S(1)} %shard_map.97.tot), channel_id=1, source_target_pairs={{0,6},{1,7},{2,0},{3,1},{4,2},{5,3},{6,4},{7,5},{8,14},{9,15},{10,... | collective-permute-start | bytes 393224 | tf_op jit(solution)/shard_map/ppermute | solution.py:331
  110.7 5.9 %collective-permute-start.25 = (bf16[2,32,8,128]{3,2,1,0:T(8,128)(2,1)S(1)}, bf16[2,32,8,128]{3,2,1,0:T(8,128)(2,1)S(1)}, u32[]{:S(2)}, u32[]{:S(2)}) collective-permute-start(bf16[2,32,8,128]{3,2,1,0:T(8,128)(2,1)S(1)} %shard_map.97.tot), channel_id=1, source_target_pairs={{0,4},{1,5},{2,6},{3,7},{4,0},{5,1},{6,2},{7,3},{8,12},{9,13},{10,... | collective-permute-start | bytes 393224 | tf_op jit(solution)/shard_map/ppermute | solution.py:334
  111.5 9.0 %collective-permute-start.26 = (bf16[2,32,8,128]{3,2,1,0:T(8,128)(2,1)S(1)}, bf16[2,32,8,128]{3,2,1,0:T(8,128)(2,1)S(1)}, u32[]{:S(2)}, u32[]{:S(2)}) collective-permute-start(bf16[2,32,8,128]{3,2,1,0:T(8,128)(2,1)S(1)} %shard_map.97.tot), channel_id=1, source_target_pairs={{0,2},{1,3},{2,4},{3,5},{4,6},{5,7},{6,0},{7,1},{8,10},{9,11},{10,... | collective-permute-start | bytes 393224 | tf_op jit(solution)/shard_map/ppermute | solution.py:328
  (11 other events, 89.3 us)

commit v7 on v6

--- a/solution.py
+++ b/solution.py
@@ -117,8 +117,11 @@
         copy.wait()
 
 
-def pack_second_kernel(where, cot, t0, t1, t2, t3, late_lo, late_hi, turned, mine, to_up, to_far, to_down):
+def pack_second_kernel(cot, late_lo, late_hi, late_far, turned):
     turned[...] = cot[...].T
+
+
+def pack_own_kernel(where, t0, t1, t2, t3, late, mine, to_up, to_far, to_down):
     for out, t in ((mine, t0), (to_up, t1), (to_far, t2), (to_down, t3)):
         out[...] = t[...]
 
@@ -163,7 +166,7 @@
     return rows
 
 
-def pick_kernel(where, pre, got_a, got_b, idx, ch, cl, late, moment, picked, keep, send):
+def pick_kernel(where, pre, got_a, got_b, idx, ch, cl, moment, picked, keep, send):
     step = pl.program_id(0)
     first = step < STEPS // 2
     got = jnp.where(first, got_a[...], got_b[...]).astype(jnp.float32)
@@ -188,8 +191,9 @@
     out[...] = (a[...] + b[...]).astype(out.dtype)
 
 
-def add_four_kernel(a, b, c, d, out):
-    out[...] = (a[...] + b[...]) + (c[...] + d[...])
+def add_release_kernel(a, b, *rest):
+    out = rest[3]
+    out[...] = a[...] + b[...]
 
 
 def pair_kernel(where, half, core, across, corner, late_0, late_1, late_2, out):
@@ -213,7 +217,7 @@
     mark[...] = back[:8, :LANES]
 
 
-def base_kernel(where, o0, o1, o2, o3, p0, p1, p2, p3, w_own, w_peer, idx, got_a, *outs):
+def base_kernel(where, o0, o1, o2, o3, p0, p1, p2, p3, w_own, w_peer, idx, got_a, late, *outs):
     mine, theirs = flat_index(idx), got_a[HALF:, :]
     first = (where[0] & 1) == 0
     left, right = jnp.where(first, mine, theirs), jnp.where(first, theirs, mine)
@@ -248,25 +252,28 @@
     for g in range(STEPS):
         expand_group(g, pairs, values, dense)
         span = slice(g * GROUP, (g + 1) * GROUP)
-        mixed[span, :] = mix(dense[span, :], tok[...], ((1,), (1,)))
         turned = dense[span, cols].T
         delta = mix(turned, ch[...], ((1,), (0,))) + mix(turned, cl[...], ((1,), (0,)))
         new = weight[:, span].astype(jnp.float32) - (step_rate / REPS) * delta
         out_weight[:, span] = new.astype(out_weight.dtype)
+    mixed[...] = mix(dense[...], tok[...], ((1,), (1,)))
 
 
 def forward_kernel(where, tok_1, tok_2, tok_3, own, hi, far, lo, tot_1, tot_2, tot_3, mixed, ch, cl, out, *scratch):
-    toks, dense, pairs, values = (tok_1, tok_2, tok_3), scratch[:3], scratch[3:6], scratch[6:]
+    toks, dense, pairs, values = (tok_1, tok_2, tok_3), scratch[:3], scratch[3:6], scratch[6:9]
+    total = scratch[9]
     for near, pair, tot, value in zip((hi, far, lo), pairs, (tot_1, tot_2, tot_3), values):
         pair[...] = near[TOK:, :].astype(jnp.float32)
         value[...] = tot[...].astype(jnp.float32)
+    before = mixed
+    for tok, pair, value, buffer in zip(toks, pairs, values, dense):
+        for g in range(STEPS):
+            expand_group(g, pair, value, buffer)
+        total[...] = before[...] + mix(buffer[...], tok[...], ((1,), (1,)))
+        before = total
     for g in range(STEPS):
         span = slice(g * GROUP, (g + 1) * GROUP)
-        total = mixed[span, :]
-        for tok, pair, value, buffer in zip(toks, pairs, values, dense):
-            expand_group(g, pair, value, buffer)
-            total += mix(buffer[span, :], tok[...], ((1,), (1,)))
-        delta = three_pass(split_pair(total.T), (ch[...], cl[...]), ((1,), (0,)))
+        delta = three_pass(split_pair(total[span, :].T), (ch[...], cl[...]), ((1,), (0,)))
         base = own[:TOK, span].astype(jnp.float32) + hi[:TOK, span].astype(jnp.float32)
         base += far[:TOK, span].astype(jnp.float32) + lo[:TOK, span].astype(jnp.float32)
         out[:, span] = (base - (step_rate / REPS) * delta).astype(out.dtype)
@@ -359,21 +366,17 @@
     first_x = across(first_far)
     firsts = (first_up, first_hi, first_x, first_lo)
 
-    cot_b, own_0, own_up, own_across, own_down = pl.pallas_call(
+    cot_b = pl.pallas_call(
         pack_second_kernel,
-        grid_spec=pltpu.PrefetchScalarGridSpec(
-            num_scalar_prefetch=1,
-            grid=(1,),
-            in_specs=[pl.BlockSpec((TOK, HALF), lambda c, *_: (0, 1))] + columns(0) + [AFTER, AFTER],
-            out_specs=[whole(HALF, TOK)] + [PIECE] * 4,
-        ),
-        out_shape=[shape(HALF, TOK)] + [shape(TOK, ROWS)] * 4,
-        compiler_params=params(),
-        cost_estimate=cost(0, 3),
-    )(place, cotangent, tokens, tokens, tokens, tokens, first_lo, first_hi)
+        grid=(1,),
+        in_specs=[pl.BlockSpec((TOK, HALF), lambda c: (0, 1)), AFTER, AFTER, AFTER],
+        out_specs=whole(HALF, TOK),
+        out_shape=shape(HALF, TOK),
+        compiler_params=params(),
+        cost_estimate=cost(0, 1),
+    )(cotangent, first_lo, first_hi, first_x)
     b_lo, b_hi, b_far = up(cot_b), down(cot_b), across(cot_b)
     cots_b = (cot_b, b_hi, b_far, b_lo)
-    owns = (own_0, down(own_down), across(own_across), up(own_up))
 
     partial_a = pl.pallas_call(
         partial_first_kernel,
@@ -396,6 +399,20 @@
     )(*cots_b, peer_0, *firsts[1:])
     got_b = swap(partial_b)
 
+    own_0, own_up, own_across, own_down = pl.pallas_call(
+        pack_own_kernel,
+        grid_spec=pltpu.PrefetchScalarGridSpec(
+            num_scalar_prefetch=1,
+            grid=(1,),
+            in_specs=columns(0) + [AFTER],
+            out_specs=[PIECE] * 4,
+        ),
+        out_shape=[shape(TOK, ROWS)] * 4,
+        compiler_params=params(),
+        cost_estimate=cost(0, 2),
+    )(place, tokens, tokens, tokens, tokens, partial_b)
+    owns = (own_0, down(own_down), across(own_across), up(own_up))
+
     pre = pl.pallas_call(
         own_kernel,
         grid=(STEPS,),
@@ -409,23 +426,6 @@
         cost_estimate=cost(2 * KV * KV * ROWS, 7),
     )(*firsts, *cots_b, *owns, momentum[0])
 
-    base, base_up, base_across, base_down = pl.pallas_call(
-        base_kernel,
-        grid_spec=pltpu.PrefetchScalarGridSpec(
-            num_scalar_prefetch=1,
-            grid=(1,),
-            in_specs=[PIECE] * 5
-            + [MESSAGE] * 3
-            + [whole(ROWS, KV)] * 2
-            + [INDEX, whole(HALF + PICKS, ROWS)],
-            out_specs=[whole(TOK + PICKS, KV)] * 4,
-        ),
-        out_shape=[shape(TOK + PICKS, KV)] * 4,
-        compiler_params=params(2 * VMEM_LIMIT),
-        cost_estimate=cost(4 * KV * KV * ROWS, 7),
-    )(place, *owns, peer_0, *firsts[1:], weight, weight_peer, index_t, got_a)
-    base_lo, base_hi, base_far = up(base_up), down(base_down), across(base_across)
-
     halves = whole(TILES // 2, 8, LANES)
     half_shape = shape(TILES // 2, 8, LANES, dtype=F32)
     moment, picked, keep, send = pl.pallas_call(
@@ -433,13 +433,13 @@
         grid_spec=pltpu.PrefetchScalarGridSpec(
             num_scalar_prefetch=1,
             grid=(STEPS,),
-            in_specs=[by_row(GROUP, ROWS)] + GOT + [INDEX_STEP] + BASIS + [AFTER],
+            in_specs=[by_row(GROUP, ROWS)] + GOT + [INDEX_STEP] + BASIS,
             out_specs=[by_row(GROUP, ROWS), by_row(PICKS // STEPS, ROWS), halves, halves],
         ),
         out_shape=[shape(KV, ROWS, dtype=F32), shape(PICKS, ROWS, dtype=F32), half_shape, half_shape],
         compiler_params=params(),
         cost_estimate=cost(6 * KV * GROUP * ROWS, 6),
-    )(place, pre, got_a, got_b, index_t, high, low, base)
+    )(place, pre, got_a, got_b, index_t, high, low)
 
     def partner(x, bits):
         return lax.ppermute(x, "rep", [(i, i ^ bits) for i in range(REPS)])
@@ -456,8 +456,36 @@
         )(*parts, *after)
 
     value = add(add_two_kernel, half_shape, keep, partner(send, 1))
-    value = add(add_two_kernel, half_shape, value, partner(value, 2))
-    value = add(add_four_kernel, half_shape, value, partner(value, 4), partner(value, 8), partner(value, 12))
+    from_hi = partner(value, 2)
+
+    base, base_up, base_across, base_down = pl.pallas_call(
+        base_kernel,
+        grid_spec=pltpu.PrefetchScalarGridSpec(
+            num_scalar_prefetch=1,
+            grid=(1,),
+            in_specs=[PIECE] * 5
+            + [MESSAGE] * 3
+            + [whole(ROWS, KV)] * 2
+            + [INDEX, whole(HALF + PICKS, ROWS), AFTER],
+            out_specs=[whole(TOK + PICKS, KV)] * 4,
+        ),
+        out_shape=[shape(TOK + PICKS, KV)] * 4,
+        compiler_params=params(2 * VMEM_LIMIT),
+        cost_estimate=cost(0, 0),
+    )(place, *owns, peer_0, *firsts[1:], weight, weight_peer, index_t, got_a, value)
+    value, base_up, base_across, base_down = pl.pallas_call(
+        add_release_kernel,
+        grid=(1,),
+        in_specs=[halves] * 2 + [AFTER] * 3,
+        out_specs=[halves] + [AFTER] * 3,
+        out_shape=[half_shape] + [shape(TOK + PICKS, KV)] * 3,
+        input_output_aliases={2: 1, 3: 2, 4: 3},
+        compiler_params=params(),
+        cost_estimate=cost(0, 0.25),
+    )(value, from_hi, base_up, base_across, base_down)
+    base_lo, base_hi, base_far = up(base_up), down(base_down), across(base_across)
+    value = add(add_two_kernel, half_shape, value, partner(value, 4))
+    value = add(add_two_kernel, half_shape, value, partner(value, 8))
     last = partner(value, 16)
     new_momentum, mark = pl.pallas_call(
         residual_kernel,
@@ -514,7 +542,7 @@
             + [whole(KV, TOK)]
             + BASIS,
             out_specs=whole(TOK, KV),
-            scratch_shapes=[DENSE] * 3 + [PAIRS] * 3 + [VALUES] * 3,
+            scratch_shapes=[DENSE] * 3 + [PAIRS] * 3 + [VALUES] * 3 + [pltpu.VMEM((KV, TOK), F32)],
         ),
         out_shape=shape(TOK, KV),
         compiler_params=params(2 * VMEM_LIMIT),

time: 127 us -> 132 us (1.039)
  waiting for transfers between devices: 44.2 us -> 65 us
  starting transfers between devices: 53 us -> 38.1 us
    ppermute x5, waiting for transfers between devices: 0.63 us -> 16.8 us  [down(): return lax.ppermute(x, 'fsdp', [(i, (i + 6) % 8) for i in range(8)])]
    ppermute x5, waiting for transfers between devices: 22.8 us -> 37.4 us  [up(): return lax.ppermute(x, 'fsdp', [(i, (i + 2) % 8) for i in range(8)])]
    ppermute x5, waiting for transfers between devices: 13.6 us -> 3.66 us  [across(): return lax.ppermute(x, 'fsdp', [(i, (i + 4) % 8) for i in range(8)])]
    ppermute x7 -> x6, starting transfers between devices: 24.4 us -> 16.1 us  [partner(): return lax.ppermute(x, 'rep', [(i, i ^ bits) for i in range(REPS)])]
    ppermute x5, starting transfers between devices: 7.49 us -> 1.27 us  [across(): return lax.ppermute(x, 'fsdp', [(i, (i + 4) % 8) for i in range(8)])]
    ppermute x5, starting transfers between devices: 5.6 us -> 2.37 us  [up(): return lax.ppermute(x, 'fsdp', [(i, (i + 2) % 8) for i in range(8)])]
    ppermute x1, starting transfers between devices: 1.07 us -> 4.12 us  [body(): lax.ppermute(half, ('rep', 'fsdp'), [(i, i ^ 9) for i in range(REPS * 8)])]
    ppermute x4, starting transfers between devices: 5.28 us -> 3.32 us  [swap(): return lax.ppermute(x, 'fsdp', [(i, i ^ 1) for i in range(8)])]
  transfers between devices with their start and end apart: 27 -> 26, of which waited for: 13 -> 16; matrix products, arithmetic and copies ran while one was open for 0% -> 0% of each run, Pallas kernels for 15% -> 12%
where the time goes in v7:
time: 132 us
  waiting for transfers between devices  65 us (49%)
  starting transfers between devices  38.1 us (29%)
  Pallas kernels  25.4 us (19%)
  local copies, waits for them, and re-layouts  2.66 us (2%)
    ppermute x5, waiting for transfers between devices, up(): return lax.ppermute(x, 'fsdp', [(i, (i + 2) % 8) for i in range(8)])  37.4 us
    ppermute x5, waiting for transfers between devices, down(): return lax.ppermute(x, 'fsdp', [(i, (i + 6) % 8) for i in range(8)])  16.8 us
    ppermute x6, starting transfers between devices, partner(): return lax.ppermute(x, 'rep', [(i, i ^ bits) for i in range(REPS)])  16.1 us
    ppermute x5, starting transfers between devices, down(): return lax.ppermute(x, 'fsdp', [(i, (i + 6) % 8) for i in range(8)])  10.9 us
    pallas_call x1, Pallas kernels, body(): pl.pallas_call(forward_kernel, grid_spec=pltpu.PrefetchScalarGridSpec(num...  6.01 us
    ppermute x6, waiting for transfers between devices, partner(): return lax.ppermute(x, 'rep', [(i, i ^ bits) for i in range(REPS)])  5.18 us
    ppermute x1, starting transfers between devices, body(): lax.ppermute(half, ('rep', 'fsdp'), [(i, i ^ 9) for i in range(REPS * 8)])  4.12 us
    pallas_call x1, Pallas kernels, body(): pl.pallas_call(residual_kernel, grid=(STEPS,), in_specs=[by_row(GROUP, RO...  3.71 us
  transfers between devices with their start and end apart: 26, of which 16 were waited for; matrix products, arithmetic and copies ran while one was open for 0% of the time, Pallas kernels for 12%

profile of v7, /device:TPU:1, one launch (start us, length us, event | category | flops | bytes accessed | tf_op | source)
XLA Modules:
  0.0 132.1 jit_solution(16587265244436664639)
XLA Ops:
  0.6 2.1 %collective-permute-start.9 = (bf16[512,1024]{1,0:T(8,128)(2,1)}, bf16[512,1024]{1,0:T(8,128)(2,1)S(1)}, u32[]{:S(2)}, u32[]{:S(2)}) collective-permute-start(bf16[512,1024]{1,0:T(8,128)(2,1)} %weight.1), channel_id=1, source_target_pairs={{0,1},{1,0},{2,3},{3,2},{4,5},{5,4},{6,7},{7,6},{8,9},{9,8},{10,11... | collective-permute-start | bytes 3145736 | tf_op jit(solution)/shard_map/ppermute | solution.py:344
  6.4 2.8 %collective-permute-start.1 = (bf16[512,512]{1,0:T(8,128)(2,1)S(1)}, bf16[512,512]{1,0:T(8,128)(2,1)S(1)}, u32[]{:S(2)}, u32[]{:S(2)}) collective-permute-start(bf16[512,512]{1,0:T(8,128)(2,1)S(1)} %get-tuple-element.28), channel_id=1, source_target_pairs={{0,6},{1,7},{2,0},{3,1},{4,2},{5,3},{6,4},{7,5},{8,14},{9,15},{10,... | collective-permute-start | bytes 1572872 | tf_op jit(solution)/shard_map/ppermute | solution.py:338
  10.3 10.6 %collective-permute-done.1.late_hi.hi.a1.p1 = bf16[512,512]{1,0:T(8,128)(2,1)S(1)} collective-permute-done((bf16[512,512]{1,0:T(8,128)(2,1)S(1)}, bf16[512,512]{1,0:T(8,128)(2,1)S(1)}, u32[]{:S(2)}, u32[]{:S(2)}) %collective-permute-start.1) | collective-permute-done | bytes 524320 | tf_op jit(solution)/shard_map/ppermute | solution.py:338
  20.8 2.1 %collective-permute-done.2.late_far.far.a2.p2 = bf16[512,512]{1,0:T(8,128)(2,1)S(1)} collective-permute-done((bf16[512,512]{1,0:T(8,128)(2,1)S(1)}, bf16[512,512]{1,0:T(8,128)(2,1)S(1)}, u32[]{:S(2)}, u32[]{:S(2)}) %collective-permute-start.2) | collective-permute-done | bytes 524320 | tf_op jit(solution)/shard_map/ppermute | solution.py:341
  23.0 12.8 %collective-permute-done.late_lo.lo.a3.p3 = bf16[512,512]{1,0:T(8,128)(2,1)S(1)} collective-permute-done((bf16[512,512]{1,0:T(8,128)(2,1)S(1)}, bf16[512,512]{1,0:T(8,128)(2,1)S(1)}, u32[]{:S(2)}, u32[]{:S(2)}) %collective-permute-start) | collective-permute-done | bytes 524320 | tf_op jit(solution)/shard_map/ppermute | solution.py:335
  36.5 2.2 %collective-permute-start.3 = (bf16[512,256]{1,0:T(8,128)(2,1)S(1)}, bf16[512,256]{1,0:T(8,128)(2,1)S(1)}, u32[]{:S(2)}, u32[]{:S(2)}) collective-permute-start(bf16[512,256]{1,0:T(8,128)(2,1)S(1)} %shard_map.86.c0.turned.b0), channel_id=1, source_target_pairs={{0,6},{1,7},{2,0},{3,1},{4,2},{5,3},{6,4},{7,5},{8,14},{9,15},{10,... | collective-permute-start | bytes 786440 | tf_op jit(solution)/shard_map/ppermute | solution.py:338
  39.8 10.5 %collective-permute-done.5.c3.b3 = bf16[512,256]{1,0:T(8,128)(2,1)S(1)} collective-permute-done((bf16[512,256]{1,0:T(8,128)(2,1)S(1)}, bf16[512,256]{1,0:T(8,128)(2,1)S(1)}, u32[]{:S(2)}, u32[]{:S(2)}) %collective-permute-start.5) | collective-permute-done | bytes 262176 | tf_op jit(solution)/shard_map/ppermute | solution.py:335
  52.3 2.9 %collective-permute-start.6 = (bf16[256,512]{1,0:T(8,128)(2,1)S(1)}, bf16[256,512]{1,0:T(8,128)(2,1)S(1)}, u32[]{:S(2)}, u32[]{:S(2)}) collective-permute-start(bf16[256,512]{1,0:T(8,128)(2,1)S(1)} %get-tuple-element.32), channel_id=1, source_target_pairs={{0,6},{1,7},{2,0},{3,1},{4,2},{5,3},{6,4},{7,5},{8,14},{9,15},{10,... | collective-permute-start | bytes 786440 | tf_op jit(solution)/shard_map/ppermute | solution.py:338
  55.9 5.8 %collective-permute-done.6.t1.o1 = bf16[256,512]{1,0:T(8,128)(2,1)S(1)} collective-permute-done((bf16[256,512]{1,0:T(8,128)(2,1)S(1)}, bf16[256,512]{1,0:T(8,128)(2,1)S(1)}, u32[]{:S(2)}, u32[]{:S(2)}) %collective-permute-start.6) | collective-permute-done | bytes 262176 | tf_op jit(solution)/shard_map/ppermute | solution.py:338
  63.2 6.7 %collective-permute-done.8.t3.o3 = bf16[256,512]{1,0:T(8,128)(2,1)S(1)} collective-permute-done((bf16[256,512]{1,0:T(8,128)(2,1)S(1)}, bf16[256,512]{1,0:T(8,128)(2,1)S(1)}, u32[]{:S(2)}, u32[]{:S(2)}) %collective-permute-start.8) | collective-permute-done | bytes 262176 | tf_op jit(solution)/shard_map/ppermute | solution.py:335
  69.9 2.3 %shard_map.90.pre = f32[1024,512]{1,0:T(8,128)S(1)} custom-call(bf16[512,512]{1,0:T(8,128)(2,1)S(1)} %get-tuple-element.27.sent.a0, bf16[512,512]{1,0:T(8,128)(2,1)S(1)} %collective-permute-done.1.late_hi.hi.a1.p1, bf16[512,512]{1,0:T(8,128)(2,1)S(1)} %collective-permute-done.2.late_far.far.a2.p2, ...), custom_call_target="tpu_custom_call" | custom-call | flops 1073741824 | bytes 7340032 | tf_op jit(solution)/shard_map/pallas_call | solution.py:416
  72.2 3.5 %shard_map.91 = (f32[1024,512]{1,0:T(8,128)S(1)}, f32[64,512]{1,0:T(8,128)S(1)}, f32[16,8,128]{2,1,0:T(8,128)S(1)}, f32[16,8,128]{2,1,0:T(8,128)S(1)}) custom-call(s32[2]{0:T(128)S(1)} %pad_add_fusion.where, f32[1024,512]{1,0:T(8,128)S(1)} %shard_map.90.pre, bf16[576,512]{1,0:T(8,128)(2,1)S(1)} %collective-permute-done.10.got_a, ...), custom_call_target="tpu_custom_call" | custom-call | flops 805306368 | bytes 6291456 | tf_op jit(solution)/shard_map/pallas_call | solution.py:431
  77.6 3.0 %collective-permute-start.13 = (f32[16,8,128]{2,1,0:T(8,128)S(1)}, f32[16,8,128]{2,1,0:T(8,128)S(1)}, u32[]{:S(2)}, u32[]{:S(2)}) collective-permute-start(f32[16,8,128]{2,1,0:T(8,128)S(1)} %shard_map.92.late.a), channel_id=1, source_target_pairs={{0,16},{8,24},{16,0},{24,8},{32,48},{40,56},{48,32},{56,40},{64,80... | collective-permute-start | bytes 196616 | tf_op jit(solution)/shard_map/ppermute | solution.py:445
  80.6 3.0 %shard_map.93 = (bf16[320,1024]{1,0:T(8,128)(2,1)S(1)}, bf16[320,1024]{1,0:T(8,128)(2,1)S(1)}, bf16[320,1024]{1,0:T(8,128)(2,1)S(1)}, bf16[320,1024]{1,0:T(8,128)(2,1)S(1)}) custom-call(s32[2]{0:T(128)S(1)} %pad_add_fusion.where, bf16[256,512]{1,0:T(8,128)(2,1)S(1)} %get-tuple-element.31.t0.o0, bf16[256,512]{1,0:T(8,128)(2,1)S(1)} %collective-permute-done.6.t1.o1, ...), custom_call_target="tpu_custom_call" | custom-call | tf_op jit(solution)/shard_map/pallas_call | solution.py:461
  88.8 3.1 %collective-permute-start.18 = (f32[16,8,128]{2,1,0:T(8,128)S(1)}, f32[16,8,128]{2,1,0:T(8,128)S(1)}, u32[]{:S(2)}, u32[]{:S(2)}) collective-permute-start(f32[16,8,128]{2,1,0:T(8,128)S(1)} %shard_map.95.a), channel_id=1, source_target_pairs={{0,64},{8,72},{16,80},{24,88},{32,96},{40,104},{48,112},{56,120},{... | collective-permute-start | bytes 196616 | tf_op jit(solution)/shard_map/ppermute | solution.py:445
  91.8 2.0 %collective-permute-done.18.b = f32[16,8,128]{2,1,0:T(8,128)S(1)} collective-permute-done((f32[16,8,128]{2,1,0:T(8,128)S(1)}, f32[16,8,128]{2,1,0:T(8,128)S(1)}, u32[]{:S(2)}, u32[]{:S(2)}) %collective-permute-start.18) | collective-permute-done | bytes 65568 | tf_op jit(solution)/shard_map/ppermute | solution.py:445
  93.8 6.9 %collective-permute-start.19 = (f32[16,8,128]{2,1,0:T(8,128)S(1)}, f32[16,8,128]{2,1,0:T(8,128)S(1)}, u32[]{:S(2)}, u32[]{:S(2)}) collective-permute-start(f32[16,8,128]{2,1,0:T(8,128)S(1)} %shard_map.96.late.a), channel_id=1, source_target_pairs={{0,128},{8,136},{16,144},{24,152},{32,160},{40,168},{48,176},{56,1... | collective-permute-start | bytes 196616 | tf_op jit(solution)/shard_map/ppermute | solution.py:445
  100.7 3.7 %shard_map.97 = (f32[512,1024]{1,0:T(8,128)}, f32[8,128]{1,0:T(8,128)S(1)}) custom-call(f32[1024,512]{1,0:T(8,128)S(1)} %get-tuple-element.45.moment, f32[64,512]{1,0:T(8,128)S(1)} %get-tuple-element.46.picked, s32[16,4,512]{2,1,0:T(4,128)S(1)} %bitcast.9, bf16[256,256]{1,0:T(8,128)(2,1)S(1)} %copy-done.7, bf16[256,256]{1,0:T(8,128)(2,1)S(1)} %copy-done.6, ...), custom_call_target="tpu_custom_call" | custom-call | flops 805306368 | bytes 5242880 | tf_op jit(solution)/shard_map/pallas_call | solution.py:490
  104.4 4.1 %collective-permute-start.22 = (bf16[16,8,128]{2,1,0:T(8,128)(2,1)S(1)}, bf16[16,8,128]{2,1,0:T(8,128)(2,1)S(1)}, u32[]{:S(2)}, u32[]{:S(2)}) collective-permute-start(bf16[16,8,128]{2,1,0:T(8,128)(2,1)S(1)} %shard_map.98.half), channel_id=1, source_target_pairs={{0,9},{1,8},{2,11},{3,10},{4,13},{5,12},{6,15},{7,14},{8,1},{9,0},... | collective-permute-start | bytes 98312 | tf_op jit(solution)/shard_map/ppermute | solution.py:501
  112.0 4.5 %collective-permute-done.16.late_0.lo = bf16[320,1024]{1,0:T(8,128)(2,1)S(1)} collective-permute-done((bf16[320,1024]{1,0:T(8,128)(2,1)S(1)}, bf16[320,1024]{1,0:T(8,128)(2,1)S(1)}, u32[]{:S(2)}, u32[]{:S(2)}) %collective-permute-start.16) | collective-permute-done | bytes 655392 | tf_op jit(solution)/shard_map/ppermute | solution.py:335
  117.6 2.2 %collective-permute-start.23 = (bf16[2,32,8,128]{3,2,1,0:T(8,128)(2,1)S(1)}, bf16[2,32,8,128]{3,2,1,0:T(8,128)(2,1)S(1)}, u32[]{:S(2)}, u32[]{:S(2)}) collective-permute-start(bf16[2,32,8,128]{3,2,1,0:T(8,128)(2,1)S(1)} %shard_map.99.tot), channel_id=1, source_target_pairs={{0,6},{1,7},{2,0},{3,1},{4,2},{5,3},{6,4},{7,5},{8,14},{9,15},{10,... | collective-permute-start | bytes 393224 | tf_op jit(solution)/shard_map/ppermute | solution.py:338
  119.8 3.3 %shard_map.100 = (f32[1024,256]{1,0:T(8,128)S(1)}, bf16[512,1024]{1,0:T(8,128)(2,1)}) custom-call(s32[2]{0:T(128)S(1)} %pad_add_fusion.where, bf16[256,4096]{1,0:T(8,128)(2,1)S(1)} %copy-done.1, bf16[320,1024]{1,0:T(8,128)(2,1)S(1)} %get-tuple-element.37.own, bf16[2,32,8,128]{3,2,1,0:T(8,128)(2,1)S(1)} %shard_map.99.tot, bf16[512,1024]{1,0:T(8,128)(2,1)S(1)} %copy-done.5, ...), custom_call_target="tpu_custom_call" | custom-call | flops 1610612736 | bytes 4194304 | tf_op jit(solution)/shard_map/pallas_call | solution.py:520
  123.1 2.9 %collective-permute-done.25.tot_3 = bf16[2,32,8,128]{3,2,1,0:T(8,128)(2,1)S(1)} collective-permute-done((bf16[2,32,8,128]{3,2,1,0:T(8,128)(2,1)S(1)}, bf16[2,32,8,128]{3,2,1,0:T(8,128)(2,1)S(1)}, u32[]{:S(2)}, u32[]{:S(2)}) %collective-permute-start.25) | collective-permute-done | bytes 131104 | tf_op jit(solution)/shard_map/ppermute | solution.py:335
  126.1 6.0 %shard_map.101 = bf16[256,1024]{1,0:T(8,128)(2,1)} custom-call(s32[2]{0:T(128)S(1)} %pad_add_fusion.where, bf16[256,4096]{1,0:T(8,128)(2,1)S(1)} %copy-done.1, bf16[256,4096]{1,0:T(8,128)(2,1)S(1)} %copy-done.1, bf16[256,4096]{1,0:T(8,128)(2,1)S(1)} %copy-done.1, bf16[320,1024]{1,0:T(8,128)(2,1)S(1)} %get-tuple-element.37.own, ...), custom_call_target="tpu_custom_call" | custom-call | flops 3221225472 | bytes 7340032 | tf_op jit(solution)/shard_map/pallas_call | solution.py:534
  (62 shorter events, 22.2 us)
Async XLA Ops:
  0.6 38.1 %collective-permute-start.9 = (bf16[512,1024]{1,0:T(8,128)(2,1)}, bf16[512,1024]{1,0:T(8,128)(2,1)S(1)}, u32[]{:S(2)}, u32[]{:S(2)}) collective-permute-start(bf16[512,1024]{1,0:T(8,128)(2,1)} %weight.1), channel_id=1, source_target_pairs={{0,1},{1,0},{2,3},{3,2},{4,5},{5,4},{6,7},{7,6},{8,9},{9,8},{10,11... | collective-permute-start | bytes 3145736 | tf_op jit(solution)/shard_map/ppermute | solution.py:344
  6.4 14.4 %collective-permute-start.1 = (bf16[512,512]{1,0:T(8,128)(2,1)S(1)}, bf16[512,512]{1,0:T(8,128)(2,1)S(1)}, u32[]{:S(2)}, u32[]{:S(2)}) collective-permute-start(bf16[512,512]{1,0:T(8,128)(2,1)S(1)} %get-tuple-element.28), channel_id=1, source_target_pairs={{0,6},{1,7},{2,0},{3,1},{4,2},{5,3},{6,4},{7,5},{8,14},{9,15},{10,... | collective-permute-start | bytes 1572872 | tf_op jit(solution)/shard_map/ppermute | solution.py:338
  9.2 13.7 %collective-permute-start.2 = (bf16[512,512]{1,0:T(8,128)(2,1)S(1)}, bf16[512,512]{1,0:T(8,128)(2,1)S(1)}, u32[]{:S(2)}, u32[]{:S(2)}) collective-permute-start(bf16[512,512]{1,0:T(8,128)(2,1)S(1)} %get-tuple-element.29), channel_id=1, source_target_pairs={{0,4},{1,5},{2,6},{3,7},{4,0},{5,1},{6,2},{7,3},{8,12},{9,13},{10,... | collective-permute-start | bytes 1572872 | tf_op jit(solution)/shard_map/ppermute | solution.py:341
  9.6 26.2 %collective-permute-start = (bf16[512,512]{1,0:T(8,128)(2,1)S(1)}, bf16[512,512]{1,0:T(8,128)(2,1)S(1)}, u32[]{:S(2)}, u32[]{:S(2)}) collective-permute-start(bf16[512,512]{1,0:T(8,128)(2,1)S(1)} %get-tuple-element.27.sent.a0), channel_id=1, source_target_pairs={{0,2},{1,3},{2,4},{3,5},{4,6},{5,7},{6,0},{7,1},{8,10},{9,11},{10,... | collective-permute-start | bytes 1572872 | tf_op jit(solution)/shard_map/ppermute | solution.py:335
  35.9 14.3 %collective-permute-start.5 = (bf16[512,256]{1,0:T(8,128)(2,1)S(1)}, bf16[512,256]{1,0:T(8,128)(2,1)S(1)}, u32[]{:S(2)}, u32[]{:S(2)}) collective-permute-start(bf16[512,256]{1,0:T(8,128)(2,1)S(1)} %shard_map.86.c0.turned.b0), channel_id=1, source_target_pairs={{0,2},{1,3},{2,4},{3,5},{4,6},{5,7},{6,0},{7,1},{8,10},{9,11},{10,... | collective-permute-start | bytes 786440 | tf_op jit(solution)/shard_map/ppermute | solution.py:335
  36.0 14.2 %collective-permute-start.4 = (bf16[512,256]{1,0:T(8,128)(2,1)S(1)}, bf16[512,256]{1,0:T(8,128)(2,1)S(1)}, u32[]{:S(2)}, u32[]{:S(2)}) collective-permute-start(bf16[512,256]{1,0:T(8,128)(2,1)S(1)} %shard_map.86.c0.turned.b0), channel_id=1, source_target_pairs={{0,4},{1,5},{2,6},{3,7},{4,0},{5,1},{6,2},{7,3},{8,12},{9,13},{10,... | collective-permute-start | bytes 786440 | tf_op jit(solution)/shard_map/ppermute | solution.py:341
  36.5 14.1 %collective-permute-start.3 = (bf16[512,256]{1,0:T(8,128)(2,1)S(1)}, bf16[512,256]{1,0:T(8,128)(2,1)S(1)}, u32[]{:S(2)}, u32[]{:S(2)}) collective-permute-start(bf16[512,256]{1,0:T(8,128)(2,1)S(1)} %shard_map.86.c0.turned.b0), channel_id=1, source_target_pairs={{0,6},{1,7},{2,0},{3,1},{4,2},{5,3},{6,4},{7,5},{8,14},{9,15},{10,... | collective-permute-start | bytes 786440 | tf_op jit(solution)/shard_map/ppermute | solution.py:338
  39.4 32.8 %collective-permute-start.10 = (bf16[576,512]{1,0:T(8,128)(2,1)S(1)}, bf16[576,512]{1,0:T(8,128)(2,1)S(1)}, u32[]{:S(2)}, u32[]{:S(2)}) collective-permute-start(bf16[576,512]{1,0:T(8,128)(2,1)S(1)} %shard_map.89), channel_id=1, source_target_pairs={{0,1},{1,0},{2,3},{3,2},{4,5},{5,4},{6,7},{7,6},{8,9},{9,8},{10,11... | collective-permute-start | bytes 1769480 | tf_op jit(solution)/shard_map/ppermute | solution.py:344
  51.3 20.9 %collective-permute-start.11 = (bf16[512,512]{1,0:T(8,128)(2,1)S(1)}, bf16[512,512]{1,0:T(8,128)(2,1)S(1)}, u32[]{:S(2)}, u32[]{:S(2)}) collective-permute-start(bf16[512,512]{1,0:T(8,128)(2,1)S(1)} %shard_map.87.late), channel_id=1, source_target_pairs={{0,1},{1,0},{2,3},{3,2},{4,5},{5,4},{6,7},{7,6},{8,9},{9,8},{10,11... | collective-permute-start | bytes 1572872 | tf_op jit(solution)/shard_map/ppermute | solution.py:344
  52.3 9.4 %collective-permute-start.6 = (bf16[256,512]{1,0:T(8,128)(2,1)S(1)}, bf16[256,512]{1,0:T(8,128)(2,1)S(1)}, u32[]{:S(2)}, u32[]{:S(2)}) collective-permute-start(bf16[256,512]{1,0:T(8,128)(2,1)S(1)} %get-tuple-element.32), channel_id=1, source_target_pairs={{0,6},{1,7},{2,0},{3,1},{4,2},{5,3},{6,4},{7,5},{8,14},{9,15},{10,... | collective-permute-start | bytes 786440 | tf_op jit(solution)/shard_map/ppermute | solution.py:338
  55.2 8.0 %collective-permute-start.7 = (bf16[256,512]{1,0:T(8,128)(2,1)S(1)}, bf16[256,512]{1,0:T(8,128)(2,1)S(1)}, u32[]{:S(2)}, u32[]{:S(2)}) collective-permute-start(bf16[256,512]{1,0:T(8,128)(2,1)S(1)} %get-tuple-element.33), channel_id=1, source_target_pairs={{0,4},{1,5},{2,6},{3,7},{4,0},{5,1},{6,2},{7,3},{8,12},{9,13},{10,... | collective-permute-start | bytes 786440 | tf_op jit(solution)/shard_map/ppermute | solution.py:341
  55.2 14.7 %collective-permute-start.8 = (bf16[256,512]{1,0:T(8,128)(2,1)S(1)}, bf16[256,512]{1,0:T(8,128)(2,1)S(1)}, u32[]{:S(2)}, u32[]{:S(2)}) collective-permute-start(bf16[256,512]{1,0:T(8,128)(2,1)S(1)} %get-tuple-element.34), channel_id=1, source_target_pairs={{0,2},{1,3},{2,4},{3,5},{4,6},{5,7},{6,0},{7,1},{8,10},{9,11},{10,... | collective-permute-start | bytes 786440 | tf_op jit(solution)/shard_map/ppermute | solution.py:335
  77.6 6.0 %collective-permute-start.13 = (f32[16,8,128]{2,1,0:T(8,128)S(1)}, f32[16,8,128]{2,1,0:T(8,128)S(1)}, u32[]{:S(2)}, u32[]{:S(2)}) collective-permute-start(f32[16,8,128]{2,1,0:T(8,128)S(1)} %shard_map.92.late.a), channel_id=1, source_target_pairs={{0,16},{8,24},{16,0},{24,8},{32,48},{40,56},{48,32},{56,40},{64,80... | collective-permute-start | bytes 196616 | tf_op jit(solution)/shard_map/ppermute | solution.py:445
  83.6 28.4 %collective-permute-start.14 = (bf16[320,1024]{1,0:T(8,128)(2,1)S(1)}, bf16[320,1024]{1,0:T(8,128)(2,1)S(1)}, u32[]{:S(2)}, u32[]{:S(2)}) collective-permute-start(bf16[320,1024]{1,0:T(8,128)(2,1)S(1)} %get-tuple-element.41), channel_id=1, source_target_pairs={{0,6},{1,7},{2,0},{3,1},{4,2},{5,3},{6,4},{7,5},{8,14},{9,15},{10,... | collective-permute-start | bytes 1966088 | tf_op jit(solution)/shard_map/ppermute | solution.py:338
  84.3 27.7 %collective-permute-start.15 = (bf16[320,1024]{1,0:T(8,128)(2,1)S(1)}, bf16[320,1024]{1,0:T(8,128)(2,1)S(1)}, u32[]{:S(2)}, u32[]{:S(2)}) collective-permute-start(bf16[320,1024]{1,0:T(8,128)(2,1)S(1)} %get-tuple-element.42), channel_id=1, source_target_pairs={{0,4},{1,5},{2,6},{3,7},{4,0},{5,1},{6,2},{7,3},{8,12},{9,13},{10,... | collective-permute-start | bytes 1966088 | tf_op jit(solution)/shard_map/ppermute | solution.py:341
  84.3 32.2 %collective-permute-start.16 = (bf16[320,1024]{1,0:T(8,128)(2,1)S(1)}, bf16[320,1024]{1,0:T(8,128)(2,1)S(1)}, u32[]{:S(2)}, u32[]{:S(2)}) collective-permute-start(bf16[320,1024]{1,0:T(8,128)(2,1)S(1)} %get-tuple-element.43), channel_id=1, source_target_pairs={{0,2},{1,3},{2,4},{3,5},{4,6},{5,7},{6,0},{7,1},{8,10},{9,11},{10,... | collective-permute-start | bytes 1966088 | tf_op jit(solution)/shard_map/ppermute | solution.py:335
  85.2 3.6 %collective-permute-start.17 = (f32[16,8,128]{2,1,0:T(8,128)S(1)}, f32[16,8,128]{2,1,0:T(8,128)S(1)}, u32[]{:S(2)}, u32[]{:S(2)}) collective-permute-start(f32[16,8,128]{2,1,0:T(8,128)S(1)} %get-tuple-element.44.a), channel_id=1, source_target_pairs={{0,32},{8,40},{16,48},{24,56},{32,0},{40,8},{48,16},{56,24},{64,96... | collective-permute-start | bytes 196616 | tf_op jit(solution)/shard_map/ppermute | solution.py:445
  88.8 5.0 %collective-permute-start.18 = (f32[16,8,128]{2,1,0:T(8,128)S(1)}, f32[16,8,128]{2,1,0:T(8,128)S(1)}, u32[]{:S(2)}, u32[]{:S(2)}) collective-permute-start(f32[16,8,128]{2,1,0:T(8,128)S(1)} %shard_map.95.a), channel_id=1, source_target_pairs={{0,64},{8,72},{16,80},{24,88},{32,96},{40,104},{48,112},{56,120},{... | collective-permute-start | bytes 196616 | tf_op jit(solution)/shard_map/ppermute | solution.py:445
  93.8 10.6 %collective-permute-start.19 = (f32[16,8,128]{2,1,0:T(8,128)S(1)}, f32[16,8,128]{2,1,0:T(8,128)S(1)}, u32[]{:S(2)}, u32[]{:S(2)}) collective-permute-start(f32[16,8,128]{2,1,0:T(8,128)S(1)} %shard_map.96.late.a), channel_id=1, source_target_pairs={{0,128},{8,136},{16,144},{24,152},{32,160},{40,168},{48,176},{56,1... | collective-permute-start | bytes 196616 | tf_op jit(solution)/shard_map/ppermute | solution.py:445
  104.4 6.2 %collective-permute-start.22 = (bf16[16,8,128]{2,1,0:T(8,128)(2,1)S(1)}, bf16[16,8,128]{2,1,0:T(8,128)(2,1)S(1)}, u32[]{:S(2)}, u32[]{:S(2)}) collective-permute-start(bf16[16,8,128]{2,1,0:T(8,128)(2,1)S(1)} %shard_map.98.half), channel_id=1, source_target_pairs={{0,9},{1,8},{2,11},{3,10},{4,13},{5,12},{6,15},{7,14},{8,1},{9,0},... | collective-permute-start | bytes 98312 | tf_op jit(solution)/shard_map/ppermute | solution.py:501
  108.5 3.1 %collective-permute-start.21 = (bf16[16,8,128]{2,1,0:T(8,128)(2,1)S(1)}, bf16[16,8,128]{2,1,0:T(8,128)(2,1)S(1)}, u32[]{:S(2)}, u32[]{:S(2)}) collective-permute-start(bf16[16,8,128]{2,1,0:T(8,128)(2,1)S(1)} %shard_map.98.half), channel_id=1, source_target_pairs={{0,1},{1,0},{2,3},{3,2},{4,5},{5,4},{6,7},{7,6},{8,9},{9,8},{10,11... | collective-permute-start | bytes 98312 | tf_op jit(solution)/shard_map/ppermute | solution.py:344
  117.1 9.0 %collective-permute-start.25 = (bf16[2,32,8,128]{3,2,1,0:T(8,128)(2,1)S(1)}, bf16[2,32,8,128]{3,2,1,0:T(8,128)(2,1)S(1)}, u32[]{:S(2)}, u32[]{:S(2)}) collective-permute-start(bf16[2,32,8,128]{3,2,1,0:T(8,128)(2,1)S(1)} %shard_map.99.tot), channel_id=1, source_target_pairs={{0,2},{1,3},{2,4},{3,5},{4,6},{5,7},{6,0},{7,1},{8,10},{9,11},{10,... | collective-permute-start | bytes 393224 | tf_op jit(solution)/shard_map/ppermute | solution.py:335
  117.2 8.9 %collective-permute-start.24 = (bf16[2,32,8,128]{3,2,1,0:T(8,128)(2,1)S(1)}, bf16[2,32,8,128]{3,2,1,0:T(8,128)(2,1)S(1)}, u32[]{:S(2)}, u32[]{:S(2)}) collective-permute-start(bf16[2,32,8,128]{3,2,1,0:T(8,128)(2,1)S(1)} %shard_map.99.tot), channel_id=1, source_target_pairs={{0,4},{1,5},{2,6},{3,7},{4,0},{5,1},{6,2},{7,3},{8,12},{9,13},{10,... | collective-permute-start | bytes 393224 | tf_op jit(solution)/shard_map/ppermute | solution.py:341
  117.6 8.5 %collective-permute-start.23 = (bf16[2,32,8,128]{3,2,1,0:T(8,128)(2,1)S(1)}, bf16[2,32,8,128]{3,2,1,0:T(8,128)(2,1)S(1)}, u32[]{:S(2)}, u32[]{:S(2)}) collective-permute-start(bf16[2,32,8,128]{3,2,1,0:T(8,128)(2,1)S(1)} %shard_map.99.tot), channel_id=1, source_target_pairs={{0,6},{1,7},{2,0},{3,1},{4,2},{5,3},{6,4},{7,5},{8,14},{9,15},{10,... | collective-permute-start | bytes 393224 | tf_op jit(solution)/shard_map/ppermute | solution.py:338
  (10 other events, 83.1 us)

commit v8 on v6

--- a/solution.py
+++ b/solution.py
@@ -94,14 +94,14 @@
     return jnp.concatenate(rows, axis=0).astype(jnp.bfloat16)
 
 
-def pack_first_kernel(where, cot, tok, to_up, to_far, to_down, mine, own_cot, sems):
+def pack_first_kernel(where, cot, tok, to_up, to_down, far, mine, own_cot, sems):
     head = pltpu.make_async_copy(cot.at[:, pl.ds(0, HALF)], own_cot, sems.at[0])
     head.start()
     copies = []
-    for d, out in enumerate((mine, to_up, to_far, to_down)):
+    for d, out in enumerate((mine, to_up, far, to_down)):
         first = pl.multiple_of((((where[0] ^ 1) + 2 * d) & 7) * ROWS, ROWS)
-        if d == 0:
-            copies.append(pltpu.make_async_copy(tok.at[:, pl.ds(first, ROWS)], out, sems.at[1]))
+        if d in (0, 2):
+            copies.append(pltpu.make_async_copy(tok.at[:, pl.ds(first, ROWS)], out, sems.at[2 * d + 1]))
             continue
         for h in range(2):
             source = tok.at[:, pl.ds(first + h * TOK, TOK)]
@@ -111,28 +111,32 @@
         copy.start()
     head.wait()
     turned = own_cot[...].T
-    for out in (to_up, to_far, to_down):
+    for out in (to_up, to_down):
         out[:, :TOK] = turned
     for copy in copies:
         copy.wait()
 
 
-def pack_second_kernel(where, cot, t0, t1, t2, t3, late_lo, late_hi, turned, mine, to_up, to_far, to_down):
+def pack_second_kernel(first, cot, late, relay, turned):
+    relay[...] = cot_of(first)
     turned[...] = cot[...].T
+
+
+def pack_own_kernel(where, t0, t1, t2, t3, late_lo, late_hi, mine, to_up, to_far, to_down):
     for out, t in ((mine, t0), (to_up, t1), (to_far, t2), (to_down, t3)):
         out[...] = t[...]
 
 
-def partial_first_kernel(sent, hi, far, lo, t0, idx, early, turned, out):
-    cots = (cot_of(sent), cot_of(hi), cot_of(far), cot_of(lo))
-    toks = (t0[...], tok_of(hi), tok_of(far), tok_of(lo))
+def partial_first_kernel(sent, hi, far, lo, t0, t2, idx, early, turned, out):
+    cots = (cot_of(sent), cot_of(hi), far[...], cot_of(lo))
+    toks = (t0[...], tok_of(hi), t2[...], tok_of(lo))
     out[:HALF, :] = four_products(cots, toks).astype(out.dtype)
     out[HALF:, :] = flat_index(idx)
 
 
-def partial_second_kernel(c0, c1, c2, c3, t0, hi, far, lo, out):
+def partial_second_kernel(c0, c1, c2, c3, t0, hi, t2, lo, out):
     cots = (c0[...], c1[...], c2[...], c3[...])
-    toks = (t0[...], tok_of(hi), tok_of(far), tok_of(lo))
+    toks = (t0[...], tok_of(hi), t2[...], tok_of(lo))
     out[...] = four_products(cots, toks).astype(out.dtype)
 
 
@@ -142,7 +146,7 @@
 
     @pl.when(step < STEPS // 2)
     def _():
-        cots = (cot_of(a0), cot_of(a1), cot_of(a2), cot_of(a3))
+        cots = (cot_of(a0), cot_of(a1), a2[...], cot_of(a3))
         out[...] = four_products(cots, toks) + beta_decay * mom[...].T
 
     @pl.when(step >= STEPS // 2)
@@ -188,10 +192,6 @@
     out[...] = (a[...] + b[...]).astype(out.dtype)
 
 
-def add_four_kernel(a, b, c, d, out):
-    out[...] = (a[...] + b[...]) + (c[...] + d[...])
-
-
 def pair_kernel(where, half, core, across, corner, late_0, late_1, late_2, out):
     side, mine = where[0] & 1, (where[1] & 1) * (TILES // 2)
     other = TILES // 2 - mine
@@ -217,7 +217,7 @@
     mine, theirs = flat_index(idx), got_a[HALF:, :]
     first = (where[0] & 1) == 0
     left, right = jnp.where(first, mine, theirs), jnp.where(first, theirs, mine)
-    peers = (p0[...], tok_of(p1), tok_of(p2), tok_of(p3))
+    peers = (p0[...], tok_of(p1), p2[...], tok_of(p3))
     for own, peer, out in zip((o0, o1, o2, o3), peers, outs):
         total = jnp.dot(own[...], w_own[...], preferred_element_type=jnp.float32)
         total += jnp.dot(peer, w_peer[...], preferred_element_type=jnp.float32)
@@ -248,25 +248,28 @@
     for g in range(STEPS):
         expand_group(g, pairs, values, dense)
         span = slice(g * GROUP, (g + 1) * GROUP)
-        mixed[span, :] = mix(dense[span, :], tok[...], ((1,), (1,)))
         turned = dense[span, cols].T
         delta = mix(turned, ch[...], ((1,), (0,))) + mix(turned, cl[...], ((1,), (0,)))
         new = weight[:, span].astype(jnp.float32) - (step_rate / REPS) * delta
         out_weight[:, span] = new.astype(out_weight.dtype)
+    mixed[...] = mix(dense[...], tok[...], ((1,), (1,)))
 
 
 def forward_kernel(where, tok_1, tok_2, tok_3, own, hi, far, lo, tot_1, tot_2, tot_3, mixed, ch, cl, out, *scratch):
-    toks, dense, pairs, values = (tok_1, tok_2, tok_3), scratch[:3], scratch[3:6], scratch[6:]
+    toks, dense, pairs, values = (tok_1, tok_2, tok_3), scratch[:3], scratch[3:6], scratch[6:9]
+    total = scratch[9]
     for near, pair, tot, value in zip((hi, far, lo), pairs, (tot_1, tot_2, tot_3), values):
         pair[...] = near[TOK:, :].astype(jnp.float32)
         value[...] = tot[...].astype(jnp.float32)
+    before = mixed
+    for tok, pair, value, buffer in zip(toks, pairs, values, dense):
+        for g in range(STEPS):
+            expand_group(g, pair, value, buffer)
+        total[...] = before[...] + mix(buffer[...], tok[...], ((1,), (1,)))
+        before = total
     for g in range(STEPS):
         span = slice(g * GROUP, (g + 1) * GROUP)
-        total = mixed[span, :]
-        for tok, pair, value, buffer in zip(toks, pairs, values, dense):
-            expand_group(g, pair, value, buffer)
-            total += mix(buffer[span, :], tok[...], ((1,), (1,)))
-        delta = three_pass(split_pair(total.T), (ch[...], cl[...]), ((1,), (0,)))
+        delta = three_pass(split_pair(total[span, :].T), (ch[...], cl[...]), ((1,), (0,)))
         base = own[:TOK, span].astype(jnp.float32) + hi[:TOK, span].astype(jnp.float32)
         base += far[:TOK, span].astype(jnp.float32) + lo[:TOK, span].astype(jnp.float32)
         out[:, span] = (base - (step_rate / REPS) * delta).astype(out.dtype)
@@ -341,65 +344,78 @@
 
     weight_peer = swap(weight)
 
-    first_up, first_far, first_down, peer_0 = pl.pallas_call(
+    first_up, first_down, far_send, peer_0 = pl.pallas_call(
         pack_first_kernel,
         grid_spec=pltpu.PrefetchScalarGridSpec(
             num_scalar_prefetch=1,
             grid=(1,),
             in_specs=[pl.BlockSpec(memory_space=pltpu.HBM)] * 2,
-            out_specs=[MESSAGE] * 3 + [PIECE],
+            out_specs=[MESSAGE] * 2 + [PIECE] * 2,
             scratch_shapes=[pltpu.VMEM((TOK, HALF), BF16), pltpu.SemaphoreType.DMA((8,))],
         ),
-        out_shape=[shape(HALF, 2 * TOK)] * 3 + [shape(TOK, ROWS)],
+        out_shape=[shape(HALF, 2 * TOK)] * 2 + [shape(TOK, ROWS)] * 2,
         compiler_params=params(),
         cost_estimate=cost(0, 4),
     )(place, cotangent, tokens)
     first_lo = up(first_up)
     first_hi = down(first_down)
-    first_x = across(first_far)
-    firsts = (first_up, first_hi, first_x, first_lo)
-
-    cot_b, own_0, own_up, own_across, own_down = pl.pallas_call(
+    peer_far = across(far_send)
+
+    relay, cot_b = pl.pallas_call(
         pack_second_kernel,
-        grid_spec=pltpu.PrefetchScalarGridSpec(
-            num_scalar_prefetch=1,
-            grid=(1,),
-            in_specs=[pl.BlockSpec((TOK, HALF), lambda c, *_: (0, 1))] + columns(0) + [AFTER, AFTER],
-            out_specs=[whole(HALF, TOK)] + [PIECE] * 4,
-        ),
-        out_shape=[shape(HALF, TOK)] + [shape(TOK, ROWS)] * 4,
-        compiler_params=params(),
-        cost_estimate=cost(0, 3),
-    )(place, cotangent, tokens, tokens, tokens, tokens, first_lo, first_hi)
-    b_lo, b_hi, b_far = up(cot_b), down(cot_b), across(cot_b)
+        grid=(1,),
+        in_specs=[MESSAGE, pl.BlockSpec((TOK, HALF), lambda c: (0, 1)), AFTER],
+        out_specs=[whole(HALF, TOK)] * 2,
+        out_shape=[shape(HALF, TOK)] * 2,
+        compiler_params=params(),
+        cost_estimate=cost(0, 1),
+    )(first_lo, cotangent, first_hi)
+    a_far = up(relay)
+    b_lo, b_hi = up(cot_b), down(cot_b)
+    b_far = down(b_hi)
+    firsts = (first_up, first_hi, a_far, first_lo)
     cots_b = (cot_b, b_hi, b_far, b_lo)
+
+    own_0, own_up, own_across, own_down = pl.pallas_call(
+        pack_own_kernel,
+        grid_spec=pltpu.PrefetchScalarGridSpec(
+            num_scalar_prefetch=1,
+            grid=(1,),
+            in_specs=columns(0) + [AFTER, AFTER],
+            out_specs=[PIECE] * 4,
+        ),
+        out_shape=[shape(TOK, ROWS)] * 4,
+        compiler_params=params(),
+        cost_estimate=cost(0, 2),
+    )(place, tokens, tokens, tokens, tokens, b_lo, b_hi)
     owns = (own_0, down(own_down), across(own_across), up(own_up))
 
     partial_a = pl.pallas_call(
         partial_first_kernel,
         grid=(1,),
-        in_specs=[MESSAGE] * 4 + [PIECE, INDEX, AFTER, AFTER],
+        in_specs=[MESSAGE] * 2 + [whole(HALF, TOK), MESSAGE, PIECE, PIECE, INDEX, AFTER, AFTER],
         out_specs=whole(HALF + PICKS, ROWS),
         out_shape=shape(HALF + PICKS, ROWS),
         compiler_params=params(),
         cost_estimate=cost(KV * KV * ROWS, 3),
-    )(*firsts, peer_0, index_t, weight_peer, cot_b)
+    )(*firsts, peer_0, peer_far, index_t, weight_peer, cot_b)
     got_a = swap(partial_a)
     partial_b = pl.pallas_call(
         partial_second_kernel,
         grid=(1,),
-        in_specs=[whole(HALF, TOK)] * 4 + [PIECE] + [MESSAGE] * 3,
+        in_specs=[whole(HALF, TOK)] * 4 + [PIECE, MESSAGE, PIECE, MESSAGE],
         out_specs=whole(HALF, ROWS),
         out_shape=shape(HALF, ROWS),
         compiler_params=params(),
         cost_estimate=cost(KV * KV * ROWS, 3),
-    )(*cots_b, peer_0, *firsts[1:])
+    )(*cots_b, peer_0, first_hi, peer_far, first_lo)
     got_b = swap(partial_b)
 
     pre = pl.pallas_call(
         own_kernel,
         grid=(STEPS,),
-        in_specs=[first_half(GROUP, 2 * TOK)] * 4
+        in_specs=[first_half(GROUP, 2 * TOK)] * 2
+        + [first_half(GROUP, TOK), first_half(GROUP, 2 * TOK)]
         + [second_half(GROUP, TOK)] * 4
         + [PIECE] * 4
         + [by_col(ROWS, GROUP)],
@@ -415,7 +431,7 @@
             num_scalar_prefetch=1,
             grid=(1,),
             in_specs=[PIECE] * 5
-            + [MESSAGE] * 3
+            + [MESSAGE, PIECE, MESSAGE]
             + [whole(ROWS, KV)] * 2
             + [INDEX, whole(HALF + PICKS, ROWS)],
             out_specs=[whole(TOK + PICKS, KV)] * 4,
@@ -423,7 +439,7 @@
         out_shape=[shape(TOK + PICKS, KV)] * 4,
         compiler_params=params(2 * VMEM_LIMIT),
         cost_estimate=cost(4 * KV * KV * ROWS, 7),
-    )(place, *owns, peer_0, *firsts[1:], weight, weight_peer, index_t, got_a)
+    )(place, *owns, peer_0, first_hi, peer_far, first_lo, weight, weight_peer, index_t, got_a)
     base_lo, base_hi, base_far = up(base_up), down(base_down), across(base_across)
 
     halves = whole(TILES // 2, 8, LANES)
@@ -457,7 +473,8 @@
 
     value = add(add_two_kernel, half_shape, keep, partner(send, 1))
     value = add(add_two_kernel, half_shape, value, partner(value, 2))
-    value = add(add_four_kernel, half_shape, value, partner(value, 4), partner(value, 8), partner(value, 12))
+    value = add(add_two_kernel, half_shape, value, partner(value, 4))
+    value = add(add_two_kernel, half_shape, value, partner(value, 8))
     last = partner(value, 16)
     new_momentum, mark = pl.pallas_call(
         residual_kernel,
@@ -514,7 +531,7 @@
             + [whole(KV, TOK)]
             + BASIS,
             out_specs=whole(TOK, KV),
-            scratch_shapes=[DENSE] * 3 + [PAIRS] * 3 + [VALUES] * 3,
+            scratch_shapes=[DENSE] * 3 + [PAIRS] * 3 + [VALUES] * 3 + [pltpu.VMEM((KV, TOK), F32)],
         ),
         out_shape=shape(TOK, KV),
         compiler_params=params(2 * VMEM_LIMIT),

time: 127 us -> 136 us (1.071)
  starting transfers between devices: 53 us -> 63.4 us
    ppermute x5 -> x6, waiting for transfers between devices: 0.63 us -> 14.7 us  [down(): return lax.ppermute(x, 'fsdp', [(i, (i + 6) % 8) for i in range(8)])]
    ppermute x5 -> x4, waiting for transfers between devices: 13.6 us -> 1.96 us  [across(): return lax.ppermute(x, 'fsdp', [(i, (i + 4) % 8) for i in range(8)])]
    ppermute x7 -> x6, starting transfers between devices: 24.4 us -> 33.6 us  [partner(): return lax.ppermute(x, 'rep', [(i, i ^ bits) for i in range(REPS)])]
    ppermute x5 -> x6, waiting for transfers between devices: 22.8 us -> 16.4 us  [up(): return lax.ppermute(x, 'fsdp', [(i, (i + 2) % 8) for i in range(8)])]
    ppermute x1, starting transfers between devices: 1.07 us -> 6.96 us  [body(): lax.ppermute(half, ('rep', 'fsdp'), [(i, i ^ 9) for i in range(REPS * 8)])]
    ppermute x5 -> x4, starting transfers between devices: 7.49 us -> 4.38 us  [across(): return lax.ppermute(x, 'fsdp', [(i, (i + 4) % 8) for i in range(8)])]
    ppermute x5 -> x6, starting transfers between devices: 9.15 us -> 11.8 us  [down(): return lax.ppermute(x, 'fsdp', [(i, (i + 6) % 8) for i in range(8)])]
    ppermute x5 -> x6, starting transfers between devices: 5.6 us -> 3.29 us  [up(): return lax.ppermute(x, 'fsdp', [(i, (i + 2) % 8) for i in range(8)])]
  transfers between devices with their start and end apart: 27 -> 27, of which waited for: 13 -> 14; matrix products, arithmetic and copies ran while one was open for 0% -> 0% of each run, Pallas kernels for 15% -> 14%
where the time goes in v8:
time: 136 us
  starting transfers between devices  63.4 us (47%)
  waiting for transfers between devices  43.1 us (32%)
  Pallas kernels  25.5 us (19%)
  local copies, waits for them, and re-layouts  2.66 us (2%)
    ppermute x6, starting transfers between devices, partner(): return lax.ppermute(x, 'rep', [(i, i ^ bits) for i in range(REPS)])  33.6 us
    ppermute x6, waiting for transfers between devices, up(): return lax.ppermute(x, 'fsdp', [(i, (i + 2) % 8) for i in range(8)])  16.4 us
    ppermute x6, waiting for transfers between devices, down(): return lax.ppermute(x, 'fsdp', [(i, (i + 6) % 8) for i in range(8)])  14.7 us
    ppermute x6, starting transfers between devices, down(): return lax.ppermute(x, 'fsdp', [(i, (i + 6) % 8) for i in range(8)])  11.8 us
    ppermute x6, waiting for transfers between devices, partner(): return lax.ppermute(x, 'rep', [(i, i ^ bits) for i in range(REPS)])  7.21 us
    ppermute x1, starting transfers between devices, body(): lax.ppermute(half, ('rep', 'fsdp'), [(i, i ^ 9) for i in range(REPS * 8)])  6.96 us
    pallas_call x1, Pallas kernels, body(): pl.pallas_call(forward_kernel, grid_spec=pltpu.PrefetchScalarGridSpec(num...  6 us
    ppermute x4, starting transfers between devices, across(): return lax.ppermute(x, 'fsdp', [(i, (i + 4) % 8) for i in range(8)])  4.38 us
  transfers between devices with their start and end apart: 27, of which 14 were waited for; matrix products, arithmetic and copies ran while one was open for 0% of the time, Pallas kernels for 14%

profile of v8, /device:TPU:1, one launch (start us, length us, event | category | flops | bytes accessed | tf_op | source)
XLA Modules:
  0.0 135.5 jit_solution(11398194220462106918)
XLA Ops:
  0.6 2.1 %collective-permute-start.8 = (bf16[512,1024]{1,0:T(8,128)(2,1)}, bf16[512,1024]{1,0:T(8,128)(2,1)S(1)}, u32[]{:S(2)}, u32[]{:S(2)}) collective-permute-start(bf16[512,1024]{1,0:T(8,128)(2,1)} %weight.1), channel_id=1, source_target_pairs={{0,1},{1,0},{2,3},{3,2},{4,5},{5,4},{6,7},{7,6},{8,9},{9,8},{10,11... | collective-permute-start | bytes 3145736 | tf_op jit(solution)/shard_map/ppermute | solution.py:340
  6.4 2.8 %collective-permute-start.1 = (bf16[512,512]{1,0:T(8,128)(2,1)S(1)}, bf16[512,512]{1,0:T(8,128)(2,1)S(1)}, u32[]{:S(2)}, u32[]{:S(2)}) collective-permute-start(bf16[512,512]{1,0:T(8,128)(2,1)S(1)} %get-tuple-element.26), channel_id=1, source_target_pairs={{0,6},{1,7},{2,0},{3,1},{4,2},{5,3},{6,4},{7,5},{8,14},{9,15},{10,... | collective-permute-start | bytes 1572872 | tf_op jit(solution)/shard_map/ppermute | solution.py:334
  10.8 10.0 %collective-permute-done.1.late.hi.p1.a1 = bf16[512,512]{1,0:T(8,128)(2,1)S(1)} collective-permute-done((bf16[512,512]{1,0:T(8,128)(2,1)S(1)}, bf16[512,512]{1,0:T(8,128)(2,1)S(1)}, u32[]{:S(2)}, u32[]{:S(2)}) %collective-permute-start.1) | collective-permute-done | bytes 524320 | tf_op jit(solution)/shard_map/ppermute | solution.py:334
  20.8 2.8 %collective-permute-done.first.lo.p3.a3 = bf16[512,512]{1,0:T(8,128)(2,1)S(1)} collective-permute-done((bf16[512,512]{1,0:T(8,128)(2,1)S(1)}, bf16[512,512]{1,0:T(8,128)(2,1)S(1)}, u32[]{:S(2)}, u32[]{:S(2)}) %collective-permute-start) | collective-permute-done | bytes 524320 | tf_op jit(solution)/shard_map/ppermute | solution.py:331
  23.8 2.7 %collective-permute-start.3 = (bf16[512,256]{1,0:T(8,128)(2,1)S(1)}, bf16[512,256]{1,0:T(8,128)(2,1)S(1)}, u32[]{:S(2)}, u32[]{:S(2)}) collective-permute-start(bf16[512,256]{1,0:T(8,128)(2,1)S(1)} %get-tuple-element.27.turned.b0.c0), channel_id=1, source_target_pairs={{0,6},{1,7},{2,0},{3,1},{4,2},{5,3},{6,4},{7,5},{8,14},{9,15},{10,... | collective-permute-start | bytes 786440 | tf_op jit(solution)/shard_map/ppermute | solution.py:334
  27.2 5.3 %collective-permute-done.9.far.a2 = bf16[512,256]{1,0:T(8,128)(2,1)S(1)} collective-permute-done((bf16[512,256]{1,0:T(8,128)(2,1)S(1)}, bf16[512,256]{1,0:T(8,128)(2,1)S(1)}, u32[]{:S(2)}, u32[]{:S(2)}) %collective-permute-start.9) | collective-permute-done | bytes 262176 | tf_op jit(solution)/shard_map/ppermute | solution.py:331
  33.5 2.7 %collective-permute-start.14 = (bf16[512,256]{1,0:T(8,128)(2,1)S(1)}, bf16[512,256]{1,0:T(8,128)(2,1)S(1)}, u32[]{:S(2)}, u32[]{:S(2)}) collective-permute-start(bf16[512,256]{1,0:T(8,128)(2,1)S(1)} %collective-permute-done.3.late_hi.b1.c1), channel_id=1, source_target_pairs={{0,6},{1,7},{2,0},{3,1},{4,2},{5,3},{6,4},{7,5},{8,14},{9,15},{10,... | collective-permute-start | bytes 786440 | tf_op jit(solution)/shard_map/ppermute | solution.py:334
  36.2 4.8 %collective-permute-done.2.late_lo.b3.c3 = bf16[512,256]{1,0:T(8,128)(2,1)S(1)} collective-permute-done((bf16[512,256]{1,0:T(8,128)(2,1)S(1)}, bf16[512,256]{1,0:T(8,128)(2,1)S(1)}, u32[]{:S(2)}, u32[]{:S(2)}) %collective-permute-start.2) | collective-permute-done | bytes 262176 | tf_op jit(solution)/shard_map/ppermute | solution.py:331
  44.9 4.7 %collective-permute-done.4.o1.t1 = bf16[256,512]{1,0:T(8,128)(2,1)S(1)} collective-permute-done((bf16[256,512]{1,0:T(8,128)(2,1)S(1)}, bf16[256,512]{1,0:T(8,128)(2,1)S(1)}, u32[]{:S(2)}, u32[]{:S(2)}) %collective-permute-start.4) | collective-permute-done | bytes 262176 | tf_op jit(solution)/shard_map/ppermute | solution.py:334
  49.6 3.6 %collective-permute-done.6.o3.t3 = bf16[256,512]{1,0:T(8,128)(2,1)S(1)} collective-permute-done((bf16[256,512]{1,0:T(8,128)(2,1)S(1)}, bf16[256,512]{1,0:T(8,128)(2,1)S(1)}, u32[]{:S(2)}, u32[]{:S(2)}) %collective-permute-start.6) | collective-permute-done | bytes 262176 | tf_op jit(solution)/shard_map/ppermute | solution.py:331
  53.2 3.1 %shard_map.89 = (bf16[320,1024]{1,0:T(8,128)(2,1)S(1)}, bf16[320,1024]{1,0:T(8,128)(2,1)S(1)}, bf16[320,1024]{1,0:T(8,128)(2,1)S(1)}, bf16[320,1024]{1,0:T(8,128)(2,1)S(1)}) custom-call(s32[2]{0:T(128)S(1)} %pad_add_fusion.where, bf16[256,512]{1,0:T(8,128)(2,1)S(1)} %get-tuple-element.28.o0.t0, bf16[256,512]{1,0:T(8,128)(2,1)S(1)} %collective-permute-done.4.o1.t1, ...), custom_call_target="tpu_custom_call" | custom-call | flops 2147483648 | bytes 7340032 | tf_op jit(solution)/shard_map/pallas_call | solution.py:428
  58.3 2.3 %shard_map.90.pre = f32[1024,512]{1,0:T(8,128)S(1)} custom-call(bf16[512,512]{1,0:T(8,128)(2,1)S(1)} %get-tuple-element.25.sent.a0, bf16[512,512]{1,0:T(8,128)(2,1)S(1)} %collective-permute-done.1.late.hi.p1.a1, bf16[512,256]{1,0:T(8,128)(2,1)S(1)} %collective-permute-done.9.far.a2, bf16[512,512]{1,0:T(8,128)(2,1)S(1)} %collective-permute-done.first.lo.p3.a3, ...), custom_call_target="tpu_custom_call" | custom-call | flops 1073741824 | bytes 7340032 | tf_op jit(solution)/shard_map/pallas_call | solution.py:414
  60.7 3.5 %shard_map.92 = (f32[1024,512]{1,0:T(8,128)S(1)}, f32[64,512]{1,0:T(8,128)S(1)}, f32[16,8,128]{2,1,0:T(8,128)S(1)}, f32[16,8,128]{2,1,0:T(8,128)S(1)}) custom-call(s32[2]{0:T(128)S(1)} %pad_add_fusion.where, f32[1024,512]{1,0:T(8,128)S(1)} %shard_map.90.pre, bf16[576,512]{1,0:T(8,128)(2,1)S(1)} %collective-permute-done.10.got_a, ...), custom_call_target="tpu_custom_call" | custom-call | flops 805306368 | bytes 6291456 | tf_op jit(solution)/shard_map/pallas_call | solution.py:447
  64.2 20.2 %collective-permute-start.16 = (f32[16,8,128]{2,1,0:T(8,128)S(1)}, f32[16,8,128]{2,1,0:T(8,128)S(1)}, u32[]{:S(2)}, u32[]{:S(2)}) collective-permute-start(f32[16,8,128]{2,1,0:T(8,128)S(1)} %get-tuple-element.40), channel_id=1, source_target_pairs={{0,8},{8,0},{16,24},{24,16},{32,40},{40,32},{48,56},{56,48},{64,72... | collective-permute-start | bytes 196616 | tf_op jit(solution)/shard_map/ppermute | solution.py:461
  85.3 2.3 %collective-permute-start.17 = (f32[16,8,128]{2,1,0:T(8,128)S(1)}, f32[16,8,128]{2,1,0:T(8,128)S(1)}, u32[]{:S(2)}, u32[]{:S(2)}) collective-permute-start(f32[16,8,128]{2,1,0:T(8,128)S(1)} %shard_map.93.a), channel_id=1, source_target_pairs={{0,16},{8,24},{16,0},{24,8},{32,48},{40,56},{48,32},{56,40},{64,80... | collective-permute-start | bytes 196616 | tf_op jit(solution)/shard_map/ppermute | solution.py:461
  87.6 2.4 %collective-permute-done.17.b = f32[16,8,128]{2,1,0:T(8,128)S(1)} collective-permute-done((f32[16,8,128]{2,1,0:T(8,128)S(1)}, f32[16,8,128]{2,1,0:T(8,128)S(1)}, u32[]{:S(2)}, u32[]{:S(2)}) %collective-permute-start.17) | collective-permute-done | bytes 65568 | tf_op jit(solution)/shard_map/ppermute | solution.py:461
  91.3 2.2 %collective-permute-done.18.b = f32[16,8,128]{2,1,0:T(8,128)S(1)} collective-permute-done((f32[16,8,128]{2,1,0:T(8,128)S(1)}, f32[16,8,128]{2,1,0:T(8,128)S(1)}, u32[]{:S(2)}, u32[]{:S(2)}) %collective-permute-start.18) | collective-permute-done | bytes 65568 | tf_op jit(solution)/shard_map/ppermute | solution.py:461
  93.5 2.8 %collective-permute-start.19 = (f32[16,8,128]{2,1,0:T(8,128)S(1)}, f32[16,8,128]{2,1,0:T(8,128)S(1)}, u32[]{:S(2)}, u32[]{:S(2)}) collective-permute-start(f32[16,8,128]{2,1,0:T(8,128)S(1)} %shard_map.95.a), channel_id=1, source_target_pairs={{0,64},{8,72},{16,80},{24,88},{32,96},{40,104},{48,112},{56,120},{... | collective-permute-start | bytes 196616 | tf_op jit(solution)/shard_map/ppermute | solution.py:461
  98.0 6.9 %collective-permute-start.20 = (f32[16,8,128]{2,1,0:T(8,128)S(1)}, f32[16,8,128]{2,1,0:T(8,128)S(1)}, u32[]{:S(2)}, u32[]{:S(2)}) collective-permute-start(f32[16,8,128]{2,1,0:T(8,128)S(1)} %shard_map.96.late.a), channel_id=1, source_target_pairs={{0,128},{8,136},{16,144},{24,152},{32,160},{40,168},{48,176},{56,1... | collective-permute-start | bytes 196616 | tf_op jit(solution)/shard_map/ppermute | solution.py:461
  104.9 3.7 %shard_map.97 = (f32[512,1024]{1,0:T(8,128)}, f32[8,128]{1,0:T(8,128)S(1)}) custom-call(f32[1024,512]{1,0:T(8,128)S(1)} %get-tuple-element.41.moment, f32[64,512]{1,0:T(8,128)S(1)} %get-tuple-element.42.picked, s32[16,4,512]{2,1,0:T(4,128)S(1)} %bitcast.9, bf16[256,256]{1,0:T(8,128)(2,1)S(1)} %copy-done.6, bf16[256,256]{1,0:T(8,128)(2,1)S(1)} %copy-done.5, ...), custom_call_target="tpu_custom_call" | custom-call | flops 805306368 | bytes 5242880 | tf_op jit(solution)/shard_map/pallas_call | solution.py:479
  108.7 7.0 %collective-permute-start.23 = (bf16[16,8,128]{2,1,0:T(8,128)(2,1)S(1)}, bf16[16,8,128]{2,1,0:T(8,128)(2,1)S(1)}, u32[]{:S(2)}, u32[]{:S(2)}) collective-permute-start(bf16[16,8,128]{2,1,0:T(8,128)(2,1)S(1)} %shard_map.98.half), channel_id=1, source_target_pairs={{0,9},{1,8},{2,11},{3,10},{4,13},{5,12},{6,15},{7,14},{8,1},{9,0},... | collective-permute-start | bytes 98312 | tf_op jit(solution)/shard_map/ppermute | solution.py:490
  120.4 2.7 %collective-permute-start.25 = (bf16[2,32,8,128]{3,2,1,0:T(8,128)(2,1)S(1)}, bf16[2,32,8,128]{3,2,1,0:T(8,128)(2,1)S(1)}, u32[]{:S(2)}, u32[]{:S(2)}) collective-permute-start(bf16[2,32,8,128]{3,2,1,0:T(8,128)(2,1)S(1)} %shard_map.99.tot), channel_id=1, source_target_pairs={{0,4},{1,5},{2,6},{3,7},{4,0},{5,1},{6,2},{7,3},{8,12},{9,13},{10,... | collective-permute-start | bytes 393224 | tf_op jit(solution)/shard_map/ppermute | solution.py:337
  125.0 3.3 %shard_map.100 = (f32[1024,256]{1,0:T(8,128)S(1)}, bf16[512,1024]{1,0:T(8,128)(2,1)}) custom-call(s32[2]{0:T(128)S(1)} %pad_add_fusion.where, bf16[256,4096]{1,0:T(8,128)(2,1)S(1)} %copy-done.1, bf16[320,1024]{1,0:T(8,128)(2,1)S(1)} %get-tuple-element.35.late.own, bf16[2,32,8,128]{3,2,1,0:T(8,128)(2,1)S(1)} %shard_map.99.tot, ...), custom_call_target="tpu_custom_call" | custom-call | flops 1610612736 | bytes 4194304 | tf_op jit(solution)/shard_map/pallas_call | solution.py:509
  129.5 6.0 %shard_map.101 = bf16[256,1024]{1,0:T(8,128)(2,1)} custom-call(s32[2]{0:T(128)S(1)} %pad_add_fusion.where, bf16[256,4096]{1,0:T(8,128)(2,1)S(1)} %copy-done.1, bf16[256,4096]{1,0:T(8,128)(2,1)S(1)} %copy-done.1, bf16[256,4096]{1,0:T(8,128)(2,1)S(1)} %copy-done.1, bf16[320,1024]{1,0:T(8,128)(2,1)S(1)} %get-tuple-element.35.late.own, ...), custom_call_target="tpu_custom_call" | custom-call | flops 3221225472 | bytes 7340032 | tf_op jit(solution)/shard_map/pallas_call | solution.py:523
  (64 shorter events, 25.0 us)
Async XLA Ops:
  0.6 31.8 %collective-permute-start.8 = (bf16[512,1024]{1,0:T(8,128)(2,1)}, bf16[512,1024]{1,0:T(8,128)(2,1)S(1)}, u32[]{:S(2)}, u32[]{:S(2)}) collective-permute-start(bf16[512,1024]{1,0:T(8,128)(2,1)} %weight.1), channel_id=1, source_target_pairs={{0,1},{1,0},{2,3},{3,2},{4,5},{5,4},{6,7},{7,6},{8,9},{9,8},{10,11... | collective-permute-start | bytes 3145736 | tf_op jit(solution)/shard_map/ppermute | solution.py:340
  6.4 14.4 %collective-permute-start.1 = (bf16[512,512]{1,0:T(8,128)(2,1)S(1)}, bf16[512,512]{1,0:T(8,128)(2,1)S(1)}, u32[]{:S(2)}, u32[]{:S(2)}) collective-permute-start(bf16[512,512]{1,0:T(8,128)(2,1)S(1)} %get-tuple-element.26), channel_id=1, source_target_pairs={{0,6},{1,7},{2,0},{3,1},{4,2},{5,3},{6,4},{7,5},{8,14},{9,15},{10,... | collective-permute-start | bytes 1572872 | tf_op jit(solution)/shard_map/ppermute | solution.py:334
  9.2 14.4 %collective-permute-start = (bf16[512,512]{1,0:T(8,128)(2,1)S(1)}, bf16[512,512]{1,0:T(8,128)(2,1)S(1)}, u32[]{:S(2)}, u32[]{:S(2)}) collective-permute-start(bf16[512,512]{1,0:T(8,128)(2,1)S(1)} %get-tuple-element.25.sent.a0), channel_id=1, source_target_pairs={{0,2},{1,3},{2,4},{3,5},{4,6},{5,7},{6,0},{7,1},{8,10},{9,11},{10,... | collective-permute-start | bytes 1572872 | tf_op jit(solution)/shard_map/ppermute | solution.py:331
  9.2 18.0 %collective-permute-start.7 = (bf16[256,512]{1,0:T(8,128)(2,1)S(1)}, bf16[256,512]{1,0:T(8,128)(2,1)S(1)}, u32[]{:S(2)}, u32[]{:S(2)}) collective-permute-start(bf16[256,512]{1,0:T(8,128)(2,1)S(1)} %get-tuple-element.33), channel_id=1, source_target_pairs={{0,4},{1,5},{2,6},{3,7},{4,0},{5,1},{6,2},{7,3},{8,12},{9,13},{10,... | collective-permute-start | bytes 786440 | tf_op jit(solution)/shard_map/ppermute | solution.py:337
  23.7 8.8 %collective-permute-start.9 = (bf16[512,256]{1,0:T(8,128)(2,1)S(1)}, bf16[512,256]{1,0:T(8,128)(2,1)S(1)}, u32[]{:S(2)}, u32[]{:S(2)}) collective-permute-start(bf16[512,256]{1,0:T(8,128)(2,1)S(1)} %get-tuple-element.34), channel_id=1, source_target_pairs={{0,2},{1,3},{2,4},{3,5},{4,6},{5,7},{6,0},{7,1},{8,10},{9,11},{10,... | collective-permute-start | bytes 786440 | tf_op jit(solution)/shard_map/ppermute | solution.py:331
  23.8 9.7 %collective-permute-start.3 = (bf16[512,256]{1,0:T(8,128)(2,1)S(1)}, bf16[512,256]{1,0:T(8,128)(2,1)S(1)}, u32[]{:S(2)}, u32[]{:S(2)}) collective-permute-start(bf16[512,256]{1,0:T(8,128)(2,1)S(1)} %get-tuple-element.27.turned.b0.c0), channel_id=1, source_target_pairs={{0,6},{1,7},{2,0},{3,1},{4,2},{5,3},{6,4},{7,5},{8,14},{9,15},{10,... | collective-permute-start | bytes 786440 | tf_op jit(solution)/shard_map/ppermute | solution.py:334
  33.2 20.0 %collective-permute-start.10 = (bf16[576,512]{1,0:T(8,128)(2,1)S(1)}, bf16[576,512]{1,0:T(8,128)(2,1)S(1)}, u32[]{:S(2)}, u32[]{:S(2)}) collective-permute-start(bf16[576,512]{1,0:T(8,128)(2,1)S(1)} %shard_map.88), channel_id=1, source_target_pairs={{0,1},{1,0},{2,3},{3,2},{4,5},{5,4},{6,7},{7,6},{8,9},{9,8},{10,11... | collective-permute-start | bytes 1769480 | tf_op jit(solution)/shard_map/ppermute | solution.py:340
  33.5 7.4 %collective-permute-start.2 = (bf16[512,256]{1,0:T(8,128)(2,1)S(1)}, bf16[512,256]{1,0:T(8,128)(2,1)S(1)}, u32[]{:S(2)}, u32[]{:S(2)}) collective-permute-start(bf16[512,256]{1,0:T(8,128)(2,1)S(1)} %get-tuple-element.27.turned.b0.c0), channel_id=1, source_target_pairs={{0,2},{1,3},{2,4},{3,5},{4,6},{5,7},{6,0},{7,1},{8,10},{9,11},{10,... | collective-permute-start | bytes 786440 | tf_op jit(solution)/shard_map/ppermute | solution.py:331
  33.5 9.6 %collective-permute-start.14 = (bf16[512,256]{1,0:T(8,128)(2,1)S(1)}, bf16[512,256]{1,0:T(8,128)(2,1)S(1)}, u32[]{:S(2)}, u32[]{:S(2)}) collective-permute-start(bf16[512,256]{1,0:T(8,128)(2,1)S(1)} %collective-permute-done.3.late_hi.b1.c1), channel_id=1, source_target_pairs={{0,6},{1,7},{2,0},{3,1},{4,2},{5,3},{6,4},{7,5},{8,14},{9,15},{10,... | collective-permute-start | bytes 786440 | tf_op jit(solution)/shard_map/ppermute | solution.py:334
  41.6 8.0 %collective-permute-start.4 = (bf16[256,512]{1,0:T(8,128)(2,1)S(1)}, bf16[256,512]{1,0:T(8,128)(2,1)S(1)}, u32[]{:S(2)}, u32[]{:S(2)}) collective-permute-start(bf16[256,512]{1,0:T(8,128)(2,1)S(1)} %get-tuple-element.29), channel_id=1, source_target_pairs={{0,6},{1,7},{2,0},{3,1},{4,2},{5,3},{6,4},{7,5},{8,14},{9,15},{10,... | collective-permute-start | bytes 786440 | tf_op jit(solution)/shard_map/ppermute | solution.py:334
  41.9 7.7 %collective-permute-start.5 = (bf16[256,512]{1,0:T(8,128)(2,1)S(1)}, bf16[256,512]{1,0:T(8,128)(2,1)S(1)}, u32[]{:S(2)}, u32[]{:S(2)}) collective-permute-start(bf16[256,512]{1,0:T(8,128)(2,1)S(1)} %get-tuple-element.30), channel_id=1, source_target_pairs={{0,4},{1,5},{2,6},{3,7},{4,0},{5,1},{6,2},{7,3},{8,12},{9,13},{10,... | collective-permute-start | bytes 786440 | tf_op jit(solution)/shard_map/ppermute | solution.py:337
  42.0 11.2 %collective-permute-start.6 = (bf16[256,512]{1,0:T(8,128)(2,1)S(1)}, bf16[256,512]{1,0:T(8,128)(2,1)S(1)}, u32[]{:S(2)}, u32[]{:S(2)}) collective-permute-start(bf16[256,512]{1,0:T(8,128)(2,1)S(1)} %get-tuple-element.31), channel_id=1, source_target_pairs={{0,2},{1,3},{2,4},{3,5},{4,6},{5,7},{6,0},{7,1},{8,10},{9,11},{10,... | collective-permute-start | bytes 786440 | tf_op jit(solution)/shard_map/ppermute | solution.py:331
  43.9 16.8 %collective-permute-start.15 = (bf16[512,512]{1,0:T(8,128)(2,1)S(1)}, bf16[512,512]{1,0:T(8,128)(2,1)S(1)}, u32[]{:S(2)}, u32[]{:S(2)}) collective-permute-start(bf16[512,512]{1,0:T(8,128)(2,1)S(1)} %shard_map.91), channel_id=1, source_target_pairs={{0,1},{1,0},{2,3},{3,2},{4,5},{5,4},{6,7},{7,6},{8,9},{9,8},{10,11... | collective-permute-start | bytes 1572872 | tf_op jit(solution)/shard_map/ppermute | solution.py:340
  56.3 62.1 %collective-permute-start.11 = (bf16[320,1024]{1,0:T(8,128)(2,1)S(1)}, bf16[320,1024]{1,0:T(8,128)(2,1)S(1)}, u32[]{:S(2)}, u32[]{:S(2)}) collective-permute-start(bf16[320,1024]{1,0:T(8,128)(2,1)S(1)} %get-tuple-element.36), channel_id=1, source_target_pairs={{0,6},{1,7},{2,0},{3,1},{4,2},{5,3},{6,4},{7,5},{8,14},{9,15},{10,... | collective-permute-start | bytes 1966088 | tf_op jit(solution)/shard_map/ppermute | solution.py:334
  57.7 60.8 %collective-permute-start.12 = (bf16[320,1024]{1,0:T(8,128)(2,1)S(1)}, bf16[320,1024]{1,0:T(8,128)(2,1)S(1)}, u32[]{:S(2)}, u32[]{:S(2)}) collective-permute-start(bf16[320,1024]{1,0:T(8,128)(2,1)S(1)} %get-tuple-element.37), channel_id=1, source_target_pairs={{0,4},{1,5},{2,6},{3,7},{4,0},{5,1},{6,2},{7,3},{8,12},{9,13},{10,... | collective-permute-start | bytes 1966088 | tf_op jit(solution)/shard_map/ppermute | solution.py:337
  57.7 60.8 %collective-permute-start.13 = (bf16[320,1024]{1,0:T(8,128)(2,1)S(1)}, bf16[320,1024]{1,0:T(8,128)(2,1)S(1)}, u32[]{:S(2)}, u32[]{:S(2)}) collective-permute-start(bf16[320,1024]{1,0:T(8,128)(2,1)S(1)} %get-tuple-element.38), channel_id=1, source_target_pairs={{0,2},{1,3},{2,4},{3,5},{4,6},{5,7},{6,0},{7,1},{8,10},{9,11},{10,... | collective-permute-start | bytes 1966088 | tf_op jit(solution)/shard_map/ppermute | solution.py:331
  64.2 21.1 %collective-permute-start.16 = (f32[16,8,128]{2,1,0:T(8,128)S(1)}, f32[16,8,128]{2,1,0:T(8,128)S(1)}, u32[]{:S(2)}, u32[]{:S(2)}) collective-permute-start(f32[16,8,128]{2,1,0:T(8,128)S(1)} %get-tuple-element.40), channel_id=1, source_target_pairs={{0,8},{8,0},{16,24},{24,16},{32,40},{40,32},{48,56},{56,48},{64,72... | collective-permute-start | bytes 196616 | tf_op jit(solution)/shard_map/ppermute | solution.py:461
  85.3 4.7 %collective-permute-start.17 = (f32[16,8,128]{2,1,0:T(8,128)S(1)}, f32[16,8,128]{2,1,0:T(8,128)S(1)}, u32[]{:S(2)}, u32[]{:S(2)}) collective-permute-start(f32[16,8,128]{2,1,0:T(8,128)S(1)} %shard_map.93.a), channel_id=1, source_target_pairs={{0,16},{8,24},{16,0},{24,8},{32,48},{40,56},{48,32},{56,40},{64,80... | collective-permute-start | bytes 196616 | tf_op jit(solution)/shard_map/ppermute | solution.py:461
  93.5 4.5 %collective-permute-start.19 = (f32[16,8,128]{2,1,0:T(8,128)S(1)}, f32[16,8,128]{2,1,0:T(8,128)S(1)}, u32[]{:S(2)}, u32[]{:S(2)}) collective-permute-start(f32[16,8,128]{2,1,0:T(8,128)S(1)} %shard_map.95.a), channel_id=1, source_target_pairs={{0,64},{8,72},{16,80},{24,88},{32,96},{40,104},{48,112},{56,120},{... | collective-permute-start | bytes 196616 | tf_op jit(solution)/shard_map/ppermute | solution.py:461
  98.0 10.6 %collective-permute-start.20 = (f32[16,8,128]{2,1,0:T(8,128)S(1)}, f32[16,8,128]{2,1,0:T(8,128)S(1)}, u32[]{:S(2)}, u32[]{:S(2)}) collective-permute-start(f32[16,8,128]{2,1,0:T(8,128)S(1)} %shard_map.96.late.a), channel_id=1, source_target_pairs={{0,128},{8,136},{16,144},{24,152},{32,160},{40,168},{48,176},{56,1... | collective-permute-start | bytes 196616 | tf_op jit(solution)/shard_map/ppermute | solution.py:461
  108.7 8.6 %collective-permute-start.23 = (bf16[16,8,128]{2,1,0:T(8,128)(2,1)S(1)}, bf16[16,8,128]{2,1,0:T(8,128)(2,1)S(1)}, u32[]{:S(2)}, u32[]{:S(2)}) collective-permute-start(bf16[16,8,128]{2,1,0:T(8,128)(2,1)S(1)} %shard_map.98.half), channel_id=1, source_target_pairs={{0,9},{1,8},{2,11},{3,10},{4,13},{5,12},{6,15},{7,14},{8,1},{9,0},... | collective-permute-start | bytes 98312 | tf_op jit(solution)/shard_map/ppermute | solution.py:490
  119.0 9.3 %collective-permute-start.26 = (bf16[2,32,8,128]{3,2,1,0:T(8,128)(2,1)S(1)}, bf16[2,32,8,128]{3,2,1,0:T(8,128)(2,1)S(1)}, u32[]{:S(2)}, u32[]{:S(2)}) collective-permute-start(bf16[2,32,8,128]{3,2,1,0:T(8,128)(2,1)S(1)} %shard_map.99.tot), channel_id=1, source_target_pairs={{0,2},{1,3},{2,4},{3,5},{4,6},{5,7},{6,0},{7,1},{8,10},{9,11},{10,... | collective-permute-start | bytes 393224 | tf_op jit(solution)/shard_map/ppermute | solution.py:331
  120.4 9.2 %collective-permute-start.25 = (bf16[2,32,8,128]{3,2,1,0:T(8,128)(2,1)S(1)}, bf16[2,32,8,128]{3,2,1,0:T(8,128)(2,1)S(1)}, u32[]{:S(2)}, u32[]{:S(2)}) collective-permute-start(bf16[2,32,8,128]{3,2,1,0:T(8,128)(2,1)S(1)} %shard_map.99.tot), channel_id=1, source_target_pairs={{0,4},{1,5},{2,6},{3,7},{4,0},{5,1},{6,2},{7,3},{8,12},{9,13},{10,... | collective-permute-start | bytes 393224 | tf_op jit(solution)/shard_map/ppermute | solution.py:337
  123.0 6.5 %collective-permute-start.24 = (bf16[2,32,8,128]{3,2,1,0:T(8,128)(2,1)S(1)}, bf16[2,32,8,128]{3,2,1,0:T(8,128)(2,1)S(1)}, u32[]{:S(2)}, u32[]{:S(2)}) collective-permute-start(bf16[2,32,8,128]{3,2,1,0:T(8,128)(2,1)S(1)} %shard_map.99.tot), channel_id=1, source_target_pairs={{0,6},{1,7},{2,0},{3,1},{4,2},{5,3},{6,4},{7,5},{8,14},{9,15},{10,... | collective-permute-start | bytes 393224 | tf_op jit(solution)/shard_map/ppermute | solution.py:334
  (11 other events, 67.0 us)

commit v9 on v4

--- a/solution.py
+++ b/solution.py
@@ -56,15 +56,15 @@
     return dense
 
 
-def spread_row(tile, row):
-    return jnp.broadcast_to(tile[row : row + 1, :], (PACK, LANES)).astype(jnp.bfloat16)
+def spread_row(row):
+    return jnp.broadcast_to(row, (PACK, LANES)).astype(jnp.bfloat16)
 
 
 def expand_tile(indices, values, dense, first, cols):
     freq = lax.broadcasted_iota(jnp.int32, (PACK, LANES), 0).astype(jnp.float32)
     for half in range(2):
-        at = [spread_row(indices, half * KEEP + j) for j in range(KEEP)]
-        have = [spread_row(values, half * KEEP + j) for j in range(KEEP)]
+        at = [spread_row(indices(half * KEEP + j)) for j in range(KEEP)]
+        have = [spread_row(values(half * KEEP + j)) for j in range(KEEP)]
         for part in range(BLOCK // PACK):
             here = (freq + part * PACK).astype(jnp.bfloat16)
             tile = jnp.zeros((PACK, LANES), jnp.bfloat16)
@@ -172,12 +172,9 @@
     pl.when(jnp.logical_not(here))(lambda: put(send))
 
 
-def add_two_kernel(a, b, out):
+def add_two_kernel(a, b, *rest):
+    out = rest[-1]
     out[...] = (a[...] + b[...]).astype(out.dtype)
-
-
-def add_four_kernel(a, b, c, d, out):
-    out[...] = (a[...] + b[...]) + (c[...] + d[...])
 
 
 def pair_kernel(where, half, core, across, corner, late_0, late_1, late_2, out):
@@ -189,7 +186,7 @@
     out[1 - side, pl.ds(other, TILES // 2)] = corner[...]
 
 
-def residual_kernel(moment, picked, idx, ch, cl, late, out):
+def residual_kernel(moment, picked, idx, ch, cl, late, out, mark):
     parts = []
     for b in range(GROUP // BLOCK):
         at = [idx[b, j : j + 1, :] for j in range(KEEP)]
@@ -198,6 +195,7 @@
     kept = jnp.concatenate(parts, axis=0)
     back = three_pass((ch[...], cl[...]), split_pair(kept), ((0,), (0,)))
     out[...] = (moment[...] - back).T
+    mark[...] = back[:8, :LANES]
 
 
 def base_kernel(where, o0, o1, o2, o3, p0, p1, p2, p3, w_own, w_peer, idx, got_a, *outs):
@@ -218,32 +216,50 @@
         for f in range(2):
             for q in range(ROWS // LANES):
                 cols = slice(f * ROWS + q * LANES, f * ROWS + (q + 1) * LANES)
-                values = tot[f, t * (ROWS // LANES) + q].astype(jnp.float32)
-                expand_tile(pairs[t * 8 : (t + 1) * 8, cols], values, dense, t * 2 * BLOCK, cols)
-
-
-def forward_own_kernel(where, tok, own, tot, weight, ch, cl, mixed, out_weight, dense):
-    pairs = own[TOK:, :].astype(jnp.float32)
+                tile = t * (ROWS // LANES) + q
+                expand_tile(
+                    lambda s, t=t, cols=cols: pairs[t * 8 + s : t * 8 + s + 1, cols],
+                    lambda s, f=f, tile=tile: tot[f, tile, s : s + 1, :],
+                    dense,
+                    t * 2 * BLOCK,
+                    cols,
+                )
+
+
+def forward_own_kernel(where, tok, own, tot, weight, ch, cl, mixed, out_weight, dense, pairs, values):
+    pairs[...] = own[TOK:, :].astype(jnp.float32)
+    values[...] = tot[...].astype(jnp.float32)
     cols = pl.ds(pl.multiple_of((where[0] & 1) * ROWS, ROWS), ROWS)
     for g in range(STEPS):
-        expand_group(g, pairs, tot, dense)
+        expand_group(g, pairs, values, dense)
         span = slice(g * GROUP, (g + 1) * GROUP)
-        mixed[span, :] = mix(dense[span, :], tok[...], ((1,), (1,)))
         turned = dense[span, cols].T
         delta = mix(turned, ch[...], ((1,), (0,))) + mix(turned, cl[...], ((1,), (0,)))
         new = weight[:, span].astype(jnp.float32) - (step_rate / REPS) * delta
         out_weight[:, span] = new.astype(out_weight.dtype)
-
-
-def forward_kernel(where, tok_1, tok_2, tok_3, own, hi, far, lo, tot_1, tot_2, tot_3, mixed, ch, cl, out, *dense):
-    pairs = [near[TOK:, :].astype(jnp.float32) for near in (hi, far, lo)]
+    mixed[...] = mix(dense[...], tok[...], ((1,), (1,)))
+
+
+def expand_all(near, tot, dense, pairs, values):
+    pairs[...] = near[TOK:, :].astype(jnp.float32)
+    values[...] = tot[...].astype(jnp.float32)
+    for g in range(STEPS):
+        expand_group(g, pairs, values, dense)
+
+
+def forward_near_kernel(where, tok_1, tok_3, hi, lo, tot_1, tot_3, before, out, *scratch):
+    expand_all(hi, tot_1, scratch[0], scratch[2], scratch[4])
+    total = before[...] + mix(scratch[0][...], tok_1[...], ((1,), (1,)))
+    expand_all(lo, tot_3, scratch[1], scratch[3], scratch[5])
+    out[...] = total + mix(scratch[1][...], tok_3[...], ((1,), (1,)))
+
+
+def forward_far_kernel(where, tok, own, hi, far, lo, tot, before, ch, cl, out, dense, pairs, values, total):
+    expand_all(far, tot, dense, pairs, values)
+    total[...] = before[...] + mix(dense[...], tok[...], ((1,), (1,)))
     for g in range(STEPS):
         span = slice(g * GROUP, (g + 1) * GROUP)
-        total = mixed[span, :]
-        for tok, index, tot, buffer in zip((tok_1, tok_2, tok_3), pairs, (tot_1, tot_2, tot_3), dense):
-            expand_group(g, index, tot, buffer)
-            total += mix(buffer[span, :], tok[...], ((1,), (1,)))
-        delta = three_pass(split_pair(total.T), (ch[...], cl[...]), ((1,), (0,)))
+        delta = three_pass(split_pair(total[span, :].T), (ch[...], cl[...]), ((1,), (0,)))
         base = own[:TOK, span].astype(jnp.float32) + hi[:TOK, span].astype(jnp.float32)
         base += far[:TOK, span].astype(jnp.float32) + lo[:TOK, span].astype(jnp.float32)
         out[:, span] = (base - (step_rate / REPS) * delta).astype(out.dtype)
@@ -285,6 +301,9 @@
 INDEX_STEP = pl.BlockSpec((GROUP // BLOCK, KEEP, ROWS), lambda c, *_: (c, 0, 0))
 MESSAGE = whole(HALF, 2 * TOK)
 PIECE = whole(TOK, ROWS)
+DENSE = pltpu.VMEM((KV, 2 * ROWS), BF16)
+PAIRS = pltpu.VMEM((PICKS, 2 * ROWS), F32)
+VALUES = pltpu.VMEM((2, TILES, 8, LANES), F32)
 
 
 def shape(*dims, dtype=BF16):
@@ -427,21 +446,34 @@
     def partner(x, bits):
         return lax.ppermute(x, "rep", [(i, i ^ bits) for i in range(REPS)])
 
-    def add(kernel, result, *parts):
+    def add(kernel, result, *parts, after=()):
         return pl.pallas_call(
             kernel,
             grid=(1,),
-            in_specs=[halves] * len(parts),
+            in_specs=[halves] * len(parts) + [AFTER] * len(after),
             out_specs=halves,
             out_shape=result,
             compiler_params=params(),
             cost_estimate=cost(0, 0.25),
-        )(*parts)
+        )(*parts, *after)
 
     value = add(add_two_kernel, half_shape, keep, partner(send, 1))
-    value = add(add_two_kernel, half_shape, value, partner(value, 2))
-    value = add(add_four_kernel, half_shape, value, partner(value, 4), partner(value, 8), partner(value, 12))
-    half = add(add_two_kernel, shape(TILES // 2, 8, LANES), value, partner(value, 16))
+    from_hi = partner(value, 2)
+
+    value = add(add_two_kernel, half_shape, value, from_hi)
+    value = add(add_two_kernel, half_shape, value, partner(value, 4))
+    value = add(add_two_kernel, half_shape, value, partner(value, 8))
+    last = partner(value, 16)
+    new_momentum, mark = pl.pallas_call(
+        residual_kernel,
+        grid=(STEPS,),
+        in_specs=[by_row(GROUP, ROWS), by_row(PICKS // STEPS, ROWS), INDEX_STEP] + BASIS + [AFTER],
+        out_specs=[by_col(ROWS, GROUP), whole(8, LANES)],
+        out_shape=[shape(ROWS, KV, dtype=F32), shape(8, LANES, dtype=F32)],
+        compiler_params=params(),
+        cost_estimate=cost(6 * KV * GROUP * ROWS, 5),
+    )(moment, picked, index_t, high, low, value)
+    half = add(add_two_kernel, shape(TILES // 2, 8, LANES), value, last, after=(mark,))
 
     corner = lax.ppermute(half, ("rep", "fsdp"), [(i, i ^ 9) for i in range(REPS * 8)])
     pair_spec = whole(2, TILES, 8, LANES)
@@ -469,40 +501,46 @@
             grid=(1,),
             in_specs=[token_block(0), whole(TOK + PICKS, KV), pair_spec, whole(ROWS, KV)] + BASIS,
             out_specs=[whole(KV, TOK), whole(ROWS, KV)],
-            scratch_shapes=[pltpu.VMEM((KV, 2 * ROWS), BF16)],
+            scratch_shapes=[DENSE, PAIRS, VALUES],
         ),
         out_shape=[shape(KV, TOK, dtype=F32), shape(ROWS, KV)],
         compiler_params=params(),
         cost_estimate=cost(3 * KV * KV * ROWS, 4),
     )(place, tokens, base, pair, weight, high, low)
 
-    new_momentum = pl.pallas_call(
-        residual_kernel,
-        grid=(STEPS,),
-        in_specs=[by_row(GROUP, ROWS), by_row(PICKS // STEPS, ROWS), INDEX_STEP] + BASIS + [AFTER],
-        out_specs=by_col(ROWS, GROUP),
-        out_shape=shape(ROWS, KV, dtype=F32),
-        compiler_params=params(),
-        cost_estimate=cost(6 * KV * GROUP * ROWS, 5),
-    )(moment, picked, index_t, high, low, pair)
+    mixed = pl.pallas_call(
+        forward_near_kernel,
+        grid_spec=pltpu.PrefetchScalarGridSpec(
+            num_scalar_prefetch=1,
+            grid=(1,),
+            in_specs=[token_block(1), token_block(3)]
+            + [whole(TOK + PICKS, KV)] * 2
+            + [pair_spec] * 2
+            + [whole(KV, TOK)],
+            out_specs=whole(KV, TOK),
+            scratch_shapes=[DENSE] * 2 + [PAIRS] * 2 + [VALUES] * 2,
+        ),
+        out_shape=shape(KV, TOK, dtype=F32),
+        compiler_params=params(2 * VMEM_LIMIT),
+        cost_estimate=cost(4 * KV * KV * ROWS, 5),
+    )(place, tokens, tokens, base_hi, base_lo, pair_hi, pair_lo, mixed)
 
     projected = pl.pallas_call(
-        forward_kernel,
-        grid_spec=pltpu.PrefetchScalarGridSpec(
-            num_scalar_prefetch=1,
-            grid=(1,),
-            in_specs=[token_block(d) for d in (1, 2, 3)]
+        forward_far_kernel,
+        grid_spec=pltpu.PrefetchScalarGridSpec(
+            num_scalar_prefetch=1,
+            grid=(1,),
+            in_specs=[token_block(2)]
             + [whole(TOK + PICKS, KV)] * 4
-            + [pair_spec] * 3
-            + [whole(KV, TOK)]
+            + [pair_spec, whole(KV, TOK)]
             + BASIS,
             out_specs=whole(TOK, KV),
-            scratch_shapes=[pltpu.VMEM((KV, 2 * ROWS), BF16)] * 3,
+            scratch_shapes=[DENSE, PAIRS, VALUES, pltpu.VMEM((KV, TOK), F32)],
         ),
         out_shape=shape(TOK, KV),
         compiler_params=params(2 * VMEM_LIMIT),
-        cost_estimate=cost(6 * KV * KV * ROWS, 7),
-    )(place, tokens, tokens, tokens, base, base_hi, base_far, base_lo, pair_hi, pair_far, pair_lo, mixed, high, low)
+        cost_estimate=cost(3 * KV * KV * ROWS, 5),
+    )(place, tokens, base, base_hi, base_far, base_lo, pair_far, mixed, high, low)
     return (projected, new_weight, new_momentum[None])
 
 

time: 126 us -> 124 us (0.984)
  starting transfers between devices: 52.1 us -> 49.2 us
    ppermute x7 -> x6, starting transfers between devices: 27 us -> 23.5 us  [partner(): return lax.ppermute(x, 'rep', [(i, i ^ bits) for i in range(REPS)])]
    ppermute x5, starting transfers between devices: 3.25 us -> 5.08 us  [across(): return lax.ppermute(x, 'fsdp', [(i, (i + 4) % 8) for i in range(8)])]
    ppermute x7 -> x6, waiting for transfers between devices: 7.23 us -> 6.98 us  [partner(): return lax.ppermute(x, 'rep', [(i, i ^ bits) for i in range(REPS)])]
    pallas_call x5 -> x7, Pallas kernels: 6.61 us -> 6.82 us  [the longest x1 3.51 us: body(): pl.pallas_call(forward_far_kernel, grid_spec=pltpu.PrefetchScalarGridSpec...]
  transfers between devices with their start and end apart: 27 -> 26, of which waited for: 13 -> 14; matrix products, arithmetic and copies ran while one was open for 0% -> 0% of each run, Pallas kernels for 15% -> 17%
where the time goes in v9:
time: 124 us
  starting transfers between devices  49.2 us (40%)
  waiting for transfers between devices  45.1 us (36%)
  Pallas kernels  26 us (21%)
  local copies, waits for them, and re-layouts  2.66 us (2%)
    ppermute x6, starting transfers between devices, partner(): return lax.ppermute(x, 'rep', [(i, i ^ bits) for i in range(REPS)])  23.5 us
    ppermute x5, waiting for transfers between devices, up(): return lax.ppermute(x, 'fsdp', [(i, (i + 2) % 8) for i in range(8)])  17 us
    ppermute x5, waiting for transfers between devices, across(): return lax.ppermute(x, 'fsdp', [(i, (i + 4) % 8) for i in range(8)])  12.5 us
    ppermute x5, starting transfers between devices, down(): return lax.ppermute(x, 'fsdp', [(i, (i + 6) % 8) for i in range(8)])  11.6 us
    ppermute x6, waiting for transfers between devices, partner(): return lax.ppermute(x, 'rep', [(i, i ^ bits) for i in range(REPS)])  6.98 us
    ppermute x5, waiting for transfers between devices, down(): return lax.ppermute(x, 'fsdp', [(i, (i + 6) % 8) for i in range(8)])  6.32 us
    ppermute x5, starting transfers between devices, across(): return lax.ppermute(x, 'fsdp', [(i, (i + 4) % 8) for i in range(8)])  5.08 us
    ppermute x4, starting transfers between devices, swap(): return lax.ppermute(x, 'fsdp', [(i, i ^ 1) for i in range(8)])  5.01 us
  transfers between devices with their start and end apart: 26, of which 14 were waited for; matrix products, arithmetic and copies ran while one was open for 0% of the time, Pallas kernels for 17%

profile of v9, /device:TPU:1, one launch (start us, length us, event | category | flops | bytes accessed | tf_op | source)
XLA Modules:
  0.0 123.9 jit_solution(15966219995136482516)
XLA Ops:
  0.6 2.1 %collective-permute-start.8 = (bf16[512,1024]{1,0:T(8,128)(2,1)}, bf16[512,1024]{1,0:T(8,128)(2,1)S(1)}, u32[]{:S(2)}, u32[]{:S(2)}) collective-permute-start(bf16[512,1024]{1,0:T(8,128)(2,1)} %weight.1), channel_id=1, source_target_pairs={{0,1},{1,0},{2,3},{3,2},{4,5},{5,4},{6,7},{7,6},{8,9},{9,8},{10,11... | collective-permute-start | bytes 3145736 | tf_op jit(solution)/shard_map/ppermute | solution.py:330
  10.6 9.2 %collective-permute-done.late_lo.lo.p3.a3 = bf16[512,512]{1,0:T(8,128)(2,1)S(1)} collective-permute-done((bf16[512,512]{1,0:T(8,128)(2,1)S(1)}, bf16[512,512]{1,0:T(8,128)(2,1)S(1)}, u32[]{:S(2)}, u32[]{:S(2)}) %collective-permute-start) | collective-permute-done | bytes 524320 | tf_op jit(solution)/shard_map/ppermute | solution.py:321
  19.9 12.5 %collective-permute-done.7.far.p2.a2 = bf16[512,512]{1,0:T(8,128)(2,1)S(1)} collective-permute-done((bf16[512,512]{1,0:T(8,128)(2,1)S(1)}, bf16[512,512]{1,0:T(8,128)(2,1)S(1)}, u32[]{:S(2)}, u32[]{:S(2)}) %collective-permute-start.7) | collective-permute-done | bytes 524320 | tf_op jit(solution)/shard_map/ppermute | solution.py:327
  34.0 2.1 %collective-permute-start.3 = (bf16[512,256]{1,0:T(8,128)(2,1)S(1)}, bf16[512,256]{1,0:T(8,128)(2,1)S(1)}, u32[]{:S(2)}, u32[]{:S(2)}) collective-permute-start(bf16[512,256]{1,0:T(8,128)(2,1)S(1)} %shard_map.86.turned.b0.c0), channel_id=1, source_target_pairs={{0,6},{1,7},{2,0},{3,1},{4,2},{5,3},{6,4},{7,5},{8,14},{9,15},{10,... | collective-permute-start | bytes 786440 | tf_op jit(solution)/shard_map/ppermute | solution.py:324
  36.2 4.2 %collective-permute-done.2.late_lo.b3.c3 = bf16[512,256]{1,0:T(8,128)(2,1)S(1)} collective-permute-done((bf16[512,256]{1,0:T(8,128)(2,1)S(1)}, bf16[512,256]{1,0:T(8,128)(2,1)S(1)}, u32[]{:S(2)}, u32[]{:S(2)}) %collective-permute-start.2) | collective-permute-done | bytes 262176 | tf_op jit(solution)/shard_map/ppermute | solution.py:321
  42.1 4.0 %collective-permute-start.4 = (bf16[256,512]{1,0:T(8,128)(2,1)S(1)}, bf16[256,512]{1,0:T(8,128)(2,1)S(1)}, u32[]{:S(2)}, u32[]{:S(2)}) collective-permute-start(bf16[256,512]{1,0:T(8,128)(2,1)S(1)} %get-tuple-element.26), channel_id=1, source_target_pairs={{0,6},{1,7},{2,0},{3,1},{4,2},{5,3},{6,4},{7,5},{8,14},{9,15},{10,... | collective-permute-start | bytes 786440 | tf_op jit(solution)/shard_map/ppermute | solution.py:324
  48.8 4.5 %collective-permute-done.4.o1.t1 = bf16[256,512]{1,0:T(8,128)(2,1)S(1)} collective-permute-done((bf16[256,512]{1,0:T(8,128)(2,1)S(1)}, bf16[256,512]{1,0:T(8,128)(2,1)S(1)}, u32[]{:S(2)}, u32[]{:S(2)}) %collective-permute-start.4) | collective-permute-done | bytes 262176 | tf_op jit(solution)/shard_map/ppermute | solution.py:324
  53.3 2.6 %collective-permute-done.6.o3.t3 = bf16[256,512]{1,0:T(8,128)(2,1)S(1)} collective-permute-done((bf16[256,512]{1,0:T(8,128)(2,1)S(1)}, bf16[256,512]{1,0:T(8,128)(2,1)S(1)}, u32[]{:S(2)}, u32[]{:S(2)}) %collective-permute-start.6) | collective-permute-done | bytes 262176 | tf_op jit(solution)/shard_map/ppermute | solution.py:321
  56.0 3.0 %shard_map.89 = (bf16[320,1024]{1,0:T(8,128)(2,1)S(1)}, bf16[320,1024]{1,0:T(8,128)(2,1)S(1)}, bf16[320,1024]{1,0:T(8,128)(2,1)S(1)}, bf16[320,1024]{1,0:T(8,128)(2,1)S(1)}) custom-call(s32[2]{0:T(128)S(1)} %pad_add_fusion.where, bf16[256,512]{1,0:T(8,128)(2,1)S(1)} %get-tuple-element.25.o0.t0, bf16[256,512]{1,0:T(8,128)(2,1)S(1)} %collective-permute-done.4.o1.t1, ...), custom_call_target="tpu_custom_call" | custom-call | flops 2147483648 | bytes 7340032 | tf_op jit(solution)/shard_map/pallas_call | solution.py:414
  58.9 2.5 %collective-permute-start.10 = (bf16[320,1024]{1,0:T(8,128)(2,1)S(1)}, bf16[320,1024]{1,0:T(8,128)(2,1)S(1)}, u32[]{:S(2)}, u32[]{:S(2)}) collective-permute-start(bf16[320,1024]{1,0:T(8,128)(2,1)S(1)} %get-tuple-element.32), channel_id=1, source_target_pairs={{0,6},{1,7},{2,0},{3,1},{4,2},{5,3},{6,4},{7,5},{8,14},{9,15},{10,... | collective-permute-start | bytes 1966088 | tf_op jit(solution)/shard_map/ppermute | solution.py:324
  62.3 2.3 %shard_map.90.pre = f32[1024,512]{1,0:T(8,128)S(1)} custom-call(bf16[512,512]{1,0:T(8,128)(2,1)S(1)} %get-tuple-element.23.sent.a0, bf16[512,512]{1,0:T(8,128)(2,1)S(1)} %collective-permute-done.1.late_hi.hi.p1.a1, bf16[512,512]{1,0:T(8,128)(2,1)S(1)} %collective-permute-done.7.far.p2.a2, bf16[512,512]{1,0:T(8,128)(2,1)S(1)} %collective-permute-done.late_lo.lo.p3.a3, ...), custom_call_target="tpu_custom_call" | custom-call | flops 1073741824 | bytes 7340032 | tf_op jit(solution)/shard_map/pallas_call | solution.py:401
  64.6 3.5 %shard_map.92 = (f32[1024,512]{1,0:T(8,128)S(1)}, f32[64,512]{1,0:T(8,128)S(1)}, f32[16,8,128]{2,1,0:T(8,128)S(1)}, f32[16,8,128]{2,1,0:T(8,128)S(1)}) custom-call(s32[2]{0:T(128)S(1)} %pad_add_fusion.where, f32[1024,512]{1,0:T(8,128)S(1)} %shard_map.90.pre, bf16[576,512]{1,0:T(8,128)(2,1)S(1)} %collective-permute-done.9.got_a, ...), custom_call_target="tpu_custom_call" | custom-call | flops 805306368 | bytes 6291456 | tf_op jit(solution)/shard_map/pallas_call | solution.py:433
  68.1 5.7 %collective-permute-start.15 = (f32[16,8,128]{2,1,0:T(8,128)S(1)}, f32[16,8,128]{2,1,0:T(8,128)S(1)}, u32[]{:S(2)}, u32[]{:S(2)}) collective-permute-start(f32[16,8,128]{2,1,0:T(8,128)S(1)} %get-tuple-element.36), channel_id=1, source_target_pairs={{0,8},{8,0},{16,24},{24,16},{32,40},{40,32},{48,56},{56,48},{64,72... | collective-permute-start | bytes 196616 | tf_op jit(solution)/shard_map/ppermute | solution.py:447
  74.7 2.8 %collective-permute-start.16 = (f32[16,8,128]{2,1,0:T(8,128)S(1)}, f32[16,8,128]{2,1,0:T(8,128)S(1)}, u32[]{:S(2)}, u32[]{:S(2)}) collective-permute-start(f32[16,8,128]{2,1,0:T(8,128)S(1)} %shard_map.93.a), channel_id=1, source_target_pairs={{0,16},{8,24},{16,0},{24,8},{32,48},{40,56},{48,32},{56,40},{64,80... | collective-permute-start | bytes 196616 | tf_op jit(solution)/shard_map/ppermute | solution.py:447
  77.5 2.2 %collective-permute-done.16.b = f32[16,8,128]{2,1,0:T(8,128)S(1)} collective-permute-done((f32[16,8,128]{2,1,0:T(8,128)S(1)}, f32[16,8,128]{2,1,0:T(8,128)S(1)}, u32[]{:S(2)}, u32[]{:S(2)}) %collective-permute-start.16) | collective-permute-done | bytes 65568 | tf_op jit(solution)/shard_map/ppermute | solution.py:447
  81.4 2.0 %collective-permute-done.17.b = f32[16,8,128]{2,1,0:T(8,128)S(1)} collective-permute-done((f32[16,8,128]{2,1,0:T(8,128)S(1)}, f32[16,8,128]{2,1,0:T(8,128)S(1)}, u32[]{:S(2)}, u32[]{:S(2)}) %collective-permute-start.17) | collective-permute-done | bytes 65568 | tf_op jit(solution)/shard_map/ppermute | solution.py:447
  83.4 3.1 %collective-permute-start.18 = (f32[16,8,128]{2,1,0:T(8,128)S(1)}, f32[16,8,128]{2,1,0:T(8,128)S(1)}, u32[]{:S(2)}, u32[]{:S(2)}) collective-permute-start(f32[16,8,128]{2,1,0:T(8,128)S(1)} %shard_map.95.a), channel_id=1, source_target_pairs={{0,64},{8,72},{16,80},{24,88},{32,96},{40,104},{48,112},{56,120},{... | collective-permute-start | bytes 196616 | tf_op jit(solution)/shard_map/ppermute | solution.py:447
  88.4 6.9 %collective-permute-start.19 = (f32[16,8,128]{2,1,0:T(8,128)S(1)}, f32[16,8,128]{2,1,0:T(8,128)S(1)}, u32[]{:S(2)}, u32[]{:S(2)}) collective-permute-start(f32[16,8,128]{2,1,0:T(8,128)S(1)} %shard_map.96.late.a), channel_id=1, source_target_pairs={{0,128},{8,136},{16,144},{24,152},{32,160},{40,168},{48,176},{56,1... | collective-permute-start | bytes 196616 | tf_op jit(solution)/shard_map/ppermute | solution.py:447
  95.3 3.7 %shard_map.97 = (f32[512,1024]{1,0:T(8,128)}, f32[8,128]{1,0:T(8,128)S(1)}) custom-call(f32[1024,512]{1,0:T(8,128)S(1)} %get-tuple-element.37.moment, f32[64,512]{1,0:T(8,128)S(1)} %get-tuple-element.38.picked, s32[16,4,512]{2,1,0:T(4,128)S(1)} %bitcast.9, bf16[256,256]{1,0:T(8,128)(2,1)S(1)} %copy-done.5, bf16[256,256]{1,0:T(8,128)(2,1)S(1)} %copy-done.6, ...), custom_call_target="tpu_custom_call" | custom-call | flops 805306368 | bytes 5242880 | tf_op jit(solution)/shard_map/pallas_call | solution.py:467
  99.1 3.3 %collective-permute-start.20 = (bf16[16,8,128]{2,1,0:T(8,128)(2,1)S(1)}, bf16[16,8,128]{2,1,0:T(8,128)(2,1)S(1)}, u32[]{:S(2)}, u32[]{:S(2)}) collective-permute-start(bf16[16,8,128]{2,1,0:T(8,128)(2,1)S(1)} %shard_map.98.half), channel_id=1, source_target_pairs={{0,8},{8,0},{16,24},{24,16},{32,40},{40,32},{48,56},{56,48},{64,72... | collective-permute-start | bytes 98312 | tf_op jit(solution)/shard_map/ppermute | solution.py:447
  107.5 3.0 %collective-permute-start.23 = (bf16[2,32,8,128]{3,2,1,0:T(8,128)(2,1)S(1)}, bf16[2,32,8,128]{3,2,1,0:T(8,128)(2,1)S(1)}, u32[]{:S(2)}, u32[]{:S(2)}) collective-permute-start(bf16[2,32,8,128]{3,2,1,0:T(8,128)(2,1)S(1)} %shard_map.99.tot), channel_id=1, source_target_pairs={{0,4},{1,5},{2,6},{3,7},{4,0},{5,1},{6,2},{7,3},{8,12},{9,13},{10,... | collective-permute-start | bytes 393224 | tf_op jit(solution)/shard_map/ppermute | solution.py:327
  112.1 3.3 %shard_map.100 = (f32[1024,256]{1,0:T(8,128)S(1)}, bf16[512,1024]{1,0:T(8,128)(2,1)}) custom-call(s32[2]{0:T(128)S(1)} %pad_add_fusion.where, bf16[256,4096]{1,0:T(8,128)(2,1)S(1)} %copy-done.1, bf16[320,1024]{1,0:T(8,128)(2,1)S(1)} %get-tuple-element.31.late.own, bf16[2,32,8,128]{3,2,1,0:T(8,128)(2,1)S(1)} %shard_map.99.tot, ...), custom_call_target="tpu_custom_call" | custom-call | flops 1610612736 | bytes 4194304 | tf_op jit(solution)/shard_map/pallas_call | solution.py:497
  117.1 3.3 %shard_map.101.before = f32[1024,256]{1,0:T(8,128)S(1)} custom-call(s32[2]{0:T(128)S(1)} %pad_add_fusion.where, bf16[256,4096]{1,0:T(8,128)(2,1)S(1)} %copy-done.1, bf16[256,4096]{1,0:T(8,128)(2,1)S(1)} %copy-done.1, bf16[320,1024]{1,0:T(8,128)(2,1)S(1)} %collective-permute-done.10.late_1.hi, bf16[320,1024]{1,0:T(8,128)(2,1)S(1)} %collective-permute-done.12.late_0.lo, ...), custom_call_target="tpu_custom_call" | custom-call | flops 2147483648 | bytes 5242880 | tf_op jit(solution)/shard_map/pallas_call | solution.py:511
  120.4 3.5 %shard_map.102 = bf16[256,1024]{1,0:T(8,128)(2,1)} custom-call(s32[2]{0:T(128)S(1)} %pad_add_fusion.where, bf16[256,4096]{1,0:T(8,128)(2,1)S(1)} %copy-done.1, bf16[320,1024]{1,0:T(8,128)(2,1)S(1)} %get-tuple-element.31.late.own, bf16[320,1024]{1,0:T(8,128)(2,1)S(1)} %collective-permute-done.10.late_1.hi, ...), custom_call_target="tpu_custom_call" | custom-call | flops 1610612736 | bytes 5242880 | tf_op jit(solution)/shard_map/pallas_call | solution.py:528
  (63 shorter events, 28.0 us)
Async XLA Ops:
  0.6 31.8 %collective-permute-start.8 = (bf16[512,1024]{1,0:T(8,128)(2,1)}, bf16[512,1024]{1,0:T(8,128)(2,1)S(1)}, u32[]{:S(2)}, u32[]{:S(2)}) collective-permute-start(bf16[512,1024]{1,0:T(8,128)(2,1)} %weight.1), channel_id=1, source_target_pairs={{0,1},{1,0},{2,3},{3,2},{4,5},{5,4},{6,7},{7,6},{8,9},{9,8},{10,11... | collective-permute-start | bytes 3145736 | tf_op jit(solution)/shard_map/ppermute | solution.py:330
  6.2 13.6 %collective-permute-start = (bf16[512,512]{1,0:T(8,128)(2,1)S(1)}, bf16[512,512]{1,0:T(8,128)(2,1)S(1)}, u32[]{:S(2)}, u32[]{:S(2)}) collective-permute-start(bf16[512,512]{1,0:T(8,128)(2,1)S(1)} %get-tuple-element.23.sent.a0), channel_id=1, source_target_pairs={{0,2},{1,3},{2,4},{3,5},{4,6},{5,7},{6,0},{7,1},{8,10},{9,11},{10,... | collective-permute-start | bytes 1572872 | tf_op jit(solution)/shard_map/ppermute | solution.py:321
  7.5 12.2 %collective-permute-start.1 = (bf16[512,512]{1,0:T(8,128)(2,1)S(1)}, bf16[512,512]{1,0:T(8,128)(2,1)S(1)}, u32[]{:S(2)}, u32[]{:S(2)}) collective-permute-start(bf16[512,512]{1,0:T(8,128)(2,1)S(1)} %get-tuple-element.24), channel_id=1, source_target_pairs={{0,6},{1,7},{2,0},{3,1},{4,2},{5,3},{6,4},{7,5},{8,14},{9,15},{10,... | collective-permute-start | bytes 1572872 | tf_op jit(solution)/shard_map/ppermute | solution.py:324
  9.1 23.3 %collective-permute-start.7 = (bf16[512,512]{1,0:T(8,128)(2,1)S(1)}, bf16[512,512]{1,0:T(8,128)(2,1)S(1)}, u32[]{:S(2)}, u32[]{:S(2)}) collective-permute-start(bf16[512,512]{1,0:T(8,128)(2,1)S(1)} %get-tuple-element.30), channel_id=1, source_target_pairs={{0,4},{1,5},{2,6},{3,7},{4,0},{5,1},{6,2},{7,3},{8,12},{9,13},{10,... | collective-permute-start | bytes 1572872 | tf_op jit(solution)/shard_map/ppermute | solution.py:327
  33.1 22.8 %collective-permute-start.9 = (bf16[576,512]{1,0:T(8,128)(2,1)S(1)}, bf16[576,512]{1,0:T(8,128)(2,1)S(1)}, u32[]{:S(2)}, u32[]{:S(2)}) collective-permute-start(bf16[576,512]{1,0:T(8,128)(2,1)S(1)} %shard_map.88), channel_id=1, source_target_pairs={{0,1},{1,0},{2,3},{3,2},{4,5},{5,4},{6,7},{7,6},{8,9},{9,8},{10,11... | collective-permute-start | bytes 1769480 | tf_op jit(solution)/shard_map/ppermute | solution.py:330
  33.5 6.9 %collective-permute-start.2 = (bf16[512,256]{1,0:T(8,128)(2,1)S(1)}, bf16[512,256]{1,0:T(8,128)(2,1)S(1)}, u32[]{:S(2)}, u32[]{:S(2)}) collective-permute-start(bf16[512,256]{1,0:T(8,128)(2,1)S(1)} %shard_map.86.turned.b0.c0), channel_id=1, source_target_pairs={{0,2},{1,3},{2,4},{3,5},{4,6},{5,7},{6,0},{7,1},{8,10},{9,11},{10,... | collective-permute-start | bytes 786440 | tf_op jit(solution)/shard_map/ppermute | solution.py:321
  34.0 7.4 %collective-permute-start.3 = (bf16[512,256]{1,0:T(8,128)(2,1)S(1)}, bf16[512,256]{1,0:T(8,128)(2,1)S(1)}, u32[]{:S(2)}, u32[]{:S(2)}) collective-permute-start(bf16[512,256]{1,0:T(8,128)(2,1)S(1)} %shard_map.86.turned.b0.c0), channel_id=1, source_target_pairs={{0,6},{1,7},{2,0},{3,1},{4,2},{5,3},{6,4},{7,5},{8,14},{9,15},{10,... | collective-permute-start | bytes 786440 | tf_op jit(solution)/shard_map/ppermute | solution.py:324
  36.2 10.6 %collective-permute-start.13 = (bf16[512,256]{1,0:T(8,128)(2,1)S(1)}, bf16[512,256]{1,0:T(8,128)(2,1)S(1)}, u32[]{:S(2)}, u32[]{:S(2)}) collective-permute-start(bf16[512,256]{1,0:T(8,128)(2,1)S(1)} %shard_map.86.turned.b0.c0), channel_id=1, source_target_pairs={{0,4},{1,5},{2,6},{3,7},{4,0},{5,1},{6,2},{7,3},{8,12},{9,13},{10,... | collective-permute-start | bytes 786440 | tf_op jit(solution)/shard_map/ppermute | solution.py:327
  42.1 11.2 %collective-permute-start.4 = (bf16[256,512]{1,0:T(8,128)(2,1)S(1)}, bf16[256,512]{1,0:T(8,128)(2,1)S(1)}, u32[]{:S(2)}, u32[]{:S(2)}) collective-permute-start(bf16[256,512]{1,0:T(8,128)(2,1)S(1)} %get-tuple-element.26), channel_id=1, source_target_pairs={{0,6},{1,7},{2,0},{3,1},{4,2},{5,3},{6,4},{7,5},{8,14},{9,15},{10,... | collective-permute-start | bytes 786440 | tf_op jit(solution)/shard_map/ppermute | solution.py:324
  46.1 7.2 %collective-permute-start.5 = (bf16[256,512]{1,0:T(8,128)(2,1)S(1)}, bf16[256,512]{1,0:T(8,128)(2,1)S(1)}, u32[]{:S(2)}, u32[]{:S(2)}) collective-permute-start(bf16[256,512]{1,0:T(8,128)(2,1)S(1)} %get-tuple-element.27), channel_id=1, source_target_pairs={{0,4},{1,5},{2,6},{3,7},{4,0},{5,1},{6,2},{7,3},{8,12},{9,13},{10,... | collective-permute-start | bytes 786440 | tf_op jit(solution)/shard_map/ppermute | solution.py:327
  46.1 9.8 %collective-permute-start.6 = (bf16[256,512]{1,0:T(8,128)(2,1)S(1)}, bf16[256,512]{1,0:T(8,128)(2,1)S(1)}, u32[]{:S(2)}, u32[]{:S(2)}) collective-permute-start(bf16[256,512]{1,0:T(8,128)(2,1)S(1)} %get-tuple-element.28), channel_id=1, source_target_pairs={{0,2},{1,3},{2,4},{3,5},{4,6},{5,7},{6,0},{7,1},{8,10},{9,11},{10,... | collective-permute-start | bytes 786440 | tf_op jit(solution)/shard_map/ppermute | solution.py:321
  47.5 17.0 %collective-permute-start.14 = (bf16[512,512]{1,0:T(8,128)(2,1)S(1)}, bf16[512,512]{1,0:T(8,128)(2,1)S(1)}, u32[]{:S(2)}, u32[]{:S(2)}) collective-permute-start(bf16[512,512]{1,0:T(8,128)(2,1)S(1)} %shard_map.91), channel_id=1, source_target_pairs={{0,1},{1,0},{2,3},{3,2},{4,5},{5,4},{6,7},{7,6},{8,9},{9,8},{10,11... | collective-permute-start | bytes 1572872 | tf_op jit(solution)/shard_map/ppermute | solution.py:330
  58.9 48.0 %collective-permute-start.10 = (bf16[320,1024]{1,0:T(8,128)(2,1)S(1)}, bf16[320,1024]{1,0:T(8,128)(2,1)S(1)}, u32[]{:S(2)}, u32[]{:S(2)}) collective-permute-start(bf16[320,1024]{1,0:T(8,128)(2,1)S(1)} %get-tuple-element.32), channel_id=1, source_target_pairs={{0,6},{1,7},{2,0},{3,1},{4,2},{5,3},{6,4},{7,5},{8,14},{9,15},{10,... | collective-permute-start | bytes 1966088 | tf_op jit(solution)/shard_map/ppermute | solution.py:324
  61.4 45.5 %collective-permute-start.11 = (bf16[320,1024]{1,0:T(8,128)(2,1)S(1)}, bf16[320,1024]{1,0:T(8,128)(2,1)S(1)}, u32[]{:S(2)}, u32[]{:S(2)}) collective-permute-start(bf16[320,1024]{1,0:T(8,128)(2,1)S(1)} %get-tuple-element.33), channel_id=1, source_target_pairs={{0,4},{1,5},{2,6},{3,7},{4,0},{5,1},{6,2},{7,3},{8,12},{9,13},{10,... | collective-permute-start | bytes 1966088 | tf_op jit(solution)/shard_map/ppermute | solution.py:327
  61.9 45.0 %collective-permute-start.12 = (bf16[320,1024]{1,0:T(8,128)(2,1)S(1)}, bf16[320,1024]{1,0:T(8,128)(2,1)S(1)}, u32[]{:S(2)}, u32[]{:S(2)}) collective-permute-start(bf16[320,1024]{1,0:T(8,128)(2,1)S(1)} %get-tuple-element.34), channel_id=1, source_target_pairs={{0,2},{1,3},{2,4},{3,5},{4,6},{5,7},{6,0},{7,1},{8,10},{9,11},{10,... | collective-permute-start | bytes 1966088 | tf_op jit(solution)/shard_map/ppermute | solution.py:321
  68.1 6.6 %collective-permute-start.15 = (f32[16,8,128]{2,1,0:T(8,128)S(1)}, f32[16,8,128]{2,1,0:T(8,128)S(1)}, u32[]{:S(2)}, u32[]{:S(2)}) collective-permute-start(f32[16,8,128]{2,1,0:T(8,128)S(1)} %get-tuple-element.36), channel_id=1, source_target_pairs={{0,8},{8,0},{16,24},{24,16},{32,40},{40,32},{48,56},{56,48},{64,72... | collective-permute-start | bytes 196616 | tf_op jit(solution)/shard_map/ppermute | solution.py:447
  74.7 5.0 %collective-permute-start.16 = (f32[16,8,128]{2,1,0:T(8,128)S(1)}, f32[16,8,128]{2,1,0:T(8,128)S(1)}, u32[]{:S(2)}, u32[]{:S(2)}) collective-permute-start(f32[16,8,128]{2,1,0:T(8,128)S(1)} %shard_map.93.a), channel_id=1, source_target_pairs={{0,16},{8,24},{16,0},{24,8},{32,48},{40,56},{48,32},{56,40},{64,80... | collective-permute-start | bytes 196616 | tf_op jit(solution)/shard_map/ppermute | solution.py:447
  79.7 3.7 %collective-permute-start.17 = (f32[16,8,128]{2,1,0:T(8,128)S(1)}, f32[16,8,128]{2,1,0:T(8,128)S(1)}, u32[]{:S(2)}, u32[]{:S(2)}) collective-permute-start(f32[16,8,128]{2,1,0:T(8,128)S(1)} %shard_map.94.a), channel_id=1, source_target_pairs={{0,32},{8,40},{16,48},{24,56},{32,0},{40,8},{48,16},{56,24},{64,96... | collective-permute-start | bytes 196616 | tf_op jit(solution)/shard_map/ppermute | solution.py:447
  83.4 5.0 %collective-permute-start.18 = (f32[16,8,128]{2,1,0:T(8,128)S(1)}, f32[16,8,128]{2,1,0:T(8,128)S(1)}, u32[]{:S(2)}, u32[]{:S(2)}) collective-permute-start(f32[16,8,128]{2,1,0:T(8,128)S(1)} %shard_map.95.a), channel_id=1, source_target_pairs={{0,64},{8,72},{16,80},{24,88},{32,96},{40,104},{48,112},{56,120},{... | collective-permute-start | bytes 196616 | tf_op jit(solution)/shard_map/ppermute | solution.py:447
  88.4 10.6 %collective-permute-start.19 = (f32[16,8,128]{2,1,0:T(8,128)S(1)}, f32[16,8,128]{2,1,0:T(8,128)S(1)}, u32[]{:S(2)}, u32[]{:S(2)}) collective-permute-start(f32[16,8,128]{2,1,0:T(8,128)S(1)} %shard_map.96.late.a), channel_id=1, source_target_pairs={{0,128},{8,136},{16,144},{24,152},{32,160},{40,168},{48,176},{56,1... | collective-permute-start | bytes 196616 | tf_op jit(solution)/shard_map/ppermute | solution.py:447
  99.1 4.5 %collective-permute-start.20 = (bf16[16,8,128]{2,1,0:T(8,128)(2,1)S(1)}, bf16[16,8,128]{2,1,0:T(8,128)(2,1)S(1)}, u32[]{:S(2)}, u32[]{:S(2)}) collective-permute-start(bf16[16,8,128]{2,1,0:T(8,128)(2,1)S(1)} %shard_map.98.half), channel_id=1, source_target_pairs={{0,8},{8,0},{16,24},{24,16},{32,40},{40,32},{48,56},{56,48},{64,72... | collective-permute-start | bytes 98312 | tf_op jit(solution)/shard_map/ppermute | solution.py:447
  107.5 12.9 %collective-permute-start.23 = (bf16[2,32,8,128]{3,2,1,0:T(8,128)(2,1)S(1)}, bf16[2,32,8,128]{3,2,1,0:T(8,128)(2,1)S(1)}, u32[]{:S(2)}, u32[]{:S(2)}) collective-permute-start(bf16[2,32,8,128]{3,2,1,0:T(8,128)(2,1)S(1)} %shard_map.99.tot), channel_id=1, source_target_pairs={{0,4},{1,5},{2,6},{3,7},{4,0},{5,1},{6,2},{7,3},{8,12},{9,13},{10,... | collective-permute-start | bytes 393224 | tf_op jit(solution)/shard_map/ppermute | solution.py:327
  110.5 5.5 %collective-permute-start.24 = (bf16[2,32,8,128]{3,2,1,0:T(8,128)(2,1)S(1)}, bf16[2,32,8,128]{3,2,1,0:T(8,128)(2,1)S(1)}, u32[]{:S(2)}, u32[]{:S(2)}) collective-permute-start(bf16[2,32,8,128]{3,2,1,0:T(8,128)(2,1)S(1)} %shard_map.99.tot), channel_id=1, source_target_pairs={{0,6},{1,7},{2,0},{3,1},{4,2},{5,3},{6,4},{7,5},{8,14},{9,15},{10,... | collective-permute-start | bytes 393224 | tf_op jit(solution)/shard_map/ppermute | solution.py:324
  112.1 5.0 %collective-permute-start.25 = (bf16[2,32,8,128]{3,2,1,0:T(8,128)(2,1)S(1)}, bf16[2,32,8,128]{3,2,1,0:T(8,128)(2,1)S(1)}, u32[]{:S(2)}, u32[]{:S(2)}) collective-permute-start(bf16[2,32,8,128]{3,2,1,0:T(8,128)(2,1)S(1)} %shard_map.99.tot), channel_id=1, source_target_pairs={{0,2},{1,3},{2,4},{3,5},{4,6},{5,7},{6,0},{7,1},{8,10},{9,11},{10,... | collective-permute-start | bytes 393224 | tf_op jit(solution)/shard_map/ppermute | solution.py:321
  (10 other events, 69.6 us)

commit v10 on v9

--- a/solution.py
+++ b/solution.py
@@ -125,23 +125,12 @@
     out[...] = four_products(cots, toks).astype(out.dtype)
 
 
-def own_kernel(a0, a1, a2, a3, b0, b1, b2, b3, t0, t1, t2, t3, mom, out):
-    step = pl.program_id(0)
-    toks = (t0[...], t1[...], t2[...], t3[...])
-
-    @pl.when(step < STEPS // 2)
-    def _():
-        cots = (cot_of(a0), cot_of(a1), cot_of(a2), cot_of(a3))
-        out[...] = four_products(cots, toks) + beta_decay * mom[...].T
-
-    @pl.when(step >= STEPS // 2)
-    def _():
-        cots = (b0[...], b1[...], b2[...], b3[...])
-        out[...] = four_products(cots, toks) + beta_decay * mom[...].T
-
-
 def pick_rows(moment, idx, ch, cl):
-    spectrum = three_pass((ch[...], cl[...]), split_pair(moment), ((1,), (0,)))
+    upper, lower = split_pair(moment)
+    both = jnp.concatenate([ch[...], cl[...]], axis=0)
+    product = jnp.dot(both, upper, preferred_element_type=jnp.float32)
+    spectrum = product[:GROUP] + product[GROUP:]
+    spectrum += jnp.dot(ch[...], lower, preferred_element_type=jnp.float32)
     freq = lax.broadcasted_iota(jnp.int32, (BLOCK, ROWS), 0)
     rows = []
     for b in range(GROUP // BLOCK):
@@ -152,11 +141,23 @@
     return rows
 
 
-def pick_kernel(where, pre, got_a, got_b, idx, ch, cl, late, moment, picked, keep, send):
+def pick_kernel(
+    where, a0, a1, a2, a3, b0, b1, b2, b3, t0, t1, t2, t3, mom, got_a, got_b, idx, ch, cl, late, moment, picked, keep, send
+):
     step = pl.program_id(0)
-    first = step < STEPS // 2
-    got = jnp.where(first, got_a[...], got_b[...]).astype(jnp.float32)
-    total = pre[...] + got
+    toks = (t0[...], t1[...], t2[...], t3[...])
+
+    @pl.when(step < STEPS // 2)
+    def _():
+        cots = (cot_of(a0), cot_of(a1), cot_of(a2), cot_of(a3))
+        moment[...] = four_products(cots, toks) + got_a[...].astype(jnp.float32)
+
+    @pl.when(step >= STEPS // 2)
+    def _():
+        cots = (b0[...], b1[...], b2[...], b3[...])
+        moment[...] = four_products(cots, toks) + got_b[...].astype(jnp.float32)
+
+    total = moment[...] + beta_decay * mom[...].T
     moment[...] = total
     values = jnp.concatenate(pick_rows(total, idx, ch, cl), axis=0)
     picked[...] = values
@@ -199,16 +200,23 @@
 
 
 def base_kernel(where, o0, o1, o2, o3, p0, p1, p2, p3, w_own, w_peer, idx, got_a, *outs):
-    mine, theirs = flat_index(idx), got_a[HALF:, :]
-    first = (where[0] & 1) == 0
-    left, right = jnp.where(first, mine, theirs), jnp.where(first, theirs, mine)
+    pairs, outs = outs[-1], outs[:-1]
+    step = pl.program_id(0)
+
+    @pl.when(step == 0)
+    def _():
+        mine, theirs = flat_index(idx), got_a[HALF:, :]
+        first = (where[0] & 1) == 0
+        pairs[:, :ROWS] = jnp.where(first, mine, theirs)
+        pairs[:, ROWS:] = jnp.where(first, theirs, mine)
+
+    here = pairs[:, pl.ds(pl.multiple_of(step * GROUP, GROUP), GROUP)]
     peers = (p0[...], tok_of(p1), tok_of(p2), tok_of(p3))
     for own, peer, out in zip((o0, o1, o2, o3), peers, outs):
         total = jnp.dot(own[...], w_own[...], preferred_element_type=jnp.float32)
         total += jnp.dot(peer, w_peer[...], preferred_element_type=jnp.float32)
         out[:TOK, :] = total.astype(out.dtype)
-        out[TOK:, :ROWS] = left
-        out[TOK:, ROWS:] = right
+        out[TOK:, :] = here
 
 
 def expand_group(g, pairs, tot, dense):
@@ -226,7 +234,7 @@
                 )
 
 
-def forward_own_kernel(where, tok, own, tot, weight, ch, cl, mixed, out_weight, dense, pairs, values):
+def forward_own_kernel(where, tok, own, hi, far, lo, tot, weight, ch, cl, mixed, out_weight, base, dense, pairs, values):
     pairs[...] = own[TOK:, :].astype(jnp.float32)
     values[...] = tot[...].astype(jnp.float32)
     cols = pl.ds(pl.multiple_of((where[0] & 1) * ROWS, ROWS), ROWS)
@@ -238,10 +246,12 @@
         new = weight[:, span].astype(jnp.float32) - (step_rate / REPS) * delta
         out_weight[:, span] = new.astype(out_weight.dtype)
     mixed[...] = mix(dense[...], tok[...], ((1,), (1,)))
-
-
-def expand_all(near, tot, dense, pairs, values):
-    pairs[...] = near[TOK:, :].astype(jnp.float32)
+    near = own[:TOK, :].astype(jnp.float32) + hi[:TOK, :].astype(jnp.float32)
+    base[...] = near + far[:TOK, :].astype(jnp.float32) + lo[:TOK, :].astype(jnp.float32)
+
+
+def expand_all(index, tot, dense, pairs, values):
+    pairs[...] = index[...].astype(jnp.float32)
     values[...] = tot[...].astype(jnp.float32)
     for g in range(STEPS):
         expand_group(g, pairs, values, dense)
@@ -254,15 +264,15 @@
     out[...] = total + mix(scratch[1][...], tok_3[...], ((1,), (1,)))
 
 
-def forward_far_kernel(where, tok, own, hi, far, lo, tot, before, ch, cl, out, dense, pairs, values, total):
+def forward_far_kernel(where, tok, base, far, tot, before, ch, cl, out, dense, pairs, values, total):
     expand_all(far, tot, dense, pairs, values)
     total[...] = before[...] + mix(dense[...], tok[...], ((1,), (1,)))
+    groups = [total[g * GROUP : (g + 1) * GROUP, :].T for g in range(STEPS)]
+    delta = three_pass(split_pair(jnp.concatenate(groups, axis=0)), (ch[...], cl[...]), ((1,), (0,)))
     for g in range(STEPS):
         span = slice(g * GROUP, (g + 1) * GROUP)
-        delta = three_pass(split_pair(total[span, :].T), (ch[...], cl[...]), ((1,), (0,)))
-        base = own[:TOK, span].astype(jnp.float32) + hi[:TOK, span].astype(jnp.float32)
-        base += far[:TOK, span].astype(jnp.float32) + lo[:TOK, span].astype(jnp.float32)
-        out[:, span] = (base - (step_rate / REPS) * delta).astype(out.dtype)
+        part = delta[g * TOK : (g + 1) * TOK]
+        out[:, span] = (base[:, span] - (step_rate / REPS) * part).astype(out.dtype)
 
 
 def params(limit=VMEM_LIMIT):
@@ -398,29 +408,17 @@
     )(*cots_b, peer_0, *firsts[1:])
     got_b = swap(partial_b)
 
-    pre = pl.pallas_call(
-        own_kernel,
-        grid=(STEPS,),
-        in_specs=[first_half(GROUP, 2 * TOK)] * 4
-        + [second_half(GROUP, TOK)] * 4
-        + [PIECE] * 4
-        + [by_col(ROWS, GROUP)],
-        out_specs=by_row(GROUP, ROWS),
-        out_shape=shape(KV, ROWS, dtype=F32),
-        compiler_params=params(),
-        cost_estimate=cost(2 * KV * KV * ROWS, 7),
-    )(*firsts, *cots_b, *owns, momentum[0])
-
     base, base_up, base_across, base_down = pl.pallas_call(
         base_kernel,
         grid_spec=pltpu.PrefetchScalarGridSpec(
             num_scalar_prefetch=1,
-            grid=(1,),
+            grid=(STEPS,),
             in_specs=[PIECE] * 5
             + [MESSAGE] * 3
-            + [whole(ROWS, KV)] * 2
+            + [by_col(ROWS, GROUP)] * 2
             + [INDEX, whole(HALF + PICKS, ROWS)],
-            out_specs=[whole(TOK + PICKS, KV)] * 4,
+            out_specs=[by_col(TOK + PICKS, GROUP)] * 4,
+            scratch_shapes=[pltpu.VMEM((PICKS, KV), BF16)],
         ),
         out_shape=[shape(TOK + PICKS, KV)] * 4,
         compiler_params=params(2 * VMEM_LIMIT),
@@ -435,13 +433,20 @@
         grid_spec=pltpu.PrefetchScalarGridSpec(
             num_scalar_prefetch=1,
             grid=(STEPS,),
-            in_specs=[by_row(GROUP, ROWS)] + GOT + [INDEX_STEP] + BASIS + [AFTER],
+            in_specs=[first_half(GROUP, 2 * TOK)] * 4
+            + [second_half(GROUP, TOK)] * 4
+            + [PIECE] * 4
+            + [by_col(ROWS, GROUP)]
+            + GOT
+            + [INDEX_STEP]
+            + BASIS
+            + [AFTER],
             out_specs=[by_row(GROUP, ROWS), by_row(PICKS // STEPS, ROWS), halves, halves],
         ),
         out_shape=[shape(KV, ROWS, dtype=F32), shape(PICKS, ROWS, dtype=F32), half_shape, half_shape],
         compiler_params=params(),
-        cost_estimate=cost(6 * KV * GROUP * ROWS, 6),
-    )(place, pre, got_a, got_b, index_t, high, low, base)
+        cost_estimate=cost(2 * KV * KV * ROWS, 12),
+    )(place, *firsts, *cots_b, *owns, momentum[0], got_a, got_b, index_t, high, low, base)
 
     def partner(x, bits):
         return lax.ppermute(x, "rep", [(i, i ^ bits) for i in range(REPS)])
@@ -494,27 +499,28 @@
     def token_block(d):
         return pl.BlockSpec((TOK, 2 * ROWS), lambda c, s: (0, ((s[0] >> 1) + d) & 3))
 
-    mixed, new_weight = pl.pallas_call(
+    mixed, new_weight, base_sum = pl.pallas_call(
         forward_own_kernel,
         grid_spec=pltpu.PrefetchScalarGridSpec(
             num_scalar_prefetch=1,
             grid=(1,),
-            in_specs=[token_block(0), whole(TOK + PICKS, KV), pair_spec, whole(ROWS, KV)] + BASIS,
-            out_specs=[whole(KV, TOK), whole(ROWS, KV)],
+            in_specs=[token_block(0)] + [whole(TOK + PICKS, KV)] * 4 + [pair_spec, whole(ROWS, KV)] + BASIS,
+            out_specs=[whole(KV, TOK), whole(ROWS, KV), whole(TOK, KV)],
             scratch_shapes=[DENSE, PAIRS, VALUES],
         ),
-        out_shape=[shape(KV, TOK, dtype=F32), shape(ROWS, KV)],
-        compiler_params=params(),
+        out_shape=[shape(KV, TOK, dtype=F32), shape(ROWS, KV), shape(TOK, KV, dtype=F32)],
+        compiler_params=params(2 * VMEM_LIMIT),
         cost_estimate=cost(3 * KV * KV * ROWS, 4),
-    )(place, tokens, base, pair, weight, high, low)
-
+    )(place, tokens, base, base_hi, base_far, base_lo, pair, weight, high, low)
+
+    tail = pl.BlockSpec((PICKS, KV), lambda c, *_: (TOK // PICKS, 0))
     mixed = pl.pallas_call(
         forward_near_kernel,
         grid_spec=pltpu.PrefetchScalarGridSpec(
             num_scalar_prefetch=1,
             grid=(1,),
             in_specs=[token_block(1), token_block(3)]
-            + [whole(TOK + PICKS, KV)] * 2
+            + [tail] * 2
             + [pair_spec] * 2
             + [whole(KV, TOK)],
             out_specs=whole(KV, TOK),
@@ -530,9 +536,7 @@
         grid_spec=pltpu.PrefetchScalarGridSpec(
             num_scalar_prefetch=1,
             grid=(1,),
-            in_specs=[token_block(2)]
-            + [whole(TOK + PICKS, KV)] * 4
-            + [pair_spec, whole(KV, TOK)]
+            in_specs=[token_block(2), whole(TOK, KV), tail, pair_spec, whole(KV, TOK)]
             + BASIS,
             out_specs=whole(TOK, KV),
             scratch_shapes=[DENSE, PAIRS, VALUES, pltpu.VMEM((KV, TOK), F32)],
@@ -540,7 +544,7 @@
         out_shape=shape(TOK, KV),
         compiler_params=params(2 * VMEM_LIMIT),
         cost_estimate=cost(3 * KV * KV * ROWS, 5),
-    )(place, tokens, base, base_hi, base_far, base_lo, pair_far, mixed, high, low)
+    )(place, tokens, base_sum, base_far, pair_far, mixed, high, low)
     return (projected, new_weight, new_momentum[None])
 
 

time: 124 us -> 126 us (1.016)
  Pallas kernels: 26 us -> 27.5 us
    pallas_call x1, Pallas kernels: 3.5 us -> 6.14 us  [body(): pl.pallas_call(pick_kernel, grid_spec=pltpu.PrefetchScalarGridSpec(num_sc...]
    pallas_call x1 -> x0, Pallas kernels: 2.27 us -> none  [body(): pl.pallas_call(own_kernel, grid=(STEPS,), in_specs=[first_half(GROUP, 2 *...]
  transfers between devices with their start and end apart: 26 -> 26, of which waited for: 14 -> 14; matrix products, arithmetic and copies ran while one was open for 0% -> 0% of each run, Pallas kernels for 17% -> 18%
where the time goes in v10:
time: 126 us; the launch traced here: 125 us
  starting transfers between devices  49.2 us (39%)
  waiting for transfers between devices  45.1 us (36%)
  Pallas kernels  27.5 us (22%)
  local copies, waits for them, and re-layouts  2.66 us (2%)
    ppermute x6, starting transfers between devices, partner(): return lax.ppermute(x, 'rep', [(i, i ^ bits) for i in range(REPS)])  23.5 us
    ppermute x5, waiting for transfers between devices, up(): return lax.ppermute(x, 'fsdp', [(i, (i + 2) % 8) for i in range(8)])  17 us
    ppermute x5, waiting for transfers between devices, across(): return lax.ppermute(x, 'fsdp', [(i, (i + 4) % 8) for i in range(8)])  12.5 us
    ppermute x5, starting transfers between devices, down(): return lax.ppermute(x, 'fsdp', [(i, (i + 6) % 8) for i in range(8)])  11.6 us
    ppermute x6, waiting for transfers between devices, partner(): return lax.ppermute(x, 'rep', [(i, i ^ bits) for i in range(REPS)])  6.99 us
    ppermute x5, waiting for transfers between devices, down(): return lax.ppermute(x, 'fsdp', [(i, (i + 6) % 8) for i in range(8)])  6.34 us
    pallas_call x1, Pallas kernels, body(): pl.pallas_call(pick_kernel, grid_spec=pltpu.PrefetchScalarGridSpec(num_sc...  6.14 us
    ppermute x5, starting transfers between devices, across(): return lax.ppermute(x, 'fsdp', [(i, (i + 4) % 8) for i in range(8)])  5.26 us
  transfers between devices with their start and end apart: 26, of which 14 were waited for; matrix products, arithmetic and copies ran while one was open for 0% of the time, Pallas kernels for 18%

profile of v10, /device:TPU:1, one launch (start us, length us, event | category | flops | bytes accessed | tf_op | source)
XLA Modules:
  0.0 125.4 jit_solution(8650407649476660108)
XLA Ops:
  0.6 2.1 %collective-permute-start.8 = (bf16[512,1024]{1,0:T(8,128)(2,1)}, bf16[512,1024]{1,0:T(8,128)(2,1)S(1)}, u32[]{:S(2)}, u32[]{:S(2)}) collective-permute-start(bf16[512,1024]{1,0:T(8,128)(2,1)} %weight.1), channel_id=1, source_target_pairs={{0,1},{1,0},{2,3},{3,2},{4,5},{5,4},{6,7},{7,6},{8,9},{9,8},{10,11... | collective-permute-start | bytes 3145736 | tf_op jit(solution)/shard_map/ppermute | solution.py:340
  10.6 9.2 %collective-permute-done.late_lo.lo.p3.a3 = bf16[512,512]{1,0:T(8,128)(2,1)S(1)} collective-permute-done((bf16[512,512]{1,0:T(8,128)(2,1)S(1)}, bf16[512,512]{1,0:T(8,128)(2,1)S(1)}, u32[]{:S(2)}, u32[]{:S(2)}) %collective-permute-start) | collective-permute-done | bytes 524320 | tf_op jit(solution)/shard_map/ppermute | solution.py:331
  19.9 12.5 %collective-permute-done.7.far.p2.a2 = bf16[512,512]{1,0:T(8,128)(2,1)S(1)} collective-permute-done((bf16[512,512]{1,0:T(8,128)(2,1)S(1)}, bf16[512,512]{1,0:T(8,128)(2,1)S(1)}, u32[]{:S(2)}, u32[]{:S(2)}) %collective-permute-start.7) | collective-permute-done | bytes 524320 | tf_op jit(solution)/shard_map/ppermute | solution.py:337
  34.0 2.1 %collective-permute-start.3 = (bf16[512,256]{1,0:T(8,128)(2,1)S(1)}, bf16[512,256]{1,0:T(8,128)(2,1)S(1)}, u32[]{:S(2)}, u32[]{:S(2)}) collective-permute-start(bf16[512,256]{1,0:T(8,128)(2,1)S(1)} %shard_map.86.turned.c0.b0), channel_id=1, source_target_pairs={{0,6},{1,7},{2,0},{3,1},{4,2},{5,3},{6,4},{7,5},{8,14},{9,15},{10,... | collective-permute-start | bytes 786440 | tf_op jit(solution)/shard_map/ppermute | solution.py:334
  36.2 4.2 %collective-permute-done.2.late_lo.c3.b3 = bf16[512,256]{1,0:T(8,128)(2,1)S(1)} collective-permute-done((bf16[512,256]{1,0:T(8,128)(2,1)S(1)}, bf16[512,256]{1,0:T(8,128)(2,1)S(1)}, u32[]{:S(2)}, u32[]{:S(2)}) %collective-permute-start.2) | collective-permute-done | bytes 262176 | tf_op jit(solution)/shard_map/ppermute | solution.py:331
  42.1 4.0 %collective-permute-start.4 = (bf16[256,512]{1,0:T(8,128)(2,1)S(1)}, bf16[256,512]{1,0:T(8,128)(2,1)S(1)}, u32[]{:S(2)}, u32[]{:S(2)}) collective-permute-start(bf16[256,512]{1,0:T(8,128)(2,1)S(1)} %get-tuple-element.27), channel_id=1, source_target_pairs={{0,6},{1,7},{2,0},{3,1},{4,2},{5,3},{6,4},{7,5},{8,14},{9,15},{10,... | collective-permute-start | bytes 786440 | tf_op jit(solution)/shard_map/ppermute | solution.py:334
  48.8 4.5 %collective-permute-done.4.o1.t1 = bf16[256,512]{1,0:T(8,128)(2,1)S(1)} collective-permute-done((bf16[256,512]{1,0:T(8,128)(2,1)S(1)}, bf16[256,512]{1,0:T(8,128)(2,1)S(1)}, u32[]{:S(2)}, u32[]{:S(2)}) %collective-permute-start.4) | collective-permute-done | bytes 262176 | tf_op jit(solution)/shard_map/ppermute | solution.py:334
  53.3 2.6 %collective-permute-done.6.o3.t3 = bf16[256,512]{1,0:T(8,128)(2,1)S(1)} collective-permute-done((bf16[256,512]{1,0:T(8,128)(2,1)S(1)}, bf16[256,512]{1,0:T(8,128)(2,1)S(1)}, u32[]{:S(2)}, u32[]{:S(2)}) %collective-permute-start.6) | collective-permute-done | bytes 262176 | tf_op jit(solution)/shard_map/ppermute | solution.py:331
  56.0 4.1 %shard_map.89 = (bf16[320,1024]{1,0:T(8,128)(2,1)S(1)}, bf16[320,1024]{1,0:T(8,128)(2,1)S(1)}, bf16[320,1024]{1,0:T(8,128)(2,1)S(1)}, bf16[320,1024]{1,0:T(8,128)(2,1)S(1)}) custom-call(s32[2]{0:T(128)S(1)} %pad_add_fusion.where, bf16[256,512]{1,0:T(8,128)(2,1)S(1)} %get-tuple-element.26.o0.t0, bf16[256,512]{1,0:T(8,128)(2,1)S(1)} %collective-permute-done.4.o1.t1, ...), custom_call_target="tpu_custom_call" | custom-call | flops 2147483648 | bytes 7340032 | tf_op jit(solution)/shard_map/pallas_call | solution.py:411
  60.1 2.5 %collective-permute-start.10 = (bf16[320,1024]{1,0:T(8,128)(2,1)S(1)}, bf16[320,1024]{1,0:T(8,128)(2,1)S(1)}, u32[]{:S(2)}, u32[]{:S(2)}) collective-permute-start(bf16[320,1024]{1,0:T(8,128)(2,1)S(1)} %get-tuple-element.33), channel_id=1, source_target_pairs={{0,6},{1,7},{2,0},{3,1},{4,2},{5,3},{6,4},{7,5},{8,14},{9,15},{10,... | collective-permute-start | bytes 1966088 | tf_op jit(solution)/shard_map/ppermute | solution.py:334
  63.3 6.1 %shard_map.91 = (f32[1024,512]{1,0:T(8,128)S(1)}, f32[64,512]{1,0:T(8,128)S(1)}, f32[16,8,128]{2,1,0:T(8,128)S(1)}, f32[16,8,128]{2,1,0:T(8,128)S(1)}) custom-call(s32[2]{0:T(128)S(1)} %pad_add_fusion.where, bf16[512,512]{1,0:T(8,128)(2,1)S(1)} %get-tuple-element.24.sent.a0, bf16[512,512]{1,0:T(8,128)(2,1)S(1)} %collective-permute-done.1.late_hi.hi.p1.a1, ...), custom_call_target="tpu_custom_call" | custom-call | flops 1073741824 | bytes 12582912 | tf_op jit(solution)/shard_map/pallas_call | solution.py:431
  69.4 5.7 %collective-permute-start.15 = (f32[16,8,128]{2,1,0:T(8,128)S(1)}, f32[16,8,128]{2,1,0:T(8,128)S(1)}, u32[]{:S(2)}, u32[]{:S(2)}) collective-permute-start(f32[16,8,128]{2,1,0:T(8,128)S(1)} %get-tuple-element.37), channel_id=1, source_target_pairs={{0,8},{8,0},{16,24},{24,16},{32,40},{40,32},{48,56},{56,48},{64,72... | collective-permute-start | bytes 196616 | tf_op jit(solution)/shard_map/ppermute | solution.py:452
  76.0 2.8 %collective-permute-start.16 = (f32[16,8,128]{2,1,0:T(8,128)S(1)}, f32[16,8,128]{2,1,0:T(8,128)S(1)}, u32[]{:S(2)}, u32[]{:S(2)}) collective-permute-start(f32[16,8,128]{2,1,0:T(8,128)S(1)} %shard_map.92.a), channel_id=1, source_target_pairs={{0,16},{8,24},{16,0},{24,8},{32,48},{40,56},{48,32},{56,40},{64,80... | collective-permute-start | bytes 196616 | tf_op jit(solution)/shard_map/ppermute | solution.py:452
  78.8 2.2 %collective-permute-done.16.b = f32[16,8,128]{2,1,0:T(8,128)S(1)} collective-permute-done((f32[16,8,128]{2,1,0:T(8,128)S(1)}, f32[16,8,128]{2,1,0:T(8,128)S(1)}, u32[]{:S(2)}, u32[]{:S(2)}) %collective-permute-start.16) | collective-permute-done | bytes 65568 | tf_op jit(solution)/shard_map/ppermute | solution.py:452
  82.8 2.0 %collective-permute-done.17.b = f32[16,8,128]{2,1,0:T(8,128)S(1)} collective-permute-done((f32[16,8,128]{2,1,0:T(8,128)S(1)}, f32[16,8,128]{2,1,0:T(8,128)S(1)}, u32[]{:S(2)}, u32[]{:S(2)}) %collective-permute-start.17) | collective-permute-done | bytes 65568 | tf_op jit(solution)/shard_map/ppermute | solution.py:452
  84.7 3.1 %collective-permute-start.18 = (f32[16,8,128]{2,1,0:T(8,128)S(1)}, f32[16,8,128]{2,1,0:T(8,128)S(1)}, u32[]{:S(2)}, u32[]{:S(2)}) collective-permute-start(f32[16,8,128]{2,1,0:T(8,128)S(1)} %shard_map.94.a), channel_id=1, source_target_pairs={{0,64},{8,72},{16,80},{24,88},{32,96},{40,104},{48,112},{56,120},{... | collective-permute-start | bytes 196616 | tf_op jit(solution)/shard_map/ppermute | solution.py:452
  87.8 2.0 %collective-permute-done.18.b = f32[16,8,128]{2,1,0:T(8,128)S(1)} collective-permute-done((f32[16,8,128]{2,1,0:T(8,128)S(1)}, f32[16,8,128]{2,1,0:T(8,128)S(1)}, u32[]{:S(2)}, u32[]{:S(2)}) %collective-permute-start.18) | collective-permute-done | bytes 65568 | tf_op jit(solution)/shard_map/ppermute | solution.py:452
  89.8 6.9 %collective-permute-start.19 = (f32[16,8,128]{2,1,0:T(8,128)S(1)}, f32[16,8,128]{2,1,0:T(8,128)S(1)}, u32[]{:S(2)}, u32[]{:S(2)}) collective-permute-start(f32[16,8,128]{2,1,0:T(8,128)S(1)} %shard_map.95.late.a), channel_id=1, source_target_pairs={{0,128},{8,136},{16,144},{24,152},{32,160},{40,168},{48,176},{56,1... | collective-permute-start | bytes 196616 | tf_op jit(solution)/shard_map/ppermute | solution.py:452
  96.7 3.7 %shard_map.96 = (f32[512,1024]{1,0:T(8,128)}, f32[8,128]{1,0:T(8,128)S(1)}) custom-call(f32[1024,512]{1,0:T(8,128)S(1)} %get-tuple-element.38.moment, f32[64,512]{1,0:T(8,128)S(1)} %get-tuple-element.39.picked, s32[16,4,512]{2,1,0:T(4,128)S(1)} %bitcast.9, bf16[256,256]{1,0:T(8,128)(2,1)S(1)} %copy-done.6, bf16[256,256]{1,0:T(8,128)(2,1)S(1)} %copy-done.7, ...), custom_call_target="tpu_custom_call" | custom-call | flops 805306368 | bytes 5242880 | tf_op jit(solution)/shard_map/pallas_call | solution.py:472
  100.4 3.3 %collective-permute-start.20 = (bf16[16,8,128]{2,1,0:T(8,128)(2,1)S(1)}, bf16[16,8,128]{2,1,0:T(8,128)(2,1)S(1)}, u32[]{:S(2)}, u32[]{:S(2)}) collective-permute-start(bf16[16,8,128]{2,1,0:T(8,128)(2,1)S(1)} %shard_map.97.half), channel_id=1, source_target_pairs={{0,8},{8,0},{16,24},{24,16},{32,40},{40,32},{48,56},{56,48},{64,72... | collective-permute-start | bytes 98312 | tf_op jit(solution)/shard_map/ppermute | solution.py:452
  108.8 3.2 %collective-permute-start.23 = (bf16[2,32,8,128]{3,2,1,0:T(8,128)(2,1)S(1)}, bf16[2,32,8,128]{3,2,1,0:T(8,128)(2,1)S(1)}, u32[]{:S(2)}, u32[]{:S(2)}) collective-permute-start(bf16[2,32,8,128]{3,2,1,0:T(8,128)(2,1)S(1)} %shard_map.98.tot), channel_id=1, source_target_pairs={{0,4},{1,5},{2,6},{3,7},{4,0},{5,1},{6,2},{7,3},{8,12},{9,13},{10,... | collective-permute-start | bytes 393224 | tf_op jit(solution)/shard_map/ppermute | solution.py:337
  113.6 3.3 %shard_map.99 = (f32[1024,256]{1,0:T(8,128)S(1)}, bf16[512,1024]{1,0:T(8,128)(2,1)}, f32[256,1024]{1,0:T(8,128)S(1)}) custom-call(s32[2]{0:T(128)S(1)} %pad_add_fusion.where, bf16[256,4096]{1,0:T(8,128)(2,1)S(1)} %copy-done.1, bf16[320,1024]{1,0:T(8,128)(2,1)S(1)} %get-tuple-element.32.late.own, bf16[320,1024]{1,0:T(8,128)(2,1)S(1)} %collective-permute-done.10.late_1.hi, ...), custom_call_target="tpu_custom_call" | custom-call | flops 1610612736 | bytes 4194304 | tf_op jit(solution)/shard_map/pallas_call | solution.py:502
  118.6 3.3 %shard_map.100.before = f32[1024,256]{1,0:T(8,128)S(1)} custom-call(s32[2]{0:T(128)S(1)} %pad_add_fusion.where, bf16[256,4096]{1,0:T(8,128)(2,1)S(1)} %copy-done.1, bf16[256,4096]{1,0:T(8,128)(2,1)S(1)} %copy-done.1, bf16[320,1024]{1,0:T(8,128)(2,1)S(1)} %collective-permute-done.10.late_1.hi, bf16[320,1024]{1,0:T(8,128)(2,1)S(1)} %collective-permute-done.12.late_0.lo, ...), custom_call_target="tpu_custom_call" | custom-call | flops 2147483648 | bytes 5242880 | tf_op jit(solution)/shard_map/pallas_call | solution.py:517
  121.9 3.5 %shard_map.101 = bf16[256,1024]{1,0:T(8,128)(2,1)} custom-call(s32[2]{0:T(128)S(1)} %pad_add_fusion.where, bf16[256,4096]{1,0:T(8,128)(2,1)S(1)} %copy-done.1, f32[256,1024]{1,0:T(8,128)S(1)} %get-tuple-element.41.base, bf16[320,1024]{1,0:T(8,128)(2,1)S(1)} %collective-permute-done.11.late_2.far, bf16[2,32,8,128]{3,2,1,0:T(8,128)(2,1)S(1)} %collective-permute-done.23.tot, ...), custom_call_target="tpu_custom_call" | custom-call | flops 1610612736 | bytes 5242880 | tf_op jit(solution)/shard_map/pallas_call | solution.py:534
  (62 shorter events, 25.9 us)
Async XLA Ops:
  0.6 31.8 %collective-permute-start.8 = (bf16[512,1024]{1,0:T(8,128)(2,1)}, bf16[512,1024]{1,0:T(8,128)(2,1)S(1)}, u32[]{:S(2)}, u32[]{:S(2)}) collective-permute-start(bf16[512,1024]{1,0:T(8,128)(2,1)} %weight.1), channel_id=1, source_target_pairs={{0,1},{1,0},{2,3},{3,2},{4,5},{5,4},{6,7},{7,6},{8,9},{9,8},{10,11... | collective-permute-start | bytes 3145736 | tf_op jit(solution)/shard_map/ppermute | solution.py:340
  6.2 13.6 %collective-permute-start = (bf16[512,512]{1,0:T(8,128)(2,1)S(1)}, bf16[512,512]{1,0:T(8,128)(2,1)S(1)}, u32[]{:S(2)}, u32[]{:S(2)}) collective-permute-start(bf16[512,512]{1,0:T(8,128)(2,1)S(1)} %get-tuple-element.24.sent.a0), channel_id=1, source_target_pairs={{0,2},{1,3},{2,4},{3,5},{4,6},{5,7},{6,0},{7,1},{8,10},{9,11},{10,... | collective-permute-start | bytes 1572872 | tf_op jit(solution)/shard_map/ppermute | solution.py:331
  7.5 12.2 %collective-permute-start.1 = (bf16[512,512]{1,0:T(8,128)(2,1)S(1)}, bf16[512,512]{1,0:T(8,128)(2,1)S(1)}, u32[]{:S(2)}, u32[]{:S(2)}) collective-permute-start(bf16[512,512]{1,0:T(8,128)(2,1)S(1)} %get-tuple-element.25), channel_id=1, source_target_pairs={{0,6},{1,7},{2,0},{3,1},{4,2},{5,3},{6,4},{7,5},{8,14},{9,15},{10,... | collective-permute-start | bytes 1572872 | tf_op jit(solution)/shard_map/ppermute | solution.py:334
  9.1 23.3 %collective-permute-start.7 = (bf16[512,512]{1,0:T(8,128)(2,1)S(1)}, bf16[512,512]{1,0:T(8,128)(2,1)S(1)}, u32[]{:S(2)}, u32[]{:S(2)}) collective-permute-start(bf16[512,512]{1,0:T(8,128)(2,1)S(1)} %get-tuple-element.31), channel_id=1, source_target_pairs={{0,4},{1,5},{2,6},{3,7},{4,0},{5,1},{6,2},{7,3},{8,12},{9,13},{10,... | collective-permute-start | bytes 1572872 | tf_op jit(solution)/shard_map/ppermute | solution.py:337
  33.1 22.8 %collective-permute-start.9 = (bf16[576,512]{1,0:T(8,128)(2,1)S(1)}, bf16[576,512]{1,0:T(8,128)(2,1)S(1)}, u32[]{:S(2)}, u32[]{:S(2)}) collective-permute-start(bf16[576,512]{1,0:T(8,128)(2,1)S(1)} %shard_map.88), channel_id=1, source_target_pairs={{0,1},{1,0},{2,3},{3,2},{4,5},{5,4},{6,7},{7,6},{8,9},{9,8},{10,11... | collective-permute-start | bytes 1769480 | tf_op jit(solution)/shard_map/ppermute | solution.py:340
  33.5 6.9 %collective-permute-start.2 = (bf16[512,256]{1,0:T(8,128)(2,1)S(1)}, bf16[512,256]{1,0:T(8,128)(2,1)S(1)}, u32[]{:S(2)}, u32[]{:S(2)}) collective-permute-start(bf16[512,256]{1,0:T(8,128)(2,1)S(1)} %shard_map.86.turned.c0.b0), channel_id=1, source_target_pairs={{0,2},{1,3},{2,4},{3,5},{4,6},{5,7},{6,0},{7,1},{8,10},{9,11},{10,... | collective-permute-start | bytes 786440 | tf_op jit(solution)/shard_map/ppermute | solution.py:331
  34.0 7.4 %collective-permute-start.3 = (bf16[512,256]{1,0:T(8,128)(2,1)S(1)}, bf16[512,256]{1,0:T(8,128)(2,1)S(1)}, u32[]{:S(2)}, u32[]{:S(2)}) collective-permute-start(bf16[512,256]{1,0:T(8,128)(2,1)S(1)} %shard_map.86.turned.c0.b0), channel_id=1, source_target_pairs={{0,6},{1,7},{2,0},{3,1},{4,2},{5,3},{6,4},{7,5},{8,14},{9,15},{10,... | collective-permute-start | bytes 786440 | tf_op jit(solution)/shard_map/ppermute | solution.py:334
  36.2 10.6 %collective-permute-start.13 = (bf16[512,256]{1,0:T(8,128)(2,1)S(1)}, bf16[512,256]{1,0:T(8,128)(2,1)S(1)}, u32[]{:S(2)}, u32[]{:S(2)}) collective-permute-start(bf16[512,256]{1,0:T(8,128)(2,1)S(1)} %shard_map.86.turned.c0.b0), channel_id=1, source_target_pairs={{0,4},{1,5},{2,6},{3,7},{4,0},{5,1},{6,2},{7,3},{8,12},{9,13},{10,... | collective-permute-start | bytes 786440 | tf_op jit(solution)/shard_map/ppermute | solution.py:337
  42.1 11.2 %collective-permute-start.4 = (bf16[256,512]{1,0:T(8,128)(2,1)S(1)}, bf16[256,512]{1,0:T(8,128)(2,1)S(1)}, u32[]{:S(2)}, u32[]{:S(2)}) collective-permute-start(bf16[256,512]{1,0:T(8,128)(2,1)S(1)} %get-tuple-element.27), channel_id=1, source_target_pairs={{0,6},{1,7},{2,0},{3,1},{4,2},{5,3},{6,4},{7,5},{8,14},{9,15},{10,... | collective-permute-start | bytes 786440 | tf_op jit(solution)/shard_map/ppermute | solution.py:334
  46.1 7.2 %collective-permute-start.5 = (bf16[256,512]{1,0:T(8,128)(2,1)S(1)}, bf16[256,512]{1,0:T(8,128)(2,1)S(1)}, u32[]{:S(2)}, u32[]{:S(2)}) collective-permute-start(bf16[256,512]{1,0:T(8,128)(2,1)S(1)} %get-tuple-element.28), channel_id=1, source_target_pairs={{0,4},{1,5},{2,6},{3,7},{4,0},{5,1},{6,2},{7,3},{8,12},{9,13},{10,... | collective-permute-start | bytes 786440 | tf_op jit(solution)/shard_map/ppermute | solution.py:337
  46.1 9.8 %collective-permute-start.6 = (bf16[256,512]{1,0:T(8,128)(2,1)S(1)}, bf16[256,512]{1,0:T(8,128)(2,1)S(1)}, u32[]{:S(2)}, u32[]{:S(2)}) collective-permute-start(bf16[256,512]{1,0:T(8,128)(2,1)S(1)} %get-tuple-element.29), channel_id=1, source_target_pairs={{0,2},{1,3},{2,4},{3,5},{4,6},{5,7},{6,0},{7,1},{8,10},{9,11},{10,... | collective-permute-start | bytes 786440 | tf_op jit(solution)/shard_map/ppermute | solution.py:331
  47.5 15.7 %collective-permute-start.14 = (bf16[512,512]{1,0:T(8,128)(2,1)S(1)}, bf16[512,512]{1,0:T(8,128)(2,1)S(1)}, u32[]{:S(2)}, u32[]{:S(2)}) collective-permute-start(bf16[512,512]{1,0:T(8,128)(2,1)S(1)} %shard_map.90), channel_id=1, source_target_pairs={{0,1},{1,0},{2,3},{3,2},{4,5},{5,4},{6,7},{7,6},{8,9},{9,8},{10,11... | collective-permute-start | bytes 1572872 | tf_op jit(solution)/shard_map/ppermute | solution.py:340
  60.1 48.2 %collective-permute-start.10 = (bf16[320,1024]{1,0:T(8,128)(2,1)S(1)}, bf16[320,1024]{1,0:T(8,128)(2,1)S(1)}, u32[]{:S(2)}, u32[]{:S(2)}) collective-permute-start(bf16[320,1024]{1,0:T(8,128)(2,1)S(1)} %get-tuple-element.33), channel_id=1, source_target_pairs={{0,6},{1,7},{2,0},{3,1},{4,2},{5,3},{6,4},{7,5},{8,14},{9,15},{10,... | collective-permute-start | bytes 1966088 | tf_op jit(solution)/shard_map/ppermute | solution.py:334
  62.6 45.7 %collective-permute-start.11 = (bf16[320,1024]{1,0:T(8,128)(2,1)S(1)}, bf16[320,1024]{1,0:T(8,128)(2,1)S(1)}, u32[]{:S(2)}, u32[]{:S(2)}) collective-permute-start(bf16[320,1024]{1,0:T(8,128)(2,1)S(1)} %get-tuple-element.34), channel_id=1, source_target_pairs={{0,4},{1,5},{2,6},{3,7},{4,0},{5,1},{6,2},{7,3},{8,12},{9,13},{10,... | collective-permute-start | bytes 1966088 | tf_op jit(solution)/shard_map/ppermute | solution.py:337
  63.1 45.2 %collective-permute-start.12 = (bf16[320,1024]{1,0:T(8,128)(2,1)S(1)}, bf16[320,1024]{1,0:T(8,128)(2,1)S(1)}, u32[]{:S(2)}, u32[]{:S(2)}) collective-permute-start(bf16[320,1024]{1,0:T(8,128)(2,1)S(1)} %get-tuple-element.35), channel_id=1, source_target_pairs={{0,2},{1,3},{2,4},{3,5},{4,6},{5,7},{6,0},{7,1},{8,10},{9,11},{10,... | collective-permute-start | bytes 1966088 | tf_op jit(solution)/shard_map/ppermute | solution.py:331
  69.4 6.6 %collective-permute-start.15 = (f32[16,8,128]{2,1,0:T(8,128)S(1)}, f32[16,8,128]{2,1,0:T(8,128)S(1)}, u32[]{:S(2)}, u32[]{:S(2)}) collective-permute-start(f32[16,8,128]{2,1,0:T(8,128)S(1)} %get-tuple-element.37), channel_id=1, source_target_pairs={{0,8},{8,0},{16,24},{24,16},{32,40},{40,32},{48,56},{56,48},{64,72... | collective-permute-start | bytes 196616 | tf_op jit(solution)/shard_map/ppermute | solution.py:452
  76.0 5.0 %collective-permute-start.16 = (f32[16,8,128]{2,1,0:T(8,128)S(1)}, f32[16,8,128]{2,1,0:T(8,128)S(1)}, u32[]{:S(2)}, u32[]{:S(2)}) collective-permute-start(f32[16,8,128]{2,1,0:T(8,128)S(1)} %shard_map.92.a), channel_id=1, source_target_pairs={{0,16},{8,24},{16,0},{24,8},{32,48},{40,56},{48,32},{56,40},{64,80... | collective-permute-start | bytes 196616 | tf_op jit(solution)/shard_map/ppermute | solution.py:452
  81.0 3.7 %collective-permute-start.17 = (f32[16,8,128]{2,1,0:T(8,128)S(1)}, f32[16,8,128]{2,1,0:T(8,128)S(1)}, u32[]{:S(2)}, u32[]{:S(2)}) collective-permute-start(f32[16,8,128]{2,1,0:T(8,128)S(1)} %shard_map.93.a), channel_id=1, source_target_pairs={{0,32},{8,40},{16,48},{24,56},{32,0},{40,8},{48,16},{56,24},{64,96... | collective-permute-start | bytes 196616 | tf_op jit(solution)/shard_map/ppermute | solution.py:452
  84.7 5.0 %collective-permute-start.18 = (f32[16,8,128]{2,1,0:T(8,128)S(1)}, f32[16,8,128]{2,1,0:T(8,128)S(1)}, u32[]{:S(2)}, u32[]{:S(2)}) collective-permute-start(f32[16,8,128]{2,1,0:T(8,128)S(1)} %shard_map.94.a), channel_id=1, source_target_pairs={{0,64},{8,72},{16,80},{24,88},{32,96},{40,104},{48,112},{56,120},{... | collective-permute-start | bytes 196616 | tf_op jit(solution)/shard_map/ppermute | solution.py:452
  89.8 10.6 %collective-permute-start.19 = (f32[16,8,128]{2,1,0:T(8,128)S(1)}, f32[16,8,128]{2,1,0:T(8,128)S(1)}, u32[]{:S(2)}, u32[]{:S(2)}) collective-permute-start(f32[16,8,128]{2,1,0:T(8,128)S(1)} %shard_map.95.late.a), channel_id=1, source_target_pairs={{0,128},{8,136},{16,144},{24,152},{32,160},{40,168},{48,176},{56,1... | collective-permute-start | bytes 196616 | tf_op jit(solution)/shard_map/ppermute | solution.py:452
  100.4 4.5 %collective-permute-start.20 = (bf16[16,8,128]{2,1,0:T(8,128)(2,1)S(1)}, bf16[16,8,128]{2,1,0:T(8,128)(2,1)S(1)}, u32[]{:S(2)}, u32[]{:S(2)}) collective-permute-start(bf16[16,8,128]{2,1,0:T(8,128)(2,1)S(1)} %shard_map.97.half), channel_id=1, source_target_pairs={{0,8},{8,0},{16,24},{24,16},{32,40},{40,32},{48,56},{56,48},{64,72... | collective-permute-start | bytes 98312 | tf_op jit(solution)/shard_map/ppermute | solution.py:452
  108.8 13.0 %collective-permute-start.23 = (bf16[2,32,8,128]{3,2,1,0:T(8,128)(2,1)S(1)}, bf16[2,32,8,128]{3,2,1,0:T(8,128)(2,1)S(1)}, u32[]{:S(2)}, u32[]{:S(2)}) collective-permute-start(bf16[2,32,8,128]{3,2,1,0:T(8,128)(2,1)S(1)} %shard_map.98.tot), channel_id=1, source_target_pairs={{0,4},{1,5},{2,6},{3,7},{4,0},{5,1},{6,2},{7,3},{8,12},{9,13},{10,... | collective-permute-start | bytes 393224 | tf_op jit(solution)/shard_map/ppermute | solution.py:337
  112.0 5.6 %collective-permute-start.24 = (bf16[2,32,8,128]{3,2,1,0:T(8,128)(2,1)S(1)}, bf16[2,32,8,128]{3,2,1,0:T(8,128)(2,1)S(1)}, u32[]{:S(2)}, u32[]{:S(2)}) collective-permute-start(bf16[2,32,8,128]{3,2,1,0:T(8,128)(2,1)S(1)} %shard_map.98.tot), channel_id=1, source_target_pairs={{0,6},{1,7},{2,0},{3,1},{4,2},{5,3},{6,4},{7,5},{8,14},{9,15},{10,... | collective-permute-start | bytes 393224 | tf_op jit(solution)/shard_map/ppermute | solution.py:334
  113.6 5.0 %collective-permute-start.25 = (bf16[2,32,8,128]{3,2,1,0:T(8,128)(2,1)S(1)}, bf16[2,32,8,128]{3,2,1,0:T(8,128)(2,1)S(1)}, u32[]{:S(2)}, u32[]{:S(2)}) collective-permute-start(bf16[2,32,8,128]{3,2,1,0:T(8,128)(2,1)S(1)} %shard_map.98.tot), channel_id=1, source_target_pairs={{0,2},{1,3},{2,4},{3,5},{4,6},{5,7},{6,0},{7,1},{8,10},{9,11},{10,... | collective-permute-start | bytes 393224 | tf_op jit(solution)/shard_map/ppermute | solution.py:331
  (10 other events, 80.5 us)

commit v11 on v9

--- a/solution.py
+++ b/solution.py
@@ -56,17 +56,17 @@
     return dense
 
 
-def spread_row(row):
-    return jnp.broadcast_to(row, (PACK, LANES)).astype(jnp.bfloat16)
+def spread_row(row, dtype):
+    return jnp.broadcast_to(row, (PACK, LANES)).astype(dtype)
 
 
 def expand_tile(indices, values, dense, first, cols):
-    freq = lax.broadcasted_iota(jnp.int32, (PACK, LANES), 0).astype(jnp.float32)
+    freq = lax.broadcasted_iota(jnp.int32, (PACK, LANES), 0)
     for half in range(2):
-        at = [spread_row(indices(half * KEEP + j)) for j in range(KEEP)]
-        have = [spread_row(values(half * KEEP + j)) for j in range(KEEP)]
+        at = [spread_row(indices(half * KEEP + j), jnp.int16) for j in range(KEEP)]
+        have = [spread_row(values(half * KEEP + j), jnp.bfloat16) for j in range(KEEP)]
         for part in range(BLOCK // PACK):
-            here = (freq + part * PACK).astype(jnp.bfloat16)
+            here = (freq + part * PACK).astype(jnp.int16)
             tile = jnp.zeros((PACK, LANES), jnp.bfloat16)
             for j in range(KEEP):
                 tile = jnp.where(at[j] == here, have[j], tile)
@@ -227,7 +227,7 @@
 
 
 def forward_own_kernel(where, tok, own, tot, weight, ch, cl, mixed, out_weight, dense, pairs, values):
-    pairs[...] = own[TOK:, :].astype(jnp.float32)
+    pairs[...] = own[TOK:, :].astype(jnp.int32)
     values[...] = tot[...].astype(jnp.float32)
     cols = pl.ds(pl.multiple_of((where[0] & 1) * ROWS, ROWS), ROWS)
     for g in range(STEPS):
@@ -241,7 +241,7 @@
 
 
 def expand_all(near, tot, dense, pairs, values):
-    pairs[...] = near[TOK:, :].astype(jnp.float32)
+    pairs[...] = near[TOK:, :].astype(jnp.int32)
     values[...] = tot[...].astype(jnp.float32)
     for g in range(STEPS):
         expand_group(g, pairs, values, dense)
@@ -302,7 +302,7 @@
 MESSAGE = whole(HALF, 2 * TOK)
 PIECE = whole(TOK, ROWS)
 DENSE = pltpu.VMEM((KV, 2 * ROWS), BF16)
-PAIRS = pltpu.VMEM((PICKS, 2 * ROWS), F32)
+PAIRS = pltpu.VMEM((PICKS, 2 * ROWS), jnp.int32)
 VALUES = pltpu.VMEM((2, TILES, 8, LANES), F32)
 
 

time: 124 us -> 124 us (level)
  no operation moved by 1% of the time
where the time goes in v11:
time: 124 us
  starting transfers between devices  49.2 us (40%)
  waiting for transfers between devices  45.1 us (36%)
  Pallas kernels  26 us (21%)
  local copies, waits for them, and re-layouts  2.66 us (2%)
    ppermute x6, starting transfers between devices, partner(): return lax.ppermute(x, 'rep', [(i, i ^ bits) for i in range(REPS)])  23.5 us
    ppermute x5, waiting for transfers between devices, up(): return lax.ppermute(x, 'fsdp', [(i, (i + 2) % 8) for i in range(8)])  17 us
    ppermute x5, waiting for transfers between devices, across(): return lax.ppermute(x, 'fsdp', [(i, (i + 4) % 8) for i in range(8)])  12.5 us
    ppermute x5, starting transfers between devices, down(): return lax.ppermute(x, 'fsdp', [(i, (i + 6) % 8) for i in range(8)])  11.6 us
    ppermute x6, waiting for transfers between devices, partner(): return lax.ppermute(x, 'rep', [(i, i ^ bits) for i in range(REPS)])  6.98 us
    ppermute x5, waiting for transfers between devices, down(): return lax.ppermute(x, 'fsdp', [(i, (i + 6) % 8) for i in range(8)])  6.3 us
    ppermute x5, starting transfers between devices, across(): return lax.ppermute(x, 'fsdp', [(i, (i + 4) % 8) for i in range(8)])  5.08 us
    ppermute x4, starting transfers between devices, swap(): return lax.ppermute(x, 'fsdp', [(i, i ^ 1) for i in range(8)])  5.01 us
  transfers between devices with their start and end apart: 26, of which 14 were waited for; matrix products, arithmetic and copies ran while one was open for 0% of the time, Pallas kernels for 17%

profile of v11, /device:TPU:1, one launch (start us, length us, event | category | flops | bytes accessed | tf_op | source)
XLA Modules:
  0.0 123.9 jit_solution(9221840803715557269)
XLA Ops:
  0.6 2.1 %collective-permute-start.8 = (bf16[512,1024]{1,0:T(8,128)(2,1)}, bf16[512,1024]{1,0:T(8,128)(2,1)S(1)}, u32[]{:S(2)}, u32[]{:S(2)}) collective-permute-start(bf16[512,1024]{1,0:T(8,128)(2,1)} %weight.1), channel_id=1, source_target_pairs={{0,1},{1,0},{2,3},{3,2},{4,5},{5,4},{6,7},{7,6},{8,9},{9,8},{10,11... | collective-permute-start | bytes 3145736 | tf_op jit(solution)/shard_map/ppermute | solution.py:330
  10.6 9.2 %collective-permute-done.late_lo.lo.p3.a3 = bf16[512,512]{1,0:T(8,128)(2,1)S(1)} collective-permute-done((bf16[512,512]{1,0:T(8,128)(2,1)S(1)}, bf16[512,512]{1,0:T(8,128)(2,1)S(1)}, u32[]{:S(2)}, u32[]{:S(2)}) %collective-permute-start) | collective-permute-done | bytes 524320 | tf_op jit(solution)/shard_map/ppermute | solution.py:321
  19.9 12.5 %collective-permute-done.7.far.p2.a2 = bf16[512,512]{1,0:T(8,128)(2,1)S(1)} collective-permute-done((bf16[512,512]{1,0:T(8,128)(2,1)S(1)}, bf16[512,512]{1,0:T(8,128)(2,1)S(1)}, u32[]{:S(2)}, u32[]{:S(2)}) %collective-permute-start.7) | collective-permute-done | bytes 524320 | tf_op jit(solution)/shard_map/ppermute | solution.py:327
  34.0 2.1 %collective-permute-start.3 = (bf16[512,256]{1,0:T(8,128)(2,1)S(1)}, bf16[512,256]{1,0:T(8,128)(2,1)S(1)}, u32[]{:S(2)}, u32[]{:S(2)}) collective-permute-start(bf16[512,256]{1,0:T(8,128)(2,1)S(1)} %shard_map.86.turned.b0.c0), channel_id=1, source_target_pairs={{0,6},{1,7},{2,0},{3,1},{4,2},{5,3},{6,4},{7,5},{8,14},{9,15},{10,... | collective-permute-start | bytes 786440 | tf_op jit(solution)/shard_map/ppermute | solution.py:324
  36.2 4.2 %collective-permute-done.2.late_lo.b3.c3 = bf16[512,256]{1,0:T(8,128)(2,1)S(1)} collective-permute-done((bf16[512,256]{1,0:T(8,128)(2,1)S(1)}, bf16[512,256]{1,0:T(8,128)(2,1)S(1)}, u32[]{:S(2)}, u32[]{:S(2)}) %collective-permute-start.2) | collective-permute-done | bytes 262176 | tf_op jit(solution)/shard_map/ppermute | solution.py:321
  42.1 4.0 %collective-permute-start.4 = (bf16[256,512]{1,0:T(8,128)(2,1)S(1)}, bf16[256,512]{1,0:T(8,128)(2,1)S(1)}, u32[]{:S(2)}, u32[]{:S(2)}) collective-permute-start(bf16[256,512]{1,0:T(8,128)(2,1)S(1)} %get-tuple-element.26), channel_id=1, source_target_pairs={{0,6},{1,7},{2,0},{3,1},{4,2},{5,3},{6,4},{7,5},{8,14},{9,15},{10,... | collective-permute-start | bytes 786440 | tf_op jit(solution)/shard_map/ppermute | solution.py:324
  48.8 4.5 %collective-permute-done.4.o1.t1 = bf16[256,512]{1,0:T(8,128)(2,1)S(1)} collective-permute-done((bf16[256,512]{1,0:T(8,128)(2,1)S(1)}, bf16[256,512]{1,0:T(8,128)(2,1)S(1)}, u32[]{:S(2)}, u32[]{:S(2)}) %collective-permute-start.4) | collective-permute-done | bytes 262176 | tf_op jit(solution)/shard_map/ppermute | solution.py:324
  53.3 2.6 %collective-permute-done.6.o3.t3 = bf16[256,512]{1,0:T(8,128)(2,1)S(1)} collective-permute-done((bf16[256,512]{1,0:T(8,128)(2,1)S(1)}, bf16[256,512]{1,0:T(8,128)(2,1)S(1)}, u32[]{:S(2)}, u32[]{:S(2)}) %collective-permute-start.6) | collective-permute-done | bytes 262176 | tf_op jit(solution)/shard_map/ppermute | solution.py:321
  56.0 3.0 %shard_map.89 = (bf16[320,1024]{1,0:T(8,128)(2,1)S(1)}, bf16[320,1024]{1,0:T(8,128)(2,1)S(1)}, bf16[320,1024]{1,0:T(8,128)(2,1)S(1)}, bf16[320,1024]{1,0:T(8,128)(2,1)S(1)}) custom-call(s32[2]{0:T(128)S(1)} %pad_add_fusion.where, bf16[256,512]{1,0:T(8,128)(2,1)S(1)} %get-tuple-element.25.o0.t0, bf16[256,512]{1,0:T(8,128)(2,1)S(1)} %collective-permute-done.4.o1.t1, ...), custom_call_target="tpu_custom_call" | custom-call | flops 2147483648 | bytes 7340032 | tf_op jit(solution)/shard_map/pallas_call | solution.py:414
  58.9 2.5 %collective-permute-start.10 = (bf16[320,1024]{1,0:T(8,128)(2,1)S(1)}, bf16[320,1024]{1,0:T(8,128)(2,1)S(1)}, u32[]{:S(2)}, u32[]{:S(2)}) collective-permute-start(bf16[320,1024]{1,0:T(8,128)(2,1)S(1)} %get-tuple-element.32), channel_id=1, source_target_pairs={{0,6},{1,7},{2,0},{3,1},{4,2},{5,3},{6,4},{7,5},{8,14},{9,15},{10,... | collective-permute-start | bytes 1966088 | tf_op jit(solution)/shard_map/ppermute | solution.py:324
  62.3 2.3 %shard_map.90.pre = f32[1024,512]{1,0:T(8,128)S(1)} custom-call(bf16[512,512]{1,0:T(8,128)(2,1)S(1)} %get-tuple-element.23.sent.a0, bf16[512,512]{1,0:T(8,128)(2,1)S(1)} %collective-permute-done.1.late_hi.hi.p1.a1, bf16[512,512]{1,0:T(8,128)(2,1)S(1)} %collective-permute-done.7.far.p2.a2, bf16[512,512]{1,0:T(8,128)(2,1)S(1)} %collective-permute-done.late_lo.lo.p3.a3, ...), custom_call_target="tpu_custom_call" | custom-call | flops 1073741824 | bytes 7340032 | tf_op jit(solution)/shard_map/pallas_call | solution.py:401
  64.6 3.5 %shard_map.92 = (f32[1024,512]{1,0:T(8,128)S(1)}, f32[64,512]{1,0:T(8,128)S(1)}, f32[16,8,128]{2,1,0:T(8,128)S(1)}, f32[16,8,128]{2,1,0:T(8,128)S(1)}) custom-call(s32[2]{0:T(128)S(1)} %pad_add_fusion.where, f32[1024,512]{1,0:T(8,128)S(1)} %shard_map.90.pre, bf16[576,512]{1,0:T(8,128)(2,1)S(1)} %collective-permute-done.9.got_a, ...), custom_call_target="tpu_custom_call" | custom-call | flops 805306368 | bytes 6291456 | tf_op jit(solution)/shard_map/pallas_call | solution.py:433
  68.1 5.7 %collective-permute-start.15 = (f32[16,8,128]{2,1,0:T(8,128)S(1)}, f32[16,8,128]{2,1,0:T(8,128)S(1)}, u32[]{:S(2)}, u32[]{:S(2)}) collective-permute-start(f32[16,8,128]{2,1,0:T(8,128)S(1)} %get-tuple-element.36), channel_id=1, source_target_pairs={{0,8},{8,0},{16,24},{24,16},{32,40},{40,32},{48,56},{56,48},{64,72... | collective-permute-start | bytes 196616 | tf_op jit(solution)/shard_map/ppermute | solution.py:447
  74.7 2.8 %collective-permute-start.16 = (f32[16,8,128]{2,1,0:T(8,128)S(1)}, f32[16,8,128]{2,1,0:T(8,128)S(1)}, u32[]{:S(2)}, u32[]{:S(2)}) collective-permute-start(f32[16,8,128]{2,1,0:T(8,128)S(1)} %shard_map.93.a), channel_id=1, source_target_pairs={{0,16},{8,24},{16,0},{24,8},{32,48},{40,56},{48,32},{56,40},{64,80... | collective-permute-start | bytes 196616 | tf_op jit(solution)/shard_map/ppermute | solution.py:447
  77.5 2.2 %collective-permute-done.16.b = f32[16,8,128]{2,1,0:T(8,128)S(1)} collective-permute-done((f32[16,8,128]{2,1,0:T(8,128)S(1)}, f32[16,8,128]{2,1,0:T(8,128)S(1)}, u32[]{:S(2)}, u32[]{:S(2)}) %collective-permute-start.16) | collective-permute-done | bytes 65568 | tf_op jit(solution)/shard_map/ppermute | solution.py:447
  81.4 2.0 %collective-permute-done.17.b = f32[16,8,128]{2,1,0:T(8,128)S(1)} collective-permute-done((f32[16,8,128]{2,1,0:T(8,128)S(1)}, f32[16,8,128]{2,1,0:T(8,128)S(1)}, u32[]{:S(2)}, u32[]{:S(2)}) %collective-permute-start.17) | collective-permute-done | bytes 65568 | tf_op jit(solution)/shard_map/ppermute | solution.py:447
  83.4 3.1 %collective-permute-start.18 = (f32[16,8,128]{2,1,0:T(8,128)S(1)}, f32[16,8,128]{2,1,0:T(8,128)S(1)}, u32[]{:S(2)}, u32[]{:S(2)}) collective-permute-start(f32[16,8,128]{2,1,0:T(8,128)S(1)} %shard_map.95.a), channel_id=1, source_target_pairs={{0,64},{8,72},{16,80},{24,88},{32,96},{40,104},{48,112},{56,120},{... | collective-permute-start | bytes 196616 | tf_op jit(solution)/shard_map/ppermute | solution.py:447
  88.4 6.9 %collective-permute-start.19 = (f32[16,8,128]{2,1,0:T(8,128)S(1)}, f32[16,8,128]{2,1,0:T(8,128)S(1)}, u32[]{:S(2)}, u32[]{:S(2)}) collective-permute-start(f32[16,8,128]{2,1,0:T(8,128)S(1)} %shard_map.96.late.a), channel_id=1, source_target_pairs={{0,128},{8,136},{16,144},{24,152},{32,160},{40,168},{48,176},{56,1... | collective-permute-start | bytes 196616 | tf_op jit(solution)/shard_map/ppermute | solution.py:447
  95.3 3.7 %shard_map.97 = (f32[512,1024]{1,0:T(8,128)}, f32[8,128]{1,0:T(8,128)S(1)}) custom-call(f32[1024,512]{1,0:T(8,128)S(1)} %get-tuple-element.37.moment, f32[64,512]{1,0:T(8,128)S(1)} %get-tuple-element.38.picked, s32[16,4,512]{2,1,0:T(4,128)S(1)} %bitcast.9, bf16[256,256]{1,0:T(8,128)(2,1)S(1)} %copy-done.5, bf16[256,256]{1,0:T(8,128)(2,1)S(1)} %copy-done.6, ...), custom_call_target="tpu_custom_call" | custom-call | flops 805306368 | bytes 5242880 | tf_op jit(solution)/shard_map/pallas_call | solution.py:467
  99.1 3.3 %collective-permute-start.20 = (bf16[16,8,128]{2,1,0:T(8,128)(2,1)S(1)}, bf16[16,8,128]{2,1,0:T(8,128)(2,1)S(1)}, u32[]{:S(2)}, u32[]{:S(2)}) collective-permute-start(bf16[16,8,128]{2,1,0:T(8,128)(2,1)S(1)} %shard_map.98.half), channel_id=1, source_target_pairs={{0,8},{8,0},{16,24},{24,16},{32,40},{40,32},{48,56},{56,48},{64,72... | collective-permute-start | bytes 98312 | tf_op jit(solution)/shard_map/ppermute | solution.py:447
  107.5 3.0 %collective-permute-start.23 = (bf16[2,32,8,128]{3,2,1,0:T(8,128)(2,1)S(1)}, bf16[2,32,8,128]{3,2,1,0:T(8,128)(2,1)S(1)}, u32[]{:S(2)}, u32[]{:S(2)}) collective-permute-start(bf16[2,32,8,128]{3,2,1,0:T(8,128)(2,1)S(1)} %shard_map.99.tot), channel_id=1, source_target_pairs={{0,4},{1,5},{2,6},{3,7},{4,0},{5,1},{6,2},{7,3},{8,12},{9,13},{10,... | collective-permute-start | bytes 393224 | tf_op jit(solution)/shard_map/ppermute | solution.py:327
  112.1 3.3 %shard_map.100 = (f32[1024,256]{1,0:T(8,128)S(1)}, bf16[512,1024]{1,0:T(8,128)(2,1)}) custom-call(s32[2]{0:T(128)S(1)} %pad_add_fusion.where, bf16[256,4096]{1,0:T(8,128)(2,1)S(1)} %copy-done.1, bf16[320,1024]{1,0:T(8,128)(2,1)S(1)} %get-tuple-element.31.late.own, bf16[2,32,8,128]{3,2,1,0:T(8,128)(2,1)S(1)} %shard_map.99.tot, ...), custom_call_target="tpu_custom_call" | custom-call | flops 1610612736 | bytes 4194304 | tf_op jit(solution)/shard_map/pallas_call | solution.py:497
  117.1 3.3 %shard_map.101.before = f32[1024,256]{1,0:T(8,128)S(1)} custom-call(s32[2]{0:T(128)S(1)} %pad_add_fusion.where, bf16[256,4096]{1,0:T(8,128)(2,1)S(1)} %copy-done.1, bf16[256,4096]{1,0:T(8,128)(2,1)S(1)} %copy-done.1, bf16[320,1024]{1,0:T(8,128)(2,1)S(1)} %collective-permute-done.10.late_1.hi, bf16[320,1024]{1,0:T(8,128)(2,1)S(1)} %collective-permute-done.12.late_0.lo, ...), custom_call_target="tpu_custom_call" | custom-call | flops 2147483648 | bytes 5242880 | tf_op jit(solution)/shard_map/pallas_call | solution.py:511
  120.4 3.5 %shard_map.102 = bf16[256,1024]{1,0:T(8,128)(2,1)} custom-call(s32[2]{0:T(128)S(1)} %pad_add_fusion.where, bf16[256,4096]{1,0:T(8,128)(2,1)S(1)} %copy-done.1, bf16[320,1024]{1,0:T(8,128)(2,1)S(1)} %get-tuple-element.31.late.own, bf16[320,1024]{1,0:T(8,128)(2,1)S(1)} %collective-permute-done.10.late_1.hi, ...), custom_call_target="tpu_custom_call" | custom-call | flops 1610612736 | bytes 5242880 | tf_op jit(solution)/shard_map/pallas_call | solution.py:528
  (63 shorter events, 28.0 us)
Async XLA Ops:
  0.6 31.8 %collective-permute-start.8 = (bf16[512,1024]{1,0:T(8,128)(2,1)}, bf16[512,1024]{1,0:T(8,128)(2,1)S(1)}, u32[]{:S(2)}, u32[]{:S(2)}) collective-permute-start(bf16[512,1024]{1,0:T(8,128)(2,1)} %weight.1), channel_id=1, source_target_pairs={{0,1},{1,0},{2,3},{3,2},{4,5},{5,4},{6,7},{7,6},{8,9},{9,8},{10,11... | collective-permute-start | bytes 3145736 | tf_op jit(solution)/shard_map/ppermute | solution.py:330
  6.2 13.6 %collective-permute-start = (bf16[512,512]{1,0:T(8,128)(2,1)S(1)}, bf16[512,512]{1,0:T(8,128)(2,1)S(1)}, u32[]{:S(2)}, u32[]{:S(2)}) collective-permute-start(bf16[512,512]{1,0:T(8,128)(2,1)S(1)} %get-tuple-element.23.sent.a0), channel_id=1, source_target_pairs={{0,2},{1,3},{2,4},{3,5},{4,6},{5,7},{6,0},{7,1},{8,10},{9,11},{10,... | collective-permute-start | bytes 1572872 | tf_op jit(solution)/shard_map/ppermute | solution.py:321
  7.5 12.2 %collective-permute-start.1 = (bf16[512,512]{1,0:T(8,128)(2,1)S(1)}, bf16[512,512]{1,0:T(8,128)(2,1)S(1)}, u32[]{:S(2)}, u32[]{:S(2)}) collective-permute-start(bf16[512,512]{1,0:T(8,128)(2,1)S(1)} %get-tuple-element.24), channel_id=1, source_target_pairs={{0,6},{1,7},{2,0},{3,1},{4,2},{5,3},{6,4},{7,5},{8,14},{9,15},{10,... | collective-permute-start | bytes 1572872 | tf_op jit(solution)/shard_map/ppermute | solution.py:324
  9.1 23.3 %collective-permute-start.7 = (bf16[512,512]{1,0:T(8,128)(2,1)S(1)}, bf16[512,512]{1,0:T(8,128)(2,1)S(1)}, u32[]{:S(2)}, u32[]{:S(2)}) collective-permute-start(bf16[512,512]{1,0:T(8,128)(2,1)S(1)} %get-tuple-element.30), channel_id=1, source_target_pairs={{0,4},{1,5},{2,6},{3,7},{4,0},{5,1},{6,2},{7,3},{8,12},{9,13},{10,... | collective-permute-start | bytes 1572872 | tf_op jit(solution)/shard_map/ppermute | solution.py:327
  33.1 22.8 %collective-permute-start.9 = (bf16[576,512]{1,0:T(8,128)(2,1)S(1)}, bf16[576,512]{1,0:T(8,128)(2,1)S(1)}, u32[]{:S(2)}, u32[]{:S(2)}) collective-permute-start(bf16[576,512]{1,0:T(8,128)(2,1)S(1)} %shard_map.88), channel_id=1, source_target_pairs={{0,1},{1,0},{2,3},{3,2},{4,5},{5,4},{6,7},{7,6},{8,9},{9,8},{10,11... | collective-permute-start | bytes 1769480 | tf_op jit(solution)/shard_map/ppermute | solution.py:330
  33.5 6.9 %collective-permute-start.2 = (bf16[512,256]{1,0:T(8,128)(2,1)S(1)}, bf16[512,256]{1,0:T(8,128)(2,1)S(1)}, u32[]{:S(2)}, u32[]{:S(2)}) collective-permute-start(bf16[512,256]{1,0:T(8,128)(2,1)S(1)} %shard_map.86.turned.b0.c0), channel_id=1, source_target_pairs={{0,2},{1,3},{2,4},{3,5},{4,6},{5,7},{6,0},{7,1},{8,10},{9,11},{10,... | collective-permute-start | bytes 786440 | tf_op jit(solution)/shard_map/ppermute | solution.py:321
  34.0 7.4 %collective-permute-start.3 = (bf16[512,256]{1,0:T(8,128)(2,1)S(1)}, bf16[512,256]{1,0:T(8,128)(2,1)S(1)}, u32[]{:S(2)}, u32[]{:S(2)}) collective-permute-start(bf16[512,256]{1,0:T(8,128)(2,1)S(1)} %shard_map.86.turned.b0.c0), channel_id=1, source_target_pairs={{0,6},{1,7},{2,0},{3,1},{4,2},{5,3},{6,4},{7,5},{8,14},{9,15},{10,... | collective-permute-start | bytes 786440 | tf_op jit(solution)/shard_map/ppermute | solution.py:324
  36.2 10.6 %collective-permute-start.13 = (bf16[512,256]{1,0:T(8,128)(2,1)S(1)}, bf16[512,256]{1,0:T(8,128)(2,1)S(1)}, u32[]{:S(2)}, u32[]{:S(2)}) collective-permute-start(bf16[512,256]{1,0:T(8,128)(2,1)S(1)} %shard_map.86.turned.b0.c0), channel_id=1, source_target_pairs={{0,4},{1,5},{2,6},{3,7},{4,0},{5,1},{6,2},{7,3},{8,12},{9,13},{10,... | collective-permute-start | bytes 786440 | tf_op jit(solution)/shard_map/ppermute | solution.py:327
  42.1 11.2 %collective-permute-start.4 = (bf16[256,512]{1,0:T(8,128)(2,1)S(1)}, bf16[256,512]{1,0:T(8,128)(2,1)S(1)}, u32[]{:S(2)}, u32[]{:S(2)}) collective-permute-start(bf16[256,512]{1,0:T(8,128)(2,1)S(1)} %get-tuple-element.26), channel_id=1, source_target_pairs={{0,6},{1,7},{2,0},{3,1},{4,2},{5,3},{6,4},{7,5},{8,14},{9,15},{10,... | collective-permute-start | bytes 786440 | tf_op jit(solution)/shard_map/ppermute | solution.py:324
  46.1 7.2 %collective-permute-start.5 = (bf16[256,512]{1,0:T(8,128)(2,1)S(1)}, bf16[256,512]{1,0:T(8,128)(2,1)S(1)}, u32[]{:S(2)}, u32[]{:S(2)}) collective-permute-start(bf16[256,512]{1,0:T(8,128)(2,1)S(1)} %get-tuple-element.27), channel_id=1, source_target_pairs={{0,4},{1,5},{2,6},{3,7},{4,0},{5,1},{6,2},{7,3},{8,12},{9,13},{10,... | collective-permute-start | bytes 786440 | tf_op jit(solution)/shard_map/ppermute | solution.py:327
  46.1 9.8 %collective-permute-start.6 = (bf16[256,512]{1,0:T(8,128)(2,1)S(1)}, bf16[256,512]{1,0:T(8,128)(2,1)S(1)}, u32[]{:S(2)}, u32[]{:S(2)}) collective-permute-start(bf16[256,512]{1,0:T(8,128)(2,1)S(1)} %get-tuple-element.28), channel_id=1, source_target_pairs={{0,2},{1,3},{2,4},{3,5},{4,6},{5,7},{6,0},{7,1},{8,10},{9,11},{10,... | collective-permute-start | bytes 786440 | tf_op jit(solution)/shard_map/ppermute | solution.py:321
  47.5 17.0 %collective-permute-start.14 = (bf16[512,512]{1,0:T(8,128)(2,1)S(1)}, bf16[512,512]{1,0:T(8,128)(2,1)S(1)}, u32[]{:S(2)}, u32[]{:S(2)}) collective-permute-start(bf16[512,512]{1,0:T(8,128)(2,1)S(1)} %shard_map.91), channel_id=1, source_target_pairs={{0,1},{1,0},{2,3},{3,2},{4,5},{5,4},{6,7},{7,6},{8,9},{9,8},{10,11... | collective-permute-start | bytes 1572872 | tf_op jit(solution)/shard_map/ppermute | solution.py:330
  58.9 48.0 %collective-permute-start.10 = (bf16[320,1024]{1,0:T(8,128)(2,1)S(1)}, bf16[320,1024]{1,0:T(8,128)(2,1)S(1)}, u32[]{:S(2)}, u32[]{:S(2)}) collective-permute-start(bf16[320,1024]{1,0:T(8,128)(2,1)S(1)} %get-tuple-element.32), channel_id=1, source_target_pairs={{0,6},{1,7},{2,0},{3,1},{4,2},{5,3},{6,4},{7,5},{8,14},{9,15},{10,... | collective-permute-start | bytes 1966088 | tf_op jit(solution)/shard_map/ppermute | solution.py:324
  61.4 45.5 %collective-permute-start.11 = (bf16[320,1024]{1,0:T(8,128)(2,1)S(1)}, bf16[320,1024]{1,0:T(8,128)(2,1)S(1)}, u32[]{:S(2)}, u32[]{:S(2)}) collective-permute-start(bf16[320,1024]{1,0:T(8,128)(2,1)S(1)} %get-tuple-element.33), channel_id=1, source_target_pairs={{0,4},{1,5},{2,6},{3,7},{4,0},{5,1},{6,2},{7,3},{8,12},{9,13},{10,... | collective-permute-start | bytes 1966088 | tf_op jit(solution)/shard_map/ppermute | solution.py:327
  61.9 45.0 %collective-permute-start.12 = (bf16[320,1024]{1,0:T(8,128)(2,1)S(1)}, bf16[320,1024]{1,0:T(8,128)(2,1)S(1)}, u32[]{:S(2)}, u32[]{:S(2)}) collective-permute-start(bf16[320,1024]{1,0:T(8,128)(2,1)S(1)} %get-tuple-element.34), channel_id=1, source_target_pairs={{0,2},{1,3},{2,4},{3,5},{4,6},{5,7},{6,0},{7,1},{8,10},{9,11},{10,... | collective-permute-start | bytes 1966088 | tf_op jit(solution)/shard_map/ppermute | solution.py:321
  68.1 6.6 %collective-permute-start.15 = (f32[16,8,128]{2,1,0:T(8,128)S(1)}, f32[16,8,128]{2,1,0:T(8,128)S(1)}, u32[]{:S(2)}, u32[]{:S(2)}) collective-permute-start(f32[16,8,128]{2,1,0:T(8,128)S(1)} %get-tuple-element.36), channel_id=1, source_target_pairs={{0,8},{8,0},{16,24},{24,16},{32,40},{40,32},{48,56},{56,48},{64,72... | collective-permute-start | bytes 196616 | tf_op jit(solution)/shard_map/ppermute | solution.py:447
  74.7 5.0 %collective-permute-start.16 = (f32[16,8,128]{2,1,0:T(8,128)S(1)}, f32[16,8,128]{2,1,0:T(8,128)S(1)}, u32[]{:S(2)}, u32[]{:S(2)}) collective-permute-start(f32[16,8,128]{2,1,0:T(8,128)S(1)} %shard_map.93.a), channel_id=1, source_target_pairs={{0,16},{8,24},{16,0},{24,8},{32,48},{40,56},{48,32},{56,40},{64,80... | collective-permute-start | bytes 196616 | tf_op jit(solution)/shard_map/ppermute | solution.py:447
  79.7 3.7 %collective-permute-start.17 = (f32[16,8,128]{2,1,0:T(8,128)S(1)}, f32[16,8,128]{2,1,0:T(8,128)S(1)}, u32[]{:S(2)}, u32[]{:S(2)}) collective-permute-start(f32[16,8,128]{2,1,0:T(8,128)S(1)} %shard_map.94.a), channel_id=1, source_target_pairs={{0,32},{8,40},{16,48},{24,56},{32,0},{40,8},{48,16},{56,24},{64,96... | collective-permute-start | bytes 196616 | tf_op jit(solution)/shard_map/ppermute | solution.py:447
  83.4 5.0 %collective-permute-start.18 = (f32[16,8,128]{2,1,0:T(8,128)S(1)}, f32[16,8,128]{2,1,0:T(8,128)S(1)}, u32[]{:S(2)}, u32[]{:S(2)}) collective-permute-start(f32[16,8,128]{2,1,0:T(8,128)S(1)} %shard_map.95.a), channel_id=1, source_target_pairs={{0,64},{8,72},{16,80},{24,88},{32,96},{40,104},{48,112},{56,120},{... | collective-permute-start | bytes 196616 | tf_op jit(solution)/shard_map/ppermute | solution.py:447
  88.4 10.6 %collective-permute-start.19 = (f32[16,8,128]{2,1,0:T(8,128)S(1)}, f32[16,8,128]{2,1,0:T(8,128)S(1)}, u32[]{:S(2)}, u32[]{:S(2)}) collective-permute-start(f32[16,8,128]{2,1,0:T(8,128)S(1)} %shard_map.96.late.a), channel_id=1, source_target_pairs={{0,128},{8,136},{16,144},{24,152},{32,160},{40,168},{48,176},{56,1... | collective-permute-start | bytes 196616 | tf_op jit(solution)/shard_map/ppermute | solution.py:447
  99.1 4.5 %collective-permute-start.20 = (bf16[16,8,128]{2,1,0:T(8,128)(2,1)S(1)}, bf16[16,8,128]{2,1,0:T(8,128)(2,1)S(1)}, u32[]{:S(2)}, u32[]{:S(2)}) collective-permute-start(bf16[16,8,128]{2,1,0:T(8,128)(2,1)S(1)} %shard_map.98.half), channel_id=1, source_target_pairs={{0,8},{8,0},{16,24},{24,16},{32,40},{40,32},{48,56},{56,48},{64,72... | collective-permute-start | bytes 98312 | tf_op jit(solution)/shard_map/ppermute | solution.py:447
  107.5 12.9 %collective-permute-start.23 = (bf16[2,32,8,128]{3,2,1,0:T(8,128)(2,1)S(1)}, bf16[2,32,8,128]{3,2,1,0:T(8,128)(2,1)S(1)}, u32[]{:S(2)}, u32[]{:S(2)}) collective-permute-start(bf16[2,32,8,128]{3,2,1,0:T(8,128)(2,1)S(1)} %shard_map.99.tot), channel_id=1, source_target_pairs={{0,4},{1,5},{2,6},{3,7},{4,0},{5,1},{6,2},{7,3},{8,12},{9,13},{10,... | collective-permute-start | bytes 393224 | tf_op jit(solution)/shard_map/ppermute | solution.py:327
  110.5 5.5 %collective-permute-start.24 = (bf16[2,32,8,128]{3,2,1,0:T(8,128)(2,1)S(1)}, bf16[2,32,8,128]{3,2,1,0:T(8,128)(2,1)S(1)}, u32[]{:S(2)}, u32[]{:S(2)}) collective-permute-start(bf16[2,32,8,128]{3,2,1,0:T(8,128)(2,1)S(1)} %shard_map.99.tot), channel_id=1, source_target_pairs={{0,6},{1,7},{2,0},{3,1},{4,2},{5,3},{6,4},{7,5},{8,14},{9,15},{10,... | collective-permute-start | bytes 393224 | tf_op jit(solution)/shard_map/ppermute | solution.py:324
  112.1 5.0 %collective-permute-start.25 = (bf16[2,32,8,128]{3,2,1,0:T(8,128)(2,1)S(1)}, bf16[2,32,8,128]{3,2,1,0:T(8,128)(2,1)S(1)}, u32[]{:S(2)}, u32[]{:S(2)}) collective-permute-start(bf16[2,32,8,128]{3,2,1,0:T(8,128)(2,1)S(1)} %shard_map.99.tot), channel_id=1, source_target_pairs={{0,2},{1,3},{2,4},{3,5},{4,6},{5,7},{6,0},{7,1},{8,10},{9,11},{10,... | collective-permute-start | bytes 393224 | tf_op jit(solution)/shard_map/ppermute | solution.py:321
  (10 other events, 69.6 us)

commit v12 on v9

--- a/solution.py
+++ b/solution.py
@@ -174,7 +174,7 @@
 
 def add_two_kernel(a, b, *rest):
     out = rest[-1]
-    out[...] = (a[...] + b[...]).astype(out.dtype)
+    out[...] = (a[...].astype(jnp.float32) + b[...].astype(jnp.float32)).astype(out.dtype)
 
 
 def pair_kernel(where, half, core, across, corner, late_0, late_1, late_2, out):
@@ -462,7 +462,7 @@
 
     value = add(add_two_kernel, half_shape, value, from_hi)
     value = add(add_two_kernel, half_shape, value, partner(value, 4))
-    value = add(add_two_kernel, half_shape, value, partner(value, 8))
+    value = add(add_two_kernel, shape(TILES // 2, 8, LANES), value, partner(value, 8))
     last = partner(value, 16)
     new_momentum, mark = pl.pallas_call(
         residual_kernel,

time: 124 us -> 124 us (level)
  no operation moved by 1% of the time
where the time goes in v12:
time: 124 us
  starting transfers between devices  49.2 us (40%)
  waiting for transfers between devices  45.1 us (36%)
  Pallas kernels  26 us (21%)
  local copies, waits for them, and re-layouts  2.66 us (2%)
    ppermute x6, starting transfers between devices, partner(): return lax.ppermute(x, 'rep', [(i, i ^ bits) for i in range(REPS)])  23.5 us
    ppermute x5, waiting for transfers between devices, up(): return lax.ppermute(x, 'fsdp', [(i, (i + 2) % 8) for i in range(8)])  17 us
    ppermute x5, waiting for transfers between devices, across(): return lax.ppermute(x, 'fsdp', [(i, (i + 4) % 8) for i in range(8)])  12.5 us
    ppermute x5, starting transfers between devices, down(): return lax.ppermute(x, 'fsdp', [(i, (i + 6) % 8) for i in range(8)])  11.6 us
    ppermute x6, waiting for transfers between devices, partner(): return lax.ppermute(x, 'rep', [(i, i ^ bits) for i in range(REPS)])  6.98 us
    ppermute x5, waiting for transfers between devices, down(): return lax.ppermute(x, 'fsdp', [(i, (i + 6) % 8) for i in range(8)])  6.31 us
    ppermute x5, starting transfers between devices, across(): return lax.ppermute(x, 'fsdp', [(i, (i + 4) % 8) for i in range(8)])  5.08 us
    ppermute x4, starting transfers between devices, swap(): return lax.ppermute(x, 'fsdp', [(i, i ^ 1) for i in range(8)])  5.01 us
  transfers between devices with their start and end apart: 26, of which 14 were waited for; matrix products, arithmetic and copies ran while one was open for 0% of the time, Pallas kernels for 17%

profile of v12, /device:TPU:1, one launch (start us, length us, event | category | flops | bytes accessed | tf_op | source)
XLA Modules:
  0.0 123.9 jit_solution(8923488846765299262)
XLA Ops:
  0.6 2.1 %collective-permute-start.8 = (bf16[512,1024]{1,0:T(8,128)(2,1)}, bf16[512,1024]{1,0:T(8,128)(2,1)S(1)}, u32[]{:S(2)}, u32[]{:S(2)}) collective-permute-start(bf16[512,1024]{1,0:T(8,128)(2,1)} %weight.1), channel_id=1, source_target_pairs={{0,1},{1,0},{2,3},{3,2},{4,5},{5,4},{6,7},{7,6},{8,9},{9,8},{10,11... | collective-permute-start | bytes 3145736 | tf_op jit(solution)/shard_map/ppermute | solution.py:330
  10.6 9.2 %collective-permute-done.late_lo.lo.p3.a3 = bf16[512,512]{1,0:T(8,128)(2,1)S(1)} collective-permute-done((bf16[512,512]{1,0:T(8,128)(2,1)S(1)}, bf16[512,512]{1,0:T(8,128)(2,1)S(1)}, u32[]{:S(2)}, u32[]{:S(2)}) %collective-permute-start) | collective-permute-done | bytes 524320 | tf_op jit(solution)/shard_map/ppermute | solution.py:321
  19.9 12.5 %collective-permute-done.7.far.p2.a2 = bf16[512,512]{1,0:T(8,128)(2,1)S(1)} collective-permute-done((bf16[512,512]{1,0:T(8,128)(2,1)S(1)}, bf16[512,512]{1,0:T(8,128)(2,1)S(1)}, u32[]{:S(2)}, u32[]{:S(2)}) %collective-permute-start.7) | collective-permute-done | bytes 524320 | tf_op jit(solution)/shard_map/ppermute | solution.py:327
  34.0 2.1 %collective-permute-start.3 = (bf16[512,256]{1,0:T(8,128)(2,1)S(1)}, bf16[512,256]{1,0:T(8,128)(2,1)S(1)}, u32[]{:S(2)}, u32[]{:S(2)}) collective-permute-start(bf16[512,256]{1,0:T(8,128)(2,1)S(1)} %shard_map.86.turned.b0.c0), channel_id=1, source_target_pairs={{0,6},{1,7},{2,0},{3,1},{4,2},{5,3},{6,4},{7,5},{8,14},{9,15},{10,... | collective-permute-start | bytes 786440 | tf_op jit(solution)/shard_map/ppermute | solution.py:324
  36.2 4.2 %collective-permute-done.2.late_lo.b3.c3 = bf16[512,256]{1,0:T(8,128)(2,1)S(1)} collective-permute-done((bf16[512,256]{1,0:T(8,128)(2,1)S(1)}, bf16[512,256]{1,0:T(8,128)(2,1)S(1)}, u32[]{:S(2)}, u32[]{:S(2)}) %collective-permute-start.2) | collective-permute-done | bytes 262176 | tf_op jit(solution)/shard_map/ppermute | solution.py:321
  42.1 4.0 %collective-permute-start.4 = (bf16[256,512]{1,0:T(8,128)(2,1)S(1)}, bf16[256,512]{1,0:T(8,128)(2,1)S(1)}, u32[]{:S(2)}, u32[]{:S(2)}) collective-permute-start(bf16[256,512]{1,0:T(8,128)(2,1)S(1)} %get-tuple-element.26), channel_id=1, source_target_pairs={{0,6},{1,7},{2,0},{3,1},{4,2},{5,3},{6,4},{7,5},{8,14},{9,15},{10,... | collective-permute-start | bytes 786440 | tf_op jit(solution)/shard_map/ppermute | solution.py:324
  48.8 4.5 %collective-permute-done.4.o1.t1 = bf16[256,512]{1,0:T(8,128)(2,1)S(1)} collective-permute-done((bf16[256,512]{1,0:T(8,128)(2,1)S(1)}, bf16[256,512]{1,0:T(8,128)(2,1)S(1)}, u32[]{:S(2)}, u32[]{:S(2)}) %collective-permute-start.4) | collective-permute-done | bytes 262176 | tf_op jit(solution)/shard_map/ppermute | solution.py:324
  53.3 2.6 %collective-permute-done.6.o3.t3 = bf16[256,512]{1,0:T(8,128)(2,1)S(1)} collective-permute-done((bf16[256,512]{1,0:T(8,128)(2,1)S(1)}, bf16[256,512]{1,0:T(8,128)(2,1)S(1)}, u32[]{:S(2)}, u32[]{:S(2)}) %collective-permute-start.6) | collective-permute-done | bytes 262176 | tf_op jit(solution)/shard_map/ppermute | solution.py:321
  56.0 3.0 %shard_map.89 = (bf16[320,1024]{1,0:T(8,128)(2,1)S(1)}, bf16[320,1024]{1,0:T(8,128)(2,1)S(1)}, bf16[320,1024]{1,0:T(8,128)(2,1)S(1)}, bf16[320,1024]{1,0:T(8,128)(2,1)S(1)}) custom-call(s32[2]{0:T(128)S(1)} %pad_add_fusion.where, bf16[256,512]{1,0:T(8,128)(2,1)S(1)} %get-tuple-element.25.o0.t0, bf16[256,512]{1,0:T(8,128)(2,1)S(1)} %collective-permute-done.4.o1.t1, ...), custom_call_target="tpu_custom_call" | custom-call | flops 2147483648 | bytes 7340032 | tf_op jit(solution)/shard_map/pallas_call | solution.py:414
  58.9 2.5 %collective-permute-start.10 = (bf16[320,1024]{1,0:T(8,128)(2,1)S(1)}, bf16[320,1024]{1,0:T(8,128)(2,1)S(1)}, u32[]{:S(2)}, u32[]{:S(2)}) collective-permute-start(bf16[320,1024]{1,0:T(8,128)(2,1)S(1)} %get-tuple-element.32), channel_id=1, source_target_pairs={{0,6},{1,7},{2,0},{3,1},{4,2},{5,3},{6,4},{7,5},{8,14},{9,15},{10,... | collective-permute-start | bytes 1966088 | tf_op jit(solution)/shard_map/ppermute | solution.py:324
  62.3 2.3 %shard_map.90.pre = f32[1024,512]{1,0:T(8,128)S(1)} custom-call(bf16[512,512]{1,0:T(8,128)(2,1)S(1)} %get-tuple-element.23.sent.a0, bf16[512,512]{1,0:T(8,128)(2,1)S(1)} %collective-permute-done.1.late_hi.hi.p1.a1, bf16[512,512]{1,0:T(8,128)(2,1)S(1)} %collective-permute-done.7.far.p2.a2, bf16[512,512]{1,0:T(8,128)(2,1)S(1)} %collective-permute-done.late_lo.lo.p3.a3, ...), custom_call_target="tpu_custom_call" | custom-call | flops 1073741824 | bytes 7340032 | tf_op jit(solution)/shard_map/pallas_call | solution.py:401
  64.6 3.5 %shard_map.92 = (f32[1024,512]{1,0:T(8,128)S(1)}, f32[64,512]{1,0:T(8,128)S(1)}, f32[16,8,128]{2,1,0:T(8,128)S(1)}, f32[16,8,128]{2,1,0:T(8,128)S(1)}) custom-call(s32[2]{0:T(128)S(1)} %pad_add_fusion.where, f32[1024,512]{1,0:T(8,128)S(1)} %shard_map.90.pre, bf16[576,512]{1,0:T(8,128)(2,1)S(1)} %collective-permute-done.9.got_a, ...), custom_call_target="tpu_custom_call" | custom-call | flops 805306368 | bytes 6291456 | tf_op jit(solution)/shard_map/pallas_call | solution.py:433
  68.1 5.7 %collective-permute-start.15 = (f32[16,8,128]{2,1,0:T(8,128)S(1)}, f32[16,8,128]{2,1,0:T(8,128)S(1)}, u32[]{:S(2)}, u32[]{:S(2)}) collective-permute-start(f32[16,8,128]{2,1,0:T(8,128)S(1)} %get-tuple-element.36), channel_id=1, source_target_pairs={{0,8},{8,0},{16,24},{24,16},{32,40},{40,32},{48,56},{56,48},{64,72... | collective-permute-start | bytes 196616 | tf_op jit(solution)/shard_map/ppermute | solution.py:447
  74.7 2.8 %collective-permute-start.16 = (f32[16,8,128]{2,1,0:T(8,128)S(1)}, f32[16,8,128]{2,1,0:T(8,128)S(1)}, u32[]{:S(2)}, u32[]{:S(2)}) collective-permute-start(f32[16,8,128]{2,1,0:T(8,128)S(1)} %shard_map.93.a), channel_id=1, source_target_pairs={{0,16},{8,24},{16,0},{24,8},{32,48},{40,56},{48,32},{56,40},{64,80... | collective-permute-start | bytes 196616 | tf_op jit(solution)/shard_map/ppermute | solution.py:447
  77.5 2.2 %collective-permute-done.16.b = f32[16,8,128]{2,1,0:T(8,128)S(1)} collective-permute-done((f32[16,8,128]{2,1,0:T(8,128)S(1)}, f32[16,8,128]{2,1,0:T(8,128)S(1)}, u32[]{:S(2)}, u32[]{:S(2)}) %collective-permute-start.16) | collective-permute-done | bytes 65568 | tf_op jit(solution)/shard_map/ppermute | solution.py:447
  81.4 2.0 %collective-permute-done.17.b = f32[16,8,128]{2,1,0:T(8,128)S(1)} collective-permute-done((f32[16,8,128]{2,1,0:T(8,128)S(1)}, f32[16,8,128]{2,1,0:T(8,128)S(1)}, u32[]{:S(2)}, u32[]{:S(2)}) %collective-permute-start.17) | collective-permute-done | bytes 65568 | tf_op jit(solution)/shard_map/ppermute | solution.py:447
  83.4 3.1 %collective-permute-start.18 = (f32[16,8,128]{2,1,0:T(8,128)S(1)}, f32[16,8,128]{2,1,0:T(8,128)S(1)}, u32[]{:S(2)}, u32[]{:S(2)}) collective-permute-start(f32[16,8,128]{2,1,0:T(8,128)S(1)} %shard_map.95.a), channel_id=1, source_target_pairs={{0,64},{8,72},{16,80},{24,88},{32,96},{40,104},{48,112},{56,120},{... | collective-permute-start | bytes 196616 | tf_op jit(solution)/shard_map/ppermute | solution.py:447
  88.4 6.9 %collective-permute-start.19 = (bf16[16,8,128]{2,1,0:T(8,128)(2,1)S(1)}, bf16[16,8,128]{2,1,0:T(8,128)(2,1)S(1)}, u32[]{:S(2)}, u32[]{:S(2)}) collective-permute-start(bf16[16,8,128]{2,1,0:T(8,128)(2,1)S(1)} %shard_map.96.late.a), channel_id=1, source_target_pairs={{0,128},{8,136},{16,144},{24,152},{32,160},{40,168},{48,176},{56,1... | collective-permute-start | bytes 98312 | tf_op jit(solution)/shard_map/ppermute | solution.py:447
  95.3 3.7 %shard_map.97 = (f32[512,1024]{1,0:T(8,128)}, f32[8,128]{1,0:T(8,128)S(1)}) custom-call(f32[1024,512]{1,0:T(8,128)S(1)} %get-tuple-element.37.moment, f32[64,512]{1,0:T(8,128)S(1)} %get-tuple-element.38.picked, s32[16,4,512]{2,1,0:T(4,128)S(1)} %bitcast.9, bf16[256,256]{1,0:T(8,128)(2,1)S(1)} %copy-done.5, bf16[256,256]{1,0:T(8,128)(2,1)S(1)} %copy-done.6, ...), custom_call_target="tpu_custom_call" | custom-call | flops 805306368 | bytes 5242880 | tf_op jit(solution)/shard_map/pallas_call | solution.py:467
  99.1 3.3 %collective-permute-start.20 = (bf16[16,8,128]{2,1,0:T(8,128)(2,1)S(1)}, bf16[16,8,128]{2,1,0:T(8,128)(2,1)S(1)}, u32[]{:S(2)}, u32[]{:S(2)}) collective-permute-start(bf16[16,8,128]{2,1,0:T(8,128)(2,1)S(1)} %shard_map.98.half), channel_id=1, source_target_pairs={{0,8},{8,0},{16,24},{24,16},{32,40},{40,32},{48,56},{56,48},{64,72... | collective-permute-start | bytes 98312 | tf_op jit(solution)/shard_map/ppermute | solution.py:447
  107.5 3.0 %collective-permute-start.23 = (bf16[2,32,8,128]{3,2,1,0:T(8,128)(2,1)S(1)}, bf16[2,32,8,128]{3,2,1,0:T(8,128)(2,1)S(1)}, u32[]{:S(2)}, u32[]{:S(2)}) collective-permute-start(bf16[2,32,8,128]{3,2,1,0:T(8,128)(2,1)S(1)} %shard_map.99.tot), channel_id=1, source_target_pairs={{0,4},{1,5},{2,6},{3,7},{4,0},{5,1},{6,2},{7,3},{8,12},{9,13},{10,... | collective-permute-start | bytes 393224 | tf_op jit(solution)/shard_map/ppermute | solution.py:327
  112.1 3.3 %shard_map.100 = (f32[1024,256]{1,0:T(8,128)S(1)}, bf16[512,1024]{1,0:T(8,128)(2,1)}) custom-call(s32[2]{0:T(128)S(1)} %pad_add_fusion.where, bf16[256,4096]{1,0:T(8,128)(2,1)S(1)} %copy-done.1, bf16[320,1024]{1,0:T(8,128)(2,1)S(1)} %get-tuple-element.31.late.own, bf16[2,32,8,128]{3,2,1,0:T(8,128)(2,1)S(1)} %shard_map.99.tot, ...), custom_call_target="tpu_custom_call" | custom-call | flops 1610612736 | bytes 4194304 | tf_op jit(solution)/shard_map/pallas_call | solution.py:497
  117.1 3.3 %shard_map.101.before = f32[1024,256]{1,0:T(8,128)S(1)} custom-call(s32[2]{0:T(128)S(1)} %pad_add_fusion.where, bf16[256,4096]{1,0:T(8,128)(2,1)S(1)} %copy-done.1, bf16[256,4096]{1,0:T(8,128)(2,1)S(1)} %copy-done.1, bf16[320,1024]{1,0:T(8,128)(2,1)S(1)} %collective-permute-done.10.late_1.hi, bf16[320,1024]{1,0:T(8,128)(2,1)S(1)} %collective-permute-done.12.late_0.lo, ...), custom_call_target="tpu_custom_call" | custom-call | flops 2147483648 | bytes 5242880 | tf_op jit(solution)/shard_map/pallas_call | solution.py:511
  120.4 3.5 %shard_map.102 = bf16[256,1024]{1,0:T(8,128)(2,1)} custom-call(s32[2]{0:T(128)S(1)} %pad_add_fusion.where, bf16[256,4096]{1,0:T(8,128)(2,1)S(1)} %copy-done.1, bf16[320,1024]{1,0:T(8,128)(2,1)S(1)} %get-tuple-element.31.late.own, bf16[320,1024]{1,0:T(8,128)(2,1)S(1)} %collective-permute-done.10.late_1.hi, ...), custom_call_target="tpu_custom_call" | custom-call | flops 1610612736 | bytes 5242880 | tf_op jit(solution)/shard_map/pallas_call | solution.py:528
  (63 shorter events, 28.0 us)
Async XLA Ops:
  0.6 31.8 %collective-permute-start.8 = (bf16[512,1024]{1,0:T(8,128)(2,1)}, bf16[512,1024]{1,0:T(8,128)(2,1)S(1)}, u32[]{:S(2)}, u32[]{:S(2)}) collective-permute-start(bf16[512,1024]{1,0:T(8,128)(2,1)} %weight.1), channel_id=1, source_target_pairs={{0,1},{1,0},{2,3},{3,2},{4,5},{5,4},{6,7},{7,6},{8,9},{9,8},{10,11... | collective-permute-start | bytes 3145736 | tf_op jit(solution)/shard_map/ppermute | solution.py:330
  6.2 13.6 %collective-permute-start = (bf16[512,512]{1,0:T(8,128)(2,1)S(1)}, bf16[512,512]{1,0:T(8,128)(2,1)S(1)}, u32[]{:S(2)}, u32[]{:S(2)}) collective-permute-start(bf16[512,512]{1,0:T(8,128)(2,1)S(1)} %get-tuple-element.23.sent.a0), channel_id=1, source_target_pairs={{0,2},{1,3},{2,4},{3,5},{4,6},{5,7},{6,0},{7,1},{8,10},{9,11},{10,... | collective-permute-start | bytes 1572872 | tf_op jit(solution)/shard_map/ppermute | solution.py:321
  7.5 12.2 %collective-permute-start.1 = (bf16[512,512]{1,0:T(8,128)(2,1)S(1)}, bf16[512,512]{1,0:T(8,128)(2,1)S(1)}, u32[]{:S(2)}, u32[]{:S(2)}) collective-permute-start(bf16[512,512]{1,0:T(8,128)(2,1)S(1)} %get-tuple-element.24), channel_id=1, source_target_pairs={{0,6},{1,7},{2,0},{3,1},{4,2},{5,3},{6,4},{7,5},{8,14},{9,15},{10,... | collective-permute-start | bytes 1572872 | tf_op jit(solution)/shard_map/ppermute | solution.py:324
  9.1 23.3 %collective-permute-start.7 = (bf16[512,512]{1,0:T(8,128)(2,1)S(1)}, bf16[512,512]{1,0:T(8,128)(2,1)S(1)}, u32[]{:S(2)}, u32[]{:S(2)}) collective-permute-start(bf16[512,512]{1,0:T(8,128)(2,1)S(1)} %get-tuple-element.30), channel_id=1, source_target_pairs={{0,4},{1,5},{2,6},{3,7},{4,0},{5,1},{6,2},{7,3},{8,12},{9,13},{10,... | collective-permute-start | bytes 1572872 | tf_op jit(solution)/shard_map/ppermute | solution.py:327
  33.1 22.8 %collective-permute-start.9 = (bf16[576,512]{1,0:T(8,128)(2,1)S(1)}, bf16[576,512]{1,0:T(8,128)(2,1)S(1)}, u32[]{:S(2)}, u32[]{:S(2)}) collective-permute-start(bf16[576,512]{1,0:T(8,128)(2,1)S(1)} %shard_map.88), channel_id=1, source_target_pairs={{0,1},{1,0},{2,3},{3,2},{4,5},{5,4},{6,7},{7,6},{8,9},{9,8},{10,11... | collective-permute-start | bytes 1769480 | tf_op jit(solution)/shard_map/ppermute | solution.py:330
  33.5 6.9 %collective-permute-start.2 = (bf16[512,256]{1,0:T(8,128)(2,1)S(1)}, bf16[512,256]{1,0:T(8,128)(2,1)S(1)}, u32[]{:S(2)}, u32[]{:S(2)}) collective-permute-start(bf16[512,256]{1,0:T(8,128)(2,1)S(1)} %shard_map.86.turned.b0.c0), channel_id=1, source_target_pairs={{0,2},{1,3},{2,4},{3,5},{4,6},{5,7},{6,0},{7,1},{8,10},{9,11},{10,... | collective-permute-start | bytes 786440 | tf_op jit(solution)/shard_map/ppermute | solution.py:321
  34.0 7.4 %collective-permute-start.3 = (bf16[512,256]{1,0:T(8,128)(2,1)S(1)}, bf16[512,256]{1,0:T(8,128)(2,1)S(1)}, u32[]{:S(2)}, u32[]{:S(2)}) collective-permute-start(bf16[512,256]{1,0:T(8,128)(2,1)S(1)} %shard_map.86.turned.b0.c0), channel_id=1, source_target_pairs={{0,6},{1,7},{2,0},{3,1},{4,2},{5,3},{6,4},{7,5},{8,14},{9,15},{10,... | collective-permute-start | bytes 786440 | tf_op jit(solution)/shard_map/ppermute | solution.py:324
  36.2 10.6 %collective-permute-start.13 = (bf16[512,256]{1,0:T(8,128)(2,1)S(1)}, bf16[512,256]{1,0:T(8,128)(2,1)S(1)}, u32[]{:S(2)}, u32[]{:S(2)}) collective-permute-start(bf16[512,256]{1,0:T(8,128)(2,1)S(1)} %shard_map.86.turned.b0.c0), channel_id=1, source_target_pairs={{0,4},{1,5},{2,6},{3,7},{4,0},{5,1},{6,2},{7,3},{8,12},{9,13},{10,... | collective-permute-start | bytes 786440 | tf_op jit(solution)/shard_map/ppermute | solution.py:327
  42.1 11.2 %collective-permute-start.4 = (bf16[256,512]{1,0:T(8,128)(2,1)S(1)}, bf16[256,512]{1,0:T(8,128)(2,1)S(1)}, u32[]{:S(2)}, u32[]{:S(2)}) collective-permute-start(bf16[256,512]{1,0:T(8,128)(2,1)S(1)} %get-tuple-element.26), channel_id=1, source_target_pairs={{0,6},{1,7},{2,0},{3,1},{4,2},{5,3},{6,4},{7,5},{8,14},{9,15},{10,... | collective-permute-start | bytes 786440 | tf_op jit(solution)/shard_map/ppermute | solution.py:324
  46.1 7.2 %collective-permute-start.5 = (bf16[256,512]{1,0:T(8,128)(2,1)S(1)}, bf16[256,512]{1,0:T(8,128)(2,1)S(1)}, u32[]{:S(2)}, u32[]{:S(2)}) collective-permute-start(bf16[256,512]{1,0:T(8,128)(2,1)S(1)} %get-tuple-element.27), channel_id=1, source_target_pairs={{0,4},{1,5},{2,6},{3,7},{4,0},{5,1},{6,2},{7,3},{8,12},{9,13},{10,... | collective-permute-start | bytes 786440 | tf_op jit(solution)/shard_map/ppermute | solution.py:327
  46.1 9.8 %collective-permute-start.6 = (bf16[256,512]{1,0:T(8,128)(2,1)S(1)}, bf16[256,512]{1,0:T(8,128)(2,1)S(1)}, u32[]{:S(2)}, u32[]{:S(2)}) collective-permute-start(bf16[256,512]{1,0:T(8,128)(2,1)S(1)} %get-tuple-element.28), channel_id=1, source_target_pairs={{0,2},{1,3},{2,4},{3,5},{4,6},{5,7},{6,0},{7,1},{8,10},{9,11},{10,... | collective-permute-start | bytes 786440 | tf_op jit(solution)/shard_map/ppermute | solution.py:321
  47.5 17.0 %collective-permute-start.14 = (bf16[512,512]{1,0:T(8,128)(2,1)S(1)}, bf16[512,512]{1,0:T(8,128)(2,1)S(1)}, u32[]{:S(2)}, u32[]{:S(2)}) collective-permute-start(bf16[512,512]{1,0:T(8,128)(2,1)S(1)} %shard_map.91), channel_id=1, source_target_pairs={{0,1},{1,0},{2,3},{3,2},{4,5},{5,4},{6,7},{7,6},{8,9},{9,8},{10,11... | collective-permute-start | bytes 1572872 | tf_op jit(solution)/shard_map/ppermute | solution.py:330
  58.9 48.0 %collective-permute-start.10 = (bf16[320,1024]{1,0:T(8,128)(2,1)S(1)}, bf16[320,1024]{1,0:T(8,128)(2,1)S(1)}, u32[]{:S(2)}, u32[]{:S(2)}) collective-permute-start(bf16[320,1024]{1,0:T(8,128)(2,1)S(1)} %get-tuple-element.32), channel_id=1, source_target_pairs={{0,6},{1,7},{2,0},{3,1},{4,2},{5,3},{6,4},{7,5},{8,14},{9,15},{10,... | collective-permute-start | bytes 1966088 | tf_op jit(solution)/shard_map/ppermute | solution.py:324
  61.4 45.5 %collective-permute-start.11 = (bf16[320,1024]{1,0:T(8,128)(2,1)S(1)}, bf16[320,1024]{1,0:T(8,128)(2,1)S(1)}, u32[]{:S(2)}, u32[]{:S(2)}) collective-permute-start(bf16[320,1024]{1,0:T(8,128)(2,1)S(1)} %get-tuple-element.33), channel_id=1, source_target_pairs={{0,4},{1,5},{2,6},{3,7},{4,0},{5,1},{6,2},{7,3},{8,12},{9,13},{10,... | collective-permute-start | bytes 1966088 | tf_op jit(solution)/shard_map/ppermute | solution.py:327
  61.9 45.0 %collective-permute-start.12 = (bf16[320,1024]{1,0:T(8,128)(2,1)S(1)}, bf16[320,1024]{1,0:T(8,128)(2,1)S(1)}, u32[]{:S(2)}, u32[]{:S(2)}) collective-permute-start(bf16[320,1024]{1,0:T(8,128)(2,1)S(1)} %get-tuple-element.34), channel_id=1, source_target_pairs={{0,2},{1,3},{2,4},{3,5},{4,6},{5,7},{6,0},{7,1},{8,10},{9,11},{10,... | collective-permute-start | bytes 1966088 | tf_op jit(solution)/shard_map/ppermute | solution.py:321
  68.1 6.6 %collective-permute-start.15 = (f32[16,8,128]{2,1,0:T(8,128)S(1)}, f32[16,8,128]{2,1,0:T(8,128)S(1)}, u32[]{:S(2)}, u32[]{:S(2)}) collective-permute-start(f32[16,8,128]{2,1,0:T(8,128)S(1)} %get-tuple-element.36), channel_id=1, source_target_pairs={{0,8},{8,0},{16,24},{24,16},{32,40},{40,32},{48,56},{56,48},{64,72... | collective-permute-start | bytes 196616 | tf_op jit(solution)/shard_map/ppermute | solution.py:447
  74.7 5.0 %collective-permute-start.16 = (f32[16,8,128]{2,1,0:T(8,128)S(1)}, f32[16,8,128]{2,1,0:T(8,128)S(1)}, u32[]{:S(2)}, u32[]{:S(2)}) collective-permute-start(f32[16,8,128]{2,1,0:T(8,128)S(1)} %shard_map.93.a), channel_id=1, source_target_pairs={{0,16},{8,24},{16,0},{24,8},{32,48},{40,56},{48,32},{56,40},{64,80... | collective-permute-start | bytes 196616 | tf_op jit(solution)/shard_map/ppermute | solution.py:447
  79.7 3.7 %collective-permute-start.17 = (f32[16,8,128]{2,1,0:T(8,128)S(1)}, f32[16,8,128]{2,1,0:T(8,128)S(1)}, u32[]{:S(2)}, u32[]{:S(2)}) collective-permute-start(f32[16,8,128]{2,1,0:T(8,128)S(1)} %shard_map.94.a), channel_id=1, source_target_pairs={{0,32},{8,40},{16,48},{24,56},{32,0},{40,8},{48,16},{56,24},{64,96... | collective-permute-start | bytes 196616 | tf_op jit(solution)/shard_map/ppermute | solution.py:447
  83.4 5.0 %collective-permute-start.18 = (f32[16,8,128]{2,1,0:T(8,128)S(1)}, f32[16,8,128]{2,1,0:T(8,128)S(1)}, u32[]{:S(2)}, u32[]{:S(2)}) collective-permute-start(f32[16,8,128]{2,1,0:T(8,128)S(1)} %shard_map.95.a), channel_id=1, source_target_pairs={{0,64},{8,72},{16,80},{24,88},{32,96},{40,104},{48,112},{56,120},{... | collective-permute-start | bytes 196616 | tf_op jit(solution)/shard_map/ppermute | solution.py:447
  88.4 10.6 %collective-permute-start.19 = (bf16[16,8,128]{2,1,0:T(8,128)(2,1)S(1)}, bf16[16,8,128]{2,1,0:T(8,128)(2,1)S(1)}, u32[]{:S(2)}, u32[]{:S(2)}) collective-permute-start(bf16[16,8,128]{2,1,0:T(8,128)(2,1)S(1)} %shard_map.96.late.a), channel_id=1, source_target_pairs={{0,128},{8,136},{16,144},{24,152},{32,160},{40,168},{48,176},{56,1... | collective-permute-start | bytes 98312 | tf_op jit(solution)/shard_map/ppermute | solution.py:447
  99.1 4.5 %collective-permute-start.20 = (bf16[16,8,128]{2,1,0:T(8,128)(2,1)S(1)}, bf16[16,8,128]{2,1,0:T(8,128)(2,1)S(1)}, u32[]{:S(2)}, u32[]{:S(2)}) collective-permute-start(bf16[16,8,128]{2,1,0:T(8,128)(2,1)S(1)} %shard_map.98.half), channel_id=1, source_target_pairs={{0,8},{8,0},{16,24},{24,16},{32,40},{40,32},{48,56},{56,48},{64,72... | collective-permute-start | bytes 98312 | tf_op jit(solution)/shard_map/ppermute | solution.py:447
  107.5 12.9 %collective-permute-start.23 = (bf16[2,32,8,128]{3,2,1,0:T(8,128)(2,1)S(1)}, bf16[2,32,8,128]{3,2,1,0:T(8,128)(2,1)S(1)}, u32[]{:S(2)}, u32[]{:S(2)}) collective-permute-start(bf16[2,32,8,128]{3,2,1,0:T(8,128)(2,1)S(1)} %shard_map.99.tot), channel_id=1, source_target_pairs={{0,4},{1,5},{2,6},{3,7},{4,0},{5,1},{6,2},{7,3},{8,12},{9,13},{10,... | collective-permute-start | bytes 393224 | tf_op jit(solution)/shard_map/ppermute | solution.py:327
  110.5 5.5 %collective-permute-start.24 = (bf16[2,32,8,128]{3,2,1,0:T(8,128)(2,1)S(1)}, bf16[2,32,8,128]{3,2,1,0:T(8,128)(2,1)S(1)}, u32[]{:S(2)}, u32[]{:S(2)}) collective-permute-start(bf16[2,32,8,128]{3,2,1,0:T(8,128)(2,1)S(1)} %shard_map.99.tot), channel_id=1, source_target_pairs={{0,6},{1,7},{2,0},{3,1},{4,2},{5,3},{6,4},{7,5},{8,14},{9,15},{10,... | collective-permute-start | bytes 393224 | tf_op jit(solution)/shard_map/ppermute | solution.py:324
  112.1 5.0 %collective-permute-start.25 = (bf16[2,32,8,128]{3,2,1,0:T(8,128)(2,1)S(1)}, bf16[2,32,8,128]{3,2,1,0:T(8,128)(2,1)S(1)}, u32[]{:S(2)}, u32[]{:S(2)}) collective-permute-start(bf16[2,32,8,128]{3,2,1,0:T(8,128)(2,1)S(1)} %shard_map.99.tot), channel_id=1, source_target_pairs={{0,2},{1,3},{2,4},{3,5},{4,6},{5,7},{6,0},{7,1},{8,10},{9,11},{10,... | collective-permute-start | bytes 393224 | tf_op jit(solution)/shard_map/ppermute | solution.py:321
  (10 other events, 69.6 us)
